TPU v7x, 256 devices: a whole 4x4x8 slice. The times are simulated.
256 devices in a mesh: dp: 4 (over z_lo, core), row: 16 (over x, y), col: 4 (over z_hi).
Axes of the slice: x: 4, y: 4, z: 8 (z_hi: 4, z_lo: 2; z = z_hi * 2 + z_lo), core: 2. Of those that a mesh axis runs over, the one named last changes fastest.
Arguments:
- activations: bfloat16 [8192, 8192], P('dp', 'row'), may hold values from -24 to 24
- out_grads: bfloat16 [8192, 16384], P(('dp', 'row'), 'col'), may hold values from -24 to 24
- weights: float32 [16384, 8192], P(('col', 'dp'), 'row'), may hold values from -0.0625 to 0.0625
- momentum: bfloat16 [16384, 8192], P(('col', 'dp'), 'row'), may hold values from -3 to 3
- scores: float32 [16384, 8192], P(('col', 'dp'), 'row'), may hold values from -6 to 6
- row_moment: float32 [16384], P(('col', 'dp')), may hold values from 0.05 to 90
- col_moment: float32 [8192], P('row'), may hold values from 0.05 to 90
Outputs:
- weights_new: float32 [16384, 8192], P(('col', 'dp'), 'row')
- momentum_new: bfloat16 [16384, 8192], P(('col', 'dp'), 'row')
- scores_new: float32 [16384, 8192], P(('col', 'dp'), 'row')
- row_moment_new: float32 [16384], P(('col', 'dp'))
- col_moment_new: float32 [8192], P('row')
All inputs are finite; a program needn't handle non-finite values.
Results may differ from a plain program's by a relative error of at most 0.004.
Values may be sent and summed in bfloat16 or wider, within the bound.
No kernel may reach another device: no remote copies, remote signals or barrier semaphores. Data moves between devices by JAX's collectives and lax.ppermute only.
A program may use at most 128 MiB of HBM per device.

v0:
```python
import math

import jax
import jax.numpy as jnp
from jax import lax
from jax.sharding import Mesh, PartitionSpec as P

D = 8192
FF = 16384
AXES = ("core", "x", "y")
STEPS = (0, -1, 1, 2)


def ring_pairs(phase, step):
    pairs = []
    for core in range(2):
        for x in range(4):
            for y in range(4):
                if core == phase:
                    to = (x + step) % 4 * 4 + y
                else:
                    to = x * 4 + (y + step) % 4
                pairs.append((core * 16 + x * 4 + y, core * 16 + to))
    return pairs


def shift(array, phase, step):
    return lax.ppermute(array, AXES, ring_pairs(phase, step))


def along_z(array, step):
    place = lambda z: z % 2 * 4 + z // 2
    return lax.ppermute(array, ("zl", "zh"), [(place(z), place((z + step) % 8)) for z in range(8)])


def swap(array, axis):
    return lax.ppermute(array, axis, [(0, 1), (1, 0)])


def ring_start(block, phase):
    return [block, shift(block, phase, 1), shift(block, phase, -1)]


def ring_end(blocks, phase):
    block, below, above = blocks
    half = block.shape[0] // 2
    return [*blocks, shift(below[:half], phase, 1), shift(above[half:], phase, -1)]


def after(blocks, *others):
    return lax.optimization_barrier((*blocks, *others))[: len(blocks)]


def product(grad_rows, act_rows):
    return lax.dot_general(
        grad_rows, act_rows, (((0,), (0,)), ((), ())), preferred_element_type=jnp.float32
    )


def token_sum(groups, acts):
    own, below, above, far_low, far_high = groups
    half = far_low.shape[0]
    total = product(own, acts[0]) + product(below, acts[1]) + product(above, acts[2])
    return total + product(far_low, acts[3][:half]) + product(far_high, acts[3][half:])


def total_over(vector, axes):
    spread = jnp.broadcast_to(vector[None], (16, vector.shape[0]))
    return jnp.sum(lax.all_to_all(spread, axes, 0, 0, tiled=True), axis=0)


def local(activations, out_grads, weights, momentum, scores, row_moment, col_moment):
    token_scale = 1.0 / math.sqrt(activations.shape[0] * 4)
    core, low = lax.axis_index("core"), lax.axis_index("zl")
    x, y = lax.axis_index("x"), lax.axis_index("y")
    rows = FF // 16

    def units(a, b):
        return lax.dynamic_slice_in_dim(out_grads, ((low ^ a) * 2 + (core ^ b)) * rows, rows, 1)

    other = swap(jnp.concatenate([units(0, 1), units(1, 1)], axis=0), "core")
    tokens = other.shape[0] // 2
    near = jnp.concatenate([units(0, 0), other[:tokens]], axis=0)
    away = swap(jnp.concatenate([units(1, 0), other[tokens:]], axis=0), "zl")

    half = activations.shape[0] // 2
    acts_core = swap(activations, "core")
    acts_below, acts_above = along_z(activations[:half], 1), along_z(activations[half:], -1)

    def arranged(first, second):
        first, second = (a.reshape(16, tokens, -1) for a in (first, second))
        groups = []
        for j in STEPS:
            parts = []
            for i in STEPS:
                at = jnp.where(
                    core == 0, (x + i) % 4 * 4 + (y + j) % 4, (x + j) % 4 * 4 + (y + i) % 4
                )
                parts += [lax.dynamic_index_in_dim(a, at, 0, False) for a in (first, second)]
            groups.append(jnp.concatenate(parts, axis=0))
        return groups

    near = ring_end(ring_start(near, 0), 0)
    near = ring_start(jnp.concatenate(after(near, away), axis=0), 1)
    away = ring_end(ring_start(away, 0), 0)
    groups_near = ring_end(after(near, *away), 1)
    groups_away = ring_end(ring_start(jnp.concatenate(away, axis=0), 1), 1)
    acts_below, acts_above = after((acts_below, acts_above), *groups_near[3:])
    acts_low = jnp.concatenate([acts_below, acts_above], axis=0)
    acts_both = swap(acts_low, "core")
    gradient = token_sum(groups_near, arranged(activations, acts_core))
    gradient = gradient + token_sum(groups_away, arranged(acts_low, acts_both))
    gradient = gradient * token_scale

    squares = gradient * gradient + 1e-30
    row_full = total_over(jnp.sum(squares, axis=1), ("x", "y"))
    row_moment_new = 0.8 * row_moment + 0.2 * row_full / D
    col_part = jnp.sum(squares, axis=0)
    sums = jnp.concatenate([col_part, jnp.full((128,), jnp.sum(row_moment_new))])
    sums = total_over(sums, ("zl", "core", "zh"))
    col_moment_new = 0.8 * col_moment + 0.2 * sums[:512] / FF
    row_average = sums[512] / FF
    update = gradient * lax.rsqrt(row_moment_new[:, None] * col_moment_new[None, :] / row_average)
    momentum_new = (0.9 * momentum.astype(jnp.float32) + 0.1 * update).astype(jnp.bfloat16)
    weights_new = weights - 0.01 * momentum_new.astype(jnp.float32)
    scores_new = scores - 50.0 * weights * gradient
    return (weights_new, momentum_new, scores_new, row_moment_new, col_moment_new)


def solution(mesh):
    fine = Mesh(mesh.devices.reshape(2, 2, 4, 4, 4), ("zl", "core", "x", "y", "zh"))
    dp, row, col = ("zl", "core"), ("x", "y"), "zh"
    return jax.shard_map(
        local,
        mesh=fine,
        in_specs=(
            P(dp, row),
            P(dp + row, col),
            P((col,) + dp, row),
            P((col,) + dp, row),
            P((col,) + dp, row),
            P((col,) + dp),
            P(row),
        ),
        out_specs=(
            P((col,) + dp, row),
            P((col,) + dp, row),
            P((col,) + dp, row),
            P((col,) + dp),
            P(row),
        ),
        check_vma=False,
    )
```

profile of v0, /device:TPU:1, one launch (start us, length us, event | category | flops | bytes accessed | tf_op | source)
XLA Modules:
  0.0 175.7 jit_solution(8366253475268187930)
XLA Ops:
  0.7 1.3 constant_dynamic-slice_fusion.3
  2.0 3.3 %collective-permute-start = (bf16[256,1024]{1,0:T(8,128)(2,1)S(1)}, bf16[256,1024]{1,0:T(8,128)(2,1)S(1)}, u32[]{:S(2)}, u32[]{:S(2)}) collective-permute-start(bf16[256,1024]{1,0:T(8,128)(2,1)S(1)} %pad_maximum_fusion), channel_id=1, source_target_pairs={{0,64},{64,0},{1,65},{65,1},{2,66},{66,2},{3,67},{67,3},{4,68},{68... | collective-permute-start | bytes 1572872 | tf_op jit(solution)/shard_map/ppermute | solution.py:37
  5.3 1.5 collective-permute-done
  7.0 2.7 %collective-permute-start.2 = (bf16[256,1024]{1,0:T(8,128)(2,1)S(1)}, bf16[256,1024]{1,0:T(8,128)(2,1)S(1)}, u32[]{:S(2)}, u32[]{:S(2)}) collective-permute-start(bf16[256,1024]{1,0:T(8,128)(2,1)S(1)} %pad_maximum_fusion.1), channel_id=1, source_target_pairs={{0,48},{4,52},{8,56},{12,60},{16,0},{20,4},{24,8},{28,12},{32,16},... | collective-permute-start | bytes 1572872 | tf_op jit(solution)/shard_map/ppermute | solution.py:28
  9.9 6.7 %collective-permute-done.1 = bf16[256,1024]{1,0:T(8,128)(2,1)S(1)} collective-permute-done((bf16[256,1024]{1,0:T(8,128)(2,1)S(1)}, bf16[256,1024]{1,0:T(8,128)(2,1)S(1)}, u32[]{:S(2)}, u32[]{:S(2)}) %collective-permute-start.1) | collective-permute-done | bytes 524320 | tf_op jit(solution)/shard_map/ppermute | solution.py:28
  16.7 2.7 %collective-permute-start.4 = (bf16[128,1024]{1,0:T(8,128)(2,1)S(1)}, bf16[128,1024]{1,0:T(8,128)(2,1)S(1)}, u32[]{:S(2)}, u32[]{:S(2)}) collective-permute-start(bf16[128,1024]{1,0:T(8,128)(2,1)S(1)} %slice.66), channel_id=1, source_target_pairs={{0,48},{4,52},{8,56},{12,60},{16,0},{20,4},{24,8},{28,12},{32,16},... | collective-permute-start | bytes 786440 | tf_op jit(solution)/shard_map/ppermute | solution.py:28
  19.4 2.9 %collective-permute-done.5 = bf16[256,1024]{1,0:T(8,128)(2,1)S(1)} collective-permute-done((bf16[256,1024]{1,0:T(8,128)(2,1)S(1)}, bf16[256,1024]{1,0:T(8,128)(2,1)S(1)}, u32[]{:S(2)}, u32[]{:S(2)}) %collective-permute-start.5) | collective-permute-done | bytes 524320 | tf_op jit(solution)/shard_map/ppermute | solution.py:37
  22.3 1.1 collective-permute-done.3
  23.7 2.7 %collective-permute-start.7 = (bf16[1024,1024]{1,0:T(8,128)(2,1)S(1)}, bf16[1024,1024]{1,0:T(8,128)(2,1)S(1)}, u32[]{:S(2)}, u32[]{:S(2)}) collective-permute-start(bf16[1024,1024]{1,0:T(8,128)(2,1)S(1)} %constant_dynamic-update-slice_fusion), channel_id=1, source_target_pairs={{0,12},{4,0},{8,4},{12,8},{16,28},{20,16},{24,20},{28,24},{32,44},... | collective-permute-start | bytes 6291464 | tf_op jit(solution)/shard_map/ppermute | solution.py:28
  26.3 2.7 %collective-permute-start.9 = (bf16[256,1024]{1,0:T(8,128)(2,1)S(1)}, bf16[256,1024]{1,0:T(8,128)(2,1)S(1)}, u32[]{:S(2)}, u32[]{:S(2)}) collective-permute-start(bf16[256,1024]{1,0:T(8,128)(2,1)S(1)} %collective-permute-done.5), channel_id=1, source_target_pairs={{0,48},{4,52},{8,56},{12,60},{16,0},{20,4},{24,8},{28,12},{32,16},... | collective-permute-start | bytes 1572872 | tf_op jit(solution)/shard_map/ppermute | solution.py:28
  29.5 12.0 %collective-permute-done.8 = bf16[256,1024]{1,0:T(8,128)(2,1)S(1)} collective-permute-done((bf16[256,1024]{1,0:T(8,128)(2,1)S(1)}, bf16[256,1024]{1,0:T(8,128)(2,1)S(1)}, u32[]{:S(2)}, u32[]{:S(2)}) %collective-permute-start.8) | collective-permute-done | bytes 524320 | tf_op jit(solution)/shard_map/ppermute | solution.py:28
  41.5 4.1 %collective-permute-start.16 = (bf16[1024,512]{1,0:T(8,128)(2,1)S(1)}, bf16[1024,512]{1,0:T(8,128)(2,1)S(1)}, u32[]{:S(2)}, u32[]{:S(2)}) collective-permute-start(bf16[1024,512]{1,0:T(8,128)(2,1)S(1)} %get-tuple-element.96), channel_id=1, source_target_pairs={{0,131},{128,0},{1,128},{129,1},{2,129},{130,2},{3,130},{131,3},{4... | collective-permute-start | bytes 3145736 | tf_op jit(solution)/shard_map/ppermute | solution.py:33
  45.8 9.6 %collective-permute-done.10 = bf16[128,1024]{1,0:T(8,128)(2,1)S(1)} collective-permute-done((bf16[128,1024]{1,0:T(8,128)(2,1)S(1)}, bf16[128,1024]{1,0:T(8,128)(2,1)S(1)}, u32[]{:S(2)}, u32[]{:S(2)}) %collective-permute-start.10) | collective-permute-done | bytes 262176 | tf_op jit(solution)/shard_map/ppermute | solution.py:28
  56.3 4.6 %collective-permute-done.11 = bf16[128,1024]{1,0:T(8,128)(2,1)S(1)} collective-permute-done((bf16[128,1024]{1,0:T(8,128)(2,1)S(1)}, bf16[128,1024]{1,0:T(8,128)(2,1)S(1)}, u32[]{:S(2)}, u32[]{:S(2)}) %collective-permute-start.11) | collective-permute-done | bytes 262176 | tf_op jit(solution)/shard_map/ppermute | solution.py:28
  60.8 4.4 %collective-permute-start.12 = (bf16[2048,512]{1,0:T(8,128)(2,1)S(1)}, bf16[2048,512]{1,0:T(8,128)(2,1)}, u32[]{:S(2)}, u32[]{:S(2)}) collective-permute-start(bf16[2048,512]{1,0:T(8,128)(2,1)S(1)} %copy-done), channel_id=1, source_target_pairs={{0,64},{64,0},{1,65},{65,1},{2,66},{66,2},{3,67},{67,3},{4,68},{68... | collective-permute-start | bytes 6291464 | tf_op jit(solution)/shard_map/ppermute | solution.py:37
  67.3 1.4 collective-permute-start.14
  71.8 2.6 %collective-permute-start.19 = (bf16[1024,1024]{1,0:T(8,128)(2,1)}, bf16[1024,1024]{1,0:T(8,128)(2,1)}, u32[]{:S(2)}, u32[]{:S(2)}) collective-permute-start(bf16[1024,1024]{1,0:T(8,128)(2,1)} %constant_dynamic-update-slice_fusion.5), channel_id=1, source_target_pairs={{0,12},{4,0},{8,4},{12,8},{16,28},{20,16},{24,20},{28,24},{32,44},... | collective-permute-start | bytes 6291464 | tf_op jit(solution)/shard_map/ppermute | solution.py:28
  74.4 6.3 %collective-permute-done.13 = bf16[512,1024]{1,0:T(8,128)(2,1)S(1)} collective-permute-done((bf16[512,1024]{1,0:T(8,128)(2,1)S(1)}, bf16[512,1024]{1,0:T(8,128)(2,1)S(1)}, u32[]{:S(2)}, u32[]{:S(2)}) %collective-permute-start.13) | collective-permute-done | bytes 1048608 | tf_op jit(solution)/shard_map/ppermute | solution.py:28
  83.4 1.1 collective-permute-start.17
  84.5 1.1 dynamic-slice_bitcast_fusion.14
  85.7 17.6 %collective-permute-done.18 = bf16[1024,1024]{1,0:T(8,128)(2,1)} collective-permute-done((bf16[1024,1024]{1,0:T(8,128)(2,1)}, bf16[1024,1024]{1,0:T(8,128)(2,1)}, u32[]{:S(2)}, u32[]{:S(2)}) %collective-permute-start.18) | collective-permute-done | bytes 2097184 | tf_op jit(solution)/shard_map/ppermute | solution.py:28
  103.3 1.3 slice.70
  104.7 1.3 slice.71
  106.0 3.0 %collective-permute-start.21 = (bf16[512,1024]{1,0:T(8,128)(2,1)S(1)}, bf16[512,1024]{1,0:T(8,128)(2,1)S(1)}, u32[]{:S(2)}, u32[]{:S(2)}) collective-permute-start(bf16[512,1024]{1,0:T(8,128)(2,1)S(1)} %slice.71), channel_id=1, source_target_pairs={{0,12},{4,0},{8,4},{12,8},{16,28},{20,16},{24,20},{28,24},{32,44},... | collective-permute-start | bytes 3145736 | tf_op jit(solution)/shard_map/ppermute | solution.py:28
  109.0 1.1 bitcast_dynamic-update-slice_fusion.15
  110.0 1.1 dynamic-slice_bitcast_fusion.3
  111.2 2.0 %fusion.10 = f32[1024,512]{1,0:T(8,128)S(1)} fusion(bf16[512,1024]{1,0:T(8,128)(2,1)} %collective-permute-done.14, bf16[128,512]{1,0:T(8,128)(2,1)S(1)} %get-tuple-element.69, bf16[128,512]{1,0:T(8,128)(2,1)S(1)} %get-tuple-element.65, bf16[128,512]{1,0:T(8,128)(2,1)S(1)} %get-tuple-element.70, bf16[128,512]{1,0:T(8,128)(2,1)S(1)} %get-tuple-element.66), kind=kOutput, calls=%fused_computation.18 | convolution fusion | flops 538968064 | bytes 3670016 | tf_op jit(solution)/shard_map/dot_general | solution.py:55
  113.9 1.3 bitcast_dynamic-update-slice_fusion.14
  115.2 1.2 bitcast_dynamic-update-slice_fusion.36
  116.5 1.1 bitcast_dynamic-update-slice_fusion.34
  117.6 1.1 bitcast_dynamic-update-slice_fusion.32
  118.7 1.3 fusion.44
  120.3 1.3 fusion.45
  121.6 1.1 bitcast_dynamic-update-slice_fusion.13
  122.6 1.1 bitcast_dynamic-update-slice_fusion.12
  123.7 1.1 bitcast_dynamic-update-slice_fusion.11
  124.8 1.1 bitcast_dynamic-update-slice_fusion.10
  125.8 1.1 bitcast_dynamic-update-slice_fusion.9
  126.9 1.1 bitcast_dynamic-update-slice_fusion.8
  128.0 3.0 %fusion.46 = f32[1024,512]{1,0:T(8,128)S(1)} fusion(bf16[1024,1024]{1,0:T(8,128)(2,1)} %constant_dynamic-update-slice_fusion.5, bf16[1024,512]{1,0:T(8,128)(2,1)S(1)} %get-tuple-element.74), kind=kOutput, calls=%fused_computation.134 | convolution fusion | flops 1073741824 | bytes 5242880 | tf_op jit(solution)/shard_map/dot_general | solution.py:55
  131.0 1.3 fusion.43
  132.3 1.1 dynamic-slice_bitcast_fusion.2
  134.2 2.9 %fusion.47 = f32[1024,512]{1,0:T(8,128)S(1)} fusion(bf16[1024,1024]{1,0:T(8,128)(2,1)} %collective-permute-done.18, bf16[1024,512]{1,0:T(8,128)(2,1)S(1)} %get-tuple-element.72), kind=kOutput, calls=%fused_computation.135 | convolution fusion | flops 1073741824 | bytes 5242880 | tf_op jit(solution)/shard_map/dot_general | solution.py:55
  137.1 2.9 %fusion.48 = f32[1024,512]{1,0:T(8,128)S(1)} fusion(bf16[1024,1024]{1,0:T(8,128)(2,1)} %collective-permute-done.19, bf16[1024,512]{1,0:T(8,128)(2,1)S(1)} %get-tuple-element.73), kind=kOutput, calls=%fused_computation.136 | convolution fusion | flops 1073741824 | bytes 5242880 | tf_op jit(solution)/shard_map/dot_general | solution.py:55
  140.0 3.2 %fusion.1 = (f32[1024]{0:T(1024)S(1)}, f32[512]{0:T(512)S(1)}, f32[1024,512]{1,0:T(8,128)S(1)}) fusion(bf16[512,1024]{1,0:T(8,128)(2,1)S(1)} %collective-permute-done.21, bf16[128,512]{1,0:T(8,128)(2,1)S(1)} %get-tuple-element.37, bf16[128,512]{1,0:T(8,128)(2,1)S(1)} %get-tuple-element.33, bf16[128,512]{1,0:T(8,128)(2,1)S(1)} %get-tuple-element.36, ...), kind=kOutput, calls=%fused_computation.6 | convolution fusion | flops 546306560 | bytes 22550528 | tf_op jit(solution)/shard_map/dot_general | solution.py:55
  143.3 10.2 %all_to_all.12 = f32[16,1,1024]{2,1,0:T(1,128)S(1)} all-to-all(f32[16,1,1024]{2,1,0:T(1,128)S(1)} %broadcast_in_dim.4), channel_id=1, replica_groups=mesh['zl'=2,'core'=2,'x'=4,'y'=4,'zh'=4] {'x','y'}, dimensions={0} | all-to-all | bytes 131072 | tf_op jit(solution)/shard_map/all_to_all | solution.py:69
  154.8 14.1 %all_to_all.13 = f32[16,1,640]{2,1,0:T(1,128)S(1)} all-to-all(f32[16,1,640]{2,1,0:T(1,128)S(1)} %broadcast_in_dim.5), channel_id=1, replica_groups=mesh['zl'=2,'core'=2,'x'=4,'y'=4,'zh'=4] {'zl','core','zh'}, dimensions={0} | all-to-all | bytes 81920 | tf_op jit(solution)/shard_map/all_to_all | solution.py:69
  170.2 5.5 %multiply_subtract_fusion.1 = (f32[1024,512]{1,0:T(8,128)}, bf16[1024,512]{1,0:T(8,128)(2,1)}, f32[1024,512]{1,0:T(8,128)}) fusion(f32[1024,512]{1,0:T(8,128)} %param.9, f32[1024,512]{1,0:T(8,128)S(1)} %get-tuple-element.104, f32[]{:T(128)} %bitcast.68, f32[512]{0:T(512)S(1)} %multiply_add_fusion.2, f32[1024]{0:T(1024)S(1)} %get-tuple-element.30, ...), kind=kLoop, calls=%fused_computation.1 | loop fusion | flops 7340032 | bytes 12589060 | tf_op jit(solution)/shard_map/sub | solution.py:125
  (86 shorter events, 14.1 us)
Async XLA Ops:
  2.0 4.9 %collective-permute-start = (bf16[256,1024]{1,0:T(8,128)(2,1)S(1)}, bf16[256,1024]{1,0:T(8,128)(2,1)S(1)}, u32[]{:S(2)}, u32[]{:S(2)}) collective-permute-start(bf16[256,1024]{1,0:T(8,128)(2,1)S(1)} %pad_maximum_fusion), channel_id=1, source_target_pairs={{0,64},{64,0},{1,65},{65,1},{2,66},{66,2},{3,67},{67,3},{4,68},{68... | collective-permute-start | bytes 1572872 | tf_op jit(solution)/shard_map/ppermute | solution.py:37
  6.9 9.6 %collective-permute-start.1 = (bf16[256,1024]{1,0:T(8,128)(2,1)S(1)}, bf16[256,1024]{1,0:T(8,128)(2,1)S(1)}, u32[]{:S(2)}, u32[]{:S(2)}) collective-permute-start(bf16[256,1024]{1,0:T(8,128)(2,1)S(1)} %pad_maximum_fusion.1), channel_id=1, source_target_pairs={{0,16},{4,20},{8,24},{12,28},{16,32},{20,36},{24,40},{28,44},{32,4... | collective-permute-start | bytes 1572872 | tf_op jit(solution)/shard_map/ppermute | solution.py:28
  7.0 9.6 %collective-permute-start.2 = (bf16[256,1024]{1,0:T(8,128)(2,1)S(1)}, bf16[256,1024]{1,0:T(8,128)(2,1)S(1)}, u32[]{:S(2)}, u32[]{:S(2)}) collective-permute-start(bf16[256,1024]{1,0:T(8,128)(2,1)S(1)} %pad_maximum_fusion.1), channel_id=1, source_target_pairs={{0,48},{4,52},{8,56},{12,60},{16,0},{20,4},{24,8},{28,12},{32,16},... | collective-permute-start | bytes 1572872 | tf_op jit(solution)/shard_map/ppermute | solution.py:28
  9.7 12.6 %collective-permute-start.5 = (bf16[256,1024]{1,0:T(8,128)(2,1)S(1)}, bf16[256,1024]{1,0:T(8,128)(2,1)S(1)}, u32[]{:S(2)}, u32[]{:S(2)}) collective-permute-start(bf16[256,1024]{1,0:T(8,128)(2,1)S(1)} %pad_maximum_fusion.2), channel_id=1, source_target_pairs={{0,128},{128,0},{1,129},{129,1},{2,130},{130,2},{3,131},{131,3},{4... | collective-permute-start | bytes 1572872 | tf_op jit(solution)/shard_map/ppermute | solution.py:37
  16.6 6.8 %collective-permute-start.3 = (bf16[128,1024]{1,0:T(8,128)(2,1)S(1)}, bf16[128,1024]{1,0:T(8,128)(2,1)S(1)}, u32[]{:S(2)}, u32[]{:S(2)}) collective-permute-start(bf16[128,1024]{1,0:T(8,128)(2,1)S(1)} %slice.65), channel_id=1, source_target_pairs={{0,16},{4,20},{8,24},{12,28},{16,32},{20,36},{24,40},{28,44},{32,4... | collective-permute-start | bytes 786440 | tf_op jit(solution)/shard_map/ppermute | solution.py:28
  16.7 12.3 %copy-start = (bf16[2048,512]{1,0:T(8,128)(2,1)S(1)}, bf16[2048,512]{1,0:T(8,128)(2,1)}, u32[]{:S(2)}) copy-start(bf16[2048,512]{1,0:T(8,128)(2,1)} %param.7) | copy-start | bytes 6291460
  16.7 6.7 %collective-permute-start.4 = (bf16[128,1024]{1,0:T(8,128)(2,1)S(1)}, bf16[128,1024]{1,0:T(8,128)(2,1)S(1)}, u32[]{:S(2)}, u32[]{:S(2)}) collective-permute-start(bf16[128,1024]{1,0:T(8,128)(2,1)S(1)} %slice.66), channel_id=1, source_target_pairs={{0,48},{4,52},{8,56},{12,60},{16,0},{20,4},{24,8},{28,12},{32,16},... | collective-permute-start | bytes 786440 | tf_op jit(solution)/shard_map/ppermute | solution.py:28
  23.5 5.6 %copy-start.6 = (bf16[1024,1024]{1,0:T(8,128)(2,1)}, bf16[1024,1024]{1,0:T(8,128)(2,1)S(1)}, u32[]{:S(2)}) copy-start(bf16[1024,1024]{1,0:T(8,128)(2,1)S(1)} %constant_dynamic-update-slice_fusion) | copy-start | bytes 6291460
  23.6 41.7 %collective-permute-start.6 = (bf16[1024,1024]{1,0:T(8,128)(2,1)S(1)}, bf16[1024,1024]{1,0:T(8,128)(2,1)S(1)}, u32[]{:S(2)}, u32[]{:S(2)}) collective-permute-start(bf16[1024,1024]{1,0:T(8,128)(2,1)S(1)} %constant_dynamic-update-slice_fusion), channel_id=1, source_target_pairs={{0,4},{4,8},{8,12},{12,0},{16,20},{20,24},{24,28},{28,16},{32,36},... | collective-permute-start | bytes 6291464 | tf_op jit(solution)/shard_map/ppermute | solution.py:28
  23.7 41.6 %collective-permute-start.7 = (bf16[1024,1024]{1,0:T(8,128)(2,1)S(1)}, bf16[1024,1024]{1,0:T(8,128)(2,1)S(1)}, u32[]{:S(2)}, u32[]{:S(2)}) collective-permute-start(bf16[1024,1024]{1,0:T(8,128)(2,1)S(1)} %constant_dynamic-update-slice_fusion), channel_id=1, source_target_pairs={{0,12},{4,0},{8,4},{12,8},{16,28},{20,16},{24,20},{28,24},{32,44},... | collective-permute-start | bytes 6291464 | tf_op jit(solution)/shard_map/ppermute | solution.py:28
  26.3 15.2 %collective-permute-start.8 = (bf16[256,1024]{1,0:T(8,128)(2,1)S(1)}, bf16[256,1024]{1,0:T(8,128)(2,1)S(1)}, u32[]{:S(2)}, u32[]{:S(2)}) collective-permute-start(bf16[256,1024]{1,0:T(8,128)(2,1)S(1)} %collective-permute-done.5), channel_id=1, source_target_pairs={{0,16},{4,20},{8,24},{12,28},{16,32},{20,36},{24,40},{28,44},{32,4... | collective-permute-start | bytes 1572872 | tf_op jit(solution)/shard_map/ppermute | solution.py:28
  26.3 19.3 %collective-permute-start.9 = (bf16[256,1024]{1,0:T(8,128)(2,1)S(1)}, bf16[256,1024]{1,0:T(8,128)(2,1)S(1)}, u32[]{:S(2)}, u32[]{:S(2)}) collective-permute-start(bf16[256,1024]{1,0:T(8,128)(2,1)S(1)} %collective-permute-done.5), channel_id=1, source_target_pairs={{0,48},{4,52},{8,56},{12,60},{16,0},{20,4},{24,8},{28,12},{32,16},... | collective-permute-start | bytes 1572872 | tf_op jit(solution)/shard_map/ppermute | solution.py:28
  29.2 42.6 %collective-permute-start.15 = (bf16[1024,512]{1,0:T(8,128)(2,1)S(1)}, bf16[1024,512]{1,0:T(8,128)(2,1)S(1)}, u32[]{:S(2)}, u32[]{:S(2)}) collective-permute-start(bf16[1024,512]{1,0:T(8,128)(2,1)S(1)} %get-tuple-element.97), channel_id=1, source_target_pairs={{0,128},{128,1},{1,129},{129,2},{2,130},{130,3},{3,131},{131,0},{4... | collective-permute-start | bytes 3145736 | tf_op jit(solution)/shard_map/ppermute | solution.py:33
  41.5 30.4 %collective-permute-start.16 = (bf16[1024,512]{1,0:T(8,128)(2,1)S(1)}, bf16[1024,512]{1,0:T(8,128)(2,1)S(1)}, u32[]{:S(2)}, u32[]{:S(2)}) collective-permute-start(bf16[1024,512]{1,0:T(8,128)(2,1)S(1)} %get-tuple-element.96), channel_id=1, source_target_pairs={{0,131},{128,0},{1,128},{129,1},{2,129},{130,2},{3,130},{131,3},{4... | collective-permute-start | bytes 3145736 | tf_op jit(solution)/shard_map/ppermute | solution.py:33
  45.6 9.7 %collective-permute-start.10 = (bf16[128,1024]{1,0:T(8,128)(2,1)S(1)}, bf16[128,1024]{1,0:T(8,128)(2,1)S(1)}, u32[]{:S(2)}, u32[]{:S(2)}) collective-permute-start(bf16[128,1024]{1,0:T(8,128)(2,1)S(1)} %slice.68), channel_id=1, source_target_pairs={{0,16},{4,20},{8,24},{12,28},{16,32},{20,36},{24,40},{28,44},{32,4... | collective-permute-start | bytes 786440 | tf_op jit(solution)/shard_map/ppermute | solution.py:28
  55.3 5.5 %collective-permute-start.11 = (bf16[128,1024]{1,0:T(8,128)(2,1)S(1)}, bf16[128,1024]{1,0:T(8,128)(2,1)S(1)}, u32[]{:S(2)}, u32[]{:S(2)}) collective-permute-start(bf16[128,1024]{1,0:T(8,128)(2,1)S(1)} %slice.69), channel_id=1, source_target_pairs={{0,48},{4,52},{8,56},{12,60},{16,0},{20,4},{24,8},{28,12},{32,16},... | collective-permute-start | bytes 786440 | tf_op jit(solution)/shard_map/ppermute | solution.py:28
  60.8 23.7 %collective-permute-start.12 = (bf16[2048,512]{1,0:T(8,128)(2,1)S(1)}, bf16[2048,512]{1,0:T(8,128)(2,1)}, u32[]{:S(2)}, u32[]{:S(2)}) collective-permute-start(bf16[2048,512]{1,0:T(8,128)(2,1)S(1)} %copy-done), channel_id=1, source_target_pairs={{0,64},{64,0},{1,65},{65,1},{2,66},{66,2},{3,67},{67,3},{4,68},{68... | collective-permute-start | bytes 6291464 | tf_op jit(solution)/shard_map/ppermute | solution.py:37
  65.2 1.4 copy-start.2
  65.2 2.0 %copy-start.4 = (bf16[1024,1024]{1,0:T(8,128)(2,1)}, bf16[1024,1024]{1,0:T(8,128)(2,1)S(1)}, u32[]{:S(2)}) copy-start(bf16[1024,1024]{1,0:T(8,128)(2,1)S(1)} %collective-permute-done.7) | copy-start | bytes 6291460
  65.3 15.4 %collective-permute-start.13 = (bf16[512,1024]{1,0:T(8,128)(2,1)S(1)}, bf16[512,1024]{1,0:T(8,128)(2,1)S(1)}, u32[]{:S(2)}, u32[]{:S(2)}) collective-permute-start(bf16[512,1024]{1,0:T(8,128)(2,1)S(1)} %slice.56), channel_id=1, source_target_pairs={{0,4},{4,8},{8,12},{12,0},{16,20},{20,24},{24,28},{28,16},{32,36},... | collective-permute-start | bytes 3145736 | tf_op jit(solution)/shard_map/ppermute | solution.py:28
  67.3 14.0 %collective-permute-start.14 = (bf16[512,1024]{1,0:T(8,128)(2,1)S(1)}, bf16[512,1024]{1,0:T(8,128)(2,1)}, u32[]{:S(2)}, u32[]{:S(2)}) collective-permute-start(bf16[512,1024]{1,0:T(8,128)(2,1)S(1)} %slice.57), channel_id=1, source_target_pairs={{0,12},{4,0},{8,4},{12,8},{16,28},{20,16},{24,20},{28,24},{32,44},... | collective-permute-start | bytes 3145736 | tf_op jit(solution)/shard_map/ppermute | solution.py:28
  71.8 31.6 %collective-permute-start.18 = (bf16[1024,1024]{1,0:T(8,128)(2,1)}, bf16[1024,1024]{1,0:T(8,128)(2,1)}, u32[]{:S(2)}, u32[]{:S(2)}) collective-permute-start(bf16[1024,1024]{1,0:T(8,128)(2,1)} %constant_dynamic-update-slice_fusion.5), channel_id=1, source_target_pairs={{0,4},{4,8},{8,12},{12,0},{16,20},{20,24},{24,28},{28,16},{32,36},... | collective-permute-start | bytes 6291464 | tf_op jit(solution)/shard_map/ppermute | solution.py:28
  71.8 32.9 %collective-permute-start.19 = (bf16[1024,1024]{1,0:T(8,128)(2,1)}, bf16[1024,1024]{1,0:T(8,128)(2,1)}, u32[]{:S(2)}, u32[]{:S(2)}) collective-permute-start(bf16[1024,1024]{1,0:T(8,128)(2,1)} %constant_dynamic-update-slice_fusion.5), channel_id=1, source_target_pairs={{0,12},{4,0},{8,4},{12,8},{16,28},{20,16},{24,20},{28,24},{32,44},... | collective-permute-start | bytes 6291464 | tf_op jit(solution)/shard_map/ppermute | solution.py:28
  83.4 30.5 %collective-permute-start.17 = (bf16[2048,512]{1,0:T(8,128)(2,1)}, bf16[2048,512]{1,0:T(8,128)(2,1)}, u32[]{:S(2)}, u32[]{:S(2)}) collective-permute-start(bf16[2048,512]{1,0:T(8,128)(2,1)} %constant_dynamic-update-slice_fusion.10), channel_id=1, source_target_pairs={{0,64},{64,0},{1,65},{65,1},{2,66},{66,2},{3,67},{67,3},{4,68},{68... | collective-permute-start | bytes 6291464 | tf_op jit(solution)/shard_map/ppermute | solution.py:37
  104.6 28.9 %collective-permute-start.20 = (bf16[512,1024]{1,0:T(8,128)(2,1)S(1)}, bf16[512,1024]{1,0:T(8,128)(2,1)S(1)}, u32[]{:S(2)}, u32[]{:S(2)}) collective-permute-start(bf16[512,1024]{1,0:T(8,128)(2,1)S(1)} %slice.70), channel_id=1, source_target_pairs={{0,4},{4,8},{8,12},{12,0},{16,20},{20,24},{24,28},{28,16},{32,36},... | collective-permute-start | bytes 3145736 | tf_op jit(solution)/shard_map/ppermute | solution.py:28
  106.0 34.0 %collective-permute-start.21 = (bf16[512,1024]{1,0:T(8,128)(2,1)S(1)}, bf16[512,1024]{1,0:T(8,128)(2,1)S(1)}, u32[]{:S(2)}, u32[]{:S(2)}) collective-permute-start(bf16[512,1024]{1,0:T(8,128)(2,1)S(1)} %slice.71), channel_id=1, source_target_pairs={{0,12},{4,0},{8,4},{12,8},{16,28},{20,16},{24,20},{28,24},{32,44},... | collective-permute-start | bytes 3145736 | tf_op jit(solution)/shard_map/ppermute | solution.py:28
  115.2 3.5 %copy-start.3 = (bf16[1024,1024]{1,0:T(8,128)(2,1)S(1)}, bf16[1024,1024]{1,0:T(8,128)(2,1)}, u32[]{:S(2)}) copy-start(bf16[1024,1024]{1,0:T(8,128)(2,1)} %copy-done.2) | copy-start | bytes 6291460
  118.7 1.6 copy-start.5
  128.0 3.0 %copy-start.7 = (bf16[1024,1024]{1,0:T(8,128)(2,1)S(1)}, bf16[1024,1024]{1,0:T(8,128)(2,1)}, u32[]{:S(2)}) copy-start(bf16[1024,1024]{1,0:T(8,128)(2,1)} %copy-done.6) | copy-start | bytes 6291460
  140.0 13.5 %copy-start.10 = (f32[1024]{0:T(1024)S(1)}, f32[1024]{0:T(1024)}, u32[]{:S(2)}) copy-start(f32[1024]{0:T(1024)} %param.12) | copy-start | bytes 12292
  140.0 29.5 %copy-start.11 = (f32[512]{0:T(512)S(1)}, f32[512]{0:T(512)}, u32[]{:S(2)}) copy-start(f32[512]{0:T(512)} %param.13) | copy-start | bytes 6148
  140.0 30.1 %copy-start.1 = (bf16[1024,512]{1,0:T(8,128)(2,1)S(1)}, bf16[1024,512]{1,0:T(8,128)(2,1)}, u32[]{:S(2)}) copy-start(bf16[1024,512]{1,0:T(8,128)(2,1)} %param.10) | copy-start | bytes 3145732
  154.1 21.6 %copy-start.8 = (f32[1024]{0:T(1024)}, f32[1024]{0:T(1024)S(1)}, u32[]{:S(2)}) copy-start(f32[1024]{0:T(1024)S(1)} %get-tuple-element.30) | copy-start | bytes 12292
  169.5 6.2 %copy-start.9 = (f32[512]{0:T(512)}, f32[512]{0:T(512)S(1)}, u32[]{:S(2)}) copy-start(f32[512]{0:T(512)S(1)} %multiply_add_fusion.2) | copy-start | bytes 6148
where the time goes:
time: 176 us
  waiting for transfers between devices  62.8 us (36%)
  starting transfers between devices  32 us (18%)
  local copies, waits for them, and re-layouts  29.2 us (17%)
  blocking collectives  24.3 us (14%)
  matrix products  19.3 us (11%)
  other arithmetic  6.34 us (4%)
  between operations  1.82 us (1%)
    ppermute x16, waiting for transfers between devices, shift(): return lax.ppermute(array, AXES, ring_pairs(phase, step))  58.4 us
    all_to_all x2, blocking collectives, total_over(): return jnp.sum(lax.all_to_all(spread, axes, 0, 0, tiled=True), axis=0)  24.3 us
    dot_general x10, matrix products, product(): lax.dot_general(grad_rows, act_rows, (((0,), (0,)), ((), ())), preferred_...  19.3 us
    ppermute x16, starting transfers between devices, shift(): return lax.ppermute(array, AXES, ring_pairs(phase, step))  18.6 us
    unnamed x46, local copies, waits for them, and re-layouts  16.4 us
    ppermute x4, starting transfers between devices, swap(): return lax.ppermute(array, axis, [(0, 1), (1, 0)])  8.89 us
    sub x1, other arithmetic, local(): weights_new = weights - 0.01 * momentum_new.astype(jnp.float32)  5.53 us
    ppermute x2, starting transfers between devices, along_z(): lax.ppermute(array, ('zl', 'zh'), [(place(z), place((z + step) % 8)) for...  4.5 us
  transfers between devices with their start and end apart: 22, of which 10 were waited for; matrix products, arithmetic and copies ran while one was open for 23% of the time, Pallas kernels for 0%

commit v1 on v0

v1 whole, which is shorter than its diff:
```python
import math

import jax
import jax.numpy as jnp
from jax import lax
from jax.experimental import pallas as pl
from jax.experimental.pallas import tpu as pltpu
from jax.sharding import Mesh, PartitionSpec as P

D = 8192
FF = 16384
AXES = ("core", "x", "y")
STEPS = (0, -1, 1, 2)


def ring_pairs(phase, step):
    pairs = []
    for core in range(2):
        for x in range(4):
            for y in range(4):
                if core == phase:
                    to = (x + step) % 4 * 4 + y
                else:
                    to = x * 4 + (y + step) % 4
                pairs.append((core * 16 + x * 4 + y, core * 16 + to))
    return pairs


def shift(array, phase, step):
    return lax.ppermute(array, AXES, ring_pairs(phase, step))


def along_z(array, step):
    place = lambda z: z % 2 * 4 + z // 2
    return lax.ppermute(array, ("zl", "zh"), [(place(z), place((z + step) % 8)) for z in range(8)])


def swap(array, axis):
    return lax.ppermute(array, axis, [(0, 1), (1, 0)])


def first_ring(block):
    return [block, shift(block, 0, 1), shift(block, 0, -1), shift(block, 0, 2)]


def second_start(block):
    return [block, shift(block, 1, 1), shift(block, 1, -1)]


def second_end(blocks):
    block, below, above = blocks
    half = block.shape[0] // 2
    return [*blocks, shift(below[:half], 1, 1), shift(above[half:], 1, -1)]


def product(grad_rows, act_rows):
    return lax.dot_general(
        grad_rows, act_rows, (((0,), (0,)), ((), ())), preferred_element_type=jnp.float32
    )


def add_products(total, groups, acts):
    half = groups[3].shape[0]
    for rows, cols in zip(groups, (*acts[:3], acts[3][:half], acts[3][half:])):
        term = product(rows, cols)
        total = term if total is None else total + term
    return total


def arrange_kernel(place, first, second, out):
    tokens = first.shape[0]
    out[:tokens] = first[...]
    out[tokens:] = second[...]


def arranged(places, first, second, tokens):
    block = pl.BlockSpec((tokens, first.shape[1]), lambda i, place: (place[i], 0))
    out = pl.pallas_call(
        arrange_kernel,
        grid_spec=pltpu.PrefetchScalarGridSpec(
            num_scalar_prefetch=1,
            grid=(16,),
            in_specs=[block, block],
            out_specs=pl.BlockSpec((2 * tokens, first.shape[1]), lambda i, place: (i, 0)),
        ),
        out_shape=jax.ShapeDtypeStruct((32 * tokens, first.shape[1]), first.dtype),
        cost_estimate=pl.CostEstimate(
            flops=0, bytes_accessed=128 * tokens * first.shape[1], transcendentals=0
        ),
    )(places, first, second)
    return out.reshape(4, 8 * tokens, first.shape[1])


def total_over(vector, axes):
    spread = jnp.broadcast_to(vector[None], (16, vector.shape[0]))
    return jnp.sum(lax.all_to_all(spread, axes, 0, 0, tiled=True), axis=0)


def local(activations, out_grads, weights, momentum, scores, row_moment, col_moment):
    token_scale = 1.0 / math.sqrt(activations.shape[0] * 4)
    core, low = lax.axis_index("core"), lax.axis_index("zl")
    x, y = lax.axis_index("x"), lax.axis_index("y")
    rows = FF // 16

    def units(a, b):
        return lax.dynamic_slice_in_dim(out_grads, ((low ^ a) * 2 + (core ^ b)) * rows, rows, 1)

    other = swap(jnp.concatenate([units(0, 1), units(1, 1)], axis=0), "core")
    tokens = other.shape[0] // 2
    near = jnp.concatenate([units(0, 0), other[:tokens]], axis=0)
    away = jnp.concatenate([units(1, 0), other[tokens:]], axis=0)
    acts_core = swap(activations, "core")

    places = []
    for j in STEPS:
        for i in STEPS:
            dx, dy = jnp.where(core == 0, i, j), jnp.where(core == 0, j, i)
            places.append((x + dx) % 4 * 4 + (y + dy) % 4)
    places = jnp.stack(places).astype(jnp.int32)

    *near, acts_core, away, sent = lax.optimization_barrier(
        (*first_ring(near), acts_core, away, activations)
    )
    near = second_start(jnp.concatenate(near, axis=0))
    away = swap(away, "zl")
    half = sent.shape[0] // 2
    acts_below, acts_above = along_z(sent[:half], 1), along_z(sent[half:], -1)
    away, acts_below, acts_above = lax.optimization_barrier((away, acts_below, acts_above))
    *away, acts_below, acts_above = lax.optimization_barrier(
        (*first_ring(away), acts_below, acts_above)
    )
    away = second_start(jnp.concatenate(away, axis=0))
    near = second_end(near)
    gradient = add_products(None, near, arranged(places, activations, acts_core, tokens))
    acts_low = jnp.concatenate([acts_below, acts_above], axis=0)
    acts_away = arranged(places, acts_low, swap(acts_low, "core"), tokens)
    *away, acts_away, gradient = lax.optimization_barrier((*away, acts_away, gradient))
    gradient = add_products(gradient, second_end(away), acts_away)
    gradient = gradient * token_scale

    squares = gradient * gradient + 1e-30
    row_full = total_over(jnp.sum(squares, axis=1), ("x", "y"))
    row_moment_new = 0.8 * row_moment + 0.2 * row_full / D
    col_part = jnp.sum(squares, axis=0)
    sums = jnp.concatenate([col_part, jnp.sum(row_moment_new.reshape(8, 128), axis=0)])
    sums = total_over(sums, ("zl", "core", "zh"))
    col_moment_new = 0.8 * col_moment + 0.2 * sums[:512] / FF
    row_average = jnp.sum(sums[512:]) / FF
    update = gradient * lax.rsqrt(row_moment_new[:, None] * col_moment_new[None, :] / row_average)
    momentum_new = (0.9 * momentum.astype(jnp.float32) + 0.1 * update).astype(jnp.bfloat16)
    weights_new = weights - 0.01 * momentum_new.astype(jnp.float32)
    scores_new = scores - 50.0 * weights * gradient
    return (weights_new, momentum_new, scores_new, row_moment_new, col_moment_new)


def solution(mesh):
    fine = Mesh(mesh.devices.reshape(2, 2, 4, 4, 4), ("zl", "core", "x", "y", "zh"))
    dp, row, col = ("zl", "core"), ("x", "y"), "zh"
    return jax.shard_map(
        local,
        mesh=fine,
        in_specs=(
            P(dp, row),
            P(dp + row, col),
            P((col,) + dp, row),
            P((col,) + dp, row),
            P((col,) + dp, row),
            P((col,) + dp),
            P(row),
        ),
        out_specs=(
            P((col,) + dp, row),
            P((col,) + dp, row),
            P((col,) + dp, row),
            P((col,) + dp),
            P(row),
        ),
        check_vma=False,
    )
```

time: 176 us -> 192 us (1.091)
  Pallas kernels: 0 us -> 22 us
  local copies, waits for them, and re-layouts: 29.2 us -> 14.4 us
  blocking collectives: 24.3 us -> 31.4 us
  starting transfers between devices: 32 us -> 28.4 us
  matrix products: 19.3 us -> 22.7 us
    ppermute x4, waiting for transfers between devices: 4.41 us -> 28.1 us  [swap(): return lax.ppermute(array, axis, [(0, 1), (1, 0)])]
    ppermute x16 -> x14, waiting for transfers between devices: 58.4 us -> 36.1 us  [shift(): return lax.ppermute(array, AXES, ring_pairs(phase, step))]
    pallas_call x0 -> x2, Pallas kernels: none -> 22 us  [arranged(): pl.pallas_call(arrange_kernel, grid_spec=pltpu.PrefetchScalarGridSpec(num...]
    unnamed x46 -> x27, local copies, waits for them, and re-layouts: 16.4 us -> 5.14 us
    all_to_all x2, blocking collectives: 24.3 us -> 31.4 us  [total_over(): return jnp.sum(lax.all_to_all(spread, axes, 0, 0, tiled=True), axis=0)]
    dot_general x10, matrix products: 19.3 us -> 22.7 us  [product(): lax.dot_general(grad_rows, act_rows, (((0,), (0,)), ((), ())), preferred_...]
    squeeze x4 -> x0, local copies, waits for them, and re-layouts: 3.47 us -> none  [arranged(): lax.dynamic_index_in_dim(a, at, 0, False)]
    ppermute x4, starting transfers between devices: 8.89 us -> 6.46 us  [swap(): return lax.ppermute(array, axis, [(0, 1), (1, 0)])]
  transfers between devices with their start and end apart: 22 -> 20, of which waited for: 10 -> 8; matrix products, arithmetic and copies ran while one was open for 23% -> 18% of each run, Pallas kernels for 0% -> 12%
where the time goes in v1:
time: 192 us; the launch traced here: 191 us
  waiting for transfers between devices  64.2 us (33%)
  blocking collectives  31.4 us (16%)
  starting transfers between devices  28.4 us (15%)
  matrix products  22.7 us (12%)
  Pallas kernels  22 us (11%)
  local copies, waits for them, and re-layouts  14.4 us (8%)
  other arithmetic  6.37 us (3%)
    ppermute x14, waiting for transfers between devices, shift(): return lax.ppermute(array, AXES, ring_pairs(phase, step))  36.1 us
    all_to_all x2, blocking collectives, total_over(): return jnp.sum(lax.all_to_all(spread, axes, 0, 0, tiled=True), axis=0)  31.4 us
    ppermute x4, waiting for transfers between devices, swap(): return lax.ppermute(array, axis, [(0, 1), (1, 0)])  28.1 us
    dot_general x10, matrix products, product(): lax.dot_general(grad_rows, act_rows, (((0,), (0,)), ((), ())), preferred_...  22.7 us
    pallas_call x2, Pallas kernels, arranged(): pl.pallas_call(arrange_kernel, grid_spec=pltpu.PrefetchScalarGridSpec(num...  22 us
    ppermute x14, starting transfers between devices, shift(): return lax.ppermute(array, AXES, ring_pairs(phase, step))  16.8 us
    ppermute x4, starting transfers between devices, swap(): return lax.ppermute(array, axis, [(0, 1), (1, 0)])  6.46 us
    sub x1, other arithmetic, local(): weights_new = weights - 0.01 * momentum_new.astype(jnp.float32)  5.53 us
  transfers between devices with their start and end apart: 20, of which 8 were waited for; matrix products, arithmetic and copies ran while one was open for 18% of the time, Pallas kernels for 12%

profile of v1, /device:TPU:1, one launch (start us, length us, event | category | flops | bytes accessed | tf_op | source)
XLA Modules:
  0.0 191.2 jit_solution(3503546321595452290)
XLA Ops:
  0.6 3.3 %collective-permute-start.4 = (bf16[2048,512]{1,0:T(8,128)(2,1)}, bf16[2048,512]{1,0:T(8,128)(2,1)}, u32[]{:S(2)}, u32[]{:S(2)}) collective-permute-start(bf16[2048,512]{1,0:T(8,128)(2,1)} %first.1), channel_id=1, source_target_pairs={{0,64},{64,0},{1,65},{65,1},{2,66},{66,2},{3,67},{67,3},{4,68},{68... | collective-permute-start | bytes 6291464 | tf_op jit(solution)/shard_map/ppermute | solution.py:39
  4.0 1.3 constant_dynamic-slice_fusion
  5.4 3.1 %collective-permute-done = bf16[256,1024]{1,0:T(8,128)(2,1)S(1)} collective-permute-done((bf16[256,1024]{1,0:T(8,128)(2,1)S(1)}, bf16[256,1024]{1,0:T(8,128)(2,1)S(1)}, u32[]{:S(2)}, u32[]{:S(2)}) %collective-permute-start) | collective-permute-done | bytes 524320 | tf_op jit(solution)/shard_map/ppermute | solution.py:39
  8.7 2.7 %collective-permute-start.2 = (bf16[256,1024]{1,0:T(8,128)(2,1)S(1)}, bf16[256,1024]{1,0:T(8,128)(2,1)S(1)}, u32[]{:S(2)}, u32[]{:S(2)}) collective-permute-start(bf16[256,1024]{1,0:T(8,128)(2,1)S(1)} %pad_maximum_fusion.1), channel_id=1, source_target_pairs={{0,48},{4,52},{8,56},{12,60},{16,0},{20,4},{24,8},{28,12},{32,16},... | collective-permute-start | bytes 1572872 | tf_op jit(solution)/shard_map/ppermute | solution.py:30
  11.4 12.4 %collective-permute-done.1 = bf16[256,1024]{1,0:T(8,128)(2,1)S(1)} collective-permute-done((bf16[256,1024]{1,0:T(8,128)(2,1)S(1)}, bf16[256,1024]{1,0:T(8,128)(2,1)S(1)}, u32[]{:S(2)}, u32[]{:S(2)}) %collective-permute-start.1) | collective-permute-done | bytes 524320 | tf_op jit(solution)/shard_map/ppermute | solution.py:30
  24.0 1.2 collective-permute-start.6
  25.2 4.0 %collective-permute-start.7 = (bf16[1024,512]{1,0:T(8,128)(2,1)S(1)}, bf16[1024,512]{1,0:T(8,128)(2,1)S(1)}, u32[]{:S(2)}, u32[]{:S(2)}) collective-permute-start(bf16[1024,512]{1,0:T(8,128)(2,1)S(1)} %get-tuple-element.54), channel_id=1, source_target_pairs={{0,131},{128,0},{1,128},{129,1},{2,129},{130,2},{3,130},{131,3},{4... | collective-permute-start | bytes 3145736 | tf_op jit(solution)/shard_map/ppermute | solution.py:35
  29.2 0.8 constant_dynamic-update-slice_fusion.9
  30.1 0.8 constant_dynamic-update-slice_fusion.8
  30.9 0.9 constant_dynamic-update-slice_fusion.7
  31.7 0.8 constant_dynamic-update-slice_fusion.6
  32.6 0.9 collective-permute-start.14
  33.5 1.8 collective-permute-start.15
  35.3 25.0 %collective-permute-done.5 = bf16[256,1024]{1,0:T(8,128)(2,1)S(1)} collective-permute-done((bf16[256,1024]{1,0:T(8,128)(2,1)S(1)}, bf16[256,1024]{1,0:T(8,128)(2,1)S(1)}, u32[]{:S(2)}, u32[]{:S(2)}) %collective-permute-start.5) | collective-permute-done | bytes 524320 | tf_op jit(solution)/shard_map/ppermute | solution.py:39
  60.3 1.0 collective-permute-start.8
  61.3 1.8 collective-permute-start.9
  63.1 7.1 %collective-permute-done.10 = bf16[256,1024]{1,0:T(8,128)(2,1)S(1)} collective-permute-done((bf16[256,1024]{1,0:T(8,128)(2,1)S(1)}, bf16[256,1024]{1,0:T(8,128)(2,1)S(1)}, u32[]{:S(2)}, u32[]{:S(2)}) %collective-permute-start.10) | collective-permute-done | bytes 524320 | tf_op jit(solution)/shard_map/ppermute | solution.py:30
  70.1 5.4 %collective-permute-done.8 = bf16[256,1024]{1,0:T(8,128)(2,1)S(1)} collective-permute-done((bf16[256,1024]{1,0:T(8,128)(2,1)S(1)}, bf16[256,1024]{1,0:T(8,128)(2,1)S(1)}, u32[]{:S(2)}, u32[]{:S(2)}) %collective-permute-start.8) | collective-permute-done | bytes 524320 | tf_op jit(solution)/shard_map/ppermute | solution.py:30
  75.7 3.0 %collective-permute-start.13 = (bf16[2048,512]{1,0:T(8,128)(2,1)S(1)}, bf16[2048,512]{1,0:T(8,128)(2,1)}, u32[]{:S(2)}, u32[]{:S(2)}) collective-permute-start(bf16[2048,512]{1,0:T(8,128)(2,1)S(1)} %constant_dynamic-update-slice_fusion.4.first), channel_id=1, source_target_pairs={{0,64},{64,0},{1,65},{65,1},{2,66},{66,2},{3,67},{67,3},{4,68},{68... | collective-permute-start | bytes 6291464 | tf_op jit(solution)/shard_map/ppermute | solution.py:39
  78.7 0.8 constant_dynamic-update-slice_fusion.3
  79.6 0.8 constant_dynamic-update-slice_fusion.2
  80.4 0.8 constant_dynamic-update-slice_fusion.1
  81.2 0.8 constant_dynamic-update-slice_fusion
  82.0 0.9 collective-permute-start.11
  83.0 1.8 collective-permute-start.12
  85.4 11.0 %shard_map.111 = bf16[4096,512]{1,0:T(8,128)(2,1)} custom-call(s32[16]{0:T(128)} %stack.67.place, bf16[2048,512]{1,0:T(8,128)(2,1)} %first.1, bf16[2048,512]{1,0:T(8,128)(2,1)} %collective-permute-done.4.second), custom_call_target="tpu_custom_call" | custom-call | bytes 8388608 | tf_op jit(solution)/shard_map/pallas_call | solution.py:78
  96.4 1.3 slice.88
  97.8 3.3 %fusion.6 = f32[1024,512]{1,0:T(8,128)S(1)} fusion(bf16[1024,1024]{1,0:T(8,128)(2,1)} %constant_dynamic-update-slice_fusion.6, bf16[4096,512]{1,0:T(8,128)(2,1)} %shard_map.111), kind=kOutput, calls=%fused_computation.12 | convolution fusion | flops 1073741824 | bytes 5242880 | tf_op jit(solution)/shard_map/dot_general | solution.py:57
  101.1 1.3 slice.90
  102.4 2.7 %collective-permute-start.17 = (bf16[512,1024]{1,0:T(8,128)(2,1)S(1)}, bf16[512,1024]{1,0:T(8,128)(2,1)S(1)}, u32[]{:S(2)}, u32[]{:S(2)}) collective-permute-start(bf16[512,1024]{1,0:T(8,128)(2,1)S(1)} %slice.90), channel_id=1, source_target_pairs={{0,12},{4,0},{8,4},{12,8},{16,28},{20,16},{24,20},{28,24},{32,44},... | collective-permute-start | bytes 3145736 | tf_op jit(solution)/shard_map/ppermute | solution.py:30
  105.2 2.9 %fusion.2 = f32[1024,512]{1,0:T(8,128)S(1)} fusion(bf16[1024,1024]{1,0:T(8,128)(2,1)} %collective-permute-done.15, bf16[4096,512]{1,0:T(8,128)(2,1)S(1)} %copy-done.3), kind=kOutput, calls=%fused_computation.8 | convolution fusion | flops 1073741824 | bytes 5242880 | tf_op jit(solution)/shard_map/dot_general | solution.py:57
  108.0 2.9 %fusion.4 = f32[1024,512]{1,0:T(8,128)S(1)} fusion(bf16[1024,1024]{1,0:T(8,128)(2,1)} %collective-permute-done.14, bf16[4096,512]{1,0:T(8,128)(2,1)S(1)} %copy-done.3), kind=kOutput, calls=%fused_computation.10 | convolution fusion | flops 1073741824 | bytes 5242880 | tf_op jit(solution)/shard_map/dot_general | solution.py:57
  110.9 8.9 %collective-permute-done.16 = bf16[512,1024]{1,0:T(8,128)(2,1)S(1)} collective-permute-done((bf16[512,1024]{1,0:T(8,128)(2,1)S(1)}, bf16[512,1024]{1,0:T(8,128)(2,1)S(1)}, u32[]{:S(2)}, u32[]{:S(2)}) %collective-permute-start.16) | collective-permute-done | bytes 1048608 | tf_op jit(solution)/shard_map/ppermute | solution.py:30
  119.9 0.7 fusion.21
  120.6 2.2 %add_add_fusion = f32[1024,512]{1,0:T(8,128)} fusion(f32[1024,512]{1,0:T(8,128)S(1)} %fusion.21, f32[1024,512]{1,0:T(8,128)S(1)} %fusion.2, f32[1024,512]{1,0:T(8,128)S(1)} %fusion.6, f32[1024,512]{1,0:T(8,128)S(1)} %fusion.4, bf16[512,1024]{1,0:T(8,128)(2,1)S(1)} %collective-permute-done.17, bf16[4096,512]{1,0:T(8,128)(2,1)S(1)} %copy-done.3), kind=kOutput, calls=%fused_computation.5 | convolution fusion | flops 538968064 | bytes 12058624 | tf_op jit(solution)/shard_map/dot_general | solution.py:57
  122.8 11.0 %shard_map.110 = bf16[4096,512]{1,0:T(8,128)(2,1)} custom-call(s32[16]{0:T(128)} %stack.67.place, bf16[2048,512]{1,0:T(8,128)(2,1)} %copy-done.4, bf16[2048,512]{1,0:T(8,128)(2,1)} %collective-permute-done.13.second), custom_call_target="tpu_custom_call" | custom-call | bytes 8388608 | tf_op jit(solution)/shard_map/pallas_call | solution.py:78
  133.9 1.4 slice.78
  135.4 1.3 slice.81
  136.7 2.9 %collective-permute-start.19 = (bf16[512,1024]{1,0:T(8,128)(2,1)S(1)}, bf16[512,1024]{1,0:T(8,128)(2,1)S(1)}, u32[]{:S(2)}, u32[]{:S(2)}) collective-permute-start(bf16[512,1024]{1,0:T(8,128)(2,1)S(1)} %slice.81), channel_id=1, source_target_pairs={{0,12},{4,0},{8,4},{12,8},{16,28},{20,16},{24,20},{28,24},{32,44},... | collective-permute-start | bytes 3145736 | tf_op jit(solution)/shard_map/ppermute | solution.py:30
  139.7 2.9 %fusion.10 = f32[1024,512]{1,0:T(8,128)S(1)} fusion(bf16[1024,1024]{1,0:T(8,128)(2,1)} %collective-permute-done.11, bf16[4,1024,512]{2,1,0:T(8,128)(2,1)S(1)} %bitcast.48), kind=kOutput, calls=%fused_computation.16 | convolution fusion | flops 1073741824 | bytes 5242880 | tf_op jit(solution)/shard_map/dot_general | solution.py:57
  142.6 2.9 %fusion.8 = f32[1024,512]{1,0:T(8,128)S(1)} fusion(bf16[1024,1024]{1,0:T(8,128)(2,1)} %collective-permute-done.12, bf16[4,1024,512]{2,1,0:T(8,128)(2,1)S(1)} %bitcast.49), kind=kOutput, calls=%fused_computation.14 | convolution fusion | flops 1073741824 | bytes 5242880 | tf_op jit(solution)/shard_map/dot_general | solution.py:57
  145.5 2.9 %fusion.12 = f32[1024,512]{1,0:T(8,128)S(1)} fusion(bf16[1024,1024]{1,0:T(8,128)(2,1)} %constant_dynamic-update-slice_fusion, bf16[4,1024,512]{2,1,0:T(8,128)(2,1)S(1)} %bitcast.50), kind=kOutput, calls=%fused_computation.18 | convolution fusion | flops 1073741824 | bytes 5242880 | tf_op jit(solution)/shard_map/dot_general | solution.py:57
  148.4 2.2 %collective-permute-done.18 = bf16[512,1024]{1,0:T(8,128)(2,1)S(1)} collective-permute-done((bf16[512,1024]{1,0:T(8,128)(2,1)S(1)}, bf16[512,1024]{1,0:T(8,128)(2,1)S(1)}, u32[]{:S(2)}, u32[]{:S(2)}) %collective-permute-start.18) | collective-permute-done | bytes 1048608 | tf_op jit(solution)/shard_map/ppermute | solution.py:30
  150.6 0.8 fusion.27
  151.4 1.3 fusion
  152.8 12.5 %all_to_all.12 = f32[16,1,1024]{2,1,0:T(1,128)S(1)} all-to-all(f32[16,1,1024]{2,1,0:T(1,128)S(1)} %broadcast_in_dim.4), channel_id=1, replica_groups=mesh['zl'=2,'core'=2,'x'=4,'y'=4,'zh'=4] {'x','y'}, dimensions={0} | all-to-all | bytes 131072 | tf_op jit(solution)/shard_map/all_to_all | solution.py:96
  165.4 18.9 %all_to_all.13 = f32[16,1,640]{2,1,0:T(1,128)S(1)} all-to-all(f32[16,1,640]{2,1,0:T(1,128)S(1)} %broadcast_in_dim.5), channel_id=1, replica_groups=mesh['zl'=2,'core'=2,'x'=4,'y'=4,'zh'=4] {'zl','core','zh'}, dimensions={0} | all-to-all | bytes 81920 | tf_op jit(solution)/shard_map/all_to_all | solution.py:96
  185.7 5.5 %multiply_subtract_fusion.1 = (f32[1024,512]{1,0:T(8,128)}, bf16[1024,512]{1,0:T(8,128)(2,1)}, f32[1024,512]{1,0:T(8,128)}) fusion(f32[1024,512]{1,0:T(8,128)} %param.9, f32[1024,512]{1,0:T(8,128)S(1)} %get-tuple-element.62, f32[]{:T(128)S(6)} %div.25, f32[512]{0:T(512)S(1)} %multiply_add_fusion.2, f32[1024]{0:T(1024)S(1)} %get-tuple-element.52, ...), kind=kLoop, calls=%fused_computation.1 | loop fusion | flops 7340032 | bytes 12589060 | tf_op jit(solution)/shard_map/sub | solution.py:151
  (56 shorter events, 2.4 us)
Async XLA Ops:
  0.6 23.2 %collective-permute-start.4 = (bf16[2048,512]{1,0:T(8,128)(2,1)}, bf16[2048,512]{1,0:T(8,128)(2,1)}, u32[]{:S(2)}, u32[]{:S(2)}) collective-permute-start(bf16[2048,512]{1,0:T(8,128)(2,1)} %first.1), channel_id=1, source_target_pairs={{0,64},{64,0},{1,65},{65,1},{2,66},{66,2},{3,67},{67,3},{4,68},{68... | collective-permute-start | bytes 6291464 | tf_op jit(solution)/shard_map/ppermute | solution.py:39
  5.2 18.6 %copy-start = (bf16[2048,512]{1,0:T(8,128)(2,1)S(1)}, bf16[2048,512]{1,0:T(8,128)(2,1)}, u32[]{:S(2)}) copy-start(bf16[2048,512]{1,0:T(8,128)(2,1)} %first.1) | copy-start | bytes 6291460
  5.3 3.2 %collective-permute-start = (bf16[256,1024]{1,0:T(8,128)(2,1)S(1)}, bf16[256,1024]{1,0:T(8,128)(2,1)S(1)}, u32[]{:S(2)}, u32[]{:S(2)}) collective-permute-start(bf16[256,1024]{1,0:T(8,128)(2,1)S(1)} %pad_maximum_fusion), channel_id=1, source_target_pairs={{0,64},{64,0},{1,65},{65,1},{2,66},{66,2},{3,67},{67,3},{4,68},{68... | collective-permute-start | bytes 1572872 | tf_op jit(solution)/shard_map/ppermute | solution.py:39
  8.6 15.2 %collective-permute-start.1 = (bf16[256,1024]{1,0:T(8,128)(2,1)S(1)}, bf16[256,1024]{1,0:T(8,128)(2,1)S(1)}, u32[]{:S(2)}, u32[]{:S(2)}) collective-permute-start(bf16[256,1024]{1,0:T(8,128)(2,1)S(1)} %pad_maximum_fusion.1), channel_id=1, source_target_pairs={{0,16},{4,20},{8,24},{12,28},{16,32},{20,36},{24,40},{28,44},{32,4... | collective-permute-start | bytes 1572872 | tf_op jit(solution)/shard_map/ppermute | solution.py:30
  8.7 15.1 %collective-permute-start.2 = (bf16[256,1024]{1,0:T(8,128)(2,1)S(1)}, bf16[256,1024]{1,0:T(8,128)(2,1)S(1)}, u32[]{:S(2)}, u32[]{:S(2)}) collective-permute-start(bf16[256,1024]{1,0:T(8,128)(2,1)S(1)} %pad_maximum_fusion.1), channel_id=1, source_target_pairs={{0,48},{4,52},{8,56},{12,60},{16,0},{20,4},{24,8},{28,12},{32,16},... | collective-permute-start | bytes 1572872 | tf_op jit(solution)/shard_map/ppermute | solution.py:30
  11.3 12.5 %collective-permute-start.3 = (bf16[256,1024]{1,0:T(8,128)(2,1)S(1)}, bf16[256,1024]{1,0:T(8,128)(2,1)S(1)}, u32[]{:S(2)}, u32[]{:S(2)}) collective-permute-start(bf16[256,1024]{1,0:T(8,128)(2,1)S(1)} %pad_maximum_fusion.1), channel_id=1, source_target_pairs={{0,32},{4,36},{8,40},{12,44},{16,48},{20,52},{24,56},{28,60},{32,0... | collective-permute-start | bytes 1572872 | tf_op jit(solution)/shard_map/ppermute | solution.py:30
  24.0 36.3 %collective-permute-start.6 = (bf16[1024,512]{1,0:T(8,128)(2,1)S(1)}, bf16[1024,512]{1,0:T(8,128)(2,1)S(1)}, u32[]{:S(2)}, u32[]{:S(2)}) collective-permute-start(bf16[1024,512]{1,0:T(8,128)(2,1)S(1)} %get-tuple-element.55), channel_id=1, source_target_pairs={{0,128},{128,1},{1,129},{129,2},{2,130},{130,3},{3,131},{131,0},{4... | collective-permute-start | bytes 3145736 | tf_op jit(solution)/shard_map/ppermute | solution.py:35
  25.2 35.1 %collective-permute-start.7 = (bf16[1024,512]{1,0:T(8,128)(2,1)S(1)}, bf16[1024,512]{1,0:T(8,128)(2,1)S(1)}, u32[]{:S(2)}, u32[]{:S(2)}) collective-permute-start(bf16[1024,512]{1,0:T(8,128)(2,1)S(1)} %get-tuple-element.54), channel_id=1, source_target_pairs={{0,131},{128,0},{1,128},{129,1},{2,129},{130,2},{3,130},{131,3},{4... | collective-permute-start | bytes 3145736 | tf_op jit(solution)/shard_map/ppermute | solution.py:35
  32.6 63.8 %collective-permute-start.14 = (bf16[1024,1024]{1,0:T(8,128)(2,1)}, bf16[1024,1024]{1,0:T(8,128)(2,1)}, u32[]{:S(2)}, u32[]{:S(2)}) collective-permute-start(bf16[1024,1024]{1,0:T(8,128)(2,1)} %constant_dynamic-update-slice_fusion.6), channel_id=1, source_target_pairs={{0,4},{4,8},{8,12},{12,0},{16,20},{20,24},{24,28},{28,16},{32,36},... | collective-permute-start | bytes 6291464 | tf_op jit(solution)/shard_map/ppermute | solution.py:30
  33.5 26.8 %collective-permute-start.5 = (bf16[256,1024]{1,0:T(8,128)(2,1)S(1)}, bf16[256,1024]{1,0:T(8,128)(2,1)S(1)}, u32[]{:S(2)}, u32[]{:S(2)}) collective-permute-start(bf16[256,1024]{1,0:T(8,128)(2,1)S(1)} %pad_maximum_fusion.2), channel_id=1, source_target_pairs={{0,128},{128,0},{1,129},{129,1},{2,130},{130,2},{3,131},{131,3},{4... | collective-permute-start | bytes 1572872 | tf_op jit(solution)/shard_map/ppermute | solution.py:39
  33.5 67.6 %collective-permute-start.15 = (bf16[1024,1024]{1,0:T(8,128)(2,1)}, bf16[1024,1024]{1,0:T(8,128)(2,1)}, u32[]{:S(2)}, u32[]{:S(2)}) collective-permute-start(bf16[1024,1024]{1,0:T(8,128)(2,1)} %constant_dynamic-update-slice_fusion.6), channel_id=1, source_target_pairs={{0,12},{4,0},{8,4},{12,8},{16,28},{20,16},{24,20},{28,24},{32,44},... | collective-permute-start | bytes 6291464 | tf_op jit(solution)/shard_map/ppermute | solution.py:30
  60.3 9.9 %collective-permute-start.10 = (bf16[256,1024]{1,0:T(8,128)(2,1)S(1)}, bf16[256,1024]{1,0:T(8,128)(2,1)S(1)}, u32[]{:S(2)}, u32[]{:S(2)}) collective-permute-start(bf16[256,1024]{1,0:T(8,128)(2,1)S(1)} %collective-permute-done.5), channel_id=1, source_target_pairs={{0,32},{4,36},{8,40},{12,44},{16,48},{20,52},{24,56},{28,60},{32,0... | collective-permute-start | bytes 1572872 | tf_op jit(solution)/shard_map/ppermute | solution.py:30
  60.3 15.3 %collective-permute-start.8 = (bf16[256,1024]{1,0:T(8,128)(2,1)S(1)}, bf16[256,1024]{1,0:T(8,128)(2,1)S(1)}, u32[]{:S(2)}, u32[]{:S(2)}) collective-permute-start(bf16[256,1024]{1,0:T(8,128)(2,1)S(1)} %collective-permute-done.5), channel_id=1, source_target_pairs={{0,16},{4,20},{8,24},{12,28},{16,32},{20,36},{24,40},{28,44},{32,4... | collective-permute-start | bytes 1572872 | tf_op jit(solution)/shard_map/ppermute | solution.py:30
  61.3 14.3 %collective-permute-start.9 = (bf16[256,1024]{1,0:T(8,128)(2,1)S(1)}, bf16[256,1024]{1,0:T(8,128)(2,1)S(1)}, u32[]{:S(2)}, u32[]{:S(2)}) collective-permute-start(bf16[256,1024]{1,0:T(8,128)(2,1)S(1)} %collective-permute-done.5), channel_id=1, source_target_pairs={{0,48},{4,52},{8,56},{12,60},{16,0},{20,4},{24,8},{28,12},{32,16},... | collective-permute-start | bytes 1572872 | tf_op jit(solution)/shard_map/ppermute | solution.py:30
  75.7 6.3 %copy-start.4 = (bf16[2048,512]{1,0:T(8,128)(2,1)}, bf16[2048,512]{1,0:T(8,128)(2,1)S(1)}, u32[]{:S(2)}) copy-start(bf16[2048,512]{1,0:T(8,128)(2,1)S(1)} %constant_dynamic-update-slice_fusion.4.first) | copy-start | bytes 6291460
  75.7 47.1 %collective-permute-start.13 = (bf16[2048,512]{1,0:T(8,128)(2,1)S(1)}, bf16[2048,512]{1,0:T(8,128)(2,1)}, u32[]{:S(2)}, u32[]{:S(2)}) collective-permute-start(bf16[2048,512]{1,0:T(8,128)(2,1)S(1)} %constant_dynamic-update-slice_fusion.4.first), channel_id=1, source_target_pairs={{0,64},{64,0},{1,65},{65,1},{2,66},{66,2},{3,67},{67,3},{4,68},{68... | collective-permute-start | bytes 6291464 | tf_op jit(solution)/shard_map/ppermute | solution.py:39
  82.0 51.8 %collective-permute-start.11 = (bf16[1024,1024]{1,0:T(8,128)(2,1)}, bf16[1024,1024]{1,0:T(8,128)(2,1)}, u32[]{:S(2)}, u32[]{:S(2)}) collective-permute-start(bf16[1024,1024]{1,0:T(8,128)(2,1)} %constant_dynamic-update-slice_fusion), channel_id=1, source_target_pairs={{0,4},{4,8},{8,12},{12,0},{16,20},{20,24},{24,28},{28,16},{32,36},... | collective-permute-start | bytes 6291464 | tf_op jit(solution)/shard_map/ppermute | solution.py:30
  83.0 50.9 %collective-permute-start.12 = (bf16[1024,1024]{1,0:T(8,128)(2,1)}, bf16[1024,1024]{1,0:T(8,128)(2,1)}, u32[]{:S(2)}, u32[]{:S(2)}) collective-permute-start(bf16[1024,1024]{1,0:T(8,128)(2,1)} %constant_dynamic-update-slice_fusion), channel_id=1, source_target_pairs={{0,12},{4,0},{8,4},{12,8},{16,28},{20,16},{24,20},{28,24},{32,44},... | collective-permute-start | bytes 6291464 | tf_op jit(solution)/shard_map/ppermute | solution.py:30
  97.7 22.2 %collective-permute-start.16 = (bf16[512,1024]{1,0:T(8,128)(2,1)S(1)}, bf16[512,1024]{1,0:T(8,128)(2,1)S(1)}, u32[]{:S(2)}, u32[]{:S(2)}) collective-permute-start(bf16[512,1024]{1,0:T(8,128)(2,1)S(1)} %slice.88), channel_id=1, source_target_pairs={{0,4},{4,8},{8,12},{12,0},{16,20},{20,24},{24,28},{28,16},{32,36},... | collective-permute-start | bytes 3145736 | tf_op jit(solution)/shard_map/ppermute | solution.py:30
  97.8 7.3 %copy-start.3 = (bf16[4096,512]{1,0:T(8,128)(2,1)S(1)}, bf16[4096,512]{1,0:T(8,128)(2,1)}, u32[]{:S(2)}) copy-start(bf16[4096,512]{1,0:T(8,128)(2,1)} %shard_map.111) | copy-start | bytes 12582916
  102.4 18.2 %collective-permute-start.17 = (bf16[512,1024]{1,0:T(8,128)(2,1)S(1)}, bf16[512,1024]{1,0:T(8,128)(2,1)S(1)}, u32[]{:S(2)}, u32[]{:S(2)}) collective-permute-start(bf16[512,1024]{1,0:T(8,128)(2,1)S(1)} %slice.90), channel_id=1, source_target_pairs={{0,12},{4,0},{8,4},{12,8},{16,28},{20,16},{24,20},{28,24},{32,44},... | collective-permute-start | bytes 3145736 | tf_op jit(solution)/shard_map/ppermute | solution.py:30
  133.9 5.8 %copy-start.2 = (bf16[4096,512]{1,0:T(8,128)(2,1)S(1)}, bf16[4096,512]{1,0:T(8,128)(2,1)}, u32[]{:S(2)}) copy-start(bf16[4096,512]{1,0:T(8,128)(2,1)} %shard_map.110) | copy-start | bytes 12582916
  135.3 15.2 %collective-permute-start.18 = (bf16[512,1024]{1,0:T(8,128)(2,1)S(1)}, bf16[512,1024]{1,0:T(8,128)(2,1)S(1)}, u32[]{:S(2)}, u32[]{:S(2)}) collective-permute-start(bf16[512,1024]{1,0:T(8,128)(2,1)S(1)} %slice.78), channel_id=1, source_target_pairs={{0,4},{4,8},{8,12},{12,0},{16,20},{20,24},{24,28},{28,16},{32,36},... | collective-permute-start | bytes 3145736 | tf_op jit(solution)/shard_map/ppermute | solution.py:30
  136.7 14.7 %collective-permute-start.19 = (bf16[512,1024]{1,0:T(8,128)(2,1)S(1)}, bf16[512,1024]{1,0:T(8,128)(2,1)S(1)}, u32[]{:S(2)}, u32[]{:S(2)}) collective-permute-start(bf16[512,1024]{1,0:T(8,128)(2,1)S(1)} %slice.81), channel_id=1, source_target_pairs={{0,12},{4,0},{8,4},{12,8},{16,28},{20,16},{24,20},{28,24},{32,44},... | collective-permute-start | bytes 3145736 | tf_op jit(solution)/shard_map/ppermute | solution.py:30
  148.3 3.1 %copy-start.1 = (f32[1024,512]{1,0:T(8,128)S(1)}, f32[1024,512]{1,0:T(8,128)}, u32[]{:S(2)}) copy-start(f32[1024,512]{1,0:T(8,128)} %add_add_fusion) | copy-start | bytes 6291460
  151.3 14.0 %copy-start.8 = (f32[1024]{0:T(1024)S(1)}, f32[1024]{0:T(1024)}, u32[]{:S(2)}) copy-start(f32[1024]{0:T(1024)} %param.12) | copy-start | bytes 12292
  151.3 33.7 %copy-start.9 = (f32[512]{0:T(512)S(1)}, f32[512]{0:T(512)}, u32[]{:S(2)}) copy-start(f32[512]{0:T(512)} %param.13) | copy-start | bytes 6148
  151.3 34.3 %copy-start.5 = (bf16[1024,512]{1,0:T(8,128)(2,1)S(1)}, bf16[1024,512]{1,0:T(8,128)(2,1)}, u32[]{:S(2)}) copy-start(bf16[1024,512]{1,0:T(8,128)(2,1)} %param.10) | copy-start | bytes 3145732
  165.4 25.8 %copy-start.6 = (f32[1024]{0:T(1024)}, f32[1024]{0:T(1024)S(1)}, u32[]{:S(2)}) copy-start(f32[1024]{0:T(1024)S(1)} %get-tuple-element.52) | copy-start | bytes 12292
  185.0 6.2 %copy-start.7 = (f32[512]{0:T(512)}, f32[512]{0:T(512)S(1)}, u32[]{:S(2)}) copy-start(f32[512]{0:T(512)S(1)} %multiply_add_fusion.2) | copy-start | bytes 6148

commit v2 on v1

--- a/solution.py
+++ b/solution.py
@@ -39,18 +39,16 @@
     return lax.ppermute(array, axis, [(0, 1), (1, 0)])
 
 
-def first_ring(block):
-    return [block, shift(block, 0, 1), shift(block, 0, -1), shift(block, 0, 2)]
+def ring_start(block, phase):
+    return [block, shift(block, phase, 1), shift(block, phase, -1)]
 
 
-def second_start(block):
-    return [block, shift(block, 1, 1), shift(block, 1, -1)]
+def ring_end(blocks, phase, step):
+    return [*blocks, shift(blocks[1] if step == 1 else blocks[2], phase, step)]
 
 
-def second_end(blocks):
-    block, below, above = blocks
-    half = block.shape[0] // 2
-    return [*blocks, shift(below[:half], 1, 1), shift(above[half:], 1, -1)]
+def after(blocks, *others):
+    return lax.optimization_barrier((*blocks, *others))[: len(blocks)]
 
 
 def product(grad_rows, act_rows):
@@ -59,36 +57,34 @@
     )
 
 
-def add_products(total, groups, acts):
-    half = groups[3].shape[0]
-    for rows, cols in zip(groups, (*acts[:3], acts[3][:half], acts[3][half:])):
-        term = product(rows, cols)
-        total = term if total is None else total + term
-    return total
+def arrange_kernel(place, first, second, out, sems):
+    tokens = first.shape[0] // 16
+    copies = []
+    for i in range(16):
+        rows = pl.ds(pl.multiple_of(place[i] * tokens, tokens), tokens)
+        for c, source in enumerate((first, second)):
+            at = pl.ds((2 * i + c) * tokens, tokens)
+            copies.append(pltpu.make_async_copy(source.at[rows], out.at[at], sems.at[2 * i + c]))
+    for copy in copies:
+        copy.start()
+    for copy in copies:
+        copy.wait()
 
 
-def arrange_kernel(place, first, second, out):
-    tokens = first.shape[0]
-    out[:tokens] = first[...]
-    out[tokens:] = second[...]
-
-
-def arranged(places, first, second, tokens):
-    block = pl.BlockSpec((tokens, first.shape[1]), lambda i, place: (place[i], 0))
+def arranged(places, first, second):
+    rows, width = first.shape
+    anywhere = pl.BlockSpec(memory_space=pl.ANY)
     out = pl.pallas_call(
         arrange_kernel,
-        grid_spec=pltpu.PrefetchScalarGridSpec(
-            num_scalar_prefetch=1,
-            grid=(16,),
-            in_specs=[block, block],
-            out_specs=pl.BlockSpec((2 * tokens, first.shape[1]), lambda i, place: (i, 0)),
-        ),
-        out_shape=jax.ShapeDtypeStruct((32 * tokens, first.shape[1]), first.dtype),
+        in_specs=[pl.BlockSpec(memory_space=pltpu.SMEM), anywhere, anywhere],
+        out_specs=anywhere,
+        out_shape=jax.ShapeDtypeStruct((2 * rows, width), first.dtype),
+        scratch_shapes=[pltpu.SemaphoreType.DMA((32,))],
         cost_estimate=pl.CostEstimate(
-            flops=0, bytes_accessed=128 * tokens * first.shape[1], transcendentals=0
+            flops=0, bytes_accessed=8 * rows * width, transcendentals=0
         ),
     )(places, first, second)
-    return out.reshape(4, 8 * tokens, first.shape[1])
+    return out.reshape(4, rows // 2, width)
 
 
 def total_over(vector, axes):
@@ -108,7 +104,7 @@
     other = swap(jnp.concatenate([units(0, 1), units(1, 1)], axis=0), "core")
     tokens = other.shape[0] // 2
     near = jnp.concatenate([units(0, 0), other[:tokens]], axis=0)
-    away = jnp.concatenate([units(1, 0), other[tokens:]], axis=0)
+    away = swap(jnp.concatenate([units(1, 0), other[tokens:]], axis=0), "zl")
     acts_core = swap(activations, "core")
 
     places = []
@@ -118,24 +114,24 @@
             places.append((x + dx) % 4 * 4 + (y + dy) % 4)
     places = jnp.stack(places).astype(jnp.int32)
 
-    *near, acts_core, away, sent = lax.optimization_barrier(
-        (*first_ring(near), acts_core, away, activations)
-    )
-    near = second_start(jnp.concatenate(near, axis=0))
-    away = swap(away, "zl")
+    near = after(ring_end(ring_start(near, 0), 0, 1), away)
+    (sent,) = after((activations,), *near)
+    near = ring_start(jnp.concatenate(near, axis=0), 1)
+    away = ring_end(ring_start(away, 0), 0, -1)
     half = sent.shape[0] // 2
-    acts_below, acts_above = along_z(sent[:half], 1), along_z(sent[half:], -1)
-    away, acts_below, acts_above = lax.optimization_barrier((away, acts_below, acts_above))
-    *away, acts_below, acts_above = lax.optimization_barrier(
-        (*first_ring(away), acts_below, acts_above)
-    )
-    away = second_start(jnp.concatenate(away, axis=0))
-    near = second_end(near)
-    gradient = add_products(None, near, arranged(places, activations, acts_core, tokens))
-    acts_low = jnp.concatenate([acts_below, acts_above], axis=0)
-    acts_away = arranged(places, acts_low, swap(acts_low, "core"), tokens)
-    *away, acts_away, gradient = lax.optimization_barrier((*away, acts_away, gradient))
-    gradient = add_products(gradient, second_end(away), acts_away)
+    acts_low = (along_z(sent[:half], 1), along_z(sent[half:], -1))
+    first = arranged(places, activations, acts_core)
+    gradient = product(near[0], first[0]) + product(near[1], first[1]) + product(near[2], first[2])
+    near = ring_end(after(near, *away), 1, 1)
+    away = ring_start(jnp.concatenate(away, axis=0), 1)
+    away[2], gradient = lax.optimization_barrier((away[2], gradient))
+    away = ring_end(away, 1, -1)
+    acts_low = jnp.concatenate(after(acts_low, away[2]), axis=0)
+    second = arranged(places, acts_low, swap(acts_low, "core"))
+    gradient = gradient + product(near[3], first[3])
+    gradient = gradient + product(away[0], second[0]) + product(away[2], second[2])
+    last = lax.optimization_barrier((product(away[1], second[1]), product(away[3], second[3])))
+    gradient = gradient + (last[0] + last[1])
     gradient = gradient * token_scale
 
     squares = gradient * gradient + 1e-30

time: 192 us -> 398 us (2.07)
  Pallas kernels: 22 us -> 258 us
  waiting for transfers between devices: 64.2 us -> 35.2 us
    pallas_call x2, Pallas kernels: 22 us -> 258 us  [arranged(): pl.pallas_call(arrange_kernel, in_specs=[pl.BlockSpec(memory_space=pltpu....]
    ppermute x4, waiting for transfers between devices: 28.1 us -> 4.05 us  [swap(): return lax.ppermute(array, axis, [(0, 1), (1, 0)])]
    ppermute x14 -> x12, starting transfers between devices: 16.8 us -> 11 us  [shift(): return lax.ppermute(array, AXES, ring_pairs(phase, step))]
    ppermute x14 -> x12, waiting for transfers between devices: 36.1 us -> 31.1 us  [shift(): return lax.ppermute(array, AXES, ring_pairs(phase, step))]
    ppermute x4, starting transfers between devices: 6.46 us -> 11.5 us  [swap(): return lax.ppermute(array, axis, [(0, 1), (1, 0)])]
    dot_general x10 -> x8, matrix products: 22.7 us -> 25.7 us  [product(): lax.dot_general(grad_rows, act_rows, (((0,), (0,)), ((), ())), preferred_...]
  transfers between devices with their start and end apart: 20 -> 18, of which waited for: 8 -> 6; matrix products, arithmetic and copies ran while one was open for 18% -> 7% of each run, Pallas kernels for 12% -> 65%
where the time goes in v2:
time: 398 us
  Pallas kernels  258 us (65%)
  waiting for transfers between devices  35.2 us (9%)
  blocking collectives  32 us (8%)
  starting transfers between devices  26.6 us (7%)
  matrix products  25.7 us (6%)
  local copies, waits for them, and re-layouts  11.5 us (3%)
  other arithmetic  7.02 us (2%)
    pallas_call x2, Pallas kernels, arranged(): pl.pallas_call(arrange_kernel, in_specs=[pl.BlockSpec(memory_space=pltpu....  258 us
    all_to_all x2, blocking collectives, total_over(): return jnp.sum(lax.all_to_all(spread, axes, 0, 0, tiled=True), axis=0)  32 us
    ppermute x12, waiting for transfers between devices, shift(): return lax.ppermute(array, AXES, ring_pairs(phase, step))  31.1 us
    dot_general x8, matrix products, product(): lax.dot_general(grad_rows, act_rows, (((0,), (0,)), ((), ())), preferred_...  25.7 us
    ppermute x4, starting transfers between devices, swap(): return lax.ppermute(array, axis, [(0, 1), (1, 0)])  11.5 us
    ppermute x12, starting transfers between devices, shift(): return lax.ppermute(array, AXES, ring_pairs(phase, step))  11 us
  transfers between devices with their start and end apart: 18, of which 6 were waited for; matrix products, arithmetic and copies ran while one was open for 7% of the time, Pallas kernels for 65%

profile of v2, /device:TPU:1, one launch (start us, length us, event | category | flops | bytes accessed | tf_op | source)
XLA Modules:
  0.0 397.9 jit_solution(15295155508311309271)
XLA Ops:
  0.7 1.3 constant_dynamic-slice_fusion
  1.9 0.0 copy-start
  2.0 3.3 collective-permute-start
  5.3 1.5 collective-permute-done
  6.9 0.1 collective-permute-start.6
  7.1 1.3 collective-permute-start.1
  8.3 1.6 collective-permute-start.7
  9.9 6.6 %collective-permute-done.6 = bf16[256,1024]{1,0:T(8,128)(2,1)S(1)} collective-permute-done((bf16[256,1024]{1,0:T(8,128)(2,1)S(1)}, bf16[256,1024]{1,0:T(8,128)(2,1)S(1)}, u32[]{:S(2)}, u32[]{:S(2)}) %collective-permute-start.6) | collective-permute-done | bytes 524320 | tf_op jit(solution)/shard_map/ppermute | solution.py:30
  16.6 1.2 collective-permute-start.9
  17.8 2.5 collective-permute-done.1
  20.3 2.9 collective-permute-start.3
  23.2 2.9 collective-permute-done.8
  26.1 0.8 constant_dynamic-update-slice_fusion.7
  26.9 0.8 constant_dynamic-update-slice_fusion.6
  27.7 0.8 constant_dynamic-update-slice_fusion.5
  28.6 0.8 constant_dynamic-update-slice_fusion.4
  29.4 2.7 collective-permute-start.11
  32.1 0.6 collective-permute-start.4
  32.7 0.8 constant_dynamic-update-slice_fusion.3
  33.5 0.8 constant_dynamic-update-slice_fusion.2
  34.4 0.8 constant_dynamic-update-slice_fusion.1
  35.2 10.9 %collective-permute-done.4 = bf16[256,1024]{1,0:T(8,128)(2,1)S(1)} collective-permute-done((bf16[256,1024]{1,0:T(8,128)(2,1)S(1)}, bf16[256,1024]{1,0:T(8,128)(2,1)S(1)}, u32[]{:S(2)}, u32[]{:S(2)}) %collective-permute-start.4) | collective-permute-done | bytes 524320 | tf_op jit(solution)/shard_map/ppermute | solution.py:30
  46.0 0.8 constant_dynamic-update-slice_fusion
  46.9 0.6 stack.67.place
  47.5 1.5 fusion.19
  49.0 0.2 collective-permute-start.13
  49.2 4.0 collective-permute-start.14
  53.2 129.1 %shard_map.110 = bf16[4096,512]{1,0:T(8,128)(2,1)} custom-call(s32[16]{0:T(128)} %stack.67.place, bf16[2048,512]{1,0:T(8,128)(2,1)} %first.1, bf16[2048,512]{1,0:T(8,128)(2,1)} %collective-permute-done.9.second), custom_call_target="tpu_custom_call" | custom-call | bytes 8388608 | tf_op jit(solution)/shard_map/pallas_call | solution.py:77
  182.3 3.3 fusion.17
  185.6 0.1 collective-permute-start.12
  185.7 2.9 fusion.15
  188.6 2.9 add_add_fusion
  191.5 0.1 constant_dynamic-update-slice_fusion.9
  191.6 1.3 constant_dynamic-update-slice_fusion.8.first
  192.9 5.6 %collective-permute-start.15 = (bf16[2048,512]{1,0:T(8,128)(2,1)S(1)}, bf16[2048,512]{1,0:T(8,128)(2,1)}, u32[]{:S(2)}, u32[]{:S(2)}) collective-permute-start(bf16[2048,512]{1,0:T(8,128)(2,1)S(1)} %constant_dynamic-update-slice_fusion.8.first), channel_id=1, source_target_pairs={{0,64},{64,0},{1,65},{65,1},{2,66},{66,2},{3,67},{67,3},{4,68},{68... | collective-permute-start | bytes 6291464 | tf_op jit(solution)/shard_map/ppermute | solution.py:39
  198.5 3.1 collective-permute-start.17
  201.6 10.7 %collective-permute-done.12 = bf16[1024,1024]{1,0:T(8,128)(2,1)S(1)} collective-permute-done((bf16[1024,1024]{1,0:T(8,128)(2,1)}, bf16[1024,1024]{1,0:T(8,128)(2,1)S(1)}, u32[]{:S(2)}, u32[]{:S(2)}) %collective-permute-start.12) | collective-permute-done | bytes 2097184 | tf_op jit(solution)/shard_map/ppermute | solution.py:30
  212.3 2.6 fusion.9
  214.9 129.1 %shard_map.111 = bf16[4096,512]{1,0:T(8,128)(2,1)} custom-call(s32[16]{0:T(128)} %stack.67.place, bf16[2048,512]{1,0:T(8,128)(2,1)} %copy-done.3, bf16[2048,512]{1,0:T(8,128)(2,1)} %collective-permute-done.15.second), custom_call_target="tpu_custom_call" | custom-call | bytes 8388608 | tf_op jit(solution)/shard_map/pallas_call | solution.py:77
  344.1 3.3 fusion.6
  347.4 2.9 fusion.2
  350.3 3.0 fusion.4
  353.3 4.8 %fusion = (f32[512]{0:T(512)S(1)}, f32[1024]{0:T(1024)S(1)}, f32[1024,512]{1,0:T(8,128)}) fusion(f32[1024,512]{1,0:T(8,128)S(1)} %fusion.4, f32[1024,512]{1,0:T(8,128)S(1)} %fusion.2, f32[1024,512]{1,0:T(8,128)S(1)} %fusion.6, bf16[1024,1024]{1,0:T(8,128)(2,1)} %constant_dynamic-update-slice_fusion, bf16[4096,512]{1,0:T(8,128)(2,1)S(1)} %copy-done.1, ...), kind=kOutput, calls=%fused_computation.6 | convolution fusion | flops 1078983168 | bytes 15734784 | tf_op jit(solution)/shard_map/dot_general | solution.py:55
  358.2 10.3 %all_to_all.12 = f32[16,1,1024]{2,1,0:T(1,128)S(1)} all-to-all(f32[16,1,1024]{2,1,0:T(1,128)S(1)} %broadcast_in_dim.4), channel_id=1, replica_groups=mesh['zl'=2,'core'=2,'x'=4,'y'=4,'zh'=4] {'x','y'}, dimensions={0} | all-to-all | bytes 131072 | tf_op jit(solution)/shard_map/all_to_all | solution.py:92
  368.5 0.1 reduce_sum.55
  368.6 21.7 %all_to_all.13 = f32[16,1,640]{2,1,0:T(1,128)S(1)} all-to-all(f32[16,1,640]{2,1,0:T(1,128)S(1)} %broadcast_in_dim.5), channel_id=1, replica_groups=mesh['zl'=2,'core'=2,'x'=4,'y'=4,'zh'=4] {'zl','core','zh'}, dimensions={0} | all-to-all | bytes 81920 | tf_op jit(solution)/shard_map/all_to_all | solution.py:92
  390.4 0.6 slice_reduce_fusion
  391.7 6.2 %multiply_subtract_fusion.1 = (f32[1024,512]{1,0:T(8,128)}, bf16[1024,512]{1,0:T(8,128)(2,1)}, f32[1024,512]{1,0:T(8,128)}) fusion(f32[1024,512]{1,0:T(8,128)} %param.9, f32[1024,512]{1,0:T(8,128)} %get-tuple-element.44, f32[]{:T(128)S(6)} %div.25, f32[512]{0:T(512)S(1)} %multiply_add_fusion.2, f32[1024]{0:T(1024)S(1)} %get-tuple-element.34, ...), kind=kLoop, calls=%fused_computation.1 | loop fusion | flops 7340032 | bytes 12589060 | tf_op jit(solution)/shard_map/sub | solution.py:147
  (46 shorter events, 0.4 us)
Async XLA Ops:
  1.9 14.6 %copy-start = (bf16[2048,512]{1,0:T(8,128)(2,1)S(1)}, bf16[2048,512]{1,0:T(8,128)(2,1)}, u32[]{:S(2)}) copy-start(bf16[2048,512]{1,0:T(8,128)(2,1)} %first.1) | copy-start | bytes 6291460
  2.0 4.9 %collective-permute-start = (bf16[256,1024]{1,0:T(8,128)(2,1)S(1)}, bf16[256,1024]{1,0:T(8,128)(2,1)S(1)}, u32[]{:S(2)}, u32[]{:S(2)}) collective-permute-start(bf16[256,1024]{1,0:T(8,128)(2,1)S(1)} %pad_maximum_fusion), channel_id=1, source_target_pairs={{0,64},{64,0},{1,65},{65,1},{2,66},{66,2},{3,67},{67,3},{4,68},{68... | collective-permute-start | bytes 1572872 | tf_op jit(solution)/shard_map/ppermute | solution.py:39
  6.9 9.6 %collective-permute-start.6 = (bf16[256,1024]{1,0:T(8,128)(2,1)S(1)}, bf16[256,1024]{1,0:T(8,128)(2,1)S(1)}, u32[]{:S(2)}, u32[]{:S(2)}) collective-permute-start(bf16[256,1024]{1,0:T(8,128)(2,1)S(1)} %pad_maximum_fusion.2), channel_id=1, source_target_pairs={{0,16},{4,20},{8,24},{12,28},{16,32},{20,36},{24,40},{28,44},{32,4... | collective-permute-start | bytes 1572872 | tf_op jit(solution)/shard_map/ppermute | solution.py:30
  7.1 13.2 %collective-permute-start.1 = (bf16[256,1024]{1,0:T(8,128)(2,1)S(1)}, bf16[256,1024]{1,0:T(8,128)(2,1)S(1)}, u32[]{:S(2)}, u32[]{:S(2)}) collective-permute-start(bf16[256,1024]{1,0:T(8,128)(2,1)S(1)} %pad_maximum_fusion.1), channel_id=1, source_target_pairs={{0,128},{128,0},{1,129},{129,1},{2,130},{130,2},{3,131},{131,3},{4... | collective-permute-start | bytes 1572872 | tf_op jit(solution)/shard_map/ppermute | solution.py:39
  8.3 14.8 %collective-permute-start.7 = (bf16[256,1024]{1,0:T(8,128)(2,1)S(1)}, bf16[256,1024]{1,0:T(8,128)(2,1)S(1)}, u32[]{:S(2)}, u32[]{:S(2)}) collective-permute-start(bf16[256,1024]{1,0:T(8,128)(2,1)S(1)} %pad_maximum_fusion.2), channel_id=1, source_target_pairs={{0,48},{4,52},{8,56},{12,60},{16,0},{20,4},{24,8},{28,12},{32,16},... | collective-permute-start | bytes 1572872 | tf_op jit(solution)/shard_map/ppermute | solution.py:30
  16.5 9.5 %collective-permute-start.8 = (bf16[256,1024]{1,0:T(8,128)(2,1)S(1)}, bf16[256,1024]{1,0:T(8,128)(2,1)S(1)}, u32[]{:S(2)}, u32[]{:S(2)}) collective-permute-start(bf16[256,1024]{1,0:T(8,128)(2,1)S(1)} %collective-permute-done.6), channel_id=1, source_target_pairs={{0,16},{4,20},{8,24},{12,28},{16,32},{20,36},{24,40},{28,44},{32,4... | collective-permute-start | bytes 1572872 | tf_op jit(solution)/shard_map/ppermute | solution.py:30
  16.6 32.7 %collective-permute-start.9 = (bf16[2048,512]{1,0:T(8,128)(2,1)S(1)}, bf16[2048,512]{1,0:T(8,128)(2,1)}, u32[]{:S(2)}, u32[]{:S(2)}) collective-permute-start(bf16[2048,512]{1,0:T(8,128)(2,1)S(1)} %copy-done), channel_id=1, source_target_pairs={{0,64},{64,0},{1,65},{65,1},{2,66},{66,2},{3,67},{67,3},{4,68},{68... | collective-permute-start | bytes 6291464 | tf_op jit(solution)/shard_map/ppermute | solution.py:39
  20.3 11.8 %collective-permute-start.3 = (bf16[256,1024]{1,0:T(8,128)(2,1)S(1)}, bf16[256,1024]{1,0:T(8,128)(2,1)S(1)}, u32[]{:S(2)}, u32[]{:S(2)}) collective-permute-start(bf16[256,1024]{1,0:T(8,128)(2,1)S(1)} %collective-permute-done.1), channel_id=1, source_target_pairs={{0,48},{4,52},{8,56},{12,60},{16,0},{20,4},{24,8},{28,12},{32,16},... | collective-permute-start | bytes 1572872 | tf_op jit(solution)/shard_map/ppermute | solution.py:30
  23.2 10.4 %collective-permute-start.2 = (bf16[256,1024]{1,0:T(8,128)(2,1)S(1)}, bf16[256,1024]{1,0:T(8,128)(2,1)S(1)}, u32[]{:S(2)}, u32[]{:S(2)}) collective-permute-start(bf16[256,1024]{1,0:T(8,128)(2,1)S(1)} %collective-permute-done.1), channel_id=1, source_target_pairs={{0,16},{4,20},{8,24},{12,28},{16,32},{20,36},{24,40},{28,44},{32,4... | collective-permute-start | bytes 1572872 | tf_op jit(solution)/shard_map/ppermute | solution.py:30
  29.4 156.2 %collective-permute-start.10 = (bf16[1024,1024]{1,0:T(8,128)(2,1)}, bf16[1024,1024]{1,0:T(8,128)(2,1)}, u32[]{:S(2)}, u32[]{:S(2)}) collective-permute-start(bf16[1024,1024]{1,0:T(8,128)(2,1)} %constant_dynamic-update-slice_fusion.4), channel_id=1, source_target_pairs={{0,4},{4,8},{8,12},{12,0},{16,20},{20,24},{24,28},{28,16},{32,36},... | collective-permute-start | bytes 6291464 | tf_op jit(solution)/shard_map/ppermute | solution.py:30
  29.4 156.2 %collective-permute-start.11 = (bf16[1024,1024]{1,0:T(8,128)(2,1)}, bf16[1024,1024]{1,0:T(8,128)(2,1)}, u32[]{:S(2)}, u32[]{:S(2)}) collective-permute-start(bf16[1024,1024]{1,0:T(8,128)(2,1)} %constant_dynamic-update-slice_fusion.4), channel_id=1, source_target_pairs={{0,12},{4,0},{8,4},{12,8},{16,28},{20,16},{24,20},{28,24},{32,44},... | collective-permute-start | bytes 6291464 | tf_op jit(solution)/shard_map/ppermute | solution.py:30
  32.1 14.0 %collective-permute-start.4 = (bf16[256,1024]{1,0:T(8,128)(2,1)S(1)}, bf16[256,1024]{1,0:T(8,128)(2,1)S(1)}, u32[]{:S(2)}, u32[]{:S(2)}) collective-permute-start(bf16[256,1024]{1,0:T(8,128)(2,1)S(1)} %collective-permute-done.3), channel_id=1, source_target_pairs={{0,48},{4,52},{8,56},{12,60},{16,0},{20,4},{24,8},{28,12},{32,16},... | collective-permute-start | bytes 1572872 | tf_op jit(solution)/shard_map/ppermute | solution.py:30
  46.9 144.6 %collective-permute-start.5 = (bf16[1024,1024]{1,0:T(8,128)(2,1)}, bf16[1024,1024]{1,0:T(8,128)(2,1)}, u32[]{:S(2)}, u32[]{:S(2)}) collective-permute-start(bf16[1024,1024]{1,0:T(8,128)(2,1)} %constant_dynamic-update-slice_fusion), channel_id=1, source_target_pairs={{0,12},{4,0},{8,4},{12,8},{16,28},{20,16},{24,20},{28,24},{32,44},... | collective-permute-start | bytes 6291464 | tf_op jit(solution)/shard_map/ppermute | solution.py:30
  49.0 142.5 %collective-permute-start.13 = (bf16[1024,512]{1,0:T(8,128)(2,1)}, bf16[1024,512]{1,0:T(8,128)(2,1)S(1)}, u32[]{:S(2)}, u32[]{:S(2)}) collective-permute-start(bf16[1024,512]{1,0:T(8,128)(2,1)} %get-tuple-element.37), channel_id=1, source_target_pairs={{0,128},{128,1},{1,129},{129,2},{2,130},{130,3},{3,131},{131,0},{4... | collective-permute-start | bytes 3145736 | tf_op jit(solution)/shard_map/ppermute | solution.py:35
  49.2 142.3 %collective-permute-start.14 = (bf16[1024,512]{1,0:T(8,128)(2,1)}, bf16[1024,512]{1,0:T(8,128)(2,1)}, u32[]{:S(2)}, u32[]{:S(2)}) collective-permute-start(bf16[1024,512]{1,0:T(8,128)(2,1)} %get-tuple-element.36), channel_id=1, source_target_pairs={{0,131},{128,0},{1,128},{129,1},{2,129},{130,2},{3,130},{131,3},{4... | collective-permute-start | bytes 3145736 | tf_op jit(solution)/shard_map/ppermute | solution.py:35
  182.3 3.4 copy-start.2
  185.6 26.7 %collective-permute-start.12 = (bf16[1024,1024]{1,0:T(8,128)(2,1)}, bf16[1024,1024]{1,0:T(8,128)(2,1)S(1)}, u32[]{:S(2)}, u32[]{:S(2)}) collective-permute-start(bf16[1024,1024]{1,0:T(8,128)(2,1)} %collective-permute-done.10), channel_id=1, source_target_pairs={{0,4},{4,8},{8,12},{12,0},{16,20},{20,24},{24,28},{28,16},{32,36},... | collective-permute-start | bytes 6291464 | tf_op jit(solution)/shard_map/ppermute | solution.py:30
  192.9 22.0 %copy-start.3 = (bf16[2048,512]{1,0:T(8,128)(2,1)}, bf16[2048,512]{1,0:T(8,128)(2,1)S(1)}, u32[]{:S(2)}) copy-start(bf16[2048,512]{1,0:T(8,128)(2,1)S(1)} %constant_dynamic-update-slice_fusion.8.first) | copy-start | bytes 6291460
  192.9 22.0 %collective-permute-start.15 = (bf16[2048,512]{1,0:T(8,128)(2,1)S(1)}, bf16[2048,512]{1,0:T(8,128)(2,1)}, u32[]{:S(2)}, u32[]{:S(2)}) collective-permute-start(bf16[2048,512]{1,0:T(8,128)(2,1)S(1)} %constant_dynamic-update-slice_fusion.8.first), channel_id=1, source_target_pairs={{0,64},{64,0},{1,65},{65,1},{2,66},{66,2},{3,67},{67,3},{4,68},{68... | collective-permute-start | bytes 6291464 | tf_op jit(solution)/shard_map/ppermute | solution.py:39
  198.5 148.8 %collective-permute-start.17 = (bf16[1024,1024]{1,0:T(8,128)(2,1)}, bf16[1024,1024]{1,0:T(8,128)(2,1)}, u32[]{:S(2)}, u32[]{:S(2)}) collective-permute-start(bf16[1024,1024]{1,0:T(8,128)(2,1)} %collective-permute-done.5), channel_id=1, source_target_pairs={{0,12},{4,0},{8,4},{12,8},{16,28},{20,16},{24,20},{28,24},{32,44},... | collective-permute-start | bytes 6291464 | tf_op jit(solution)/shard_map/ppermute | solution.py:30
  201.6 148.6 %collective-permute-start.16 = (bf16[1024,1024]{1,0:T(8,128)(2,1)}, bf16[1024,1024]{1,0:T(8,128)(2,1)}, u32[]{:S(2)}, u32[]{:S(2)}) collective-permute-start(bf16[1024,1024]{1,0:T(8,128)(2,1)} %constant_dynamic-update-slice_fusion), channel_id=1, source_target_pairs={{0,4},{4,8},{8,12},{12,0},{16,20},{20,24},{24,28},{28,16},{32,36},... | collective-permute-start | bytes 6291464 | tf_op jit(solution)/shard_map/ppermute | solution.py:30
  344.1 3.3 copy-start.1
  350.3 3.0 copy-start.4
  353.3 15.3 %copy-start.8 = (f32[1024]{0:T(1024)S(1)}, f32[1024]{0:T(1024)}, u32[]{:S(2)}) copy-start(f32[1024]{0:T(1024)} %param.12) | copy-start | bytes 12292
  353.3 37.7 %copy-start.9 = (f32[512]{0:T(512)S(1)}, f32[512]{0:T(512)}, u32[]{:S(2)}) copy-start(f32[512]{0:T(512)} %param.13) | copy-start | bytes 6148
  353.3 38.3 %copy-start.5 = (bf16[1024,512]{1,0:T(8,128)(2,1)S(1)}, bf16[1024,512]{1,0:T(8,128)(2,1)}, u32[]{:S(2)}) copy-start(bf16[1024,512]{1,0:T(8,128)(2,1)} %param.10) | copy-start | bytes 3145732
  368.6 29.3 %copy-start.6 = (f32[1024]{0:T(1024)}, f32[1024]{0:T(1024)S(1)}, u32[]{:S(2)}) copy-start(f32[1024]{0:T(1024)S(1)} %get-tuple-element.34) | copy-start | bytes 12292
  391.0 6.9 %copy-start.7 = (f32[512]{0:T(512)}, f32[512]{0:T(512)S(1)}, u32[]{:S(2)}) copy-start(f32[512]{0:T(512)S(1)} %multiply_add_fusion.2) | copy-start | bytes 6148

commit v3 on v2

--- a/solution.py
+++ b/solution.py
@@ -77,9 +77,10 @@
     out = pl.pallas_call(
         arrange_kernel,
         in_specs=[pl.BlockSpec(memory_space=pltpu.SMEM), anywhere, anywhere],
-        out_specs=anywhere,
+        out_specs=pl.BlockSpec(memory_space=pltpu.VMEM),
         out_shape=jax.ShapeDtypeStruct((2 * rows, width), first.dtype),
         scratch_shapes=[pltpu.SemaphoreType.DMA((32,))],
+        compiler_params=pltpu.CompilerParams(vmem_limit_bytes=8 << 20),
         cost_estimate=pl.CostEstimate(
             flops=0, bytes_accessed=8 * rows * width, transcendentals=0
         ),

time: 398 us -> 154 us (0.39)
  Pallas kernels: 258 us -> 10.8 us
  waiting for transfers between devices: 35.2 us -> 57.5 us
  matrix products: 25.7 us -> 18.9 us
  starting transfers between devices: 26.6 us -> 22.1 us
  blocking collectives: 32 us -> 27.8 us
    pallas_call x2, Pallas kernels: 258 us -> 10.8 us  [arranged(): pl.pallas_call(arrange_kernel, in_specs=[pl.BlockSpec(memory_space=pltpu....]
    ppermute x12, waiting for transfers between devices: 31.1 us -> 53.1 us  [shift(): return lax.ppermute(array, AXES, ring_pairs(phase, step))]
    dot_general x8, matrix products: 25.7 us -> 18.9 us  [product(): lax.dot_general(grad_rows, act_rows, (((0,), (0,)), ((), ())), preferred_...]
    all_to_all x2, blocking collectives: 32 us -> 27.8 us  [total_over(): return jnp.sum(lax.all_to_all(spread, axes, 0, 0, tiled=True), axis=0)]
  transfers between devices with their start and end apart: 18 -> 18, of which waited for: 6 -> 11; matrix products, arithmetic and copies ran while one was open for 7% -> 14% of each run, Pallas kernels for 65% -> 7%
where the time goes in v3:
time: 154 us; the launch traced here: 153 us
  waiting for transfers between devices  57.5 us (37%)
  blocking collectives  27.8 us (18%)
  starting transfers between devices  22.1 us (14%)
  matrix products  18.9 us (12%)
  Pallas kernels  10.8 us (7%)
  local copies, waits for them, and re-layouts  8.38 us (5%)
  other arithmetic  6.37 us (4%)
    ppermute x12, waiting for transfers between devices, shift(): return lax.ppermute(array, AXES, ring_pairs(phase, step))  53.1 us
    all_to_all x2, blocking collectives, total_over(): return jnp.sum(lax.all_to_all(spread, axes, 0, 0, tiled=True), axis=0)  27.8 us
    dot_general x8, matrix products, product(): lax.dot_general(grad_rows, act_rows, (((0,), (0,)), ((), ())), preferred_...  18.9 us
    pallas_call x2, Pallas kernels, arranged(): pl.pallas_call(arrange_kernel, in_specs=[pl.BlockSpec(memory_space=pltpu....  10.8 us
    ppermute x12, starting transfers between devices, shift(): return lax.ppermute(array, AXES, ring_pairs(phase, step))  9.29 us
    ppermute x4, starting transfers between devices, swap(): return lax.ppermute(array, axis, [(0, 1), (1, 0)])  8.3 us
    sub x1, other arithmetic, local(): weights_new = weights - 0.01 * momentum_new.astype(jnp.float32)  5.53 us
    unnamed x19, local copies, waits for them, and re-layouts  5.06 us
  transfers between devices with their start and end apart: 18, of which 11 were waited for; matrix products, arithmetic and copies ran while one was open for 14% of the time, Pallas kernels for 7%

profile of v3, /device:TPU:1, one launch (start us, length us, event | category | flops | bytes accessed | tf_op | source)
XLA Modules:
  0.0 153.4 jit_solution(9004031336261072844)
XLA Ops:
  0.7 1.3 constant_dynamic-slice_fusion
  2.0 3.3 %collective-permute-start = (bf16[256,1024]{1,0:T(8,128)(2,1)S(1)}, bf16[256,1024]{1,0:T(8,128)(2,1)S(1)}, u32[]{:S(2)}, u32[]{:S(2)}) collective-permute-start(bf16[256,1024]{1,0:T(8,128)(2,1)S(1)} %pad_maximum_fusion), channel_id=1, source_target_pairs={{0,64},{64,0},{1,65},{65,1},{2,66},{66,2},{3,67},{67,3},{4,68},{68... | collective-permute-start | bytes 1572872 | tf_op jit(solution)/shard_map/ppermute | solution.py:39
  5.3 1.5 %collective-permute-done = bf16[256,1024]{1,0:T(8,128)(2,1)S(1)} collective-permute-done((bf16[256,1024]{1,0:T(8,128)(2,1)S(1)}, bf16[256,1024]{1,0:T(8,128)(2,1)S(1)}, u32[]{:S(2)}, u32[]{:S(2)}) %collective-permute-start) | collective-permute-done | bytes 524320 | tf_op jit(solution)/shard_map/ppermute | solution.py:39
  7.1 1.3 collective-permute-start.1
  8.3 1.6 %collective-permute-start.7 = (bf16[256,1024]{1,0:T(8,128)(2,1)S(1)}, bf16[256,1024]{1,0:T(8,128)(2,1)S(1)}, u32[]{:S(2)}, u32[]{:S(2)}) collective-permute-start(bf16[256,1024]{1,0:T(8,128)(2,1)S(1)} %pad_maximum_fusion.2), channel_id=1, source_target_pairs={{0,48},{4,52},{8,56},{12,60},{16,0},{20,4},{24,8},{28,12},{32,16},... | collective-permute-start | bytes 1572872 | tf_op jit(solution)/shard_map/ppermute | solution.py:30
  9.9 6.6 %collective-permute-done.6 = bf16[256,1024]{1,0:T(8,128)(2,1)S(1)} collective-permute-done((bf16[256,1024]{1,0:T(8,128)(2,1)S(1)}, bf16[256,1024]{1,0:T(8,128)(2,1)S(1)}, u32[]{:S(2)}, u32[]{:S(2)}) %collective-permute-start.6) | collective-permute-done | bytes 524320 | tf_op jit(solution)/shard_map/ppermute | solution.py:30
  16.6 1.2 collective-permute-start.9
  17.8 2.5 %collective-permute-done.1 = bf16[256,1024]{1,0:T(8,128)(2,1)S(1)} collective-permute-done((bf16[256,1024]{1,0:T(8,128)(2,1)S(1)}, bf16[256,1024]{1,0:T(8,128)(2,1)S(1)}, u32[]{:S(2)}, u32[]{:S(2)}) %collective-permute-start.1) | collective-permute-done | bytes 524320 | tf_op jit(solution)/shard_map/ppermute | solution.py:39
  20.3 2.9 %collective-permute-start.3 = (bf16[256,1024]{1,0:T(8,128)(2,1)S(1)}, bf16[256,1024]{1,0:T(8,128)(2,1)S(1)}, u32[]{:S(2)}, u32[]{:S(2)}) collective-permute-start(bf16[256,1024]{1,0:T(8,128)(2,1)S(1)} %collective-permute-done.1), channel_id=1, source_target_pairs={{0,48},{4,52},{8,56},{12,60},{16,0},{20,4},{24,8},{28,12},{32,16},... | collective-permute-start | bytes 1572872 | tf_op jit(solution)/shard_map/ppermute | solution.py:30
  23.2 2.9 %collective-permute-done.8 = bf16[256,1024]{1,0:T(8,128)(2,1)S(1)} collective-permute-done((bf16[256,1024]{1,0:T(8,128)(2,1)S(1)}, bf16[256,1024]{1,0:T(8,128)(2,1)S(1)}, u32[]{:S(2)}, u32[]{:S(2)}) %collective-permute-start.8) | collective-permute-done | bytes 524320 | tf_op jit(solution)/shard_map/ppermute | solution.py:30
  26.1 0.8 constant_dynamic-update-slice_fusion.7
  26.9 0.8 constant_dynamic-update-slice_fusion.6
  27.7 0.8 constant_dynamic-update-slice_fusion.5
  28.6 0.8 constant_dynamic-update-slice_fusion.4
  29.4 2.7 %collective-permute-start.11 = (bf16[1024,1024]{1,0:T(8,128)(2,1)}, bf16[1024,1024]{1,0:T(8,128)(2,1)}, u32[]{:S(2)}, u32[]{:S(2)}) collective-permute-start(bf16[1024,1024]{1,0:T(8,128)(2,1)} %constant_dynamic-update-slice_fusion.4), channel_id=1, source_target_pairs={{0,12},{4,0},{8,4},{12,8},{16,28},{20,16},{24,20},{28,24},{32,44},... | collective-permute-start | bytes 6291464 | tf_op jit(solution)/shard_map/ppermute | solution.py:30
  32.1 0.6 collective-permute-start.4
  32.7 0.8 constant_dynamic-update-slice_fusion.3
  33.5 0.8 constant_dynamic-update-slice_fusion.2
  34.4 0.8 constant_dynamic-update-slice_fusion.1
  35.2 10.9 %collective-permute-done.4 = bf16[256,1024]{1,0:T(8,128)(2,1)S(1)} collective-permute-done((bf16[256,1024]{1,0:T(8,128)(2,1)S(1)}, bf16[256,1024]{1,0:T(8,128)(2,1)S(1)}, u32[]{:S(2)}, u32[]{:S(2)}) %collective-permute-start.4) | collective-permute-done | bytes 524320 | tf_op jit(solution)/shard_map/ppermute | solution.py:30
  46.0 0.8 constant_dynamic-update-slice_fusion
  46.9 0.1 stack.67.place
  47.0 0.1 fusion.19
  47.1 0.3 collective-permute-start.13
  47.4 4.2 %collective-permute-start.14 = (bf16[1024,512]{1,0:T(8,128)(2,1)S(1)}, bf16[1024,512]{1,0:T(8,128)(2,1)S(1)}, u32[]{:S(2)}, u32[]{:S(2)}) collective-permute-start(bf16[1024,512]{1,0:T(8,128)(2,1)S(1)} %get-tuple-element.36), channel_id=1, source_target_pairs={{0,131},{128,0},{1,128},{129,1},{2,129},{130,2},{3,130},{131,3},{4... | collective-permute-start | bytes 3145736 | tf_op jit(solution)/shard_map/ppermute | solution.py:35
  51.6 4.5 %shard_map.110 = bf16[4096,512]{1,0:T(8,128)(2,1)S(1)} custom-call(s32[16]{0:T(128)S(1)} %stack.67.place, bf16[2048,512]{1,0:T(8,128)(2,1)S(1)} %copy-done, bf16[2048,512]{1,0:T(8,128)(2,1)} %collective-permute-done.9.second), custom_call_target="tpu_custom_call" | custom-call | bytes 8388608 | tf_op jit(solution)/shard_map/pallas_call | solution.py:77
  56.1 2.9 %fusion.17 = f32[1024,512]{1,0:T(8,128)S(1)} fusion(bf16[1024,1024]{1,0:T(8,128)(2,1)} %constant_dynamic-update-slice_fusion.4, bf16[4096,512]{1,0:T(8,128)(2,1)S(1)} %shard_map.110), kind=kOutput, calls=%fused_computation.21 | convolution fusion | flops 1073741824 | bytes 5242880 | tf_op jit(solution)/shard_map/dot_general | solution.py:55
  59.0 1.9 %collective-permute-done.11 = bf16[1024,1024]{1,0:T(8,128)(2,1)} collective-permute-done((bf16[1024,1024]{1,0:T(8,128)(2,1)}, bf16[1024,1024]{1,0:T(8,128)(2,1)}, u32[]{:S(2)}, u32[]{:S(2)}) %collective-permute-start.11) | collective-permute-done | bytes 2097184 | tf_op jit(solution)/shard_map/ppermute | solution.py:30
  61.0 2.9 %fusion.15 = f32[1024,512]{1,0:T(8,128)S(1)} fusion(bf16[1024,1024]{1,0:T(8,128)(2,1)} %collective-permute-done.10, bf16[4096,512]{1,0:T(8,128)(2,1)S(1)} %shard_map.110), kind=kOutput, calls=%fused_computation.19 | convolution fusion | flops 1073741824 | bytes 5242880 | tf_op jit(solution)/shard_map/dot_general | solution.py:55
  63.9 2.9 %add_add_fusion = f32[1024,512]{1,0:T(8,128)S(1)} fusion(f32[1024,512]{1,0:T(8,128)S(1)} %fusion.17, f32[1024,512]{1,0:T(8,128)S(1)} %fusion.15, bf16[1024,1024]{1,0:T(8,128)(2,1)} %collective-permute-done.11, bf16[4096,512]{1,0:T(8,128)(2,1)S(1)} %shard_map.110), kind=kOutput, calls=%fused_computation.5 | convolution fusion | flops 1074790400 | bytes 9437184 | tf_op jit(solution)/shard_map/dot_general | solution.py:55
  66.8 16.7 %collective-permute-done.5 = bf16[1024,1024]{1,0:T(8,128)(2,1)} collective-permute-done((bf16[1024,1024]{1,0:T(8,128)(2,1)}, bf16[1024,1024]{1,0:T(8,128)(2,1)}, u32[]{:S(2)}, u32[]{:S(2)}) %collective-permute-start.5) | collective-permute-done | bytes 2097184 | tf_op jit(solution)/shard_map/ppermute | solution.py:30
  83.6 2.5 %collective-permute-start.15 = (bf16[2048,512]{1,0:T(8,128)(2,1)S(1)}, bf16[2048,512]{1,0:T(8,128)(2,1)S(1)}, u32[]{:S(2)}, u32[]{:S(2)}) collective-permute-start(bf16[2048,512]{1,0:T(8,128)(2,1)S(1)} %constant_dynamic-update-slice_fusion.8.first), channel_id=1, source_target_pairs={{0,64},{64,0},{1,65},{65,1},{2,66},{66,2},{3,67},{67,3},{4,68},{68... | collective-permute-start | bytes 6291464 | tf_op jit(solution)/shard_map/ppermute | solution.py:39
  86.1 1.0 collective-permute-start.17
  87.1 0.5 collective-permute-start.16
  87.6 0.7 collective-permute-done.12
  88.2 1.3 fusion.9
  89.5 0.4 collective-permute-done.15.second
  89.9 6.3 %shard_map.111 = bf16[4096,512]{1,0:T(8,128)(2,1)S(1)} custom-call(s32[16]{0:T(128)S(1)} %stack.67.place, bf16[2048,512]{1,0:T(8,128)(2,1)S(1)} %constant_dynamic-update-slice_fusion.8.first, bf16[2048,512]{1,0:T(8,128)(2,1)S(1)} %collective-permute-done.15.second), custom_call_target="tpu_custom_call" | custom-call | bytes 8388608 | tf_op jit(solution)/shard_map/pallas_call | solution.py:77
  96.2 2.9 %fusion.6 = f32[1024,512]{1,0:T(8,128)S(1)} fusion(bf16[1024,1024]{1,0:T(8,128)(2,1)} %collective-permute-done.5, bf16[4096,512]{1,0:T(8,128)(2,1)S(1)} %shard_map.111), kind=kOutput, calls=%fused_computation.12 | convolution fusion | flops 1073741824 | bytes 5242880 | tf_op jit(solution)/shard_map/dot_general | solution.py:55
  99.1 12.4 %collective-permute-done.17 = bf16[1024,1024]{1,0:T(8,128)(2,1)S(1)} collective-permute-done((bf16[1024,1024]{1,0:T(8,128)(2,1)}, bf16[1024,1024]{1,0:T(8,128)(2,1)S(1)}, u32[]{:S(2)}, u32[]{:S(2)}) %collective-permute-start.17) | collective-permute-done | bytes 2097184 | tf_op jit(solution)/shard_map/ppermute | solution.py:30
  111.5 1.3 fusion.2
  112.8 0.9 collective-permute-done.16
  113.7 1.3 fusion.4
  115.0 3.6 %fusion = (f32[512]{0:T(512)S(1)}, f32[1024]{0:T(1024)S(1)}, f32[1024,512]{1,0:T(8,128)S(1)}) fusion(f32[1024,512]{1,0:T(8,128)S(1)} %fusion.4, f32[1024,512]{1,0:T(8,128)S(1)} %fusion.2, f32[1024,512]{1,0:T(8,128)S(1)} %fusion.6, bf16[1024,1024]{1,0:T(8,128)(2,1)} %constant_dynamic-update-slice_fusion, bf16[4096,512]{1,0:T(8,128)(2,1)S(1)} %shard_map.111, ...), kind=kOutput, calls=%fused_computation.6 | convolution fusion | flops 1078983168 | bytes 15734784 | tf_op jit(solution)/shard_map/dot_general | solution.py:55
  118.6 10.0 %all_to_all.12 = f32[16,1,1024]{2,1,0:T(1,128)S(1)} all-to-all(f32[16,1,1024]{2,1,0:T(1,128)S(1)} %broadcast_in_dim.4), channel_id=1, replica_groups=mesh['zl'=2,'core'=2,'x'=4,'y'=4,'zh'=4] {'x','y'}, dimensions={0} | all-to-all | bytes 131072 | tf_op jit(solution)/shard_map/all_to_all | solution.py:93
  128.8 17.8 %all_to_all.13 = f32[16,1,640]{2,1,0:T(1,128)S(1)} all-to-all(f32[16,1,640]{2,1,0:T(1,128)S(1)} %broadcast_in_dim.5), channel_id=1, replica_groups=mesh['zl'=2,'core'=2,'x'=4,'y'=4,'zh'=4] {'zl','core','zh'}, dimensions={0} | all-to-all | bytes 81920 | tf_op jit(solution)/shard_map/all_to_all | solution.py:93
  146.6 0.6 slice_reduce_fusion
  147.9 5.5 %multiply_subtract_fusion.1 = (f32[1024,512]{1,0:T(8,128)}, bf16[1024,512]{1,0:T(8,128)(2,1)}, f32[1024,512]{1,0:T(8,128)}) fusion(f32[1024,512]{1,0:T(8,128)} %param.9, f32[1024,512]{1,0:T(8,128)S(1)} %get-tuple-element.44, f32[]{:T(128)S(6)} %div.25, f32[512]{0:T(512)S(1)} %multiply_add_fusion.2, f32[1024]{0:T(1024)S(1)} %get-tuple-element.34, ...), kind=kLoop, calls=%fused_computation.1 | loop fusion | flops 7340032 | bytes 12589060 | tf_op jit(solution)/shard_map/sub | solution.py:148
  (38 shorter events, 0.6 us)
Async XLA Ops:
  1.9 14.6 %copy-start = (bf16[2048,512]{1,0:T(8,128)(2,1)S(1)}, bf16[2048,512]{1,0:T(8,128)(2,1)}, u32[]{:S(2)}) copy-start(bf16[2048,512]{1,0:T(8,128)(2,1)} %first.1) | copy-start | bytes 6291460
  2.0 4.9 %collective-permute-start = (bf16[256,1024]{1,0:T(8,128)(2,1)S(1)}, bf16[256,1024]{1,0:T(8,128)(2,1)S(1)}, u32[]{:S(2)}, u32[]{:S(2)}) collective-permute-start(bf16[256,1024]{1,0:T(8,128)(2,1)S(1)} %pad_maximum_fusion), channel_id=1, source_target_pairs={{0,64},{64,0},{1,65},{65,1},{2,66},{66,2},{3,67},{67,3},{4,68},{68... | collective-permute-start | bytes 1572872 | tf_op jit(solution)/shard_map/ppermute | solution.py:39
  6.9 9.6 %collective-permute-start.6 = (bf16[256,1024]{1,0:T(8,128)(2,1)S(1)}, bf16[256,1024]{1,0:T(8,128)(2,1)S(1)}, u32[]{:S(2)}, u32[]{:S(2)}) collective-permute-start(bf16[256,1024]{1,0:T(8,128)(2,1)S(1)} %pad_maximum_fusion.2), channel_id=1, source_target_pairs={{0,16},{4,20},{8,24},{12,28},{16,32},{20,36},{24,40},{28,44},{32,4... | collective-permute-start | bytes 1572872 | tf_op jit(solution)/shard_map/ppermute | solution.py:30
  7.1 13.2 %collective-permute-start.1 = (bf16[256,1024]{1,0:T(8,128)(2,1)S(1)}, bf16[256,1024]{1,0:T(8,128)(2,1)S(1)}, u32[]{:S(2)}, u32[]{:S(2)}) collective-permute-start(bf16[256,1024]{1,0:T(8,128)(2,1)S(1)} %pad_maximum_fusion.1), channel_id=1, source_target_pairs={{0,128},{128,0},{1,129},{129,1},{2,130},{130,2},{3,131},{131,3},{4... | collective-permute-start | bytes 1572872 | tf_op jit(solution)/shard_map/ppermute | solution.py:39
  8.3 14.8 %collective-permute-start.7 = (bf16[256,1024]{1,0:T(8,128)(2,1)S(1)}, bf16[256,1024]{1,0:T(8,128)(2,1)S(1)}, u32[]{:S(2)}, u32[]{:S(2)}) collective-permute-start(bf16[256,1024]{1,0:T(8,128)(2,1)S(1)} %pad_maximum_fusion.2), channel_id=1, source_target_pairs={{0,48},{4,52},{8,56},{12,60},{16,0},{20,4},{24,8},{28,12},{32,16},... | collective-permute-start | bytes 1572872 | tf_op jit(solution)/shard_map/ppermute | solution.py:30
  16.5 9.5 %collective-permute-start.8 = (bf16[256,1024]{1,0:T(8,128)(2,1)S(1)}, bf16[256,1024]{1,0:T(8,128)(2,1)S(1)}, u32[]{:S(2)}, u32[]{:S(2)}) collective-permute-start(bf16[256,1024]{1,0:T(8,128)(2,1)S(1)} %collective-permute-done.6), channel_id=1, source_target_pairs={{0,16},{4,20},{8,24},{12,28},{16,32},{20,36},{24,40},{28,44},{32,4... | collective-permute-start | bytes 1572872 | tf_op jit(solution)/shard_map/ppermute | solution.py:30
  16.6 30.8 %collective-permute-start.9 = (bf16[2048,512]{1,0:T(8,128)(2,1)S(1)}, bf16[2048,512]{1,0:T(8,128)(2,1)}, u32[]{:S(2)}, u32[]{:S(2)}) collective-permute-start(bf16[2048,512]{1,0:T(8,128)(2,1)S(1)} %copy-done), channel_id=1, source_target_pairs={{0,64},{64,0},{1,65},{65,1},{2,66},{66,2},{3,67},{67,3},{4,68},{68... | collective-permute-start | bytes 6291464 | tf_op jit(solution)/shard_map/ppermute | solution.py:39
  20.3 11.8 %collective-permute-start.3 = (bf16[256,1024]{1,0:T(8,128)(2,1)S(1)}, bf16[256,1024]{1,0:T(8,128)(2,1)S(1)}, u32[]{:S(2)}, u32[]{:S(2)}) collective-permute-start(bf16[256,1024]{1,0:T(8,128)(2,1)S(1)} %collective-permute-done.1), channel_id=1, source_target_pairs={{0,48},{4,52},{8,56},{12,60},{16,0},{20,4},{24,8},{28,12},{32,16},... | collective-permute-start | bytes 1572872 | tf_op jit(solution)/shard_map/ppermute | solution.py:30
  23.2 10.4 %collective-permute-start.2 = (bf16[256,1024]{1,0:T(8,128)(2,1)S(1)}, bf16[256,1024]{1,0:T(8,128)(2,1)S(1)}, u32[]{:S(2)}, u32[]{:S(2)}) collective-permute-start(bf16[256,1024]{1,0:T(8,128)(2,1)S(1)} %collective-permute-done.1), channel_id=1, source_target_pairs={{0,16},{4,20},{8,24},{12,28},{16,32},{20,36},{24,40},{28,44},{32,4... | collective-permute-start | bytes 1572872 | tf_op jit(solution)/shard_map/ppermute | solution.py:30
  29.4 29.6 %collective-permute-start.10 = (bf16[1024,1024]{1,0:T(8,128)(2,1)}, bf16[1024,1024]{1,0:T(8,128)(2,1)}, u32[]{:S(2)}, u32[]{:S(2)}) collective-permute-start(bf16[1024,1024]{1,0:T(8,128)(2,1)} %constant_dynamic-update-slice_fusion.4), channel_id=1, source_target_pairs={{0,4},{4,8},{8,12},{12,0},{16,20},{20,24},{24,28},{28,16},{32,36},... | collective-permute-start | bytes 6291464 | tf_op jit(solution)/shard_map/ppermute | solution.py:30
  29.4 31.6 %collective-permute-start.11 = (bf16[1024,1024]{1,0:T(8,128)(2,1)}, bf16[1024,1024]{1,0:T(8,128)(2,1)}, u32[]{:S(2)}, u32[]{:S(2)}) collective-permute-start(bf16[1024,1024]{1,0:T(8,128)(2,1)} %constant_dynamic-update-slice_fusion.4), channel_id=1, source_target_pairs={{0,12},{4,0},{8,4},{12,8},{16,28},{20,16},{24,20},{28,24},{32,44},... | collective-permute-start | bytes 6291464 | tf_op jit(solution)/shard_map/ppermute | solution.py:30
  32.1 14.0 %collective-permute-start.4 = (bf16[256,1024]{1,0:T(8,128)(2,1)S(1)}, bf16[256,1024]{1,0:T(8,128)(2,1)S(1)}, u32[]{:S(2)}, u32[]{:S(2)}) collective-permute-start(bf16[256,1024]{1,0:T(8,128)(2,1)S(1)} %collective-permute-done.3), channel_id=1, source_target_pairs={{0,48},{4,52},{8,56},{12,60},{16,0},{20,4},{24,8},{28,12},{32,16},... | collective-permute-start | bytes 1572872 | tf_op jit(solution)/shard_map/ppermute | solution.py:30
  46.9 36.6 %collective-permute-start.5 = (bf16[1024,1024]{1,0:T(8,128)(2,1)}, bf16[1024,1024]{1,0:T(8,128)(2,1)}, u32[]{:S(2)}, u32[]{:S(2)}) collective-permute-start(bf16[1024,1024]{1,0:T(8,128)(2,1)} %constant_dynamic-update-slice_fusion), channel_id=1, source_target_pairs={{0,12},{4,0},{8,4},{12,8},{16,28},{20,16},{24,20},{28,24},{32,44},... | collective-permute-start | bytes 6291464 | tf_op jit(solution)/shard_map/ppermute | solution.py:30
  47.1 36.3 %collective-permute-start.13 = (bf16[1024,512]{1,0:T(8,128)(2,1)S(1)}, bf16[1024,512]{1,0:T(8,128)(2,1)S(1)}, u32[]{:S(2)}, u32[]{:S(2)}) collective-permute-start(bf16[1024,512]{1,0:T(8,128)(2,1)S(1)} %get-tuple-element.37), channel_id=1, source_target_pairs={{0,128},{128,1},{1,129},{129,2},{2,130},{130,3},{3,131},{131,0},{4... | collective-permute-start | bytes 3145736 | tf_op jit(solution)/shard_map/ppermute | solution.py:35
  47.4 36.1 %collective-permute-start.14 = (bf16[1024,512]{1,0:T(8,128)(2,1)S(1)}, bf16[1024,512]{1,0:T(8,128)(2,1)S(1)}, u32[]{:S(2)}, u32[]{:S(2)}) collective-permute-start(bf16[1024,512]{1,0:T(8,128)(2,1)S(1)} %get-tuple-element.36), channel_id=1, source_target_pairs={{0,131},{128,0},{1,128},{129,1},{2,129},{130,2},{3,130},{131,3},{4... | collective-permute-start | bytes 3145736 | tf_op jit(solution)/shard_map/ppermute | solution.py:35
  61.0 27.2 %collective-permute-start.12 = (bf16[1024,1024]{1,0:T(8,128)(2,1)}, bf16[1024,1024]{1,0:T(8,128)(2,1)S(1)}, u32[]{:S(2)}, u32[]{:S(2)}) collective-permute-start(bf16[1024,1024]{1,0:T(8,128)(2,1)} %collective-permute-done.10), channel_id=1, source_target_pairs={{0,4},{4,8},{8,12},{12,0},{16,20},{20,24},{24,28},{28,16},{32,36},... | collective-permute-start | bytes 6291464 | tf_op jit(solution)/shard_map/ppermute | solution.py:30
  83.6 6.3 %collective-permute-start.15 = (bf16[2048,512]{1,0:T(8,128)(2,1)S(1)}, bf16[2048,512]{1,0:T(8,128)(2,1)S(1)}, u32[]{:S(2)}, u32[]{:S(2)}) collective-permute-start(bf16[2048,512]{1,0:T(8,128)(2,1)S(1)} %constant_dynamic-update-slice_fusion.8.first), channel_id=1, source_target_pairs={{0,64},{64,0},{1,65},{65,1},{2,66},{66,2},{3,67},{67,3},{4,68},{68... | collective-permute-start | bytes 6291464 | tf_op jit(solution)/shard_map/ppermute | solution.py:39
  86.1 25.4 %collective-permute-start.17 = (bf16[1024,1024]{1,0:T(8,128)(2,1)}, bf16[1024,1024]{1,0:T(8,128)(2,1)S(1)}, u32[]{:S(2)}, u32[]{:S(2)}) collective-permute-start(bf16[1024,1024]{1,0:T(8,128)(2,1)} %collective-permute-done.5), channel_id=1, source_target_pairs={{0,12},{4,0},{8,4},{12,8},{16,28},{20,16},{24,20},{28,24},{32,44},... | collective-permute-start | bytes 6291464 | tf_op jit(solution)/shard_map/ppermute | solution.py:30
  87.1 26.6 %collective-permute-start.16 = (bf16[1024,1024]{1,0:T(8,128)(2,1)}, bf16[1024,1024]{1,0:T(8,128)(2,1)S(1)}, u32[]{:S(2)}, u32[]{:S(2)}) collective-permute-start(bf16[1024,1024]{1,0:T(8,128)(2,1)} %constant_dynamic-update-slice_fusion), channel_id=1, source_target_pairs={{0,4},{4,8},{8,12},{12,0},{16,20},{20,24},{24,28},{28,16},{32,36},... | collective-permute-start | bytes 6291464 | tf_op jit(solution)/shard_map/ppermute | solution.py:30
  115.0 13.7 %copy-start.4 = (f32[1024]{0:T(1024)S(1)}, f32[1024]{0:T(1024)}, u32[]{:S(2)}) copy-start(f32[1024]{0:T(1024)} %param.12) | copy-start | bytes 12292
  115.0 32.2 %copy-start.5 = (f32[512]{0:T(512)S(1)}, f32[512]{0:T(512)}, u32[]{:S(2)}) copy-start(f32[512]{0:T(512)} %param.13) | copy-start | bytes 6148
  115.0 32.8 %copy-start.1 = (bf16[1024,512]{1,0:T(8,128)(2,1)S(1)}, bf16[1024,512]{1,0:T(8,128)(2,1)}, u32[]{:S(2)}) copy-start(bf16[1024,512]{1,0:T(8,128)(2,1)} %param.10) | copy-start | bytes 3145732
  128.7 24.7 %copy-start.2 = (f32[1024]{0:T(1024)}, f32[1024]{0:T(1024)S(1)}, u32[]{:S(2)}) copy-start(f32[1024]{0:T(1024)S(1)} %get-tuple-element.34) | copy-start | bytes 12292
  147.2 6.2 %copy-start.3 = (f32[512]{0:T(512)}, f32[512]{0:T(512)S(1)}, u32[]{:S(2)}) copy-start(f32[512]{0:T(512)S(1)} %multiply_add_fusion.2) | copy-start | bytes 6148

commit v4 on v3

--- a/solution.py
+++ b/solution.py
@@ -40,11 +40,16 @@
 
 
 def ring_start(block, phase):
-    return [block, shift(block, phase, 1), shift(block, phase, -1)]
+    return [block, *lax.optimization_barrier((shift(block, phase, 1), shift(block, phase, -1)))]
 
 
-def ring_end(blocks, phase, step):
-    return [*blocks, shift(blocks[1] if step == 1 else blocks[2], phase, step)]
+def ring_up(blocks, phase):
+    return [*blocks, shift(blocks[1], phase, 1)]
+
+
+def ring_both(blocks, phase):
+    half = blocks[0].shape[0] // 2
+    return [*blocks, shift(blocks[1][:half], phase, 1), shift(blocks[2][half:], phase, -1)]
 
 
 def after(blocks, *others):
@@ -57,35 +62,38 @@
     )
 
 
-def arrange_kernel(place, first, second, out, sems):
-    tokens = first.shape[0] // 16
+def arrange_kernel(place, *refs):
+    *sources, out, sems = refs
+    tokens = sources[0].shape[0] // 16
     copies = []
     for i in range(16):
         rows = pl.ds(pl.multiple_of(place[i] * tokens, tokens), tokens)
-        for c, source in enumerate((first, second)):
-            at = pl.ds((2 * i + c) * tokens, tokens)
-            copies.append(pltpu.make_async_copy(source.at[rows], out.at[at], sems.at[2 * i + c]))
+        for source in sources:
+            at = pl.ds(len(copies) * tokens, tokens)
+            copies.append(
+                pltpu.make_async_copy(source.at[rows], out.at[at], sems.at[len(copies)])
+            )
     for copy in copies:
         copy.start()
     for copy in copies:
         copy.wait()
 
 
-def arranged(places, first, second):
-    rows, width = first.shape
-    anywhere = pl.BlockSpec(memory_space=pl.ANY)
+def arranged(places, *sources):
+    rows, width = sources[0].shape
+    rows *= len(sources)
+    size = rows * width * 2
     out = pl.pallas_call(
         arrange_kernel,
-        in_specs=[pl.BlockSpec(memory_space=pltpu.SMEM), anywhere, anywhere],
+        in_specs=[pl.BlockSpec(memory_space=pltpu.SMEM)]
+        + [pl.BlockSpec(memory_space=pl.ANY)] * len(sources),
         out_specs=pl.BlockSpec(memory_space=pltpu.VMEM),
-        out_shape=jax.ShapeDtypeStruct((2 * rows, width), first.dtype),
-        scratch_shapes=[pltpu.SemaphoreType.DMA((32,))],
-        compiler_params=pltpu.CompilerParams(vmem_limit_bytes=8 << 20),
-        cost_estimate=pl.CostEstimate(
-            flops=0, bytes_accessed=8 * rows * width, transcendentals=0
-        ),
-    )(places, first, second)
-    return out.reshape(4, rows // 2, width)
+        out_shape=jax.ShapeDtypeStruct((rows, width), sources[0].dtype),
+        scratch_shapes=[pltpu.SemaphoreType.DMA((16 * len(sources),))],
+        compiler_params=pltpu.CompilerParams(vmem_limit_bytes=size + (2 << 20)),
+        cost_estimate=pl.CostEstimate(flops=0, bytes_accessed=2 * size, transcendentals=0),
+    )(places, *sources)
+    return out.reshape(4, rows // 4, width)
 
 
 def total_over(vector, axes):
@@ -102,10 +110,11 @@
     def units(a, b):
         return lax.dynamic_slice_in_dim(out_grads, ((low ^ a) * 2 + (core ^ b)) * rows, rows, 1)
 
+    near = units(0, 0)
     other = swap(jnp.concatenate([units(0, 1), units(1, 1)], axis=0), "core")
-    tokens = other.shape[0] // 2
-    near = jnp.concatenate([units(0, 0), other[:tokens]], axis=0)
+    tokens = near.shape[0]
     away = swap(jnp.concatenate([units(1, 0), other[tokens:]], axis=0), "zl")
+    away = jnp.concatenate([other[:tokens], away], axis=0)
     acts_core = swap(activations, "core")
 
     places = []
@@ -115,23 +124,27 @@
             places.append((x + dx) % 4 * 4 + (y + dy) % 4)
     places = jnp.stack(places).astype(jnp.int32)
 
-    near = after(ring_end(ring_start(near, 0), 0, 1), away)
-    (sent,) = after((activations,), *near)
+    near = ring_up(ring_start(near, 0), 0)
+    near[3], away, sent = lax.optimization_barrier((near[3], away, activations))
     near = ring_start(jnp.concatenate(near, axis=0), 1)
-    away = ring_end(ring_start(away, 0), 0, -1)
+    away = ring_both(ring_start(away, 0), 0)
     half = sent.shape[0] // 2
     acts_low = (along_z(sent[:half], 1), along_z(sent[half:], -1))
-    first = arranged(places, activations, acts_core)
-    gradient = product(near[0], first[0]) + product(near[1], first[1]) + product(near[2], first[2])
-    near = ring_end(after(near, *away), 1, 1)
+    near = ring_up(near, 1)
     away = ring_start(jnp.concatenate(away, axis=0), 1)
-    away[2], gradient = lax.optimization_barrier((away[2], gradient))
-    away = ring_end(away, 1, -1)
-    acts_low = jnp.concatenate(after(acts_low, away[2]), axis=0)
-    second = arranged(places, acts_low, swap(acts_low, "core"))
-    gradient = gradient + product(near[3], first[3])
-    gradient = gradient + product(away[0], second[0]) + product(away[2], second[2])
-    last = lax.optimization_barrier((product(away[1], second[1]), product(away[3], second[3])))
+    first = arranged(places, activations)
+    gradient = product(near[0], first[0])
+    for k in (2, 1, 3):
+        gradient = gradient + product(near[k], first[k])
+    acts_low = jnp.concatenate(after(acts_low, near[3]), axis=0)
+    second = arranged(places, acts_core, acts_low, swap(acts_low, "core"))
+    gradient = gradient + product(away[0], second[0])
+    *away, gradient = lax.optimization_barrier((*away, gradient))
+    away = ring_both(away, 1)
+    half = away[3].shape[0]
+    gradient = gradient + product(away[1], second[1]) + product(away[2], second[2])
+    last = (product(away[3], second[3][:half]), product(away[4], second[3][half:]))
+    last = lax.optimization_barrier(last)
     gradient = gradient + (last[0] + last[1])
     gradient = gradient * token_scale
 
@@ -140,13 +153,14 @@
     row_moment_new = 0.8 * row_moment + 0.2 * row_full / D
     col_part = jnp.sum(squares, axis=0)
     sums = jnp.concatenate([col_part, jnp.sum(row_moment_new.reshape(8, 128), axis=0)])
+    scores_new = scores - 50.0 * weights * gradient
     sums = total_over(sums, ("zl", "core", "zh"))
+    sums, weights, gradient = lax.optimization_barrier((sums, weights, gradient))
     col_moment_new = 0.8 * col_moment + 0.2 * sums[:512] / FF
     row_average = jnp.sum(sums[512:]) / FF
-    update = gradient * lax.rsqrt(row_moment_new[:, None] * col_moment_new[None, :] / row_average)
-    momentum_new = (0.9 * momentum.astype(jnp.float32) + 0.1 * update).astype(jnp.bfloat16)
+    scale = lax.rsqrt(row_moment_new)[:, None] * lax.rsqrt(col_moment_new / row_average)[None, :]
+    momentum_new = (0.9 * momentum.astype(jnp.float32) + 0.1 * (gradient * scale)).astype(jnp.bfloat16)
     weights_new = weights - 0.01 * momentum_new.astype(jnp.float32)
-    scores_new = scores - 50.0 * weights * gradient
     return (weights_new, momentum_new, scores_new, row_moment_new, col_moment_new)
 
 

time: 154 us -> 165 us (1.071)
  starting transfers between devices: 22.1 us -> 36.9 us
  Pallas kernels: 10.8 us -> 7.26 us
  local copies, waits for them, and re-layouts: 8.38 us -> 11.8 us
  blocking collectives: 27.8 us -> 25 us
  other arithmetic: 6.37 us -> 8.93 us
  waiting for transfers between devices: 57.5 us -> 55.7 us
    ppermute x12 -> x14, starting transfers between devices: 9.29 us -> 16.1 us  [shift(): return lax.ppermute(array, AXES, ring_pairs(phase, step))]
    ppermute x4, starting transfers between devices: 8.3 us -> 15 us  [swap(): return lax.ppermute(array, axis, [(0, 1), (1, 0)])]
    ppermute x12 -> x14, waiting for transfers between devices: 53.1 us -> 49.1 us  [shift(): return lax.ppermute(array, AXES, ring_pairs(phase, step))]
    pallas_call x2, Pallas kernels: 10.8 us -> 7.26 us  [arranged(): pl.pallas_call(arrange_kernel, in_specs=[pl.BlockSpec(memory_space=pltpu....]
    sub x0 -> x1, other arithmetic: none -> 3.16 us  [local(): scores_new = scores - 50.0 * weights * gradient]
    slice x1 -> x5, local copies, waits for them, and re-layouts: 0.03 us -> 3.14 us  [the longest x2 1.55 us: ring_both(): blocks[1][:half]]
    all_to_all x2, blocking collectives: 27.8 us -> 25 us  [total_over(): return jnp.sum(lax.all_to_all(spread, axes, 0, 0, tiled=True), axis=0)]
    ppermute x4, waiting for transfers between devices: 4.43 us -> 6.66 us  [swap(): return lax.ppermute(array, axis, [(0, 1), (1, 0)])]
  transfers between devices with their start and end apart: 18 -> 20, of which waited for: 11 -> 10; matrix products, arithmetic and copies ran while one was open for 14% -> 15% of each run, Pallas kernels for 7% -> 4%
where the time goes in v4:
time: 165 us
  waiting for transfers between devices  55.7 us (34%)
  starting transfers between devices  36.9 us (22%)
  blocking collectives  25 us (15%)
  matrix products  17.5 us (11%)
  local copies, waits for them, and re-layouts  11.8 us (7%)
  other arithmetic  8.93 us (5%)
  Pallas kernels  7.26 us (4%)
    ppermute x14, waiting for transfers between devices, shift(): return lax.ppermute(array, AXES, ring_pairs(phase, step))  49.1 us
    all_to_all x2, blocking collectives, total_over(): return jnp.sum(lax.all_to_all(spread, axes, 0, 0, tiled=True), axis=0)  25 us
    dot_general x9, matrix products, product(): lax.dot_general(grad_rows, act_rows, (((0,), (0,)), ((), ())), preferred_...  17.5 us
    ppermute x14, starting transfers between devices, shift(): return lax.ppermute(array, AXES, ring_pairs(phase, step))  16.1 us
    ppermute x4, starting transfers between devices, swap(): return lax.ppermute(array, axis, [(0, 1), (1, 0)])  15 us
    pallas_call x2, Pallas kernels, arranged(): pl.pallas_call(arrange_kernel, in_specs=[pl.BlockSpec(memory_space=pltpu....  7.26 us
    ppermute x4, waiting for transfers between devices, swap(): return lax.ppermute(array, axis, [(0, 1), (1, 0)])  6.66 us
    ppermute x2, starting transfers between devices, along_z(): lax.ppermute(array, ('zl', 'zh'), [(place(z), place((z + step) % 8)) for...  5.86 us
  transfers between devices with their start and end apart: 20, of which 10 were waited for; matrix products, arithmetic and copies ran while one was open for 15% of the time, Pallas kernels for 4%

profile of v4, /device:TPU:1, one launch (start us, length us, event | category | flops | bytes accessed | tf_op | source)
XLA Modules:
  0.0 164.8 jit_solution(2911339163687149679)
XLA Ops:
  0.7 1.3 constant_dynamic-slice_fusion
  2.0 3.3 %collective-permute-start.3 = (bf16[256,1024]{1,0:T(8,128)(2,1)S(1)}, bf16[256,1024]{1,0:T(8,128)(2,1)S(1)}, u32[]{:S(2)}, u32[]{:S(2)}) collective-permute-start(bf16[256,1024]{1,0:T(8,128)(2,1)S(1)} %pad_maximum_fusion.2), channel_id=1, source_target_pairs={{0,64},{64,0},{1,65},{65,1},{2,66},{66,2},{3,67},{67,3},{4,68},{68... | collective-permute-start | bytes 1572872 | tf_op jit(solution)/shard_map/ppermute | solution.py:39
  5.3 1.5 collective-permute-done.3
  7.0 1.2 collective-permute-start
  8.2 1.6 collective-permute-start.1
  9.8 4.1 %collective-permute-done = bf16[128,1024]{1,0:T(8,128)(2,1)S(1)} collective-permute-done((bf16[128,1024]{1,0:T(8,128)(2,1)S(1)}, bf16[128,1024]{1,0:T(8,128)(2,1)S(1)}, u32[]{:S(2)}, u32[]{:S(2)}) %collective-permute-start) | collective-permute-done | bytes 262176 | tf_op jit(solution)/shard_map/ppermute | solution.py:30
  13.9 1.2 collective-permute-start.2
  15.0 5.1 %collective-permute-done.4 = bf16[256,1024]{1,0:T(8,128)(2,1)S(1)} collective-permute-done((bf16[256,1024]{1,0:T(8,128)(2,1)S(1)}, bf16[256,1024]{1,0:T(8,128)(2,1)S(1)}, u32[]{:S(2)}, u32[]{:S(2)}) %collective-permute-start.4) | collective-permute-done | bytes 524320 | tf_op jit(solution)/shard_map/ppermute | solution.py:39
  20.7 0.8 collective-permute-start.11
  21.5 1.9 %collective-permute-start.12 = (bf16[512,1024]{1,0:T(8,128)(2,1)S(1)}, bf16[512,1024]{1,0:T(8,128)(2,1)S(1)}, u32[]{:S(2)}, u32[]{:S(2)}) collective-permute-start(bf16[512,1024]{1,0:T(8,128)(2,1)S(1)} %pad_maximum_fusion), channel_id=1, source_target_pairs={{0,12},{4,0},{8,4},{12,8},{16,28},{20,16},{24,20},{28,24},{32,44},... | collective-permute-start | bytes 3145736 | tf_op jit(solution)/shard_map/ppermute | solution.py:30
  23.5 2.7 %collective-permute-start.6 = (bf16[384,1024]{1,0:T(8,128)(2,1)S(1)}, bf16[384,1024]{1,0:T(8,128)(2,1)S(1)}, u32[]{:S(2)}, u32[]{:S(2)}) collective-permute-start(bf16[384,1024]{1,0:T(8,128)(2,1)S(1)} %pad_maximum_fusion.1), channel_id=1, source_target_pairs={{0,48},{4,52},{8,56},{12,60},{16,0},{20,4},{24,8},{28,12},{32,16},... | collective-permute-start | bytes 2359304 | tf_op jit(solution)/shard_map/ppermute | solution.py:30
  26.4 1.5 collective-permute-start.15
  27.8 13.2 %collective-permute-done.11 = bf16[512,1024]{1,0:T(8,128)(2,1)S(1)} collective-permute-done((bf16[512,1024]{1,0:T(8,128)(2,1)S(1)}, bf16[512,1024]{1,0:T(8,128)(2,1)S(1)}, u32[]{:S(2)}, u32[]{:S(2)}) %collective-permute-start.11) | collective-permute-done | bytes 1048608 | tf_op jit(solution)/shard_map/ppermute | solution.py:30
  41.1 4.4 %collective-permute-start.16 = (bf16[1024,512]{1,0:T(8,128)(2,1)S(1)}, bf16[1024,512]{1,0:T(8,128)(2,1)S(1)}, u32[]{:S(2)}, u32[]{:S(2)}) collective-permute-start(bf16[1024,512]{1,0:T(8,128)(2,1)S(1)} %get-tuple-element.57), channel_id=1, source_target_pairs={{0,131},{128,0},{1,128},{129,1},{2,129},{130,2},{3,130},{131,3},{4... | collective-permute-start | bytes 3145736 | tf_op jit(solution)/shard_map/ppermute | solution.py:35
  46.0 1.1 collective-permute-start.7
  47.1 1.8 %collective-permute-start.8 = (bf16[192,1024]{1,0:T(8,128)(2,1)S(1)}, bf16[192,1024]{1,0:T(8,128)(2,1)S(1)}, u32[]{:S(2)}, u32[]{:S(2)}) collective-permute-start(bf16[192,1024]{1,0:T(8,128)(2,1)S(1)} %slice.73), channel_id=1, source_target_pairs={{0,48},{4,52},{8,56},{12,60},{16,0},{20,4},{24,8},{28,12},{32,16},... | collective-permute-start | bytes 1179656 | tf_op jit(solution)/shard_map/ppermute | solution.py:30
  48.9 0.9 constant_dynamic-update-slice_fusion.4
  49.8 0.9 constant_dynamic-update-slice_fusion.3
  50.8 1.0 constant_dynamic-update-slice_fusion.2
  51.8 2.5 %collective-permute-done.7 = bf16[192,1024]{1,0:T(8,128)(2,1)S(1)} collective-permute-done((bf16[192,1024]{1,0:T(8,128)(2,1)S(1)}, bf16[192,1024]{1,0:T(8,128)(2,1)S(1)}, u32[]{:S(2)}, u32[]{:S(2)}) %collective-permute-start.7) | collective-permute-done | bytes 393248 | tf_op jit(solution)/shard_map/ppermute | solution.py:30
  54.2 11.0 %collective-permute-start.14 = (bf16[2048,512]{1,0:T(8,128)(2,1)S(1)}, bf16[2048,512]{1,0:T(8,128)(2,1)}, u32[]{:S(2)}, u32[]{:S(2)}) collective-permute-start(bf16[2048,512]{1,0:T(8,128)(2,1)S(1)} %copy-done), channel_id=1, source_target_pairs={{0,64},{64,0},{1,65},{65,1},{2,66},{66,2},{3,67},{67,3},{4,68},{68... | collective-permute-start | bytes 6291464 | tf_op jit(solution)/shard_map/ppermute | solution.py:39
  65.2 0.8 constant_dynamic-update-slice_fusion.1
  66.0 0.8 constant_dynamic-update-slice_fusion
  67.0 1.2 collective-permute-start.9
  68.3 1.0 constant_dynamic-update-slice_fusion.6
  69.3 1.0 constant_dynamic-update-slice_fusion.5.refs_1_
  71.1 3.4 %shard_map.110 = bf16[2048,512]{1,0:T(8,128)(2,1)S(1)} custom-call(s32[16]{0:T(128)S(1)} %stack.67.place, bf16[2048,512]{1,0:T(8,128)(2,1)S(1)} %copy-done), custom_call_target="tpu_custom_call" | custom-call | bytes 4194304 | tf_op jit(solution)/shard_map/pallas_call | solution.py:86
  74.5 0.7 fusion.20
  75.3 0.8 fusion.16
  76.5 0.8 fusion.18
  77.3 2.0 %fusion.14 = f32[1024,512]{1,0:T(8,128)S(1)} fusion(bf16[512,1024]{1,0:T(8,128)(2,1)} %collective-permute-done.13, bf16[2048,512]{1,0:T(8,128)(2,1)S(1)} %shard_map.110), kind=kOutput, calls=%fused_computation.20 | convolution fusion | flops 536870912 | bytes 3670016 | tf_op jit(solution)/shard_map/dot_general | solution.py:60
  79.3 3.8 %shard_map.111 = bf16[6144,512]{1,0:T(8,128)(2,1)S(1)} custom-call(s32[16]{0:T(128)S(1)} %stack.67.place, bf16[2048,512]{1,0:T(8,128)(2,1)} %collective-permute-done.14.refs_0_, bf16[2048,512]{1,0:T(8,128)(2,1)} %constant_dynamic-update-slice_fusion.5.refs_1_, bf16[2048,512]{1,0:T(8,128)(2,1)} %collective-permute-done.17.refs_2_), custom_call_target="tpu_custom_call" | custom-call | bytes 12582912 | tf_op jit(solution)/shard_map/pallas_call | solution.py:86
  83.1 3.8 %add_add_fusion = f32[1024,512]{1,0:T(8,128)S(1)} fusion(f32[1024,512]{1,0:T(8,128)S(1)} %fusion.14, f32[1024,512]{1,0:T(8,128)S(1)} %fusion.16, f32[1024,512]{1,0:T(8,128)S(1)} %fusion.20, f32[1024,512]{1,0:T(8,128)S(1)} %fusion.18, bf16[1536,1024]{1,0:T(8,128)(2,1)} %constant_dynamic-update-slice_fusion, bf16[6144,512]{1,0:T(8,128)(2,1)S(1)} %shard_map.111), kind=kOutput, calls=%fused_computation.5 | convolution fusion | flops 1612709888 | bytes 15204352 | tf_op jit(solution)/shard_map/dot_general | solution.py:60
  86.9 16.6 %collective-permute-done.10 = bf16[1536,1024]{1,0:T(8,128)(2,1)} collective-permute-done((bf16[1536,1024]{1,0:T(8,128)(2,1)}, bf16[1536,1024]{1,0:T(8,128)(2,1)}, u32[]{:S(2)}, u32[]{:S(2)}) %collective-permute-start.10) | collective-permute-done | bytes 3145760 | tf_op jit(solution)/shard_map/ppermute | solution.py:30
  103.6 1.4 collective-permute-done.9
  105.0 1.5 slice.85
  106.6 1.5 slice.83
  108.1 1.8 %collective-permute-start.18 = (bf16[768,1024]{1,0:T(8,128)(2,1)S(1)}, bf16[768,1024]{1,0:T(8,128)(2,1)S(1)}, u32[]{:S(2)}, u32[]{:S(2)}) collective-permute-start(bf16[768,1024]{1,0:T(8,128)(2,1)S(1)} %slice.83), channel_id=1, source_target_pairs={{0,4},{4,8},{8,12},{12,0},{16,20},{20,24},{24,28},{28,16},{32,36},... | collective-permute-start | bytes 4718600 | tf_op jit(solution)/shard_map/ppermute | solution.py:30
  109.9 3.7 %fusion.4 = f32[1024,512]{1,0:T(8,128)S(1)} fusion(bf16[1536,1024]{1,0:T(8,128)(2,1)} %collective-permute-done.9, bf16[6144,512]{1,0:T(8,128)(2,1)S(1)} %shard_map.111), kind=kOutput, calls=%fused_computation.10 | convolution fusion | flops 1610612736 | bytes 6815744 | tf_op jit(solution)/shard_map/dot_general | solution.py:60
  113.6 3.7 %fusion.2 = f32[1024,512]{1,0:T(8,128)S(1)} fusion(bf16[1536,1024]{1,0:T(8,128)(2,1)} %collective-permute-done.10, bf16[6144,512]{1,0:T(8,128)(2,1)S(1)} %shard_map.111), kind=kOutput, calls=%fused_computation.8 | convolution fusion | flops 1610612736 | bytes 6815744 | tf_op jit(solution)/shard_map/dot_general | solution.py:60
  117.3 8.8 %collective-permute-done.19 = bf16[768,1024]{1,0:T(8,128)(2,1)S(1)} collective-permute-done((bf16[768,1024]{1,0:T(8,128)(2,1)S(1)}, bf16[768,1024]{1,0:T(8,128)(2,1)S(1)}, u32[]{:S(2)}, u32[]{:S(2)}) %collective-permute-start.19) | collective-permute-done | bytes 1572896 | tf_op jit(solution)/shard_map/ppermute | solution.py:30
  126.2 1.0 fusion.10
  127.2 2.0 %collective-permute-done.18 = bf16[768,1024]{1,0:T(8,128)(2,1)S(1)} collective-permute-done((bf16[768,1024]{1,0:T(8,128)(2,1)S(1)}, bf16[768,1024]{1,0:T(8,128)(2,1)S(1)}, u32[]{:S(2)}, u32[]{:S(2)}) %collective-permute-start.18) | collective-permute-done | bytes 1572896 | tf_op jit(solution)/shard_map/ppermute | solution.py:30
  129.2 1.0 fusion.12
  130.3 3.2 %multiply_subtract_fusion = (f32[1024,512]{1,0:T(8,128)}, f32[1024,512]{1,0:T(8,128)S(1)}) fusion(f32[1024,512]{1,0:T(8,128)S(1)} %copy-done.2, f32[1024,512]{1,0:T(8,128)S(1)} %copy-done.1, f32[1024,512]{1,0:T(8,128)S(1)} %fusion.12, f32[1024,512]{1,0:T(8,128)S(1)} %fusion.10, f32[1024,512]{1,0:T(8,128)S(1)} %fusion.2, f32[1024,512]{1,0:T(8,128)S(1)} %add_add_fusion, ...), kind=kLoop, calls=%fused_computation | loop fusion | flops 4194304 | bytes 18874368 | tf_op jit(solution)/shard_map/sub | solution.py:156
  133.9 10.4 %all_to_all.12 = f32[16,1,1024]{2,1,0:T(1,128)S(1)} all-to-all(f32[16,1,1024]{2,1,0:T(1,128)S(1)} %broadcast_in_dim.4), channel_id=1, replica_groups=mesh['zl'=2,'core'=2,'x'=4,'y'=4,'zh'=4] {'x','y'}, dimensions={0} | all-to-all | bytes 131072 | tf_op jit(solution)/shard_map/all_to_all | solution.py:101
  144.4 14.7 %all_to_all.13 = f32[16,1,640]{2,1,0:T(1,128)S(1)} all-to-all(f32[16,1,640]{2,1,0:T(1,128)S(1)} %broadcast_in_dim.5), channel_id=1, replica_groups=mesh['zl'=2,'core'=2,'x'=4,'y'=4,'zh'=4] {'zl','core','zh'}, dimensions={0} | all-to-all | bytes 81920 | tf_op jit(solution)/shard_map/all_to_all | solution.py:101
  160.9 3.9 %multiply_subtract_fusion.1 = (f32[1024,512]{1,0:T(8,128)}, bf16[1024,512]{1,0:T(8,128)(2,1)}) fusion(f32[1024,512]{1,0:T(8,128)} %param.9, f32[1024,512]{1,0:T(8,128)S(1)} %get-tuple-element.45, f32[512]{0:T(512)S(1)} %get-tuple-element.55, f32[1024]{0:T(1024)S(1)} %get-tuple-element.53, bf16[1024,512]{1,0:T(8,128)(2,1)S(1)} %copy-done.3), kind=kLoop, calls=%fused_computation.1 | loop fusion | flops 5242880 | bytes 8394752 | tf_op jit(solution)/shard_map/sub | solution.py:163
  (66 shorter events, 4.7 us)
Async XLA Ops:
  2.0 4.9 %collective-permute-start.3 = (bf16[256,1024]{1,0:T(8,128)(2,1)S(1)}, bf16[256,1024]{1,0:T(8,128)(2,1)S(1)}, u32[]{:S(2)}, u32[]{:S(2)}) collective-permute-start(bf16[256,1024]{1,0:T(8,128)(2,1)S(1)} %pad_maximum_fusion.2), channel_id=1, source_target_pairs={{0,64},{64,0},{1,65},{65,1},{2,66},{66,2},{3,67},{67,3},{4,68},{68... | collective-permute-start | bytes 1572872 | tf_op jit(solution)/shard_map/ppermute | solution.py:39
  6.9 19.3 %copy-start = (bf16[2048,512]{1,0:T(8,128)(2,1)S(1)}, bf16[2048,512]{1,0:T(8,128)(2,1)}, u32[]{:S(2)}) copy-start(bf16[2048,512]{1,0:T(8,128)(2,1)} %refs_0_.1) | copy-start | bytes 6291460
  6.9 13.2 %collective-permute-start.4 = (bf16[256,1024]{1,0:T(8,128)(2,1)S(1)}, bf16[256,1024]{1,0:T(8,128)(2,1)S(1)}, u32[]{:S(2)}, u32[]{:S(2)}) collective-permute-start(bf16[256,1024]{1,0:T(8,128)(2,1)S(1)} %pad_maximum_fusion.3), channel_id=1, source_target_pairs={{0,128},{128,0},{1,129},{129,1},{2,130},{130,2},{3,131},{131,3},{4... | collective-permute-start | bytes 1572872 | tf_op jit(solution)/shard_map/ppermute | solution.py:39
  7.0 6.8 %collective-permute-start = (bf16[128,1024]{1,0:T(8,128)(2,1)S(1)}, bf16[128,1024]{1,0:T(8,128)(2,1)S(1)}, u32[]{:S(2)}, u32[]{:S(2)}) collective-permute-start(bf16[128,1024]{1,0:T(8,128)(2,1)S(1)} %get-tuple-element.61), channel_id=1, source_target_pairs={{0,16},{4,20},{8,24},{12,28},{16,32},{20,36},{24,40},{28,44},{32,4... | collective-permute-start | bytes 786440 | tf_op jit(solution)/shard_map/ppermute | solution.py:30
  8.2 5.6 %collective-permute-start.1 = (bf16[128,1024]{1,0:T(8,128)(2,1)S(1)}, bf16[128,1024]{1,0:T(8,128)(2,1)S(1)}, u32[]{:S(2)}, u32[]{:S(2)}) collective-permute-start(bf16[128,1024]{1,0:T(8,128)(2,1)S(1)} %get-tuple-element.61), channel_id=1, source_target_pairs={{0,48},{4,52},{8,56},{12,60},{16,0},{20,4},{24,8},{28,12},{32,16},... | collective-permute-start | bytes 786440 | tf_op jit(solution)/shard_map/ppermute | solution.py:30
  13.9 9.6 %copy-start.6 = (bf16[128,1024]{1,0:T(8,128)(2,1)}, bf16[128,1024]{1,0:T(8,128)(2,1)S(1)}, u32[]{:S(2)}) copy-start(bf16[128,1024]{1,0:T(8,128)(2,1)S(1)} %collective-permute-done) | copy-start | bytes 786436
  13.9 9.6 %copy-start.8 = (bf16[128,1024]{1,0:T(8,128)(2,1)}, bf16[128,1024]{1,0:T(8,128)(2,1)S(1)}, u32[]{:S(2)}) copy-start(bf16[128,1024]{1,0:T(8,128)(2,1)S(1)} %collective-permute-done.1) | copy-start | bytes 786436
  13.9 6.8 %collective-permute-start.2 = (bf16[128,1024]{1,0:T(8,128)(2,1)S(1)}, bf16[128,1024]{1,0:T(8,128)(2,1)S(1)}, u32[]{:S(2)}, u32[]{:S(2)}) collective-permute-start(bf16[128,1024]{1,0:T(8,128)(2,1)S(1)} %collective-permute-done), channel_id=1, source_target_pairs={{0,16},{4,20},{8,24},{12,28},{16,32},{20,36},{24,40},{28,44},{32,4... | collective-permute-start | bytes 786440 | tf_op jit(solution)/shard_map/ppermute | solution.py:30
  20.7 2.8 %copy-start.10 = (bf16[128,1024]{1,0:T(8,128)(2,1)}, bf16[128,1024]{1,0:T(8,128)(2,1)S(1)}, u32[]{:S(2)}) copy-start(bf16[128,1024]{1,0:T(8,128)(2,1)S(1)} %collective-permute-done.2) | copy-start | bytes 786436
  20.7 20.3 %collective-permute-start.11 = (bf16[512,1024]{1,0:T(8,128)(2,1)S(1)}, bf16[512,1024]{1,0:T(8,128)(2,1)S(1)}, u32[]{:S(2)}, u32[]{:S(2)}) collective-permute-start(bf16[512,1024]{1,0:T(8,128)(2,1)S(1)} %pad_maximum_fusion), channel_id=1, source_target_pairs={{0,4},{4,8},{8,12},{12,0},{16,20},{20,24},{24,28},{28,16},{32,36},... | collective-permute-start | bytes 3145736 | tf_op jit(solution)/shard_map/ppermute | solution.py:30
  21.5 23.9 %collective-permute-start.12 = (bf16[512,1024]{1,0:T(8,128)(2,1)S(1)}, bf16[512,1024]{1,0:T(8,128)(2,1)S(1)}, u32[]{:S(2)}, u32[]{:S(2)}) collective-permute-start(bf16[512,1024]{1,0:T(8,128)(2,1)S(1)} %pad_maximum_fusion), channel_id=1, source_target_pairs={{0,12},{4,0},{8,4},{12,8},{16,28},{20,16},{24,20},{28,24},{32,44},... | collective-permute-start | bytes 3145736 | tf_op jit(solution)/shard_map/ppermute | solution.py:30
  23.5 22.5 %collective-permute-start.5 = (bf16[384,1024]{1,0:T(8,128)(2,1)S(1)}, bf16[384,1024]{1,0:T(8,128)(2,1)S(1)}, u32[]{:S(2)}, u32[]{:S(2)}) collective-permute-start(bf16[384,1024]{1,0:T(8,128)(2,1)S(1)} %pad_maximum_fusion.1), channel_id=1, source_target_pairs={{0,16},{4,20},{8,24},{12,28},{16,32},{20,36},{24,40},{28,44},{32,4... | collective-permute-start | bytes 2359304 | tf_op jit(solution)/shard_map/ppermute | solution.py:30
  23.5 22.5 %collective-permute-start.6 = (bf16[384,1024]{1,0:T(8,128)(2,1)S(1)}, bf16[384,1024]{1,0:T(8,128)(2,1)S(1)}, u32[]{:S(2)}, u32[]{:S(2)}) collective-permute-start(bf16[384,1024]{1,0:T(8,128)(2,1)S(1)} %pad_maximum_fusion.1), channel_id=1, source_target_pairs={{0,48},{4,52},{8,56},{12,60},{16,0},{20,4},{24,8},{28,12},{32,16},... | collective-permute-start | bytes 2359304 | tf_op jit(solution)/shard_map/ppermute | solution.py:30
  26.4 40.6 %collective-permute-start.15 = (bf16[1024,512]{1,0:T(8,128)(2,1)S(1)}, bf16[1024,512]{1,0:T(8,128)(2,1)S(1)}, u32[]{:S(2)}, u32[]{:S(2)}) collective-permute-start(bf16[1024,512]{1,0:T(8,128)(2,1)S(1)} %get-tuple-element.58), channel_id=1, source_target_pairs={{0,128},{128,1},{1,129},{129,2},{2,130},{130,3},{3,131},{131,0},{4... | collective-permute-start | bytes 3145736 | tf_op jit(solution)/shard_map/ppermute | solution.py:35
  41.1 27.2 %collective-permute-start.16 = (bf16[1024,512]{1,0:T(8,128)(2,1)S(1)}, bf16[1024,512]{1,0:T(8,128)(2,1)S(1)}, u32[]{:S(2)}, u32[]{:S(2)}) collective-permute-start(bf16[1024,512]{1,0:T(8,128)(2,1)S(1)} %get-tuple-element.57), channel_id=1, source_target_pairs={{0,131},{128,0},{1,128},{129,1},{2,129},{130,2},{3,130},{131,3},{4... | collective-permute-start | bytes 3145736 | tf_op jit(solution)/shard_map/ppermute | solution.py:35
  45.5 5.3 %copy-start.4 = (bf16[512,1024]{1,0:T(8,128)(2,1)}, bf16[512,1024]{1,0:T(8,128)(2,1)S(1)}, u32[]{:S(2)}) copy-start(bf16[512,1024]{1,0:T(8,128)(2,1)S(1)} %collective-permute-done.12) | copy-start | bytes 3145732
  45.5 22.8 %collective-permute-start.13 = (bf16[512,1024]{1,0:T(8,128)(2,1)S(1)}, bf16[512,1024]{1,0:T(8,128)(2,1)}, u32[]{:S(2)}, u32[]{:S(2)}) collective-permute-start(bf16[512,1024]{1,0:T(8,128)(2,1)S(1)} %collective-permute-done.11), channel_id=1, source_target_pairs={{0,4},{4,8},{8,12},{12,0},{16,20},{20,24},{24,28},{28,16},{32,36},... | collective-permute-start | bytes 3145736 | tf_op jit(solution)/shard_map/ppermute | solution.py:30
  46.0 8.2 %collective-permute-start.7 = (bf16[192,1024]{1,0:T(8,128)(2,1)S(1)}, bf16[192,1024]{1,0:T(8,128)(2,1)S(1)}, u32[]{:S(2)}, u32[]{:S(2)}) collective-permute-start(bf16[192,1024]{1,0:T(8,128)(2,1)S(1)} %slice.72), channel_id=1, source_target_pairs={{0,16},{4,20},{8,24},{12,28},{16,32},{20,36},{24,40},{28,44},{32,4... | collective-permute-start | bytes 1179656 | tf_op jit(solution)/shard_map/ppermute | solution.py:30
  47.1 18.9 %collective-permute-start.8 = (bf16[192,1024]{1,0:T(8,128)(2,1)S(1)}, bf16[192,1024]{1,0:T(8,128)(2,1)S(1)}, u32[]{:S(2)}, u32[]{:S(2)}) collective-permute-start(bf16[192,1024]{1,0:T(8,128)(2,1)S(1)} %slice.73), channel_id=1, source_target_pairs={{0,48},{4,52},{8,56},{12,60},{16,0},{20,4},{24,8},{28,12},{32,16},... | collective-permute-start | bytes 1179656 | tf_op jit(solution)/shard_map/ppermute | solution.py:30
  54.2 25.0 %collective-permute-start.14 = (bf16[2048,512]{1,0:T(8,128)(2,1)S(1)}, bf16[2048,512]{1,0:T(8,128)(2,1)}, u32[]{:S(2)}, u32[]{:S(2)}) collective-permute-start(bf16[2048,512]{1,0:T(8,128)(2,1)S(1)} %copy-done), channel_id=1, source_target_pairs={{0,64},{64,0},{1,65},{65,1},{2,66},{66,2},{3,67},{67,3},{4,68},{68... | collective-permute-start | bytes 6291464 | tf_op jit(solution)/shard_map/ppermute | solution.py:39
  66.8 36.7 %collective-permute-start.10 = (bf16[1536,1024]{1,0:T(8,128)(2,1)}, bf16[1536,1024]{1,0:T(8,128)(2,1)}, u32[]{:S(2)}, u32[]{:S(2)}) collective-permute-start(bf16[1536,1024]{1,0:T(8,128)(2,1)} %constant_dynamic-update-slice_fusion), channel_id=1, source_target_pairs={{0,12},{4,0},{8,4},{12,8},{16,28},{20,16},{24,20},{28,24},{32,44},... | collective-permute-start | bytes 9437192 | tf_op jit(solution)/shard_map/ppermute | solution.py:30
  67.0 37.9 %collective-permute-start.9 = (bf16[1536,1024]{1,0:T(8,128)(2,1)}, bf16[1536,1024]{1,0:T(8,128)(2,1)}, u32[]{:S(2)}, u32[]{:S(2)}) collective-permute-start(bf16[1536,1024]{1,0:T(8,128)(2,1)} %constant_dynamic-update-slice_fusion), channel_id=1, source_target_pairs={{0,4},{4,8},{8,12},{12,0},{16,20},{20,24},{24,28},{28,16},{32,36},... | collective-permute-start | bytes 9437192 | tf_op jit(solution)/shard_map/ppermute | solution.py:30
  70.4 8.9 %collective-permute-start.17 = (bf16[2048,512]{1,0:T(8,128)(2,1)}, bf16[2048,512]{1,0:T(8,128)(2,1)}, u32[]{:S(2)}, u32[]{:S(2)}) collective-permute-start(bf16[2048,512]{1,0:T(8,128)(2,1)} %constant_dynamic-update-slice_fusion.5.refs_1_), channel_id=1, source_target_pairs={{0,64},{64,0},{1,65},{65,1},{2,66},{66,2},{3,67},{67,3},{4,68},{68... | collective-permute-start | bytes 6291464 | tf_op jit(solution)/shard_map/ppermute | solution.py:39
  71.0 3.5 %copy-start.7 = (bf16[128,1024]{1,0:T(8,128)(2,1)S(1)}, bf16[128,1024]{1,0:T(8,128)(2,1)}, u32[]{:S(2)}) copy-start(bf16[128,1024]{1,0:T(8,128)(2,1)} %copy-done.6) | copy-start | bytes 786436
  71.0 3.5 %copy-start.9 = (bf16[128,1024]{1,0:T(8,128)(2,1)S(1)}, bf16[128,1024]{1,0:T(8,128)(2,1)}, u32[]{:S(2)}) copy-start(bf16[128,1024]{1,0:T(8,128)(2,1)} %copy-done.8) | copy-start | bytes 786436
  71.1 3.5 %copy-start.11 = (bf16[128,1024]{1,0:T(8,128)(2,1)S(1)}, bf16[128,1024]{1,0:T(8,128)(2,1)}, u32[]{:S(2)}) copy-start(bf16[128,1024]{1,0:T(8,128)(2,1)} %copy-done.10) | copy-start | bytes 786436
  75.3 1.2 copy-start.5
  106.5 19.6 %collective-permute-start.19 = (bf16[768,1024]{1,0:T(8,128)(2,1)S(1)}, bf16[768,1024]{1,0:T(8,128)(2,1)S(1)}, u32[]{:S(2)}, u32[]{:S(2)}) collective-permute-start(bf16[768,1024]{1,0:T(8,128)(2,1)S(1)} %slice.85), channel_id=1, source_target_pairs={{0,12},{4,0},{8,4},{12,8},{16,28},{20,16},{24,20},{28,24},{32,44},... | collective-permute-start | bytes 4718600 | tf_op jit(solution)/shard_map/ppermute | solution.py:30
  108.1 21.1 %collective-permute-start.18 = (bf16[768,1024]{1,0:T(8,128)(2,1)S(1)}, bf16[768,1024]{1,0:T(8,128)(2,1)S(1)}, u32[]{:S(2)}, u32[]{:S(2)}) collective-permute-start(bf16[768,1024]{1,0:T(8,128)(2,1)S(1)} %slice.83), channel_id=1, source_target_pairs={{0,4},{4,8},{8,12},{12,0},{16,20},{20,24},{24,28},{28,16},{32,36},... | collective-permute-start | bytes 4718600 | tf_op jit(solution)/shard_map/ppermute | solution.py:30
  127.2 3.1 %copy-start.1 = (f32[1024,512]{1,0:T(8,128)S(1)}, f32[1024,512]{1,0:T(8,128)}, u32[]{:S(2)}) copy-start(f32[1024,512]{1,0:T(8,128)} %param.9) | copy-start | bytes 6291460
  127.2 3.1 %copy-start.2 = (f32[1024,512]{1,0:T(8,128)S(1)}, f32[1024,512]{1,0:T(8,128)}, u32[]{:S(2)}) copy-start(f32[1024,512]{1,0:T(8,128)} %param.11) | copy-start | bytes 6291460
  133.4 10.9 %copy-start.13 = (f32[1024]{0:T(1024)S(1)}, f32[1024]{0:T(1024)}, u32[]{:S(2)}) copy-start(f32[1024]{0:T(1024)} %param.12) | copy-start | bytes 12292
  133.4 26.9 %copy-start.14 = (f32[512]{0:T(512)S(1)}, f32[512]{0:T(512)}, u32[]{:S(2)}) copy-start(f32[512]{0:T(512)} %param.13) | copy-start | bytes 6148
  133.4 27.5 %copy-start.3 = (bf16[1024,512]{1,0:T(8,128)(2,1)S(1)}, bf16[1024,512]{1,0:T(8,128)(2,1)}, u32[]{:S(2)}) copy-start(bf16[1024,512]{1,0:T(8,128)(2,1)} %param.10) | copy-start | bytes 3145732
  144.3 20.5 %copy-start.12 = (f32[1024]{0:T(1024)}, f32[1024]{0:T(1024)S(1)}, u32[]{:S(2)}) copy-start(f32[1024]{0:T(1024)S(1)} %get-tuple-element.54) | copy-start | bytes 12292

commit v5 on v4

--- a/solution.py
+++ b/solution.py
@@ -30,11 +30,6 @@
     return lax.ppermute(array, AXES, ring_pairs(phase, step))
 
 
-def along_z(array, step):
-    place = lambda z: z % 2 * 4 + z // 2
-    return lax.ppermute(array, ("zl", "zh"), [(place(z), place((z + step) % 8)) for z in range(8)])
-
-
 def swap(array, axis):
     return lax.ppermute(array, axis, [(0, 1), (1, 0)])
 
@@ -49,11 +44,8 @@
 
 def ring_both(blocks, phase):
     half = blocks[0].shape[0] // 2
-    return [*blocks, shift(blocks[1][:half], phase, 1), shift(blocks[2][half:], phase, -1)]
-
-
-def after(blocks, *others):
-    return lax.optimization_barrier((*blocks, *others))[: len(blocks)]
+    far = (shift(blocks[1][:half], phase, 1), shift(blocks[2][half:], phase, -1))
+    return [*blocks, *lax.optimization_barrier(far)]
 
 
 def product(grad_rows, act_rows):
@@ -97,8 +89,8 @@
 
 
 def total_over(vector, axes):
-    spread = jnp.broadcast_to(vector[None], (16, vector.shape[0]))
-    return jnp.sum(lax.all_to_all(spread, axes, 0, 0, tiled=True), axis=0)
+    spread = jnp.broadcast_to(vector.reshape(1, 8, 128), (16, 8, 128))
+    return jnp.sum(lax.all_to_all(spread, axes, 0, 0, tiled=True), axis=0).reshape(1024)
 
 
 def local(activations, out_grads, weights, momentum, scores, row_moment, col_moment):
@@ -110,11 +102,10 @@
     def units(a, b):
         return lax.dynamic_slice_in_dim(out_grads, ((low ^ a) * 2 + (core ^ b)) * rows, rows, 1)
 
-    near = units(0, 0)
     other = swap(jnp.concatenate([units(0, 1), units(1, 1)], axis=0), "core")
-    tokens = near.shape[0]
+    tokens = other.shape[0] // 2
+    near = jnp.concatenate([units(0, 0), other[:tokens]], axis=0)
     away = swap(jnp.concatenate([units(1, 0), other[tokens:]], axis=0), "zl")
-    away = jnp.concatenate([other[:tokens], away], axis=0)
     acts_core = swap(activations, "core")
 
     places = []
@@ -125,23 +116,26 @@
     places = jnp.stack(places).astype(jnp.int32)
 
     near = ring_up(ring_start(near, 0), 0)
-    near[3], away, sent = lax.optimization_barrier((near[3], away, activations))
+    near[3], away, acts_core, sent = lax.optimization_barrier(
+        (near[3], away, acts_core, activations)
+    )
     near = ring_start(jnp.concatenate(near, axis=0), 1)
-    away = ring_both(ring_start(away, 0), 0)
-    half = sent.shape[0] // 2
-    acts_low = (along_z(sent[:half], 1), along_z(sent[half:], -1))
-    near = ring_up(near, 1)
+    away = ring_up(ring_start(away, 0), 0)
+    acts_low = swap(sent, "zl")
+    first = arranged(places, activations, acts_core)
+    *near, away[3] = lax.optimization_barrier((*near, away[3]))
+    near = ring_both(near, 1)
+    gradient = product(near[0], first[0]) + product(near[1], first[1]) + product(near[2], first[2])
     away = ring_start(jnp.concatenate(away, axis=0), 1)
-    first = arranged(places, activations)
-    gradient = product(near[0], first[0])
-    for k in (2, 1, 3):
-        gradient = gradient + product(near[k], first[k])
-    acts_low = jnp.concatenate(after(acts_low, near[3]), axis=0)
-    second = arranged(places, acts_core, acts_low, swap(acts_low, "core"))
+    near[3], near[4], acts_low = lax.optimization_barrier((near[3], near[4], acts_low))
+    second = arranged(places, acts_low, swap(acts_low, "core"))
+    *away, near[3], near[4], second, gradient = lax.optimization_barrier(
+        (*away, near[3], near[4], second, gradient)
+    )
+    away = ring_both(away, 1)
+    half = near[3].shape[0]
+    gradient = gradient + product(near[3], first[3][:half]) + product(near[4], first[3][half:])
     gradient = gradient + product(away[0], second[0])
-    *away, gradient = lax.optimization_barrier((*away, gradient))
-    away = ring_both(away, 1)
-    half = away[3].shape[0]
     gradient = gradient + product(away[1], second[1]) + product(away[2], second[2])
     last = (product(away[3], second[3][:half]), product(away[4], second[3][half:]))
     last = lax.optimization_barrier(last)
@@ -152,7 +146,7 @@
     row_full = total_over(jnp.sum(squares, axis=1), ("x", "y"))
     row_moment_new = 0.8 * row_moment + 0.2 * row_full / D
     col_part = jnp.sum(squares, axis=0)
-    sums = jnp.concatenate([col_part, jnp.sum(row_moment_new.reshape(8, 128), axis=0)])
+    sums = jnp.concatenate([col_part, jnp.sum(row_moment_new.reshape(2, 512), axis=0)])
     scores_new = scores - 50.0 * weights * gradient
     sums = total_over(sums, ("zl", "core", "zh"))
     sums, weights, gradient = lax.optimization_barrier((sums, weights, gradient))

time: 165 us -> 174 us (1.055)
  waiting for transfers between devices: 55.7 us -> 71.6 us
  starting transfers between devices: 36.9 us -> 23.8 us
  blocking collectives: 25 us -> 33.3 us
  other arithmetic: 8.93 us -> 5.25 us
    ppermute x14, waiting for transfers between devices: 49.1 us -> 62.9 us  [shift(): return lax.ppermute(array, AXES, ring_pairs(phase, step))]
    all_to_all x2, blocking collectives: 25 us -> 33.3 us  [total_over(): lax.all_to_all(spread, axes, 0, 0, tiled=True)]
    ppermute x4 -> x5, starting transfers between devices: 15 us -> 7.45 us  [swap(): return lax.ppermute(array, axis, [(0, 1), (1, 0)])]
    ppermute x2 -> x0, starting transfers between devices: 5.86 us -> none  [along_z(): lax.ppermute(array, ('zl', 'zh'), [(place(z), place((z + step) % 8)) for...]
    sub x1 -> x0, other arithmetic: 3.16 us -> none  [local(): scores_new = scores - 50.0 * weights * gradient]
    unnamed x35 -> x36, local copies, waits for them, and re-layouts: 5.27 us -> 7.29 us
    ppermute x4 -> x5, waiting for transfers between devices: 6.66 us -> 8.68 us  [swap(): return lax.ppermute(array, axis, [(0, 1), (1, 0)])]
    dot_general x9 -> x10, matrix products: 17.5 us -> 18.6 us  [product(): lax.dot_general(grad_rows, act_rows, (((0,), (0,)), ((), ())), preferred_...]
  transfers between devices with their start and end apart: 20 -> 19, of which waited for: 10 -> 10; matrix products, arithmetic and copies ran while one was open for 15% -> 10% of each run, Pallas kernels for 4% -> 3%
where the time goes in v5:
time: 174 us
  waiting for transfers between devices  71.6 us (41%)
  blocking collectives  33.3 us (19%)
  starting transfers between devices  23.8 us (14%)
  matrix products  18.6 us (11%)
  local copies, waits for them, and re-layouts  12.3 us (7%)
  Pallas kernels  7.59 us (4%)
  other arithmetic  5.25 us (3%)
    ppermute x14, waiting for transfers between devices, shift(): return lax.ppermute(array, AXES, ring_pairs(phase, step))  62.9 us
    all_to_all x2, blocking collectives, total_over(): lax.all_to_all(spread, axes, 0, 0, tiled=True)  33.3 us
    dot_general x10, matrix products, product(): lax.dot_general(grad_rows, act_rows, (((0,), (0,)), ((), ())), preferred_...  18.6 us
    ppermute x14, starting transfers between devices, shift(): return lax.ppermute(array, AXES, ring_pairs(phase, step))  16.3 us
    ppermute x5, waiting for transfers between devices, swap(): return lax.ppermute(array, axis, [(0, 1), (1, 0)])  8.68 us
    pallas_call x2, Pallas kernels, arranged(): pl.pallas_call(arrange_kernel, in_specs=[pl.BlockSpec(memory_space=pltpu....  7.59 us
    ppermute x5, starting transfers between devices, swap(): return lax.ppermute(array, axis, [(0, 1), (1, 0)])  7.45 us
    unnamed x36, local copies, waits for them, and re-layouts  7.29 us
  transfers between devices with their start and end apart: 19, of which 10 were waited for; matrix products, arithmetic and copies ran while one was open for 10% of the time, Pallas kernels for 3%

profile of v5, /device:TPU:1, one launch (start us, length us, event | category | flops | bytes accessed | tf_op | source)
XLA Modules:
  0.0 173.9 jit_solution(2817358989613224453)
XLA Ops:
  0.6 3.3 %collective-permute-start.5 = (bf16[2048,512]{1,0:T(8,128)(2,1)}, bf16[2048,512]{1,0:T(8,128)(2,1)}, u32[]{:S(2)}, u32[]{:S(2)}) collective-permute-start(bf16[2048,512]{1,0:T(8,128)(2,1)} %refs_0_.1), channel_id=1, source_target_pairs={{0,64},{64,0},{1,65},{65,1},{2,66},{66,2},{3,67},{67,3},{4,68},{68... | collective-permute-start | bytes 6291464 | tf_op jit(solution)/shard_map/ppermute | solution.py:34
  4.0 1.3 constant_dynamic-slice_fusion
  5.5 3.0 %collective-permute-done = bf16[256,1024]{1,0:T(8,128)(2,1)S(1)} collective-permute-done((bf16[256,1024]{1,0:T(8,128)(2,1)S(1)}, bf16[256,1024]{1,0:T(8,128)(2,1)S(1)}, u32[]{:S(2)}, u32[]{:S(2)}) %collective-permute-start) | collective-permute-done | bytes 524320 | tf_op jit(solution)/shard_map/ppermute | solution.py:34
  8.7 2.7 %collective-permute-start.2 = (bf16[256,1024]{1,0:T(8,128)(2,1)S(1)}, bf16[256,1024]{1,0:T(8,128)(2,1)S(1)}, u32[]{:S(2)}, u32[]{:S(2)}) collective-permute-start(bf16[256,1024]{1,0:T(8,128)(2,1)S(1)} %pad_maximum_fusion.1), channel_id=1, source_target_pairs={{0,48},{4,52},{8,56},{12,60},{16,0},{20,4},{24,8},{28,12},{32,16},... | collective-permute-start | bytes 1572872 | tf_op jit(solution)/shard_map/ppermute | solution.py:30
  11.6 6.7 %collective-permute-done.1 = bf16[256,1024]{1,0:T(8,128)(2,1)S(1)} collective-permute-done((bf16[256,1024]{1,0:T(8,128)(2,1)S(1)}, bf16[256,1024]{1,0:T(8,128)(2,1)S(1)}, u32[]{:S(2)}, u32[]{:S(2)}) %collective-permute-start.1) | collective-permute-done | bytes 524320 | tf_op jit(solution)/shard_map/ppermute | solution.py:30
  18.3 5.7 %collective-permute-done.4 = bf16[256,1024]{1,0:T(8,128)(2,1)S(1)} collective-permute-done((bf16[256,1024]{1,0:T(8,128)(2,1)S(1)}, bf16[256,1024]{1,0:T(8,128)(2,1)S(1)}, u32[]{:S(2)}, u32[]{:S(2)}) %collective-permute-start.4) | collective-permute-done | bytes 524320 | tf_op jit(solution)/shard_map/ppermute | solution.py:34
  24.0 3.8 %collective-permute-done.3 = bf16[256,1024]{1,0:T(8,128)(2,1)S(1)} collective-permute-done((bf16[256,1024]{1,0:T(8,128)(2,1)S(1)}, bf16[256,1024]{1,0:T(8,128)(2,1)S(1)}, u32[]{:S(2)}, u32[]{:S(2)}) %collective-permute-start.3) | collective-permute-done | bytes 524320 | tf_op jit(solution)/shard_map/ppermute | solution.py:30
  27.9 2.7 %collective-permute-start.9 = (bf16[1024,1024]{1,0:T(8,128)(2,1)S(1)}, bf16[1024,1024]{1,0:T(8,128)(2,1)S(1)}, u32[]{:S(2)}, u32[]{:S(2)}) collective-permute-start(bf16[1024,1024]{1,0:T(8,128)(2,1)S(1)} %constant_dynamic-update-slice_fusion), channel_id=1, source_target_pairs={{0,12},{4,0},{8,4},{12,8},{16,28},{20,16},{24,20},{28,24},{32,44},... | collective-permute-start | bytes 6291464 | tf_op jit(solution)/shard_map/ppermute | solution.py:30
  30.6 2.7 %collective-permute-start.7 = (bf16[256,1024]{1,0:T(8,128)(2,1)S(1)}, bf16[256,1024]{1,0:T(8,128)(2,1)S(1)}, u32[]{:S(2)}, u32[]{:S(2)}) collective-permute-start(bf16[256,1024]{1,0:T(8,128)(2,1)S(1)} %collective-permute-done.4), channel_id=1, source_target_pairs={{0,48},{4,52},{8,56},{12,60},{16,0},{20,4},{24,8},{28,12},{32,16},... | collective-permute-start | bytes 1572872 | tf_op jit(solution)/shard_map/ppermute | solution.py:30
  33.3 12.4 %collective-permute-done.6 = bf16[256,1024]{1,0:T(8,128)(2,1)S(1)} collective-permute-done((bf16[256,1024]{1,0:T(8,128)(2,1)S(1)}, bf16[256,1024]{1,0:T(8,128)(2,1)S(1)}, u32[]{:S(2)}, u32[]{:S(2)}) %collective-permute-start.6) | collective-permute-done | bytes 524320 | tf_op jit(solution)/shard_map/ppermute | solution.py:30
  45.8 19.8 %collective-permute-done.8 = bf16[1024,1024]{1,0:T(8,128)(2,1)S(1)} collective-permute-done((bf16[1024,1024]{1,0:T(8,128)(2,1)S(1)}, bf16[1024,1024]{1,0:T(8,128)(2,1)S(1)}, u32[]{:S(2)}, u32[]{:S(2)}) %collective-permute-start.8) | collective-permute-done | bytes 2097184 | tf_op jit(solution)/shard_map/ppermute | solution.py:30
  65.6 1.3 copy-done.8
  67.0 0.5 copy-done.1
  67.5 2.3 %collective-permute-start.14 = (bf16[512,1024]{1,0:T(8,128)(2,1)S(1)}, bf16[512,1024]{1,0:T(8,128)(2,1)S(1)}, u32[]{:S(2)}, u32[]{:S(2)}) collective-permute-start(bf16[512,1024]{1,0:T(8,128)(2,1)S(1)} %slice.76), channel_id=1, source_target_pairs={{0,12},{4,0},{8,4},{12,8},{16,28},{20,16},{24,20},{28,24},{32,44},... | collective-permute-start | bytes 3145736 | tf_op jit(solution)/shard_map/ppermute | solution.py:30
  69.8 0.8 constant_dynamic-update-slice_fusion.8
  70.6 0.8 constant_dynamic-update-slice_fusion.7
  71.4 0.8 constant_dynamic-update-slice_fusion.6
  72.3 0.8 constant_dynamic-update-slice_fusion.5
  73.1 2.7 %collective-permute-start.12 = (bf16[1024,1024]{1,0:T(8,128)(2,1)}, bf16[1024,1024]{1,0:T(8,128)(2,1)}, u32[]{:S(2)}, u32[]{:S(2)}) collective-permute-start(bf16[1024,1024]{1,0:T(8,128)(2,1)} %constant_dynamic-update-slice_fusion.5), channel_id=1, source_target_pairs={{0,12},{4,0},{8,4},{12,8},{16,28},{20,16},{24,20},{28,24},{32,44},... | collective-permute-start | bytes 6291464 | tf_op jit(solution)/shard_map/ppermute | solution.py:30
  75.8 6.3 %collective-permute-done.13 = bf16[512,1024]{1,0:T(8,128)(2,1)S(1)} collective-permute-done((bf16[512,1024]{1,0:T(8,128)(2,1)S(1)}, bf16[512,1024]{1,0:T(8,128)(2,1)S(1)}, u32[]{:S(2)}, u32[]{:S(2)}) %collective-permute-start.13) | collective-permute-done | bytes 1048608 | tf_op jit(solution)/shard_map/ppermute | solution.py:30
  82.1 1.0 copy-done.6
  83.1 3.8 %collective-permute-start.16 = (bf16[2048,512]{1,0:T(8,128)(2,1)}, bf16[2048,512]{1,0:T(8,128)(2,1)}, u32[]{:S(2)}, u32[]{:S(2)}) collective-permute-start(bf16[2048,512]{1,0:T(8,128)(2,1)} %collective-permute-done.15.refs_0_), channel_id=1, source_target_pairs={{0,64},{64,0},{1,65},{65,1},{2,66},{66,2},{3,67},{67,3},{4,68},{68... | collective-permute-start | bytes 6291464 | tf_op jit(solution)/shard_map/ppermute | solution.py:34
  87.0 4.5 %shard_map.111 = bf16[4096,512]{1,0:T(8,128)(2,1)S(1)} custom-call(s32[16]{0:T(128)S(1)} %stack.67.place, bf16[2048,512]{1,0:T(8,128)(2,1)S(1)} %copy-done, bf16[2048,512]{1,0:T(8,128)(2,1)} %collective-permute-done.5.refs_1_), custom_call_target="tpu_custom_call" | custom-call | bytes 8388608 | tf_op jit(solution)/shard_map/pallas_call | solution.py:78
  91.5 1.3 fusion.6
  92.8 0.3 copy-done.11
  93.1 1.3 fusion.8
  94.4 0.3 copy-done.2
  94.7 1.3 add_add_fusion
  96.0 8.7 %collective-permute-done.11 = bf16[1024,1024]{1,0:T(8,128)(2,1)} collective-permute-done((bf16[1024,1024]{1,0:T(8,128)(2,1)}, bf16[1024,1024]{1,0:T(8,128)(2,1)}, u32[]{:S(2)}, u32[]{:S(2)}) %collective-permute-start.11) | collective-permute-done | bytes 2097184 | tf_op jit(solution)/shard_map/ppermute | solution.py:30
  104.7 3.1 %shard_map.110 = bf16[4096,512]{1,0:T(8,128)(2,1)S(1)} custom-call(s32[16]{0:T(128)S(1)} %stack.67.place, bf16[2048,512]{1,0:T(8,128)(2,1)} %collective-permute-done.15.refs_0_, bf16[2048,512]{1,0:T(8,128)(2,1)} %collective-permute-done.16.refs_1_), custom_call_target="tpu_custom_call" | custom-call | bytes 8388608 | tf_op jit(solution)/shard_map/pallas_call | solution.py:78
  107.7 1.3 slice.85
  109.0 2.9 %fusion.12 = f32[1024,512]{1,0:T(8,128)S(1)} fusion(bf16[1024,1024]{1,0:T(8,128)(2,1)} %collective-permute-done.11, bf16[4,1024,512]{2,1,0:T(8,128)(2,1)S(1)} %bitcast.49), kind=kOutput, calls=%fused_computation.16 | convolution fusion | flops 1073741824 | bytes 5242880 | tf_op jit(solution)/shard_map/dot_general | solution.py:52
  112.0 1.3 slice.86
  113.3 3.1 %collective-permute-start.18 = (bf16[512,1024]{1,0:T(8,128)(2,1)S(1)}, bf16[512,1024]{1,0:T(8,128)(2,1)S(1)}, u32[]{:S(2)}, u32[]{:S(2)}) collective-permute-start(bf16[512,1024]{1,0:T(8,128)(2,1)S(1)} %slice.86), channel_id=1, source_target_pairs={{0,12},{4,0},{8,4},{12,8},{16,28},{20,16},{24,20},{28,24},{32,44},... | collective-permute-start | bytes 3145736 | tf_op jit(solution)/shard_map/ppermute | solution.py:30
  116.5 0.7 fusion.23
  117.2 2.9 %fusion.10 = f32[1024,512]{1,0:T(8,128)S(1)} fusion(bf16[1024,1024]{1,0:T(8,128)(2,1)} %collective-permute-done.12, bf16[4,1024,512]{2,1,0:T(8,128)(2,1)S(1)} %bitcast.50), kind=kOutput, calls=%fused_computation.14 | convolution fusion | flops 1073741824 | bytes 5242880 | tf_op jit(solution)/shard_map/dot_general | solution.py:52
  120.1 2.9 %fusion.14 = f32[1024,512]{1,0:T(8,128)S(1)} fusion(bf16[1024,1024]{1,0:T(8,128)(2,1)} %constant_dynamic-update-slice_fusion.5, bf16[4,1024,512]{2,1,0:T(8,128)(2,1)S(1)} %bitcast.51), kind=kOutput, calls=%fused_computation.18 | convolution fusion | flops 1073741824 | bytes 5242880 | tf_op jit(solution)/shard_map/dot_general | solution.py:52
  123.0 4.3 %collective-permute-done.17 = bf16[512,1024]{1,0:T(8,128)(2,1)S(1)} collective-permute-done((bf16[512,1024]{1,0:T(8,128)(2,1)S(1)}, bf16[512,1024]{1,0:T(8,128)(2,1)S(1)}, u32[]{:S(2)}, u32[]{:S(2)}) %collective-permute-start.17) | collective-permute-done | bytes 1048608 | tf_op jit(solution)/shard_map/ppermute | solution.py:30
  127.3 0.9 collective-permute-done.18
  128.2 0.8 fusion.25
  129.0 0.7 fusion.27
  129.8 0.9 copy-done.3
  131.0 3.8 %fusion.1 = (f32[512]{0:T(512)S(1)}, f32[1024]{0:T(1024)S(1)}, f32[1024,512]{1,0:T(8,128)}, f32[1024,512]{1,0:T(8,128)}) fusion(f32[1024,512]{1,0:T(8,128)S(1)} %copy-done.4, f32[1024,512]{1,0:T(8,128)S(1)} %copy-done.3, f32[1024,512]{1,0:T(8,128)S(1)} %fusion.27, f32[1024,512]{1,0:T(8,128)S(1)} %fusion.25, f32[1024,512]{1,0:T(8,128)S(1)} %fusion.10, ...), kind=kOutput, calls=%fused_computation.7 | convolution fusion | flops 544733696 | bytes 24647680 | tf_op jit(solution)/shard_map/dot_general | solution.py:52
  134.8 11.7 %all_to_all.10 = f32[16,8,128]{2,1,0:T(8,128)S(1)} all-to-all(f32[16,8,128]{2,1,0:T(8,128)S(1)} %broadcast_in_dim.7), channel_id=1, replica_groups=mesh['zl'=2,'core'=2,'x'=4,'y'=4,'zh'=4] {'x','y'}, dimensions={0} | all-to-all | bytes 131072 | tf_op jit(solution)/shard_map/all_to_all | solution.py:93
  146.6 21.6 %all_to_all.11 = f32[16,8,128]{2,1,0:T(8,128)S(1)} all-to-all(f32[16,8,128]{2,1,0:T(8,128)S(1)} %broadcast_in_dim.16), channel_id=1, replica_groups=mesh['zl'=2,'core'=2,'x'=4,'y'=4,'zh'=4] {'zl','core','zh'}, dimensions={0} | all-to-all | bytes 131072 | tf_op jit(solution)/shard_map/all_to_all | solution.py:93
  168.2 0.6 slice_reduce_fusion
  169.5 0.6 divide_rsqrt_fusion
  170.0 3.9 %multiply_subtract_fusion.1 = (f32[1024,512]{1,0:T(8,128)}, bf16[1024,512]{1,0:T(8,128)(2,1)}) fusion(f32[1024,512]{1,0:T(8,128)S(1)} %copy-done.3, f32[1024,512]{1,0:T(8,128)} %get-tuple-element.73, f32[512]{0:T(512)S(1)} %get-tuple-element.81, f32[1024]{0:T(1024)S(1)} %get-tuple-element.79, bf16[1024,512]{1,0:T(8,128)(2,1)S(1)} %copy-done.5), kind=kLoop, calls=%fused_computation.1 | loop fusion | flops 5242880 | bytes 8394752 | tf_op jit(solution)/shard_map/sub | solution.py:157
  (62 shorter events, 1.6 us)
Async XLA Ops:
  0.6 27.2 %collective-permute-start.5 = (bf16[2048,512]{1,0:T(8,128)(2,1)}, bf16[2048,512]{1,0:T(8,128)(2,1)}, u32[]{:S(2)}, u32[]{:S(2)}) collective-permute-start(bf16[2048,512]{1,0:T(8,128)(2,1)} %refs_0_.1), channel_id=1, source_target_pairs={{0,64},{64,0},{1,65},{65,1},{2,66},{66,2},{3,67},{67,3},{4,68},{68... | collective-permute-start | bytes 6291464 | tf_op jit(solution)/shard_map/ppermute | solution.py:34
  5.3 3.1 %collective-permute-start = (bf16[256,1024]{1,0:T(8,128)(2,1)S(1)}, bf16[256,1024]{1,0:T(8,128)(2,1)S(1)}, u32[]{:S(2)}, u32[]{:S(2)}) collective-permute-start(bf16[256,1024]{1,0:T(8,128)(2,1)S(1)} %pad_maximum_fusion), channel_id=1, source_target_pairs={{0,64},{64,0},{1,65},{65,1},{2,66},{66,2},{3,67},{67,3},{4,68},{68... | collective-permute-start | bytes 1572872 | tf_op jit(solution)/shard_map/ppermute | solution.py:34
  8.6 9.6 %collective-permute-start.1 = (bf16[256,1024]{1,0:T(8,128)(2,1)S(1)}, bf16[256,1024]{1,0:T(8,128)(2,1)S(1)}, u32[]{:S(2)}, u32[]{:S(2)}) collective-permute-start(bf16[256,1024]{1,0:T(8,128)(2,1)S(1)} %pad_maximum_fusion.1), channel_id=1, source_target_pairs={{0,16},{4,20},{8,24},{12,28},{16,32},{20,36},{24,40},{28,44},{32,4... | collective-permute-start | bytes 1572872 | tf_op jit(solution)/shard_map/ppermute | solution.py:30
  8.7 9.5 %collective-permute-start.2 = (bf16[256,1024]{1,0:T(8,128)(2,1)S(1)}, bf16[256,1024]{1,0:T(8,128)(2,1)S(1)}, u32[]{:S(2)}, u32[]{:S(2)}) collective-permute-start(bf16[256,1024]{1,0:T(8,128)(2,1)S(1)} %pad_maximum_fusion.1), channel_id=1, source_target_pairs={{0,48},{4,52},{8,56},{12,60},{16,0},{20,4},{24,8},{28,12},{32,16},... | collective-permute-start | bytes 1572872 | tf_op jit(solution)/shard_map/ppermute | solution.py:30
  11.4 21.9 %copy-start = (bf16[2048,512]{1,0:T(8,128)(2,1)S(1)}, bf16[2048,512]{1,0:T(8,128)(2,1)}, u32[]{:S(2)}) copy-start(bf16[2048,512]{1,0:T(8,128)(2,1)} %refs_0_.1) | copy-start | bytes 6291460
  11.4 12.6 %collective-permute-start.4 = (bf16[256,1024]{1,0:T(8,128)(2,1)S(1)}, bf16[256,1024]{1,0:T(8,128)(2,1)S(1)}, u32[]{:S(2)}, u32[]{:S(2)}) collective-permute-start(bf16[256,1024]{1,0:T(8,128)(2,1)S(1)} %pad_maximum_fusion.2), channel_id=1, source_target_pairs={{0,128},{128,0},{1,129},{129,1},{2,130},{130,2},{3,131},{131,3},{4... | collective-permute-start | bytes 1572872 | tf_op jit(solution)/shard_map/ppermute | solution.py:34
  18.2 9.5 %collective-permute-start.3 = (bf16[256,1024]{1,0:T(8,128)(2,1)S(1)}, bf16[256,1024]{1,0:T(8,128)(2,1)S(1)}, u32[]{:S(2)}, u32[]{:S(2)}) collective-permute-start(bf16[256,1024]{1,0:T(8,128)(2,1)S(1)} %collective-permute-done.1), channel_id=1, source_target_pairs={{0,16},{4,20},{8,24},{12,28},{16,32},{20,36},{24,40},{28,44},{32,4... | collective-permute-start | bytes 1572872 | tf_op jit(solution)/shard_map/ppermute | solution.py:30
  27.8 54.3 %copy-start.10 = (bf16[1024,1024]{1,0:T(8,128)(2,1)}, bf16[1024,1024]{1,0:T(8,128)(2,1)S(1)}, u32[]{:S(2)}) copy-start(bf16[1024,1024]{1,0:T(8,128)(2,1)S(1)} %constant_dynamic-update-slice_fusion) | copy-start | bytes 6291460
  27.8 37.7 %collective-permute-start.8 = (bf16[1024,1024]{1,0:T(8,128)(2,1)S(1)}, bf16[1024,1024]{1,0:T(8,128)(2,1)S(1)}, u32[]{:S(2)}, u32[]{:S(2)}) collective-permute-start(bf16[1024,1024]{1,0:T(8,128)(2,1)S(1)} %constant_dynamic-update-slice_fusion), channel_id=1, source_target_pairs={{0,4},{4,8},{8,12},{12,0},{16,20},{20,24},{24,28},{28,16},{32,36},... | collective-permute-start | bytes 6291464 | tf_op jit(solution)/shard_map/ppermute | solution.py:30
  27.9 37.6 %collective-permute-start.9 = (bf16[1024,1024]{1,0:T(8,128)(2,1)S(1)}, bf16[1024,1024]{1,0:T(8,128)(2,1)S(1)}, u32[]{:S(2)}, u32[]{:S(2)}) collective-permute-start(bf16[1024,1024]{1,0:T(8,128)(2,1)S(1)} %constant_dynamic-update-slice_fusion), channel_id=1, source_target_pairs={{0,12},{4,0},{8,4},{12,8},{16,28},{20,16},{24,20},{28,24},{32,44},... | collective-permute-start | bytes 6291464 | tf_op jit(solution)/shard_map/ppermute | solution.py:30
  30.6 15.2 %collective-permute-start.6 = (bf16[256,1024]{1,0:T(8,128)(2,1)S(1)}, bf16[256,1024]{1,0:T(8,128)(2,1)S(1)}, u32[]{:S(2)}, u32[]{:S(2)}) collective-permute-start(bf16[256,1024]{1,0:T(8,128)(2,1)S(1)} %collective-permute-done.4), channel_id=1, source_target_pairs={{0,16},{4,20},{8,24},{12,28},{16,32},{20,36},{24,40},{28,44},{32,4... | collective-permute-start | bytes 1572872 | tf_op jit(solution)/shard_map/ppermute | solution.py:30
  30.6 15.2 %collective-permute-start.7 = (bf16[256,1024]{1,0:T(8,128)(2,1)S(1)}, bf16[256,1024]{1,0:T(8,128)(2,1)S(1)}, u32[]{:S(2)}, u32[]{:S(2)}) collective-permute-start(bf16[256,1024]{1,0:T(8,128)(2,1)S(1)} %collective-permute-done.4), channel_id=1, source_target_pairs={{0,48},{4,52},{8,56},{12,60},{16,0},{20,4},{24,8},{28,12},{32,16},... | collective-permute-start | bytes 1572872 | tf_op jit(solution)/shard_map/ppermute | solution.py:30
  33.3 48.8 %collective-permute-start.15 = (bf16[2048,512]{1,0:T(8,128)(2,1)S(1)}, bf16[2048,512]{1,0:T(8,128)(2,1)}, u32[]{:S(2)}, u32[]{:S(2)}) collective-permute-start(bf16[2048,512]{1,0:T(8,128)(2,1)S(1)} %copy-done), channel_id=1, source_target_pairs={{0,128},{128,0},{1,129},{129,1},{2,130},{130,2},{3,131},{131,3},{4... | collective-permute-start | bytes 6291464 | tf_op jit(solution)/shard_map/ppermute | solution.py:34
  45.8 19.8 %collective-permute-start.10 = (bf16[256,1024]{1,0:T(8,128)(2,1)S(1)}, bf16[256,1024]{1,0:T(8,128)(2,1)S(1)}, u32[]{:S(2)}, u32[]{:S(2)}) collective-permute-start(bf16[256,1024]{1,0:T(8,128)(2,1)S(1)} %collective-permute-done.6), channel_id=1, source_target_pairs={{0,16},{4,20},{8,24},{12,28},{16,32},{20,36},{24,40},{28,44},{32,4... | collective-permute-start | bytes 1572872 | tf_op jit(solution)/shard_map/ppermute | solution.py:30
  65.5 1.4 copy-start.8
  65.6 2.0 %copy-start.1 = (bf16[1024,1024]{1,0:T(8,128)(2,1)}, bf16[1024,1024]{1,0:T(8,128)(2,1)S(1)}, u32[]{:S(2)}) copy-start(bf16[1024,1024]{1,0:T(8,128)(2,1)S(1)} %collective-permute-done.9) | copy-start | bytes 6291460
  66.9 15.2 %collective-permute-start.13 = (bf16[512,1024]{1,0:T(8,128)(2,1)S(1)}, bf16[512,1024]{1,0:T(8,128)(2,1)S(1)}, u32[]{:S(2)}, u32[]{:S(2)}) collective-permute-start(bf16[512,1024]{1,0:T(8,128)(2,1)S(1)} %slice.75), channel_id=1, source_target_pairs={{0,4},{4,8},{8,12},{12,0},{16,20},{20,24},{24,28},{28,16},{32,36},... | collective-permute-start | bytes 3145736 | tf_op jit(solution)/shard_map/ppermute | solution.py:30
  67.5 14.6 %collective-permute-start.14 = (bf16[512,1024]{1,0:T(8,128)(2,1)S(1)}, bf16[512,1024]{1,0:T(8,128)(2,1)S(1)}, u32[]{:S(2)}, u32[]{:S(2)}) collective-permute-start(bf16[512,1024]{1,0:T(8,128)(2,1)S(1)} %slice.76), channel_id=1, source_target_pairs={{0,12},{4,0},{8,4},{12,8},{16,28},{20,16},{24,20},{28,24},{32,44},... | collective-permute-start | bytes 3145736 | tf_op jit(solution)/shard_map/ppermute | solution.py:30
  73.1 31.6 %collective-permute-start.11 = (bf16[1024,1024]{1,0:T(8,128)(2,1)}, bf16[1024,1024]{1,0:T(8,128)(2,1)}, u32[]{:S(2)}, u32[]{:S(2)}) collective-permute-start(bf16[1024,1024]{1,0:T(8,128)(2,1)} %constant_dynamic-update-slice_fusion.5), channel_id=1, source_target_pairs={{0,4},{4,8},{8,12},{12,0},{16,20},{20,24},{24,28},{28,16},{32,36},... | collective-permute-start | bytes 6291464 | tf_op jit(solution)/shard_map/ppermute | solution.py:30
  73.1 31.6 %collective-permute-start.12 = (bf16[1024,1024]{1,0:T(8,128)(2,1)}, bf16[1024,1024]{1,0:T(8,128)(2,1)}, u32[]{:S(2)}, u32[]{:S(2)}) collective-permute-start(bf16[1024,1024]{1,0:T(8,128)(2,1)} %constant_dynamic-update-slice_fusion.5), channel_id=1, source_target_pairs={{0,12},{4,0},{8,4},{12,8},{16,28},{20,16},{24,20},{28,24},{32,44},... | collective-permute-start | bytes 6291464 | tf_op jit(solution)/shard_map/ppermute | solution.py:30
  82.1 1.0 copy-start.6
  83.1 21.6 %collective-permute-start.16 = (bf16[2048,512]{1,0:T(8,128)(2,1)}, bf16[2048,512]{1,0:T(8,128)(2,1)}, u32[]{:S(2)}, u32[]{:S(2)}) collective-permute-start(bf16[2048,512]{1,0:T(8,128)(2,1)} %collective-permute-done.15.refs_0_), channel_id=1, source_target_pairs={{0,64},{64,0},{1,65},{65,1},{2,66},{66,2},{3,67},{67,3},{4,68},{68... | collective-permute-start | bytes 6291464 | tf_op jit(solution)/shard_map/ppermute | solution.py:34
  87.0 4.6 %copy-start.9 = (bf16[1024,1024]{1,0:T(8,128)(2,1)S(1)}, bf16[1024,1024]{1,0:T(8,128)(2,1)}, u32[]{:S(2)}) copy-start(bf16[1024,1024]{1,0:T(8,128)(2,1)} %copy-done.8) | copy-start | bytes 6291460
  91.5 1.6 copy-start.11
  93.1 1.6 copy-start.2
  111.9 15.4 %collective-permute-start.17 = (bf16[512,1024]{1,0:T(8,128)(2,1)S(1)}, bf16[512,1024]{1,0:T(8,128)(2,1)S(1)}, u32[]{:S(2)}, u32[]{:S(2)}) collective-permute-start(bf16[512,1024]{1,0:T(8,128)(2,1)S(1)} %slice.85), channel_id=1, source_target_pairs={{0,4},{4,8},{8,12},{12,0},{16,20},{20,24},{24,28},{28,16},{32,36},... | collective-permute-start | bytes 3145736 | tf_op jit(solution)/shard_map/ppermute | solution.py:30
  113.3 14.9 %collective-permute-start.18 = (bf16[512,1024]{1,0:T(8,128)(2,1)S(1)}, bf16[512,1024]{1,0:T(8,128)(2,1)S(1)}, u32[]{:S(2)}, u32[]{:S(2)}) collective-permute-start(bf16[512,1024]{1,0:T(8,128)(2,1)S(1)} %slice.86), channel_id=1, source_target_pairs={{0,12},{4,0},{8,4},{12,8},{16,28},{20,16},{24,20},{28,24},{32,44},... | collective-permute-start | bytes 3145736 | tf_op jit(solution)/shard_map/ppermute | solution.py:30
  128.2 1.6 copy-start.4
  129.0 1.8 %copy-start.3 = (f32[1024,512]{1,0:T(8,128)S(1)}, f32[1024,512]{1,0:T(8,128)}, u32[]{:S(2)}) copy-start(f32[1024,512]{1,0:T(8,128)} %param.9) | copy-start | bytes 6291460
  129.0 2.0 %copy-start.7 = (bf16[512,1024]{1,0:T(8,128)(2,1)S(1)}, bf16[512,1024]{1,0:T(8,128)(2,1)}, u32[]{:S(2)}) copy-start(bf16[512,1024]{1,0:T(8,128)(2,1)} %copy-done.6) | copy-start | bytes 3145732
  131.0 15.5 %copy-start.13 = (f32[1024]{0:T(1024)S(1)}, f32[1024]{0:T(1024)}, u32[]{:S(2)}) copy-start(f32[1024]{0:T(1024)} %param.12) | copy-start | bytes 12292
  131.0 38.5 %copy-start.14 = (f32[512]{0:T(512)S(1)}, f32[512]{0:T(512)}, u32[]{:S(2)}) copy-start(f32[512]{0:T(512)} %param.13) | copy-start | bytes 6148
  131.0 39.1 %copy-start.5 = (bf16[1024,512]{1,0:T(8,128)(2,1)S(1)}, bf16[1024,512]{1,0:T(8,128)(2,1)}, u32[]{:S(2)}) copy-start(bf16[1024,512]{1,0:T(8,128)(2,1)} %param.10) | copy-start | bytes 3145732
  146.5 27.4 %copy-start.12 = (f32[1024]{0:T(1024)}, f32[1024]{0:T(1024)S(1)}, u32[]{:S(2)}) copy-start(f32[1024]{0:T(1024)S(1)} %get-tuple-element.80) | copy-start | bytes 12292

commit v6 on v3

--- a/solution.py
+++ b/solution.py
@@ -40,7 +40,8 @@
 
 
 def ring_start(block, phase):
-    return [block, shift(block, phase, 1), shift(block, phase, -1)]
+    pair = (shift(block, phase, 1), shift(block, phase, -1))
+    return [block, *(pair if phase else lax.optimization_barrier(pair))]
 
 
 def ring_end(blocks, phase, step):
@@ -115,9 +116,12 @@
             places.append((x + dx) % 4 * 4 + (y + dy) % 4)
     places = jnp.stack(places).astype(jnp.int32)
 
-    near = after(ring_end(ring_start(near, 0), 0, 1), away)
-    (sent,) = after((activations,), *near)
+    near = ring_end(ring_start(near, 0), 0, 1)
+    near[3], away, acts_core, sent = lax.optimization_barrier(
+        (near[3], away, acts_core, activations)
+    )
     near = ring_start(jnp.concatenate(near, axis=0), 1)
+    near[1], near[2] = lax.optimization_barrier((near[1], near[2]))
     away = ring_end(ring_start(away, 0), 0, -1)
     half = sent.shape[0] // 2
     acts_low = (along_z(sent[:half], 1), along_z(sent[half:], -1))
@@ -140,13 +144,14 @@
     row_moment_new = 0.8 * row_moment + 0.2 * row_full / D
     col_part = jnp.sum(squares, axis=0)
     sums = jnp.concatenate([col_part, jnp.sum(row_moment_new.reshape(8, 128), axis=0)])
+    scores_new = scores - 50.0 * weights * gradient
     sums = total_over(sums, ("zl", "core", "zh"))
+    sums, weights, gradient = lax.optimization_barrier((sums, weights, gradient))
     col_moment_new = 0.8 * col_moment + 0.2 * sums[:512] / FF
     row_average = jnp.sum(sums[512:]) / FF
-    update = gradient * lax.rsqrt(row_moment_new[:, None] * col_moment_new[None, :] / row_average)
-    momentum_new = (0.9 * momentum.astype(jnp.float32) + 0.1 * update).astype(jnp.bfloat16)
+    scale = lax.rsqrt(row_moment_new)[:, None] * lax.rsqrt(col_moment_new / row_average)[None, :]
+    momentum_new = (0.9 * momentum.astype(jnp.float32) + 0.1 * (gradient * scale)).astype(jnp.bfloat16)
     weights_new = weights - 0.01 * momentum_new.astype(jnp.float32)
-    scores_new = scores - 50.0 * weights * gradient
     return (weights_new, momentum_new, scores_new, row_moment_new, col_moment_new)
 
 

time: 154 us -> 173 us (1.12)
  blocking collectives: 27.8 us -> 34.7 us
  other arithmetic: 6.37 us -> 13.2 us
  matrix products: 18.9 us -> 24.9 us
  waiting for transfers between devices: 57.5 us -> 51.6 us
  starting transfers between devices: 22.1 us -> 24.6 us
  Pallas kernels: 10.8 us -> 12.6 us
    ppermute x12, waiting for transfers between devices: 53.1 us -> 43.6 us  [shift(): return lax.ppermute(array, AXES, ring_pairs(phase, step))]
    sub x0 -> x1, other arithmetic: none -> 7.49 us  [local(): scores_new = scores - 50.0 * weights * gradient]
    all_to_all x2, blocking collectives: 27.8 us -> 34.7 us  [total_over(): return jnp.sum(lax.all_to_all(spread, axes, 0, 0, tiled=True), axis=0)]
    dot_general x8, matrix products: 18.9 us -> 24.9 us  [product(): lax.dot_general(grad_rows, act_rows, (((0,), (0,)), ((), ())), preferred_...]
    ppermute x12, starting transfers between devices: 9.29 us -> 14.2 us  [shift(): return lax.ppermute(array, AXES, ring_pairs(phase, step))]
    ppermute x4, starting transfers between devices: 8.3 us -> 4.4 us  [swap(): return lax.ppermute(array, axis, [(0, 1), (1, 0)])]
    ppermute x4, waiting for transfers between devices: 4.43 us -> 8.07 us  [swap(): return lax.ppermute(array, axis, [(0, 1), (1, 0)])]
    pallas_call x2, Pallas kernels: 10.8 us -> 12.6 us  [arranged(): pl.pallas_call(arrange_kernel, in_specs=[pl.BlockSpec(memory_space=pltpu....]
  transfers between devices with their start and end apart: 18 -> 18, of which waited for: 11 -> 10; matrix products, arithmetic and copies ran while one was open for 14% -> 18% of each run, Pallas kernels for 7% -> 7%
where the time goes in v6:
time: 173 us; the launch traced here: 172 us
  waiting for transfers between devices  51.6 us (30%)
  blocking collectives  34.7 us (20%)
  matrix products  24.9 us (14%)
  starting transfers between devices  24.6 us (14%)
  other arithmetic  13.2 us (8%)
  Pallas kernels  12.6 us (7%)
  local copies, waits for them, and re-layouts  9.09 us (5%)
    ppermute x12, waiting for transfers between devices, shift(): return lax.ppermute(array, AXES, ring_pairs(phase, step))  43.6 us
    all_to_all x2, blocking collectives, total_over(): return jnp.sum(lax.all_to_all(spread, axes, 0, 0, tiled=True), axis=0)  34.7 us
    dot_general x8, matrix products, product(): lax.dot_general(grad_rows, act_rows, (((0,), (0,)), ((), ())), preferred_...  24.9 us
    ppermute x12, starting transfers between devices, shift(): return lax.ppermute(array, AXES, ring_pairs(phase, step))  14.2 us
    pallas_call x2, Pallas kernels, arranged(): pl.pallas_call(arrange_kernel, in_specs=[pl.BlockSpec(memory_space=pltpu....  12.6 us
    ppermute x4, waiting for transfers between devices, swap(): return lax.ppermute(array, axis, [(0, 1), (1, 0)])  8.07 us
    sub x1, other arithmetic, local(): scores_new = scores - 50.0 * weights * gradient  7.49 us
    ppermute x2, starting transfers between devices, along_z(): lax.ppermute(array, ('zl', 'zh'), [(place(z), place((z + step) % 8)) for...  6.01 us
  transfers between devices with their start and end apart: 18, of which 10 were waited for; matrix products, arithmetic and copies ran while one was open for 18% of the time, Pallas kernels for 7%

profile of v6, /device:TPU:1, one launch (start us, length us, event | category | flops | bytes accessed | tf_op | source)
XLA Modules:
  0.0 172.2 jit_solution(10566653123498266887)
XLA Ops:
  0.6 3.3 %collective-permute-start.5 = (bf16[2048,512]{1,0:T(8,128)(2,1)}, bf16[2048,512]{1,0:T(8,128)(2,1)S(1)}, u32[]{:S(2)}, u32[]{:S(2)}) collective-permute-start(bf16[2048,512]{1,0:T(8,128)(2,1)} %first.1), channel_id=1, source_target_pairs={{0,64},{64,0},{1,65},{65,1},{2,66},{66,2},{3,67},{67,3},{4,68},{68... | collective-permute-start | bytes 6291464 | tf_op jit(solution)/shard_map/ppermute | solution.py:39
  4.0 2.0 %constant_dynamic-slice_fusion = (bf16[128,1024]{1,0:T(8,128)(2,1)S(1)}, bf16[128,1024]{1,0:T(8,128)(2,1)S(1)}, bf16[1024,1024]{1,0:T(8,128)(2,1)}, bf16[128,1024]{1,0:T(8,128)(2,1)S(1)}, bf16[128,1024]{1,0:T(8,128)(2,1)S(1)}) fusion(bf16[128,4096]{1,0:T(8,128)(2,1)} %param.8, s32[]{:T(128)S(6)} %select_n.203, s32[]{:T(128)S(6)} %select_n.201, ...), kind=kLoop, calls=%fused_computation.42 | loop fusion | bytes 2359312 | tf_op jit(solution)/shard_map/dynamic_slice | solution.py:104
  6.0 0.1 collective-permute-start
  6.2 2.3 %collective-permute-done = bf16[256,1024]{1,0:T(8,128)(2,1)S(1)} collective-permute-done((bf16[256,1024]{1,0:T(8,128)(2,1)S(1)}, bf16[256,1024]{1,0:T(8,128)(2,1)S(1)}, u32[]{:S(2)}, u32[]{:S(2)}) %collective-permute-start) | collective-permute-done | bytes 524320 | tf_op jit(solution)/shard_map/ppermute | solution.py:39
  8.5 0.8 constant_dynamic-update-slice_fusion.7
  9.4 2.7 %collective-permute-start.2 = (bf16[256,1024]{1,0:T(8,128)(2,1)S(1)}, bf16[256,1024]{1,0:T(8,128)(2,1)S(1)}, u32[]{:S(2)}, u32[]{:S(2)}) collective-permute-start(bf16[256,1024]{1,0:T(8,128)(2,1)S(1)} %pad_maximum_fusion.1), channel_id=1, source_target_pairs={{0,48},{4,52},{8,56},{12,60},{16,0},{20,4},{24,8},{28,12},{32,16},... | collective-permute-start | bytes 1572872 | tf_op jit(solution)/shard_map/ppermute | solution.py:30
  12.3 6.7 %collective-permute-done.1 = bf16[256,1024]{1,0:T(8,128)(2,1)S(1)} collective-permute-done((bf16[256,1024]{1,0:T(8,128)(2,1)S(1)}, bf16[256,1024]{1,0:T(8,128)(2,1)S(1)}, u32[]{:S(2)}, u32[]{:S(2)}) %collective-permute-start.1) | collective-permute-done | bytes 524320 | tf_op jit(solution)/shard_map/ppermute | solution.py:30
  19.0 5.7 %collective-permute-done.4 = bf16[256,1024]{1,0:T(8,128)(2,1)S(1)} collective-permute-done((bf16[256,1024]{1,0:T(8,128)(2,1)S(1)}, bf16[256,1024]{1,0:T(8,128)(2,1)S(1)}, u32[]{:S(2)}, u32[]{:S(2)}) %collective-permute-start.4) | collective-permute-done | bytes 524320 | tf_op jit(solution)/shard_map/ppermute | solution.py:39
  24.7 3.8 %collective-permute-done.3 = bf16[256,1024]{1,0:T(8,128)(2,1)S(1)} collective-permute-done((bf16[256,1024]{1,0:T(8,128)(2,1)S(1)}, bf16[256,1024]{1,0:T(8,128)(2,1)S(1)}, u32[]{:S(2)}, u32[]{:S(2)}) %collective-permute-start.3) | collective-permute-done | bytes 524320 | tf_op jit(solution)/shard_map/ppermute | solution.py:30
  28.5 2.7 %collective-permute-start.7 = (bf16[256,1024]{1,0:T(8,128)(2,1)S(1)}, bf16[256,1024]{1,0:T(8,128)(2,1)S(1)}, u32[]{:S(2)}, u32[]{:S(2)}) collective-permute-start(bf16[256,1024]{1,0:T(8,128)(2,1)S(1)} %collective-permute-done.4), channel_id=1, source_target_pairs={{0,48},{4,52},{8,56},{12,60},{16,0},{20,4},{24,8},{28,12},{32,16},... | collective-permute-start | bytes 1572872 | tf_op jit(solution)/shard_map/ppermute | solution.py:30
  31.2 0.8 constant_dynamic-update-slice_fusion.6
  32.0 0.8 constant_dynamic-update-slice_fusion.5
  32.8 0.8 constant_dynamic-update-slice_fusion.4
  33.7 2.7 %collective-permute-start.11 = (bf16[1024,1024]{1,0:T(8,128)(2,1)}, bf16[1024,1024]{1,0:T(8,128)(2,1)}, u32[]{:S(2)}, u32[]{:S(2)}) collective-permute-start(bf16[1024,1024]{1,0:T(8,128)(2,1)} %constant_dynamic-update-slice_fusion.4), channel_id=1, source_target_pairs={{0,12},{4,0},{8,4},{12,8},{16,28},{20,16},{24,20},{28,24},{32,44},... | collective-permute-start | bytes 6291464 | tf_op jit(solution)/shard_map/ppermute | solution.py:30
  36.3 1.7 collective-permute-done.6
  38.0 2.7 %collective-permute-start.8 = (bf16[256,1024]{1,0:T(8,128)(2,1)S(1)}, bf16[256,1024]{1,0:T(8,128)(2,1)S(1)}, u32[]{:S(2)}, u32[]{:S(2)}) collective-permute-start(bf16[256,1024]{1,0:T(8,128)(2,1)S(1)} %collective-permute-done.7), channel_id=1, source_target_pairs={{0,48},{4,52},{8,56},{12,60},{16,0},{20,4},{24,8},{28,12},{32,16},... | collective-permute-start | bytes 1572872 | tf_op jit(solution)/shard_map/ppermute | solution.py:30
  40.7 0.8 constant_dynamic-update-slice_fusion.3
  41.5 0.8 constant_dynamic-update-slice_fusion.2
  42.4 0.8 constant_dynamic-update-slice_fusion.1
  43.2 9.2 %collective-permute-done.8 = bf16[256,1024]{1,0:T(8,128)(2,1)S(1)} collective-permute-done((bf16[256,1024]{1,0:T(8,128)(2,1)S(1)}, bf16[256,1024]{1,0:T(8,128)(2,1)S(1)}, u32[]{:S(2)}, u32[]{:S(2)}) %collective-permute-start.8) | collective-permute-done | bytes 524320 | tf_op jit(solution)/shard_map/ppermute | solution.py:30
  52.4 0.8 constant_dynamic-update-slice_fusion
  53.2 0.6 collective-permute-start.9
  54.0 0.1 fusion.18
  54.1 1.8 %collective-permute-start.13 = (bf16[1024,512]{1,0:T(8,128)(2,1)S(1)}, bf16[1024,512]{1,0:T(8,128)(2,1)S(1)}, u32[]{:S(2)}, u32[]{:S(2)}) collective-permute-start(bf16[1024,512]{1,0:T(8,128)(2,1)S(1)} %get-tuple-element.58), channel_id=1, source_target_pairs={{0,128},{128,1},{1,129},{129,2},{2,130},{130,3},{3,131},{131,0},{4... | collective-permute-start | bytes 3145736 | tf_op jit(solution)/shard_map/ppermute | solution.py:35
  55.9 4.2 %collective-permute-start.14 = (bf16[1024,512]{1,0:T(8,128)(2,1)S(1)}, bf16[1024,512]{1,0:T(8,128)(2,1)S(1)}, u32[]{:S(2)}, u32[]{:S(2)}) collective-permute-start(bf16[1024,512]{1,0:T(8,128)(2,1)S(1)} %get-tuple-element.57), channel_id=1, source_target_pairs={{0,131},{128,0},{1,128},{129,1},{2,129},{130,2},{3,130},{131,3},{4... | collective-permute-start | bytes 3145736 | tf_op jit(solution)/shard_map/ppermute | solution.py:35
  60.1 6.3 %shard_map.110 = bf16[4096,512]{1,0:T(8,128)(2,1)S(1)} custom-call(s32[16]{0:T(128)S(1)} %stack.67.place, bf16[2048,512]{1,0:T(8,128)(2,1)S(1)} %copy-done, bf16[2048,512]{1,0:T(8,128)(2,1)S(1)} %copy-done.2), custom_call_target="tpu_custom_call" | custom-call | bytes 8388608 | tf_op jit(solution)/shard_map/pallas_call | solution.py:78
  66.4 2.9 %fusion.15 = f32[1024,512]{1,0:T(8,128)S(1)} fusion(bf16[1024,1024]{1,0:T(8,128)(2,1)} %constant_dynamic-update-slice_fusion.4, bf16[4096,512]{1,0:T(8,128)(2,1)S(1)} %shard_map.110), kind=kOutput, calls=%fused_computation.21 | convolution fusion | flops 1073741824 | bytes 5242880 | tf_op jit(solution)/shard_map/dot_general | solution.py:56
  69.4 2.9 %fusion.13 = f32[1024,512]{1,0:T(8,128)S(1)} fusion(bf16[1024,1024]{1,0:T(8,128)(2,1)} %collective-permute-done.10, bf16[4096,512]{1,0:T(8,128)(2,1)S(1)} %shard_map.110), kind=kOutput, calls=%fused_computation.19 | convolution fusion | flops 1073741824 | bytes 5242880 | tf_op jit(solution)/shard_map/dot_general | solution.py:56
  72.3 2.9 %add_add_fusion = f32[1024,512]{1,0:T(8,128)S(1)} fusion(f32[1024,512]{1,0:T(8,128)S(1)} %fusion.15, f32[1024,512]{1,0:T(8,128)S(1)} %fusion.13, bf16[1024,1024]{1,0:T(8,128)(2,1)} %collective-permute-done.11, bf16[4096,512]{1,0:T(8,128)(2,1)S(1)} %shard_map.110), kind=kOutput, calls=%fused_computation.5 | convolution fusion | flops 1074790400 | bytes 9437184 | tf_op jit(solution)/shard_map/dot_general | solution.py:56
  75.2 15.6 %collective-permute-done.9 = bf16[1024,1024]{1,0:T(8,128)(2,1)} collective-permute-done((bf16[1024,1024]{1,0:T(8,128)(2,1)}, bf16[1024,1024]{1,0:T(8,128)(2,1)}, u32[]{:S(2)}, u32[]{:S(2)}) %collective-permute-start.9) | collective-permute-done | bytes 2097184 | tf_op jit(solution)/shard_map/ppermute | solution.py:30
  90.9 0.8 collective-permute-start.15
  91.7 2.7 %collective-permute-start.17 = (bf16[1024,1024]{1,0:T(8,128)(2,1)}, bf16[1024,1024]{1,0:T(8,128)(2,1)S(1)}, u32[]{:S(2)}, u32[]{:S(2)}) collective-permute-start(bf16[1024,1024]{1,0:T(8,128)(2,1)} %collective-permute-done.9), channel_id=1, source_target_pairs={{0,12},{4,0},{8,4},{12,8},{16,28},{20,16},{24,20},{28,24},{32,44},... | collective-permute-start | bytes 6291464 | tf_op jit(solution)/shard_map/ppermute | solution.py:30
  94.4 1.6 collective-permute-done.12
  96.0 2.6 %fusion.10 = f32[1024,512]{1,0:T(8,128)} fusion(bf16[1024,1024]{1,0:T(8,128)(2,1)S(1)} %collective-permute-done.12, bf16[4096,512]{1,0:T(8,128)(2,1)S(1)} %shard_map.110), kind=kOutput, calls=%fused_computation.16 | convolution fusion | flops 1073741824 | bytes 5242880 | tf_op jit(solution)/shard_map/dot_general | solution.py:56
  98.7 6.3 %shard_map.111 = bf16[4096,512]{1,0:T(8,128)(2,1)S(1)} custom-call(s32[16]{0:T(128)S(1)} %stack.67.place, bf16[2048,512]{1,0:T(8,128)(2,1)S(1)} %constant_dynamic-update-slice_fusion.9.first, bf16[2048,512]{1,0:T(8,128)(2,1)S(1)} %collective-permute-done.15.second), custom_call_target="tpu_custom_call" | custom-call | bytes 8388608 | tf_op jit(solution)/shard_map/pallas_call | solution.py:78
  105.0 4.2 %fusion.8 = f32[1024,512]{1,0:T(8,128)} fusion(bf16[1024,1024]{1,0:T(8,128)(2,1)} %constant_dynamic-update-slice_fusion, bf16[4096,512]{1,0:T(8,128)(2,1)S(1)} %shard_map.111), kind=kOutput, calls=%fused_computation.14 | convolution fusion | flops 1073741824 | bytes 5242880 | tf_op jit(solution)/shard_map/dot_general | solution.py:56
  109.2 4.2 %fusion.6 = f32[1024,512]{1,0:T(8,128)} fusion(bf16[1024,1024]{1,0:T(8,128)(2,1)} %collective-permute-done.9, bf16[4096,512]{1,0:T(8,128)(2,1)S(1)} %shard_map.111), kind=kOutput, calls=%fused_computation.12 | convolution fusion | flops 1073741824 | bytes 5242880 | tf_op jit(solution)/shard_map/dot_general | solution.py:56
  113.4 4.3 %collective-permute-done.17 = bf16[1024,1024]{1,0:T(8,128)(2,1)S(1)} collective-permute-done((bf16[1024,1024]{1,0:T(8,128)(2,1)}, bf16[1024,1024]{1,0:T(8,128)(2,1)S(1)}, u32[]{:S(2)}, u32[]{:S(2)}) %collective-permute-start.17) | collective-permute-done | bytes 2097184 | tf_op jit(solution)/shard_map/ppermute | solution.py:30
  117.7 2.6 %fusion.2 = f32[1024,512]{1,0:T(8,128)} fusion(bf16[1024,1024]{1,0:T(8,128)(2,1)S(1)} %collective-permute-done.17, bf16[4096,512]{1,0:T(8,128)(2,1)S(1)} %shard_map.111), kind=kOutput, calls=%fused_computation.8 | convolution fusion | flops 1073741824 | bytes 5242880 | tf_op jit(solution)/shard_map/dot_general | solution.py:56
  120.3 0.7 collective-permute-done.16
  121.0 2.6 %fusion.4 = f32[1024,512]{1,0:T(8,128)} fusion(bf16[1024,1024]{1,0:T(8,128)(2,1)S(1)} %collective-permute-done.16, bf16[4096,512]{1,0:T(8,128)(2,1)S(1)} %shard_map.111), kind=kOutput, calls=%fused_computation.10 | convolution fusion | flops 1073741824 | bytes 5242880 | tf_op jit(solution)/shard_map/dot_general | solution.py:56
  123.7 7.5 %multiply_subtract_fusion = (f32[1024,512]{1,0:T(8,128)}, f32[1024,512]{1,0:T(8,128)S(1)}) fusion(f32[1024,512]{1,0:T(8,128)S(1)} %copy-done.4, f32[1024,512]{1,0:T(8,128)S(1)} %copy-done.3, f32[1024,512]{1,0:T(8,128)} %fusion.4, f32[1024,512]{1,0:T(8,128)} %fusion.2, f32[1024,512]{1,0:T(8,128)} %fusion.6, f32[1024,512]{1,0:T(8,128)} %fusion.8, ...), kind=kLoop, calls=%fused_computation | loop fusion | flops 4718592 | bytes 20971520 | tf_op jit(solution)/shard_map/sub | solution.py:147
  131.2 0.4 fusion.1
  131.6 11.3 %all_to_all.12 = f32[16,1,1024]{2,1,0:T(1,128)S(1)} all-to-all(f32[16,1,1024]{2,1,0:T(1,128)S(1)} %broadcast_in_dim.4), channel_id=1, replica_groups=mesh['zl'=2,'core'=2,'x'=4,'y'=4,'zh'=4] {'x','y'}, dimensions={0} | all-to-all | bytes 131072 | tf_op jit(solution)/shard_map/all_to_all | solution.py:94
  143.0 23.4 %all_to_all.13 = f32[16,1,640]{2,1,0:T(1,128)S(1)} all-to-all(f32[16,1,640]{2,1,0:T(1,128)S(1)} %broadcast_in_dim.5), channel_id=1, replica_groups=mesh['zl'=2,'core'=2,'x'=4,'y'=4,'zh'=4] {'zl','core','zh'}, dimensions={0} | all-to-all | bytes 81920 | tf_op jit(solution)/shard_map/all_to_all | solution.py:94
  166.4 0.6 slice_reduce_fusion
  167.7 0.6 divide_rsqrt_fusion
  168.3 3.9 %multiply_subtract_fusion.1 = (f32[1024,512]{1,0:T(8,128)}, bf16[1024,512]{1,0:T(8,128)(2,1)}) fusion(f32[1024,512]{1,0:T(8,128)} %param.9, f32[1024,512]{1,0:T(8,128)S(1)} %get-tuple-element.43, f32[512]{0:T(512)S(1)} %get-tuple-element.53, f32[1024]{0:T(1024)S(1)} %get-tuple-element.51, bf16[1024,512]{1,0:T(8,128)(2,1)S(1)} %copy-done.5), kind=kLoop, calls=%fused_computation.1 | loop fusion | flops 5242880 | bytes 8394752 | tf_op jit(solution)/shard_map/sub | solution.py:154
  (46 shorter events, 0.9 us)
Async XLA Ops:
  0.6 27.9 %collective-permute-start.5 = (bf16[2048,512]{1,0:T(8,128)(2,1)}, bf16[2048,512]{1,0:T(8,128)(2,1)S(1)}, u32[]{:S(2)}, u32[]{:S(2)}) collective-permute-start(bf16[2048,512]{1,0:T(8,128)(2,1)} %first.1), channel_id=1, source_target_pairs={{0,64},{64,0},{1,65},{65,1},{2,66},{66,2},{3,67},{67,3},{4,68},{68... | collective-permute-start | bytes 6291464 | tf_op jit(solution)/shard_map/ppermute | solution.py:39
  6.0 2.5 %collective-permute-start = (bf16[256,1024]{1,0:T(8,128)(2,1)S(1)}, bf16[256,1024]{1,0:T(8,128)(2,1)S(1)}, u32[]{:S(2)}, u32[]{:S(2)}) collective-permute-start(bf16[256,1024]{1,0:T(8,128)(2,1)S(1)} %pad_maximum_fusion), channel_id=1, source_target_pairs={{0,64},{64,0},{1,65},{65,1},{2,66},{66,2},{3,67},{67,3},{4,68},{68... | collective-permute-start | bytes 1572872 | tf_op jit(solution)/shard_map/ppermute | solution.py:39
  9.3 9.6 %collective-permute-start.1 = (bf16[256,1024]{1,0:T(8,128)(2,1)S(1)}, bf16[256,1024]{1,0:T(8,128)(2,1)S(1)}, u32[]{:S(2)}, u32[]{:S(2)}) collective-permute-start(bf16[256,1024]{1,0:T(8,128)(2,1)S(1)} %pad_maximum_fusion.1), channel_id=1, source_target_pairs={{0,16},{4,20},{8,24},{12,28},{16,32},{20,36},{24,40},{28,44},{32,4... | collective-permute-start | bytes 1572872 | tf_op jit(solution)/shard_map/ppermute | solution.py:30
  9.4 9.5 %collective-permute-start.2 = (bf16[256,1024]{1,0:T(8,128)(2,1)S(1)}, bf16[256,1024]{1,0:T(8,128)(2,1)S(1)}, u32[]{:S(2)}, u32[]{:S(2)}) collective-permute-start(bf16[256,1024]{1,0:T(8,128)(2,1)S(1)} %pad_maximum_fusion.1), channel_id=1, source_target_pairs={{0,48},{4,52},{8,56},{12,60},{16,0},{20,4},{24,8},{28,12},{32,16},... | collective-permute-start | bytes 1572872 | tf_op jit(solution)/shard_map/ppermute | solution.py:30
  12.1 12.6 %collective-permute-start.4 = (bf16[256,1024]{1,0:T(8,128)(2,1)S(1)}, bf16[256,1024]{1,0:T(8,128)(2,1)S(1)}, u32[]{:S(2)}, u32[]{:S(2)}) collective-permute-start(bf16[256,1024]{1,0:T(8,128)(2,1)S(1)} %pad_maximum_fusion.2), channel_id=1, source_target_pairs={{0,128},{128,0},{1,129},{129,1},{2,130},{130,2},{3,131},{131,3},{4... | collective-permute-start | bytes 1572872 | tf_op jit(solution)/shard_map/ppermute | solution.py:39
  18.9 9.5 %collective-permute-start.3 = (bf16[256,1024]{1,0:T(8,128)(2,1)S(1)}, bf16[256,1024]{1,0:T(8,128)(2,1)S(1)}, u32[]{:S(2)}, u32[]{:S(2)}) collective-permute-start(bf16[256,1024]{1,0:T(8,128)(2,1)S(1)} %collective-permute-done.1), channel_id=1, source_target_pairs={{0,16},{4,20},{8,24},{12,28},{16,32},{20,36},{24,40},{28,44},{32,4... | collective-permute-start | bytes 1572872 | tf_op jit(solution)/shard_map/ppermute | solution.py:30
  28.5 12.2 %copy-start.1 = (bf16[2048,512]{1,0:T(8,128)(2,1)}, bf16[2048,512]{1,0:T(8,128)(2,1)S(1)}, u32[]{:S(2)}) copy-start(bf16[2048,512]{1,0:T(8,128)(2,1)S(1)} %collective-permute-done.5.second) | copy-start | bytes 6291460
  28.5 9.5 %collective-permute-start.6 = (bf16[256,1024]{1,0:T(8,128)(2,1)S(1)}, bf16[256,1024]{1,0:T(8,128)(2,1)S(1)}, u32[]{:S(2)}, u32[]{:S(2)}) collective-permute-start(bf16[256,1024]{1,0:T(8,128)(2,1)S(1)} %collective-permute-done.4), channel_id=1, source_target_pairs={{0,16},{4,20},{8,24},{12,28},{16,32},{20,36},{24,40},{28,44},{32,4... | collective-permute-start | bytes 1572872 | tf_op jit(solution)/shard_map/ppermute | solution.py:30
  28.5 9.5 %collective-permute-start.7 = (bf16[256,1024]{1,0:T(8,128)(2,1)S(1)}, bf16[256,1024]{1,0:T(8,128)(2,1)S(1)}, u32[]{:S(2)}, u32[]{:S(2)}) collective-permute-start(bf16[256,1024]{1,0:T(8,128)(2,1)S(1)} %collective-permute-done.4), channel_id=1, source_target_pairs={{0,48},{4,52},{8,56},{12,60},{16,0},{20,4},{24,8},{28,12},{32,16},... | collective-permute-start | bytes 1572872 | tf_op jit(solution)/shard_map/ppermute | solution.py:30
  33.7 35.7 %collective-permute-start.10 = (bf16[1024,1024]{1,0:T(8,128)(2,1)}, bf16[1024,1024]{1,0:T(8,128)(2,1)}, u32[]{:S(2)}, u32[]{:S(2)}) collective-permute-start(bf16[1024,1024]{1,0:T(8,128)(2,1)} %constant_dynamic-update-slice_fusion.4), channel_id=1, source_target_pairs={{0,4},{4,8},{8,12},{12,0},{16,20},{20,24},{24,28},{28,16},{32,36},... | collective-permute-start | bytes 6291464 | tf_op jit(solution)/shard_map/ppermute | solution.py:30
  33.7 35.7 %collective-permute-start.11 = (bf16[1024,1024]{1,0:T(8,128)(2,1)}, bf16[1024,1024]{1,0:T(8,128)(2,1)}, u32[]{:S(2)}, u32[]{:S(2)}) collective-permute-start(bf16[1024,1024]{1,0:T(8,128)(2,1)} %constant_dynamic-update-slice_fusion.4), channel_id=1, source_target_pairs={{0,12},{4,0},{8,4},{12,8},{16,28},{20,16},{24,20},{28,24},{32,44},... | collective-permute-start | bytes 6291464 | tf_op jit(solution)/shard_map/ppermute | solution.py:30
  38.0 14.4 %collective-permute-start.8 = (bf16[256,1024]{1,0:T(8,128)(2,1)S(1)}, bf16[256,1024]{1,0:T(8,128)(2,1)S(1)}, u32[]{:S(2)}, u32[]{:S(2)}) collective-permute-start(bf16[256,1024]{1,0:T(8,128)(2,1)S(1)} %collective-permute-done.7), channel_id=1, source_target_pairs={{0,48},{4,52},{8,56},{12,60},{16,0},{20,4},{24,8},{28,12},{32,16},... | collective-permute-start | bytes 1572872 | tf_op jit(solution)/shard_map/ppermute | solution.py:30
  41.5 12.4 %copy-start = (bf16[2048,512]{1,0:T(8,128)(2,1)S(1)}, bf16[2048,512]{1,0:T(8,128)(2,1)}, u32[]{:S(2)}) copy-start(bf16[2048,512]{1,0:T(8,128)(2,1)} %first.1) | copy-start | bytes 6291460
  53.2 37.5 %collective-permute-start.9 = (bf16[1024,1024]{1,0:T(8,128)(2,1)}, bf16[1024,1024]{1,0:T(8,128)(2,1)}, u32[]{:S(2)}, u32[]{:S(2)}) collective-permute-start(bf16[1024,1024]{1,0:T(8,128)(2,1)} %constant_dynamic-update-slice_fusion), channel_id=1, source_target_pairs={{0,12},{4,0},{8,4},{12,8},{16,28},{20,16},{24,20},{28,24},{32,44},... | collective-permute-start | bytes 6291464 | tf_op jit(solution)/shard_map/ppermute | solution.py:30
  54.0 6.2 %copy-start.2 = (bf16[2048,512]{1,0:T(8,128)(2,1)S(1)}, bf16[2048,512]{1,0:T(8,128)(2,1)}, u32[]{:S(2)}) copy-start(bf16[2048,512]{1,0:T(8,128)(2,1)} %copy-done.1) | copy-start | bytes 6291460
  54.1 36.7 %collective-permute-start.13 = (bf16[1024,512]{1,0:T(8,128)(2,1)S(1)}, bf16[1024,512]{1,0:T(8,128)(2,1)S(1)}, u32[]{:S(2)}, u32[]{:S(2)}) collective-permute-start(bf16[1024,512]{1,0:T(8,128)(2,1)S(1)} %get-tuple-element.58), channel_id=1, source_target_pairs={{0,128},{128,1},{1,129},{129,2},{2,130},{130,3},{3,131},{131,0},{4... | collective-permute-start | bytes 3145736 | tf_op jit(solution)/shard_map/ppermute | solution.py:35
  55.9 34.9 %collective-permute-start.14 = (bf16[1024,512]{1,0:T(8,128)(2,1)S(1)}, bf16[1024,512]{1,0:T(8,128)(2,1)S(1)}, u32[]{:S(2)}, u32[]{:S(2)}) collective-permute-start(bf16[1024,512]{1,0:T(8,128)(2,1)S(1)} %get-tuple-element.57), channel_id=1, source_target_pairs={{0,131},{128,0},{1,128},{129,1},{2,129},{130,2},{3,130},{131,3},{4... | collective-permute-start | bytes 3145736 | tf_op jit(solution)/shard_map/ppermute | solution.py:35
  69.3 26.7 %collective-permute-start.12 = (bf16[1024,1024]{1,0:T(8,128)(2,1)}, bf16[1024,1024]{1,0:T(8,128)(2,1)S(1)}, u32[]{:S(2)}, u32[]{:S(2)}) collective-permute-start(bf16[1024,1024]{1,0:T(8,128)(2,1)} %collective-permute-done.10), channel_id=1, source_target_pairs={{0,4},{4,8},{8,12},{12,0},{16,20},{20,24},{24,28},{28,16},{32,36},... | collective-permute-start | bytes 6291464 | tf_op jit(solution)/shard_map/ppermute | solution.py:30
  90.9 7.7 %collective-permute-start.15 = (bf16[2048,512]{1,0:T(8,128)(2,1)S(1)}, bf16[2048,512]{1,0:T(8,128)(2,1)S(1)}, u32[]{:S(2)}, u32[]{:S(2)}) collective-permute-start(bf16[2048,512]{1,0:T(8,128)(2,1)S(1)} %constant_dynamic-update-slice_fusion.9.first), channel_id=1, source_target_pairs={{0,64},{64,0},{1,65},{65,1},{2,66},{66,2},{3,67},{67,3},{4,68},{68... | collective-permute-start | bytes 6291464 | tf_op jit(solution)/shard_map/ppermute | solution.py:39
  91.7 26.0 %collective-permute-start.17 = (bf16[1024,1024]{1,0:T(8,128)(2,1)}, bf16[1024,1024]{1,0:T(8,128)(2,1)S(1)}, u32[]{:S(2)}, u32[]{:S(2)}) collective-permute-start(bf16[1024,1024]{1,0:T(8,128)(2,1)} %collective-permute-done.9), channel_id=1, source_target_pairs={{0,12},{4,0},{8,4},{12,8},{16,28},{20,16},{24,20},{28,24},{32,44},... | collective-permute-start | bytes 6291464 | tf_op jit(solution)/shard_map/ppermute | solution.py:30
  94.4 26.6 %collective-permute-start.16 = (bf16[1024,1024]{1,0:T(8,128)(2,1)}, bf16[1024,1024]{1,0:T(8,128)(2,1)S(1)}, u32[]{:S(2)}, u32[]{:S(2)}) collective-permute-start(bf16[1024,1024]{1,0:T(8,128)(2,1)} %constant_dynamic-update-slice_fusion), channel_id=1, source_target_pairs={{0,4},{4,8},{8,12},{12,0},{16,20},{20,24},{24,28},{28,16},{32,36},... | collective-permute-start | bytes 6291464 | tf_op jit(solution)/shard_map/ppermute | solution.py:30
  120.3 3.3 %copy-start.3 = (f32[1024,512]{1,0:T(8,128)S(1)}, f32[1024,512]{1,0:T(8,128)}, u32[]{:S(2)}) copy-start(f32[1024,512]{1,0:T(8,128)} %param.9) | copy-start | bytes 6291460
  120.3 3.3 %copy-start.4 = (f32[1024,512]{1,0:T(8,128)S(1)}, f32[1024,512]{1,0:T(8,128)}, u32[]{:S(2)}) copy-start(f32[1024,512]{1,0:T(8,128)} %param.11) | copy-start | bytes 6291460
  131.1 11.8 %copy-start.7 = (f32[1024]{0:T(1024)S(1)}, f32[1024]{0:T(1024)}, u32[]{:S(2)}) copy-start(f32[1024]{0:T(1024)} %param.12) | copy-start | bytes 12292
  131.1 36.6 %copy-start.8 = (f32[512]{0:T(512)S(1)}, f32[512]{0:T(512)}, u32[]{:S(2)}) copy-start(f32[512]{0:T(512)} %param.13) | copy-start | bytes 6148
  131.2 37.1 %copy-start.5 = (bf16[1024,512]{1,0:T(8,128)(2,1)S(1)}, bf16[1024,512]{1,0:T(8,128)(2,1)}, u32[]{:S(2)}) copy-start(bf16[1024,512]{1,0:T(8,128)(2,1)} %param.10) | copy-start | bytes 3145732
  143.0 29.2 %copy-start.6 = (f32[1024]{0:T(1024)}, f32[1024]{0:T(1024)S(1)}, u32[]{:S(2)}) copy-start(f32[1024]{0:T(1024)S(1)} %get-tuple-element.52) | copy-start | bytes 12292

commit v7 on v3

--- a/solution.py
+++ b/solution.py
@@ -115,7 +115,8 @@
             places.append((x + dx) % 4 * 4 + (y + dy) % 4)
     places = jnp.stack(places).astype(jnp.int32)
 
-    near = after(ring_end(ring_start(near, 0), 0, 1), away)
+    near = ring_end(ring_start(near, 0), 0, 1)
+    near[3:] = after(near[3:], away)
     (sent,) = after((activations,), *near)
     near = ring_start(jnp.concatenate(near, axis=0), 1)
     away = ring_end(ring_start(away, 0), 0, -1)
@@ -143,7 +144,8 @@
     sums = total_over(sums, ("zl", "core", "zh"))
     col_moment_new = 0.8 * col_moment + 0.2 * sums[:512] / FF
     row_average = jnp.sum(sums[512:]) / FF
-    update = gradient * lax.rsqrt(row_moment_new[:, None] * col_moment_new[None, :] / row_average)
+    row_scale, col_scale = lax.rsqrt(row_moment_new), lax.rsqrt(col_moment_new / row_average)
+    update = gradient * (row_scale[:, None] * col_scale[None, :])
     momentum_new = (0.9 * momentum.astype(jnp.float32) + 0.1 * update).astype(jnp.bfloat16)
     weights_new = weights - 0.01 * momentum_new.astype(jnp.float32)
     scores_new = scores - 50.0 * weights * gradient

time: 154 us -> 156 us (1.013)
  waiting for transfers between devices: 57.5 us -> 50.6 us
  starting transfers between devices: 22.1 us -> 27.9 us
  blocking collectives: 27.8 us -> 29.6 us
    ppermute x12, waiting for transfers between devices: 53.1 us -> 46.2 us  [shift(): return lax.ppermute(array, AXES, ring_pairs(phase, step))]
    ppermute x12, starting transfers between devices: 9.29 us -> 12.7 us  [shift(): return lax.ppermute(array, AXES, ring_pairs(phase, step))]
    unnamed x19 -> x18, local copies, waits for them, and re-layouts: 5.06 us -> 7.09 us
    all_to_all x2, blocking collectives: 27.8 us -> 29.6 us  [total_over(): return jnp.sum(lax.all_to_all(spread, axes, 0, 0, tiled=True), axis=0)]
    ppermute x2, starting transfers between devices: 4.48 us -> 6.05 us  [along_z(): lax.ppermute(array, ('zl', 'zh'), [(place(z), place((z + step) % 8)) for...]
  transfers between devices with their start and end apart: 18 -> 18, of which waited for: 11 -> 10; matrix products, arithmetic and copies ran while one was open for 14% -> 13% of each run, Pallas kernels for 7% -> 7%
where the time goes in v7:
time: 156 us; the launch traced here: 155 us
  waiting for transfers between devices  50.6 us (32%)
  blocking collectives  29.6 us (19%)
  starting transfers between devices  27.9 us (18%)
  matrix products  19 us (12%)
  Pallas kernels  10.8 us (7%)
  local copies, waits for them, and re-layouts  9.1 us (6%)
  other arithmetic  6.8 us (4%)
    ppermute x12, waiting for transfers between devices, shift(): return lax.ppermute(array, AXES, ring_pairs(phase, step))  46.2 us
    all_to_all x2, blocking collectives, total_over(): return jnp.sum(lax.all_to_all(spread, axes, 0, 0, tiled=True), axis=0)  29.6 us
    dot_general x8, matrix products, product(): lax.dot_general(grad_rows, act_rows, (((0,), (0,)), ((), ())), preferred_...  19 us
    ppermute x12, starting transfers between devices, shift(): return lax.ppermute(array, AXES, ring_pairs(phase, step))  12.7 us
    pallas_call x2, Pallas kernels, arranged(): pl.pallas_call(arrange_kernel, in_specs=[pl.BlockSpec(memory_space=pltpu....  10.8 us
    ppermute x4, starting transfers between devices, swap(): return lax.ppermute(array, axis, [(0, 1), (1, 0)])  9.13 us
    unnamed x18, local copies, waits for them, and re-layouts  7.09 us
    ppermute x2, starting transfers between devices, along_z(): lax.ppermute(array, ('zl', 'zh'), [(place(z), place((z + step) % 8)) for...  6.05 us
  transfers between devices with their start and end apart: 18, of which 10 were waited for; matrix products, arithmetic and copies ran while one was open for 13% of the time, Pallas kernels for 7%

profile of v7, /device:TPU:1, one launch (start us, length us, event | category | flops | bytes accessed | tf_op | source)
XLA Modules:
  0.0 155.3 jit_solution(2653613363713585274)
XLA Ops:
  0.7 2.1 %constant_dynamic-update-slice_fusion.8 = (bf16[1024,1024]{1,0:T(8,128)(2,1)}, bf16[128,1024]{1,0:T(8,128)(2,1)S(1)}, bf16[128,1024]{1,0:T(8,128)(2,1)S(1)}, bf1...) fusion(bf16[128,4096]{1,0:T(8,128)(2,1)} %param.8, s32[]{:T(128)S(6)} %select_n.203, s32[]{:T(128)S(6)} %select_n.201, ...), kind=kLoop, calls=%fused_computation.34 | loop fusion | bytes 2359312
  2.8 3.3 %collective-permute-start = (bf16[256,1024]{1,0:T(8,128)(2,1)S(1)}, bf16[256,1024]{1,0:T(8,128)(2,1)S(1)}, u32[]{:S(2)}, u32[]{:S(2)}) collective-permute-start(bf16[256,1024]{1,0:T(8,128)(2,1)S(1)} %pad_maximum_fusion), channel_id=1, source_target_pairs={{0,64},{64,0},{1,65},{65,1},{2,66},{66,2},{3,67},{67,3},{4,68},{68... | collective-permute-start | bytes 1572872 | tf_op jit(solution)/shard_map/ppermute | solution.py:39
  6.1 1.5 collective-permute-done
  7.6 0.8 constant_dynamic-update-slice_fusion.7
  8.6 1.3 collective-permute-start.1
  9.9 1.6 %collective-permute-start.7 = (bf16[256,1024]{1,0:T(8,128)(2,1)S(1)}, bf16[256,1024]{1,0:T(8,128)(2,1)S(1)}, u32[]{:S(2)}, u32[]{:S(2)}) collective-permute-start(bf16[256,1024]{1,0:T(8,128)(2,1)S(1)} %pad_maximum_fusion.2), channel_id=1, source_target_pairs={{0,48},{4,52},{8,56},{12,60},{16,0},{20,4},{24,8},{28,12},{32,16},... | collective-permute-start | bytes 1572872 | tf_op jit(solution)/shard_map/ppermute | solution.py:30
  11.4 6.6 %collective-permute-done.6 = bf16[256,1024]{1,0:T(8,128)(2,1)S(1)} collective-permute-done((bf16[256,1024]{1,0:T(8,128)(2,1)S(1)}, bf16[256,1024]{1,0:T(8,128)(2,1)S(1)}, u32[]{:S(2)}, u32[]{:S(2)}) %collective-permute-start.6) | collective-permute-done | bytes 524320 | tf_op jit(solution)/shard_map/ppermute | solution.py:30
  18.1 1.2 collective-permute-start.9
  19.3 2.5 %collective-permute-done.1 = bf16[256,1024]{1,0:T(8,128)(2,1)S(1)} collective-permute-done((bf16[256,1024]{1,0:T(8,128)(2,1)S(1)}, bf16[256,1024]{1,0:T(8,128)(2,1)S(1)}, u32[]{:S(2)}, u32[]{:S(2)}) %collective-permute-start.1) | collective-permute-done | bytes 524320 | tf_op jit(solution)/shard_map/ppermute | solution.py:39
  21.8 2.9 %collective-permute-start.3 = (bf16[256,1024]{1,0:T(8,128)(2,1)S(1)}, bf16[256,1024]{1,0:T(8,128)(2,1)S(1)}, u32[]{:S(2)}, u32[]{:S(2)}) collective-permute-start(bf16[256,1024]{1,0:T(8,128)(2,1)S(1)} %collective-permute-done.1), channel_id=1, source_target_pairs={{0,48},{4,52},{8,56},{12,60},{16,0},{20,4},{24,8},{28,12},{32,16},... | collective-permute-start | bytes 1572872 | tf_op jit(solution)/shard_map/ppermute | solution.py:30
  24.7 0.8 constant_dynamic-update-slice_fusion.6
  25.5 0.8 constant_dynamic-update-slice_fusion.5
  26.3 1.3 collective-permute-done.8
  27.6 0.8 constant_dynamic-update-slice_fusion.4
  28.4 2.7 %collective-permute-start.11 = (bf16[1024,1024]{1,0:T(8,128)(2,1)}, bf16[1024,1024]{1,0:T(8,128)(2,1)}, u32[]{:S(2)}, u32[]{:S(2)}) collective-permute-start(bf16[1024,1024]{1,0:T(8,128)(2,1)} %constant_dynamic-update-slice_fusion.4), channel_id=1, source_target_pairs={{0,12},{4,0},{8,4},{12,8},{16,28},{20,16},{24,20},{28,24},{32,44},... | collective-permute-start | bytes 6291464 | tf_op jit(solution)/shard_map/ppermute | solution.py:30
  31.1 3.1 %collective-permute-start.4 = (bf16[256,1024]{1,0:T(8,128)(2,1)S(1)}, bf16[256,1024]{1,0:T(8,128)(2,1)S(1)}, u32[]{:S(2)}, u32[]{:S(2)}) collective-permute-start(bf16[256,1024]{1,0:T(8,128)(2,1)S(1)} %collective-permute-done.3), channel_id=1, source_target_pairs={{0,48},{4,52},{8,56},{12,60},{16,0},{20,4},{24,8},{28,12},{32,16},... | collective-permute-start | bytes 1572872 | tf_op jit(solution)/shard_map/ppermute | solution.py:30
  34.2 0.8 constant_dynamic-update-slice_fusion.3
  35.0 0.8 constant_dynamic-update-slice_fusion.2
  35.9 0.8 constant_dynamic-update-slice_fusion.1
  36.7 9.3 %collective-permute-done.4 = bf16[256,1024]{1,0:T(8,128)(2,1)S(1)} collective-permute-done((bf16[256,1024]{1,0:T(8,128)(2,1)S(1)}, bf16[256,1024]{1,0:T(8,128)(2,1)S(1)}, u32[]{:S(2)}, u32[]{:S(2)}) %collective-permute-start.4) | collective-permute-done | bytes 524320 | tf_op jit(solution)/shard_map/ppermute | solution.py:30
  46.0 0.8 constant_dynamic-update-slice_fusion
  46.8 0.9 collective-permute-start.5
  47.7 0.1 fusion.20
  47.9 1.8 %collective-permute-start.13 = (bf16[1024,512]{1,0:T(8,128)(2,1)S(1)}, bf16[1024,512]{1,0:T(8,128)(2,1)S(1)}, u32[]{:S(2)}, u32[]{:S(2)}) collective-permute-start(bf16[1024,512]{1,0:T(8,128)(2,1)S(1)} %get-tuple-element.35), channel_id=1, source_target_pairs={{0,128},{128,1},{1,129},{129,2},{2,130},{130,3},{3,131},{131,0},{4... | collective-permute-start | bytes 3145736 | tf_op jit(solution)/shard_map/ppermute | solution.py:35
  49.7 4.2 %collective-permute-start.14 = (bf16[1024,512]{1,0:T(8,128)(2,1)S(1)}, bf16[1024,512]{1,0:T(8,128)(2,1)S(1)}, u32[]{:S(2)}, u32[]{:S(2)}) collective-permute-start(bf16[1024,512]{1,0:T(8,128)(2,1)S(1)} %get-tuple-element.34), channel_id=1, source_target_pairs={{0,131},{128,0},{1,128},{129,1},{2,129},{130,2},{3,130},{131,3},{4... | collective-permute-start | bytes 3145736 | tf_op jit(solution)/shard_map/ppermute | solution.py:35
  53.9 4.5 %shard_map.110 = bf16[4096,512]{1,0:T(8,128)(2,1)S(1)} custom-call(s32[16]{0:T(128)S(1)} %stack.67.place, bf16[2048,512]{1,0:T(8,128)(2,1)S(1)} %copy-done, bf16[2048,512]{1,0:T(8,128)(2,1)} %collective-permute-done.9.second), custom_call_target="tpu_custom_call" | custom-call | bytes 8388608 | tf_op jit(solution)/shard_map/pallas_call | solution.py:77
  58.5 2.9 %fusion.17 = f32[1024,512]{1,0:T(8,128)S(1)} fusion(bf16[1024,1024]{1,0:T(8,128)(2,1)} %constant_dynamic-update-slice_fusion.4, bf16[4096,512]{1,0:T(8,128)(2,1)S(1)} %shard_map.110), kind=kOutput, calls=%fused_computation.21 | convolution fusion | flops 1073741824 | bytes 5242880 | tf_op jit(solution)/shard_map/dot_general | solution.py:55
  61.5 2.9 %fusion.15 = f32[1024,512]{1,0:T(8,128)S(1)} fusion(bf16[1024,1024]{1,0:T(8,128)(2,1)} %collective-permute-done.10, bf16[4096,512]{1,0:T(8,128)(2,1)S(1)} %shard_map.110), kind=kOutput, calls=%fused_computation.19 | convolution fusion | flops 1073741824 | bytes 5242880 | tf_op jit(solution)/shard_map/dot_general | solution.py:55
  64.4 3.0 %add_add_fusion = f32[1024,512]{1,0:T(8,128)S(1)} fusion(f32[1024,512]{1,0:T(8,128)S(1)} %fusion.17, f32[1024,512]{1,0:T(8,128)S(1)} %fusion.15, bf16[1024,1024]{1,0:T(8,128)(2,1)} %collective-permute-done.11, bf16[4096,512]{1,0:T(8,128)(2,1)S(1)} %shard_map.110), kind=kOutput, calls=%fused_computation.5 | convolution fusion | flops 1074790400 | bytes 9437184 | tf_op jit(solution)/shard_map/dot_general | solution.py:55
  67.3 15.2 %collective-permute-done.5 = bf16[1024,1024]{1,0:T(8,128)(2,1)} collective-permute-done((bf16[1024,1024]{1,0:T(8,128)(2,1)}, bf16[1024,1024]{1,0:T(8,128)(2,1)}, u32[]{:S(2)}, u32[]{:S(2)}) %collective-permute-start.5) | collective-permute-done | bytes 2097184 | tf_op jit(solution)/shard_map/ppermute | solution.py:30
  82.7 3.3 %collective-permute-start.15 = (bf16[2048,512]{1,0:T(8,128)(2,1)S(1)}, bf16[2048,512]{1,0:T(8,128)(2,1)S(1)}, u32[]{:S(2)}, u32[]{:S(2)}) collective-permute-start(bf16[2048,512]{1,0:T(8,128)(2,1)S(1)} %constant_dynamic-update-slice_fusion.9.first), channel_id=1, source_target_pairs={{0,64},{64,0},{1,65},{65,1},{2,66},{66,2},{3,67},{67,3},{4,68},{68... | collective-permute-start | bytes 6291464 | tf_op jit(solution)/shard_map/ppermute | solution.py:39
  86.0 0.9 collective-permute-start.17
  86.8 0.6 collective-permute-start.16
  87.4 0.6 collective-permute-done.12
  88.1 1.3 fusion.9
  89.3 0.4 collective-permute-done.15.second
  89.7 6.3 %shard_map.111 = bf16[4096,512]{1,0:T(8,128)(2,1)S(1)} custom-call(s32[16]{0:T(128)S(1)} %stack.67.place, bf16[2048,512]{1,0:T(8,128)(2,1)S(1)} %constant_dynamic-update-slice_fusion.9.first, bf16[2048,512]{1,0:T(8,128)(2,1)S(1)} %collective-permute-done.15.second), custom_call_target="tpu_custom_call" | custom-call | bytes 8388608 | tf_op jit(solution)/shard_map/pallas_call | solution.py:77
  96.1 2.9 %fusion.6 = f32[1024,512]{1,0:T(8,128)S(1)} fusion(bf16[1024,1024]{1,0:T(8,128)(2,1)} %collective-permute-done.5, bf16[4096,512]{1,0:T(8,128)(2,1)S(1)} %shard_map.111), kind=kOutput, calls=%fused_computation.12 | convolution fusion | flops 1073741824 | bytes 5242880 | tf_op jit(solution)/shard_map/dot_general | solution.py:55
  98.9 12.4 %collective-permute-done.17 = bf16[1024,1024]{1,0:T(8,128)(2,1)S(1)} collective-permute-done((bf16[1024,1024]{1,0:T(8,128)(2,1)}, bf16[1024,1024]{1,0:T(8,128)(2,1)S(1)}, u32[]{:S(2)}, u32[]{:S(2)}) %collective-permute-start.17) | collective-permute-done | bytes 2097184 | tf_op jit(solution)/shard_map/ppermute | solution.py:30
  111.3 1.3 fusion.2
  112.6 0.8 collective-permute-done.16
  113.4 1.3 fusion.4
  114.8 3.6 %fusion = (f32[512]{0:T(512)S(1)}, f32[1024]{0:T(1024)S(1)}, f32[1024,512]{1,0:T(8,128)S(1)}) fusion(f32[1024,512]{1,0:T(8,128)S(1)} %fusion.4, f32[1024,512]{1,0:T(8,128)S(1)} %fusion.2, f32[1024,512]{1,0:T(8,128)S(1)} %fusion.6, bf16[1024,1024]{1,0:T(8,128)(2,1)} %constant_dynamic-update-slice_fusion, bf16[4096,512]{1,0:T(8,128)(2,1)S(1)} %shard_map.111, ...), kind=kOutput, calls=%fused_computation.6 | convolution fusion | flops 1078983168 | bytes 15734784 | tf_op jit(solution)/shard_map/dot_general | solution.py:55
  118.4 11.7 %all_to_all.12 = f32[16,1,1024]{2,1,0:T(1,128)S(1)} all-to-all(f32[16,1,1024]{2,1,0:T(1,128)S(1)} %broadcast_in_dim.4), channel_id=1, replica_groups=mesh['zl'=2,'core'=2,'x'=4,'y'=4,'zh'=4] {'x','y'}, dimensions={0} | all-to-all | bytes 131072 | tf_op jit(solution)/shard_map/all_to_all | solution.py:93
  130.2 17.9 %all_to_all.13 = f32[16,1,640]{2,1,0:T(1,128)S(1)} all-to-all(f32[16,1,640]{2,1,0:T(1,128)S(1)} %broadcast_in_dim.5), channel_id=1, replica_groups=mesh['zl'=2,'core'=2,'x'=4,'y'=4,'zh'=4] {'zl','core','zh'}, dimensions={0} | all-to-all | bytes 81920 | tf_op jit(solution)/shard_map/all_to_all | solution.py:93
  148.1 0.6 slice_reduce_fusion
  149.4 0.6 divide_rsqrt_fusion
  150.0 5.4 %multiply_subtract_fusion.1 = (f32[1024,512]{1,0:T(8,128)}, bf16[1024,512]{1,0:T(8,128)(2,1)}, f32[1024,512]{1,0:T(8,128)}) fusion(f32[1024,512]{1,0:T(8,128)} %param.9, f32[1024,512]{1,0:T(8,128)S(1)} %get-tuple-element.42, f32[512]{0:T(512)S(1)} %get-tuple-element.29, f32[1024]{0:T(1024)S(1)} %get-tuple-element.27, bf16[1024,512]{1,0:T(8,128)(2,1)S(1)} %copy-done.1, ...), kind=kLoop, calls=%fused_computation.1 | loop fusion | flops 6815744 | bytes 12589056 | tf_op jit(solution)/shard_map/sub | solution.py:150
  (36 shorter events, 0.7 us)
Async XLA Ops:
  2.7 15.4 %copy-start = (bf16[2048,512]{1,0:T(8,128)(2,1)S(1)}, bf16[2048,512]{1,0:T(8,128)(2,1)}, u32[]{:S(2)}) copy-start(bf16[2048,512]{1,0:T(8,128)(2,1)} %first.1) | copy-start | bytes 6291460
  2.8 4.9 %collective-permute-start = (bf16[256,1024]{1,0:T(8,128)(2,1)S(1)}, bf16[256,1024]{1,0:T(8,128)(2,1)S(1)}, u32[]{:S(2)}, u32[]{:S(2)}) collective-permute-start(bf16[256,1024]{1,0:T(8,128)(2,1)S(1)} %pad_maximum_fusion), channel_id=1, source_target_pairs={{0,64},{64,0},{1,65},{65,1},{2,66},{66,2},{3,67},{67,3},{4,68},{68... | collective-permute-start | bytes 1572872 | tf_op jit(solution)/shard_map/ppermute | solution.py:39
  8.5 9.6 %collective-permute-start.6 = (bf16[256,1024]{1,0:T(8,128)(2,1)S(1)}, bf16[256,1024]{1,0:T(8,128)(2,1)S(1)}, u32[]{:S(2)}, u32[]{:S(2)}) collective-permute-start(bf16[256,1024]{1,0:T(8,128)(2,1)S(1)} %pad_maximum_fusion.2), channel_id=1, source_target_pairs={{0,16},{4,20},{8,24},{12,28},{16,32},{20,36},{24,40},{28,44},{32,4... | collective-permute-start | bytes 1572872 | tf_op jit(solution)/shard_map/ppermute | solution.py:30
  8.6 13.2 %collective-permute-start.1 = (bf16[256,1024]{1,0:T(8,128)(2,1)S(1)}, bf16[256,1024]{1,0:T(8,128)(2,1)S(1)}, u32[]{:S(2)}, u32[]{:S(2)}) collective-permute-start(bf16[256,1024]{1,0:T(8,128)(2,1)S(1)} %pad_maximum_fusion.1), channel_id=1, source_target_pairs={{0,128},{128,0},{1,129},{129,1},{2,130},{130,2},{3,131},{131,3},{4... | collective-permute-start | bytes 1572872 | tf_op jit(solution)/shard_map/ppermute | solution.py:39
  9.9 15.7 %collective-permute-start.7 = (bf16[256,1024]{1,0:T(8,128)(2,1)S(1)}, bf16[256,1024]{1,0:T(8,128)(2,1)S(1)}, u32[]{:S(2)}, u32[]{:S(2)}) collective-permute-start(bf16[256,1024]{1,0:T(8,128)(2,1)S(1)} %pad_maximum_fusion.2), channel_id=1, source_target_pairs={{0,48},{4,52},{8,56},{12,60},{16,0},{20,4},{24,8},{28,12},{32,16},... | collective-permute-start | bytes 1572872 | tf_op jit(solution)/shard_map/ppermute | solution.py:30
  18.1 9.5 %collective-permute-start.8 = (bf16[256,1024]{1,0:T(8,128)(2,1)S(1)}, bf16[256,1024]{1,0:T(8,128)(2,1)S(1)}, u32[]{:S(2)}, u32[]{:S(2)}) collective-permute-start(bf16[256,1024]{1,0:T(8,128)(2,1)S(1)} %collective-permute-done.6), channel_id=1, source_target_pairs={{0,16},{4,20},{8,24},{12,28},{16,32},{20,36},{24,40},{28,44},{32,4... | collective-permute-start | bytes 1572872 | tf_op jit(solution)/shard_map/ppermute | solution.py:30
  18.1 31.6 %collective-permute-start.9 = (bf16[2048,512]{1,0:T(8,128)(2,1)S(1)}, bf16[2048,512]{1,0:T(8,128)(2,1)}, u32[]{:S(2)}, u32[]{:S(2)}) collective-permute-start(bf16[2048,512]{1,0:T(8,128)(2,1)S(1)} %copy-done), channel_id=1, source_target_pairs={{0,64},{64,0},{1,65},{65,1},{2,66},{66,2},{3,67},{67,3},{4,68},{68... | collective-permute-start | bytes 6291464 | tf_op jit(solution)/shard_map/ppermute | solution.py:39
  21.8 9.3 %collective-permute-start.3 = (bf16[256,1024]{1,0:T(8,128)(2,1)S(1)}, bf16[256,1024]{1,0:T(8,128)(2,1)S(1)}, u32[]{:S(2)}, u32[]{:S(2)}) collective-permute-start(bf16[256,1024]{1,0:T(8,128)(2,1)S(1)} %collective-permute-done.1), channel_id=1, source_target_pairs={{0,48},{4,52},{8,56},{12,60},{16,0},{20,4},{24,8},{28,12},{32,16},... | collective-permute-start | bytes 1572872 | tf_op jit(solution)/shard_map/ppermute | solution.py:30
  24.7 10.4 %collective-permute-start.2 = (bf16[256,1024]{1,0:T(8,128)(2,1)S(1)}, bf16[256,1024]{1,0:T(8,128)(2,1)S(1)}, u32[]{:S(2)}, u32[]{:S(2)}) collective-permute-start(bf16[256,1024]{1,0:T(8,128)(2,1)S(1)} %collective-permute-done.1), channel_id=1, source_target_pairs={{0,16},{4,20},{8,24},{12,28},{16,32},{20,36},{24,40},{28,44},{32,4... | collective-permute-start | bytes 1572872 | tf_op jit(solution)/shard_map/ppermute | solution.py:30
  28.4 32.9 %collective-permute-start.10 = (bf16[1024,1024]{1,0:T(8,128)(2,1)}, bf16[1024,1024]{1,0:T(8,128)(2,1)}, u32[]{:S(2)}, u32[]{:S(2)}) collective-permute-start(bf16[1024,1024]{1,0:T(8,128)(2,1)} %constant_dynamic-update-slice_fusion.4), channel_id=1, source_target_pairs={{0,4},{4,8},{8,12},{12,0},{16,20},{20,24},{24,28},{28,16},{32,36},... | collective-permute-start | bytes 6291464 | tf_op jit(solution)/shard_map/ppermute | solution.py:30
  28.4 32.9 %collective-permute-start.11 = (bf16[1024,1024]{1,0:T(8,128)(2,1)}, bf16[1024,1024]{1,0:T(8,128)(2,1)}, u32[]{:S(2)}, u32[]{:S(2)}) collective-permute-start(bf16[1024,1024]{1,0:T(8,128)(2,1)} %constant_dynamic-update-slice_fusion.4), channel_id=1, source_target_pairs={{0,12},{4,0},{8,4},{12,8},{16,28},{20,16},{24,20},{28,24},{32,44},... | collective-permute-start | bytes 6291464 | tf_op jit(solution)/shard_map/ppermute | solution.py:30
  31.1 14.8 %collective-permute-start.4 = (bf16[256,1024]{1,0:T(8,128)(2,1)S(1)}, bf16[256,1024]{1,0:T(8,128)(2,1)S(1)}, u32[]{:S(2)}, u32[]{:S(2)}) collective-permute-start(bf16[256,1024]{1,0:T(8,128)(2,1)S(1)} %collective-permute-done.3), channel_id=1, source_target_pairs={{0,48},{4,52},{8,56},{12,60},{16,0},{20,4},{24,8},{28,12},{32,16},... | collective-permute-start | bytes 1572872 | tf_op jit(solution)/shard_map/ppermute | solution.py:30
  46.8 35.7 %collective-permute-start.5 = (bf16[1024,1024]{1,0:T(8,128)(2,1)}, bf16[1024,1024]{1,0:T(8,128)(2,1)}, u32[]{:S(2)}, u32[]{:S(2)}) collective-permute-start(bf16[1024,1024]{1,0:T(8,128)(2,1)} %constant_dynamic-update-slice_fusion), channel_id=1, source_target_pairs={{0,12},{4,0},{8,4},{12,8},{16,28},{20,16},{24,20},{28,24},{32,44},... | collective-permute-start | bytes 6291464 | tf_op jit(solution)/shard_map/ppermute | solution.py:30
  47.9 34.6 %collective-permute-start.13 = (bf16[1024,512]{1,0:T(8,128)(2,1)S(1)}, bf16[1024,512]{1,0:T(8,128)(2,1)S(1)}, u32[]{:S(2)}, u32[]{:S(2)}) collective-permute-start(bf16[1024,512]{1,0:T(8,128)(2,1)S(1)} %get-tuple-element.35), channel_id=1, source_target_pairs={{0,128},{128,1},{1,129},{129,2},{2,130},{130,3},{3,131},{131,0},{4... | collective-permute-start | bytes 3145736 | tf_op jit(solution)/shard_map/ppermute | solution.py:35
  49.7 32.8 %collective-permute-start.14 = (bf16[1024,512]{1,0:T(8,128)(2,1)S(1)}, bf16[1024,512]{1,0:T(8,128)(2,1)S(1)}, u32[]{:S(2)}, u32[]{:S(2)}) collective-permute-start(bf16[1024,512]{1,0:T(8,128)(2,1)S(1)} %get-tuple-element.34), channel_id=1, source_target_pairs={{0,131},{128,0},{1,128},{129,1},{2,129},{130,2},{3,130},{131,3},{4... | collective-permute-start | bytes 3145736 | tf_op jit(solution)/shard_map/ppermute | solution.py:35
  61.4 26.7 %collective-permute-start.12 = (bf16[1024,1024]{1,0:T(8,128)(2,1)}, bf16[1024,1024]{1,0:T(8,128)(2,1)S(1)}, u32[]{:S(2)}, u32[]{:S(2)}) collective-permute-start(bf16[1024,1024]{1,0:T(8,128)(2,1)} %collective-permute-done.10), channel_id=1, source_target_pairs={{0,4},{4,8},{8,12},{12,0},{16,20},{20,24},{24,28},{28,16},{32,36},... | collective-permute-start | bytes 6291464 | tf_op jit(solution)/shard_map/ppermute | solution.py:30
  82.7 7.1 %collective-permute-start.15 = (bf16[2048,512]{1,0:T(8,128)(2,1)S(1)}, bf16[2048,512]{1,0:T(8,128)(2,1)S(1)}, u32[]{:S(2)}, u32[]{:S(2)}) collective-permute-start(bf16[2048,512]{1,0:T(8,128)(2,1)S(1)} %constant_dynamic-update-slice_fusion.9.first), channel_id=1, source_target_pairs={{0,64},{64,0},{1,65},{65,1},{2,66},{66,2},{3,67},{67,3},{4,68},{68... | collective-permute-start | bytes 6291464 | tf_op jit(solution)/shard_map/ppermute | solution.py:39
  86.0 25.4 %collective-permute-start.17 = (bf16[1024,1024]{1,0:T(8,128)(2,1)}, bf16[1024,1024]{1,0:T(8,128)(2,1)S(1)}, u32[]{:S(2)}, u32[]{:S(2)}) collective-permute-start(bf16[1024,1024]{1,0:T(8,128)(2,1)} %collective-permute-done.5), channel_id=1, source_target_pairs={{0,12},{4,0},{8,4},{12,8},{16,28},{20,16},{24,20},{28,24},{32,44},... | collective-permute-start | bytes 6291464 | tf_op jit(solution)/shard_map/ppermute | solution.py:30
  86.8 26.6 %collective-permute-start.16 = (bf16[1024,1024]{1,0:T(8,128)(2,1)}, bf16[1024,1024]{1,0:T(8,128)(2,1)S(1)}, u32[]{:S(2)}, u32[]{:S(2)}) collective-permute-start(bf16[1024,1024]{1,0:T(8,128)(2,1)} %constant_dynamic-update-slice_fusion), channel_id=1, source_target_pairs={{0,4},{4,8},{8,12},{12,0},{16,20},{20,24},{24,28},{28,16},{32,36},... | collective-permute-start | bytes 6291464 | tf_op jit(solution)/shard_map/ppermute | solution.py:30
  114.7 15.4 %copy-start.3 = (f32[1024]{0:T(1024)S(1)}, f32[1024]{0:T(1024)}, u32[]{:S(2)}) copy-start(f32[1024]{0:T(1024)} %param.12) | copy-start | bytes 12292
  114.7 34.6 %copy-start.4 = (f32[512]{0:T(512)S(1)}, f32[512]{0:T(512)}, u32[]{:S(2)}) copy-start(f32[512]{0:T(512)} %param.13) | copy-start | bytes 6148
  114.7 35.2 %copy-start.1 = (bf16[1024,512]{1,0:T(8,128)(2,1)S(1)}, bf16[1024,512]{1,0:T(8,128)(2,1)}, u32[]{:S(2)}) copy-start(bf16[1024,512]{1,0:T(8,128)(2,1)} %param.10) | copy-start | bytes 3145732
  130.1 25.2 %copy-start.2 = (f32[1024]{0:T(1024)}, f32[1024]{0:T(1024)S(1)}, u32[]{:S(2)}) copy-start(f32[1024]{0:T(1024)S(1)} %get-tuple-element.28) | copy-start | bytes 12292

commit v8 on v7

--- a/solution.py
+++ b/solution.py
@@ -115,7 +115,7 @@
             places.append((x + dx) % 4 * 4 + (y + dy) % 4)
     places = jnp.stack(places).astype(jnp.int32)
 
-    near = ring_end(ring_start(near, 0), 0, 1)
+    near = [*ring_start(near, 0), shift(near, 0, 2)]
     near[3:] = after(near[3:], away)
     (sent,) = after((activations,), *near)
     near = ring_start(jnp.concatenate(near, axis=0), 1)
@@ -141,14 +141,14 @@
     row_moment_new = 0.8 * row_moment + 0.2 * row_full / D
     col_part = jnp.sum(squares, axis=0)
     sums = jnp.concatenate([col_part, jnp.sum(row_moment_new.reshape(8, 128), axis=0)])
+    scores_new = scores - 50.0 * weights * gradient
     sums = total_over(sums, ("zl", "core", "zh"))
+    sums, weights, gradient = lax.optimization_barrier((sums, weights, gradient))
     col_moment_new = 0.8 * col_moment + 0.2 * sums[:512] / FF
     row_average = jnp.sum(sums[512:]) / FF
-    row_scale, col_scale = lax.rsqrt(row_moment_new), lax.rsqrt(col_moment_new / row_average)
-    update = gradient * (row_scale[:, None] * col_scale[None, :])
-    momentum_new = (0.9 * momentum.astype(jnp.float32) + 0.1 * update).astype(jnp.bfloat16)
+    scale = lax.rsqrt(row_moment_new)[:, None] * lax.rsqrt(col_moment_new / row_average)[None, :]
+    momentum_new = (0.9 * momentum.astype(jnp.float32) + 0.1 * (gradient * scale)).astype(jnp.bfloat16)
     weights_new = weights - 0.01 * momentum_new.astype(jnp.float32)
-    scores_new = scores - 50.0 * weights * gradient
     return (weights_new, momentum_new, scores_new, row_moment_new, col_moment_new)
 
 

time: 156 us -> 158 us (1.013)
  matrix products: 19 us -> 21.4 us
    dot_general x8, matrix products: 19 us -> 21.4 us  [product(): lax.dot_general(grad_rows, act_rows, (((0,), (0,)), ((), ())), preferred_...]
    ppermute x12, starting transfers between devices: 12.7 us -> 14.7 us  [shift(): return lax.ppermute(array, AXES, ring_pairs(phase, step))]
    ppermute x4, waiting for transfers between devices: 4.46 us -> 6.36 us  [swap(): return lax.ppermute(array, axis, [(0, 1), (1, 0)])]
    ppermute x4, starting transfers between devices: 9.13 us -> 7.38 us  [swap(): return lax.ppermute(array, axis, [(0, 1), (1, 0)])]
    unnamed x18 -> x22, local copies, waits for them, and re-layouts: 7.09 us -> 7.17 us
  transfers between devices with their start and end apart: 18 -> 18, of which waited for: 10 -> 9; matrix products, arithmetic and copies ran while one was open for 13% -> 13% of each run, Pallas kernels for 7% -> 7%
where the time goes in v8:
time: 158 us; the launch traced here: 157 us
  waiting for transfers between devices  51.5 us (33%)
  blocking collectives  29.8 us (19%)
  starting transfers between devices  28 us (18%)
  matrix products  21.4 us (14%)
  Pallas kernels  10.9 us (7%)
  local copies, waits for them, and re-layouts  9.18 us (6%)
  other arithmetic  5.3 us (3%)
    ppermute x12, waiting for transfers between devices, shift(): return lax.ppermute(array, AXES, ring_pairs(phase, step))  45.1 us
    all_to_all x2, blocking collectives, total_over(): return jnp.sum(lax.all_to_all(spread, axes, 0, 0, tiled=True), axis=0)  29.8 us
    dot_general x8, matrix products, product(): lax.dot_general(grad_rows, act_rows, (((0,), (0,)), ((), ())), preferred_...  21.4 us
    ppermute x12, starting transfers between devices, shift(): return lax.ppermute(array, AXES, ring_pairs(phase, step))  14.7 us
    pallas_call x2, Pallas kernels, arranged(): pl.pallas_call(arrange_kernel, in_specs=[pl.BlockSpec(memory_space=pltpu....  10.9 us
    ppermute x4, starting transfers between devices, swap(): return lax.ppermute(array, axis, [(0, 1), (1, 0)])  7.38 us
    unnamed x22, local copies, waits for them, and re-layouts  7.17 us
    ppermute x4, waiting for transfers between devices, swap(): return lax.ppermute(array, axis, [(0, 1), (1, 0)])  6.36 us
  transfers between devices with their start and end apart: 18, of which 9 were waited for; matrix products, arithmetic and copies ran while one was open for 13% of the time, Pallas kernels for 7%

profile of v8, /device:TPU:1, one launch (start us, length us, event | category | flops | bytes accessed | tf_op | source)
XLA Modules:
  0.0 157.5 jit_solution(9245356207135694297)
XLA Ops:
  0.7 2.1 %constant_dynamic-update-slice_fusion.8 = (bf16[1024,1024]{1,0:T(8,128)(2,1)}, bf16[128,1024]{1,0:T(8,128)(2,1)S(1)}, bf16[128,1024]{1,0:T(8,128)(2,1)S(1)}, bf1...) fusion(bf16[128,4096]{1,0:T(8,128)(2,1)} %param.8, s32[]{:T(128)S(6)} %select_n.203, s32[]{:T(128)S(6)} %select_n.201, ...), kind=kLoop, calls=%fused_computation.34 | loop fusion | bytes 2359312
  2.8 3.3 %collective-permute-start = (bf16[256,1024]{1,0:T(8,128)(2,1)S(1)}, bf16[256,1024]{1,0:T(8,128)(2,1)S(1)}, u32[]{:S(2)}, u32[]{:S(2)}) collective-permute-start(bf16[256,1024]{1,0:T(8,128)(2,1)S(1)} %pad_maximum_fusion), channel_id=1, source_target_pairs={{0,64},{64,0},{1,65},{65,1},{2,66},{66,2},{3,67},{67,3},{4,68},{68... | collective-permute-start | bytes 1572872 | tf_op jit(solution)/shard_map/ppermute | solution.py:39
  6.1 1.5 collective-permute-done
  7.6 0.8 constant_dynamic-update-slice_fusion.7
  8.5 1.3 collective-permute-start.8
  9.8 1.7 %collective-permute-start.1 = (bf16[256,1024]{1,0:T(8,128)(2,1)S(1)}, bf16[256,1024]{1,0:T(8,128)(2,1)S(1)}, u32[]{:S(2)}, u32[]{:S(2)}) collective-permute-start(bf16[256,1024]{1,0:T(8,128)(2,1)S(1)} %pad_maximum_fusion.1), channel_id=1, source_target_pairs={{0,128},{128,0},{1,129},{129,1},{2,130},{130,2},{3,131},{131,3},{4... | collective-permute-start | bytes 1572872 | tf_op jit(solution)/shard_map/ppermute | solution.py:39
  11.5 0.4 collective-permute-start.6
  11.9 2.3 %collective-permute-start.7 = (bf16[256,1024]{1,0:T(8,128)(2,1)S(1)}, bf16[256,1024]{1,0:T(8,128)(2,1)S(1)}, u32[]{:S(2)}, u32[]{:S(2)}) collective-permute-start(bf16[256,1024]{1,0:T(8,128)(2,1)S(1)} %pad_maximum_fusion.2), channel_id=1, source_target_pairs={{0,48},{4,52},{8,56},{12,60},{16,0},{20,4},{24,8},{28,12},{32,16},... | collective-permute-start | bytes 1572872 | tf_op jit(solution)/shard_map/ppermute | solution.py:30
  14.2 1.3 collective-permute-start.9
  15.5 2.9 %collective-permute-done.8 = bf16[256,1024]{1,0:T(8,128)(2,1)S(1)} collective-permute-done((bf16[256,1024]{1,0:T(8,128)(2,1)S(1)}, bf16[256,1024]{1,0:T(8,128)(2,1)S(1)}, u32[]{:S(2)}, u32[]{:S(2)}) %collective-permute-start.8) | collective-permute-done | bytes 524320 | tf_op jit(solution)/shard_map/ppermute | solution.py:30
  18.4 4.8 %collective-permute-done.1 = bf16[256,1024]{1,0:T(8,128)(2,1)S(1)} collective-permute-done((bf16[256,1024]{1,0:T(8,128)(2,1)S(1)}, bf16[256,1024]{1,0:T(8,128)(2,1)S(1)}, u32[]{:S(2)}, u32[]{:S(2)}) %collective-permute-start.1) | collective-permute-done | bytes 524320 | tf_op jit(solution)/shard_map/ppermute | solution.py:39
  23.2 1.5 collective-permute-start.2
  24.7 0.8 constant_dynamic-update-slice_fusion.6
  25.5 0.8 constant_dynamic-update-slice_fusion.5
  26.4 0.8 constant_dynamic-update-slice_fusion.4
  27.2 1.7 %collective-permute-start.10 = (bf16[1024,1024]{1,0:T(8,128)(2,1)}, bf16[1024,1024]{1,0:T(8,128)(2,1)}, u32[]{:S(2)}, u32[]{:S(2)}) collective-permute-start(bf16[1024,1024]{1,0:T(8,128)(2,1)} %constant_dynamic-update-slice_fusion.4), channel_id=1, source_target_pairs={{0,4},{4,8},{8,12},{12,0},{16,20},{20,24},{24,28},{28,16},{32,36},... | collective-permute-start | bytes 6291464 | tf_op jit(solution)/shard_map/ppermute | solution.py:30
  28.9 1.0 collective-permute-start.11
  29.9 1.7 %collective-permute-done.3 = bf16[256,1024]{1,0:T(8,128)(2,1)S(1)} collective-permute-done((bf16[256,1024]{1,0:T(8,128)(2,1)S(1)}, bf16[256,1024]{1,0:T(8,128)(2,1)S(1)}, u32[]{:S(2)}, u32[]{:S(2)}) %collective-permute-start.3) | collective-permute-done | bytes 524320 | tf_op jit(solution)/shard_map/ppermute | solution.py:30
  31.6 1.2 collective-permute-start.4
  32.8 0.9 constant_dynamic-update-slice_fusion.3
  33.6 0.9 constant_dynamic-update-slice_fusion.2
  34.5 0.8 constant_dynamic-update-slice_fusion.1
  35.3 10.2 %collective-permute-done.4 = bf16[256,1024]{1,0:T(8,128)(2,1)S(1)} collective-permute-done((bf16[256,1024]{1,0:T(8,128)(2,1)S(1)}, bf16[256,1024]{1,0:T(8,128)(2,1)S(1)}, u32[]{:S(2)}, u32[]{:S(2)}) %collective-permute-start.4) | collective-permute-done | bytes 524320 | tf_op jit(solution)/shard_map/ppermute | solution.py:30
  45.5 0.8 constant_dynamic-update-slice_fusion
  46.4 2.4 %collective-permute-start.5 = (bf16[1024,1024]{1,0:T(8,128)(2,1)}, bf16[1024,1024]{1,0:T(8,128)(2,1)}, u32[]{:S(2)}, u32[]{:S(2)}) collective-permute-start(bf16[1024,1024]{1,0:T(8,128)(2,1)} %constant_dynamic-update-slice_fusion), channel_id=1, source_target_pairs={{0,12},{4,0},{8,4},{12,8},{16,28},{20,16},{24,20},{28,24},{32,44},... | collective-permute-start | bytes 6291464 | tf_op jit(solution)/shard_map/ppermute | solution.py:30
  49.0 1.7 %collective-permute-start.13 = (bf16[1024,512]{1,0:T(8,128)(2,1)S(1)}, bf16[1024,512]{1,0:T(8,128)(2,1)S(1)}, u32[]{:S(2)}, u32[]{:S(2)}) collective-permute-start(bf16[1024,512]{1,0:T(8,128)(2,1)S(1)} %get-tuple-element.41), channel_id=1, source_target_pairs={{0,128},{128,1},{1,129},{129,2},{2,130},{130,3},{3,131},{131,0},{4... | collective-permute-start | bytes 3145736 | tf_op jit(solution)/shard_map/ppermute | solution.py:35
  50.7 4.2 %collective-permute-start.14 = (bf16[1024,512]{1,0:T(8,128)(2,1)S(1)}, bf16[1024,512]{1,0:T(8,128)(2,1)S(1)}, u32[]{:S(2)}, u32[]{:S(2)}) collective-permute-start(bf16[1024,512]{1,0:T(8,128)(2,1)S(1)} %get-tuple-element.40), channel_id=1, source_target_pairs={{0,131},{128,0},{1,128},{129,1},{2,129},{130,2},{3,130},{131,3},{4... | collective-permute-start | bytes 3145736 | tf_op jit(solution)/shard_map/ppermute | solution.py:35
  54.9 4.5 %shard_map.110 = bf16[4096,512]{1,0:T(8,128)(2,1)S(1)} custom-call(s32[16]{0:T(128)S(1)} %stack.67.place, bf16[2048,512]{1,0:T(8,128)(2,1)S(1)} %copy-done, bf16[2048,512]{1,0:T(8,128)(2,1)} %collective-permute-done.9.second), custom_call_target="tpu_custom_call" | custom-call | bytes 8388608 | tf_op jit(solution)/shard_map/pallas_call | solution.py:77
  59.5 2.9 %fusion.17 = f32[1024,512]{1,0:T(8,128)S(1)} fusion(bf16[1024,1024]{1,0:T(8,128)(2,1)} %constant_dynamic-update-slice_fusion.4, bf16[4096,512]{1,0:T(8,128)(2,1)S(1)} %shard_map.110), kind=kOutput, calls=%fused_computation.21 | convolution fusion | flops 1073741824 | bytes 5242880 | tf_op jit(solution)/shard_map/dot_general | solution.py:55
  62.5 2.9 %fusion.15 = f32[1024,512]{1,0:T(8,128)S(1)} fusion(bf16[1024,1024]{1,0:T(8,128)(2,1)} %collective-permute-done.10, bf16[4096,512]{1,0:T(8,128)(2,1)S(1)} %shard_map.110), kind=kOutput, calls=%fused_computation.19 | convolution fusion | flops 1073741824 | bytes 5242880 | tf_op jit(solution)/shard_map/dot_general | solution.py:55
  65.4 3.0 %add_add_fusion = f32[1024,512]{1,0:T(8,128)S(1)} fusion(f32[1024,512]{1,0:T(8,128)S(1)} %fusion.17, f32[1024,512]{1,0:T(8,128)S(1)} %fusion.15, bf16[1024,1024]{1,0:T(8,128)(2,1)} %collective-permute-done.11, bf16[4096,512]{1,0:T(8,128)(2,1)S(1)} %shard_map.110), kind=kOutput, calls=%fused_computation.5 | convolution fusion | flops 1074790400 | bytes 9437184 | tf_op jit(solution)/shard_map/dot_general | solution.py:55
  68.4 15.5 %collective-permute-done.5 = bf16[1024,1024]{1,0:T(8,128)(2,1)} collective-permute-done((bf16[1024,1024]{1,0:T(8,128)(2,1)}, bf16[1024,1024]{1,0:T(8,128)(2,1)}, u32[]{:S(2)}, u32[]{:S(2)}) %collective-permute-start.5) | collective-permute-done | bytes 2097184 | tf_op jit(solution)/shard_map/ppermute | solution.py:30
  84.0 1.0 collective-permute-start.15
  85.0 2.9 %collective-permute-start.17 = (bf16[1024,1024]{1,0:T(8,128)(2,1)}, bf16[1024,1024]{1,0:T(8,128)(2,1)S(1)}, u32[]{:S(2)}, u32[]{:S(2)}) collective-permute-start(bf16[1024,1024]{1,0:T(8,128)(2,1)} %collective-permute-done.5), channel_id=1, source_target_pairs={{0,12},{4,0},{8,4},{12,8},{16,28},{20,16},{24,20},{28,24},{32,44},... | collective-permute-start | bytes 6291464 | tf_op jit(solution)/shard_map/ppermute | solution.py:30
  87.9 1.2 collective-permute-done.12
  89.1 1.3 fusion.9
  90.4 6.3 %shard_map.111 = bf16[4096,512]{1,0:T(8,128)(2,1)S(1)} custom-call(s32[16]{0:T(128)S(1)} %stack.67.place, bf16[2048,512]{1,0:T(8,128)(2,1)S(1)} %constant_dynamic-update-slice_fusion.9.first, bf16[2048,512]{1,0:T(8,128)(2,1)S(1)} %collective-permute-done.15.second), custom_call_target="tpu_custom_call" | custom-call | bytes 8388608 | tf_op jit(solution)/shard_map/pallas_call | solution.py:77
  96.7 2.9 %fusion.6 = f32[1024,512]{1,0:T(8,128)S(1)} fusion(bf16[1024,1024]{1,0:T(8,128)(2,1)} %collective-permute-done.5, bf16[4096,512]{1,0:T(8,128)(2,1)S(1)} %shard_map.111), kind=kOutput, calls=%fused_computation.12 | convolution fusion | flops 1073741824 | bytes 5242880 | tf_op jit(solution)/shard_map/dot_general | solution.py:55
  99.6 11.6 %collective-permute-done.17 = bf16[1024,1024]{1,0:T(8,128)(2,1)S(1)} collective-permute-done((bf16[1024,1024]{1,0:T(8,128)(2,1)}, bf16[1024,1024]{1,0:T(8,128)(2,1)S(1)}, u32[]{:S(2)}, u32[]{:S(2)}) %collective-permute-start.17) | collective-permute-done | bytes 2097184 | tf_op jit(solution)/shard_map/ppermute | solution.py:30
  111.2 1.3 fusion.2
  112.5 2.0 %collective-permute-done.16 = bf16[1024,1024]{1,0:T(8,128)(2,1)S(1)} collective-permute-done((bf16[1024,1024]{1,0:T(8,128)(2,1)}, bf16[1024,1024]{1,0:T(8,128)(2,1)S(1)}, u32[]{:S(2)}, u32[]{:S(2)}) %collective-permute-start.16) | collective-permute-done | bytes 2097184 | tf_op jit(solution)/shard_map/ppermute | solution.py:30
  114.5 1.3 fusion.4
  115.8 5.9 %fusion.1 = (f32[512]{0:T(512)S(1)}, f32[1024]{0:T(1024)S(1)}, f32[1024,512]{1,0:T(8,128)}, f32[1024,512]{1,0:T(8,128)}) fusion(f32[1024,512]{1,0:T(8,128)S(1)} %copy-done.2, f32[1024,512]{1,0:T(8,128)S(1)} %copy-done.1, f32[1024,512]{1,0:T(8,128)S(1)} %fusion.4, f32[1024,512]{1,0:T(8,128)S(1)} %fusion.2, f32[1024,512]{1,0:T(8,128)S(1)} %fusion.6, ...), kind=kOutput, calls=%fused_computation.7 | convolution fusion | flops 1080556032 | bytes 22026240 | tf_op jit(solution)/shard_map/dot_general | solution.py:55
  121.8 11.4 %all_to_all.12 = f32[16,1,1024]{2,1,0:T(1,128)S(1)} all-to-all(f32[16,1,1024]{2,1,0:T(1,128)S(1)} %broadcast_in_dim.4), channel_id=1, replica_groups=mesh['zl'=2,'core'=2,'x'=4,'y'=4,'zh'=4] {'x','y'}, dimensions={0} | all-to-all | bytes 131072 | tf_op jit(solution)/shard_map/all_to_all | solution.py:93
  133.3 18.4 %all_to_all.13 = f32[16,1,640]{2,1,0:T(1,128)S(1)} all-to-all(f32[16,1,640]{2,1,0:T(1,128)S(1)} %broadcast_in_dim.5), channel_id=1, replica_groups=mesh['zl'=2,'core'=2,'x'=4,'y'=4,'zh'=4] {'zl','core','zh'}, dimensions={0} | all-to-all | bytes 81920 | tf_op jit(solution)/shard_map/all_to_all | solution.py:93
  151.7 0.6 slice_reduce_fusion
  153.0 0.6 divide_rsqrt_fusion
  153.6 3.9 %multiply_subtract_fusion.1 = (f32[1024,512]{1,0:T(8,128)}, bf16[1024,512]{1,0:T(8,128)(2,1)}) fusion(f32[1024,512]{1,0:T(8,128)S(1)} %copy-done.1, f32[1024,512]{1,0:T(8,128)} %get-tuple-element.27, f32[512]{0:T(512)S(1)} %get-tuple-element.35, f32[1024]{0:T(1024)S(1)} %get-tuple-element.33, bf16[1024,512]{1,0:T(8,128)(2,1)S(1)} %copy-done.3), kind=kLoop, calls=%fused_computation.1 | loop fusion | flops 5242880 | bytes 8394752 | tf_op jit(solution)/shard_map/sub | solution.py:151
  (40 shorter events, 0.8 us)
Async XLA Ops:
  2.7 11.4 %copy-start = (bf16[2048,512]{1,0:T(8,128)(2,1)S(1)}, bf16[2048,512]{1,0:T(8,128)(2,1)}, u32[]{:S(2)}) copy-start(bf16[2048,512]{1,0:T(8,128)(2,1)} %first.1) | copy-start | bytes 6291460
  2.8 4.9 %collective-permute-start = (bf16[256,1024]{1,0:T(8,128)(2,1)S(1)}, bf16[256,1024]{1,0:T(8,128)(2,1)S(1)}, u32[]{:S(2)}, u32[]{:S(2)}) collective-permute-start(bf16[256,1024]{1,0:T(8,128)(2,1)S(1)} %pad_maximum_fusion), channel_id=1, source_target_pairs={{0,64},{64,0},{1,65},{65,1},{2,66},{66,2},{3,67},{67,3},{4,68},{68... | collective-permute-start | bytes 1572872 | tf_op jit(solution)/shard_map/ppermute | solution.py:39
  8.5 10.0 %collective-permute-start.8 = (bf16[256,1024]{1,0:T(8,128)(2,1)S(1)}, bf16[256,1024]{1,0:T(8,128)(2,1)S(1)}, u32[]{:S(2)}, u32[]{:S(2)}) collective-permute-start(bf16[256,1024]{1,0:T(8,128)(2,1)S(1)} %pad_maximum_fusion.2), channel_id=1, source_target_pairs={{0,32},{4,36},{8,40},{12,44},{16,48},{20,52},{24,56},{28,60},{32,0... | collective-permute-start | bytes 1572872 | tf_op jit(solution)/shard_map/ppermute | solution.py:30
  9.8 13.5 %collective-permute-start.1 = (bf16[256,1024]{1,0:T(8,128)(2,1)S(1)}, bf16[256,1024]{1,0:T(8,128)(2,1)S(1)}, u32[]{:S(2)}, u32[]{:S(2)}) collective-permute-start(bf16[256,1024]{1,0:T(8,128)(2,1)S(1)} %pad_maximum_fusion.1), channel_id=1, source_target_pairs={{0,128},{128,0},{1,129},{129,1},{2,130},{130,2},{3,131},{131,3},{4... | collective-permute-start | bytes 1572872 | tf_op jit(solution)/shard_map/ppermute | solution.py:39
  11.5 13.2 %collective-permute-start.6 = (bf16[256,1024]{1,0:T(8,128)(2,1)S(1)}, bf16[256,1024]{1,0:T(8,128)(2,1)S(1)}, u32[]{:S(2)}, u32[]{:S(2)}) collective-permute-start(bf16[256,1024]{1,0:T(8,128)(2,1)S(1)} %pad_maximum_fusion.2), channel_id=1, source_target_pairs={{0,16},{4,20},{8,24},{12,28},{16,32},{20,36},{24,40},{28,44},{32,4... | collective-permute-start | bytes 1572872 | tf_op jit(solution)/shard_map/ppermute | solution.py:30
  11.9 13.7 %collective-permute-start.7 = (bf16[256,1024]{1,0:T(8,128)(2,1)S(1)}, bf16[256,1024]{1,0:T(8,128)(2,1)S(1)}, u32[]{:S(2)}, u32[]{:S(2)}) collective-permute-start(bf16[256,1024]{1,0:T(8,128)(2,1)S(1)} %pad_maximum_fusion.2), channel_id=1, source_target_pairs={{0,48},{4,52},{8,56},{12,60},{16,0},{20,4},{24,8},{28,12},{32,16},... | collective-permute-start | bytes 1572872 | tf_op jit(solution)/shard_map/ppermute | solution.py:30
  14.2 36.6 %collective-permute-start.9 = (bf16[2048,512]{1,0:T(8,128)(2,1)S(1)}, bf16[2048,512]{1,0:T(8,128)(2,1)}, u32[]{:S(2)}, u32[]{:S(2)}) collective-permute-start(bf16[2048,512]{1,0:T(8,128)(2,1)S(1)} %copy-done), channel_id=1, source_target_pairs={{0,64},{64,0},{1,65},{65,1},{2,66},{66,2},{3,67},{67,3},{4,68},{68... | collective-permute-start | bytes 6291464 | tf_op jit(solution)/shard_map/ppermute | solution.py:39
  23.2 8.3 %collective-permute-start.3 = (bf16[256,1024]{1,0:T(8,128)(2,1)S(1)}, bf16[256,1024]{1,0:T(8,128)(2,1)S(1)}, u32[]{:S(2)}, u32[]{:S(2)}) collective-permute-start(bf16[256,1024]{1,0:T(8,128)(2,1)S(1)} %collective-permute-done.1), channel_id=1, source_target_pairs={{0,48},{4,52},{8,56},{12,60},{16,0},{20,4},{24,8},{28,12},{32,16},... | collective-permute-start | bytes 1572872 | tf_op jit(solution)/shard_map/ppermute | solution.py:30
  23.2 10.4 %collective-permute-start.2 = (bf16[256,1024]{1,0:T(8,128)(2,1)S(1)}, bf16[256,1024]{1,0:T(8,128)(2,1)S(1)}, u32[]{:S(2)}, u32[]{:S(2)}) collective-permute-start(bf16[256,1024]{1,0:T(8,128)(2,1)S(1)} %collective-permute-done.1), channel_id=1, source_target_pairs={{0,16},{4,20},{8,24},{12,28},{16,32},{20,36},{24,40},{28,44},{32,4... | collective-permute-start | bytes 1572872 | tf_op jit(solution)/shard_map/ppermute | solution.py:30
  27.2 35.2 %collective-permute-start.10 = (bf16[1024,1024]{1,0:T(8,128)(2,1)}, bf16[1024,1024]{1,0:T(8,128)(2,1)}, u32[]{:S(2)}, u32[]{:S(2)}) collective-permute-start(bf16[1024,1024]{1,0:T(8,128)(2,1)} %constant_dynamic-update-slice_fusion.4), channel_id=1, source_target_pairs={{0,4},{4,8},{8,12},{12,0},{16,20},{20,24},{24,28},{28,16},{32,36},... | collective-permute-start | bytes 6291464 | tf_op jit(solution)/shard_map/ppermute | solution.py:30
  28.9 33.5 %collective-permute-start.11 = (bf16[1024,1024]{1,0:T(8,128)(2,1)}, bf16[1024,1024]{1,0:T(8,128)(2,1)}, u32[]{:S(2)}, u32[]{:S(2)}) collective-permute-start(bf16[1024,1024]{1,0:T(8,128)(2,1)} %constant_dynamic-update-slice_fusion.4), channel_id=1, source_target_pairs={{0,12},{4,0},{8,4},{12,8},{16,28},{20,16},{24,20},{28,24},{32,44},... | collective-permute-start | bytes 6291464 | tf_op jit(solution)/shard_map/ppermute | solution.py:30
  31.6 14.0 %collective-permute-start.4 = (bf16[256,1024]{1,0:T(8,128)(2,1)S(1)}, bf16[256,1024]{1,0:T(8,128)(2,1)S(1)}, u32[]{:S(2)}, u32[]{:S(2)}) collective-permute-start(bf16[256,1024]{1,0:T(8,128)(2,1)S(1)} %collective-permute-done.3), channel_id=1, source_target_pairs={{0,48},{4,52},{8,56},{12,60},{16,0},{20,4},{24,8},{28,12},{32,16},... | collective-permute-start | bytes 1572872 | tf_op jit(solution)/shard_map/ppermute | solution.py:30
  46.4 37.4 %collective-permute-start.5 = (bf16[1024,1024]{1,0:T(8,128)(2,1)}, bf16[1024,1024]{1,0:T(8,128)(2,1)}, u32[]{:S(2)}, u32[]{:S(2)}) collective-permute-start(bf16[1024,1024]{1,0:T(8,128)(2,1)} %constant_dynamic-update-slice_fusion), channel_id=1, source_target_pairs={{0,12},{4,0},{8,4},{12,8},{16,28},{20,16},{24,20},{28,24},{32,44},... | collective-permute-start | bytes 6291464 | tf_op jit(solution)/shard_map/ppermute | solution.py:30
  49.0 34.8 %collective-permute-start.13 = (bf16[1024,512]{1,0:T(8,128)(2,1)S(1)}, bf16[1024,512]{1,0:T(8,128)(2,1)S(1)}, u32[]{:S(2)}, u32[]{:S(2)}) collective-permute-start(bf16[1024,512]{1,0:T(8,128)(2,1)S(1)} %get-tuple-element.41), channel_id=1, source_target_pairs={{0,128},{128,1},{1,129},{129,2},{2,130},{130,3},{3,131},{131,0},{4... | collective-permute-start | bytes 3145736 | tf_op jit(solution)/shard_map/ppermute | solution.py:35
  50.7 33.1 %collective-permute-start.14 = (bf16[1024,512]{1,0:T(8,128)(2,1)S(1)}, bf16[1024,512]{1,0:T(8,128)(2,1)S(1)}, u32[]{:S(2)}, u32[]{:S(2)}) collective-permute-start(bf16[1024,512]{1,0:T(8,128)(2,1)S(1)} %get-tuple-element.40), channel_id=1, source_target_pairs={{0,131},{128,0},{1,128},{129,1},{2,129},{130,2},{3,130},{131,3},{4... | collective-permute-start | bytes 3145736 | tf_op jit(solution)/shard_map/ppermute | solution.py:35
  62.4 26.7 %collective-permute-start.12 = (bf16[1024,1024]{1,0:T(8,128)(2,1)}, bf16[1024,1024]{1,0:T(8,128)(2,1)S(1)}, u32[]{:S(2)}, u32[]{:S(2)}) collective-permute-start(bf16[1024,1024]{1,0:T(8,128)(2,1)} %collective-permute-done.10), channel_id=1, source_target_pairs={{0,4},{4,8},{8,12},{12,0},{16,20},{20,24},{24,28},{28,16},{32,36},... | collective-permute-start | bytes 6291464 | tf_op jit(solution)/shard_map/ppermute | solution.py:30
  84.0 6.4 %collective-permute-start.15 = (bf16[2048,512]{1,0:T(8,128)(2,1)S(1)}, bf16[2048,512]{1,0:T(8,128)(2,1)S(1)}, u32[]{:S(2)}, u32[]{:S(2)}) collective-permute-start(bf16[2048,512]{1,0:T(8,128)(2,1)S(1)} %constant_dynamic-update-slice_fusion.9.first), channel_id=1, source_target_pairs={{0,64},{64,0},{1,65},{65,1},{2,66},{66,2},{3,67},{67,3},{4,68},{68... | collective-permute-start | bytes 6291464 | tf_op jit(solution)/shard_map/ppermute | solution.py:39
  85.0 26.2 %collective-permute-start.17 = (bf16[1024,1024]{1,0:T(8,128)(2,1)}, bf16[1024,1024]{1,0:T(8,128)(2,1)S(1)}, u32[]{:S(2)}, u32[]{:S(2)}) collective-permute-start(bf16[1024,1024]{1,0:T(8,128)(2,1)} %collective-permute-done.5), channel_id=1, source_target_pairs={{0,12},{4,0},{8,4},{12,8},{16,28},{20,16},{24,20},{28,24},{32,44},... | collective-permute-start | bytes 6291464 | tf_op jit(solution)/shard_map/ppermute | solution.py:30
  87.9 26.6 %collective-permute-start.16 = (bf16[1024,1024]{1,0:T(8,128)(2,1)}, bf16[1024,1024]{1,0:T(8,128)(2,1)S(1)}, u32[]{:S(2)}, u32[]{:S(2)}) collective-permute-start(bf16[1024,1024]{1,0:T(8,128)(2,1)} %constant_dynamic-update-slice_fusion), channel_id=1, source_target_pairs={{0,4},{4,8},{8,12},{12,0},{16,20},{20,24},{24,28},{28,16},{32,36},... | collective-permute-start | bytes 6291464 | tf_op jit(solution)/shard_map/ppermute | solution.py:30
  112.5 3.3 %copy-start.1 = (f32[1024,512]{1,0:T(8,128)S(1)}, f32[1024,512]{1,0:T(8,128)}, u32[]{:S(2)}) copy-start(f32[1024,512]{1,0:T(8,128)} %param.9) | copy-start | bytes 6291460
  112.5 3.3 %copy-start.2 = (f32[1024,512]{1,0:T(8,128)S(1)}, f32[1024,512]{1,0:T(8,128)}, u32[]{:S(2)}) copy-start(f32[1024,512]{1,0:T(8,128)} %param.11) | copy-start | bytes 6291460
  115.8 17.4 %copy-start.5 = (f32[1024]{0:T(1024)S(1)}, f32[1024]{0:T(1024)}, u32[]{:S(2)}) copy-start(f32[1024]{0:T(1024)} %param.12) | copy-start | bytes 12292
  115.8 37.2 %copy-start.6 = (f32[512]{0:T(512)S(1)}, f32[512]{0:T(512)}, u32[]{:S(2)}) copy-start(f32[512]{0:T(512)} %param.13) | copy-start | bytes 6148
  115.8 37.8 %copy-start.3 = (bf16[1024,512]{1,0:T(8,128)(2,1)S(1)}, bf16[1024,512]{1,0:T(8,128)(2,1)}, u32[]{:S(2)}) copy-start(bf16[1024,512]{1,0:T(8,128)(2,1)} %param.10) | copy-start | bytes 3145732
  133.3 24.2 %copy-start.4 = (f32[1024]{0:T(1024)}, f32[1024]{0:T(1024)S(1)}, u32[]{:S(2)}) copy-start(f32[1024]{0:T(1024)S(1)} %get-tuple-element.34) | copy-start | bytes 12292

commit v9 on v7

--- a/solution.py
+++ b/solution.py
@@ -102,10 +102,11 @@
     def units(a, b):
         return lax.dynamic_slice_in_dim(out_grads, ((low ^ a) * 2 + (core ^ b)) * rows, rows, 1)
 
-    other = swap(jnp.concatenate([units(0, 1), units(1, 1)], axis=0), "core")
-    tokens = other.shape[0] // 2
-    near = jnp.concatenate([units(0, 0), other[:tokens]], axis=0)
-    away = swap(jnp.concatenate([units(1, 0), other[tokens:]], axis=0), "zl")
+    low_blocks = swap(jnp.concatenate([units(1, 0), units(1, 1)], axis=0), "zl")
+    near = units(0, 0)
+    tokens = near.shape[0]
+    near = jnp.concatenate([near, swap(units(0, 1), "core")], axis=0)
+    away = jnp.concatenate([low_blocks[:tokens], swap(low_blocks[tokens:], "core")], axis=0)
     acts_core = swap(activations, "core")
 
     places = []
@@ -115,7 +116,7 @@
             places.append((x + dx) % 4 * 4 + (y + dy) % 4)
     places = jnp.stack(places).astype(jnp.int32)
 
-    near = ring_end(ring_start(near, 0), 0, 1)
+    near = [*ring_start(near, 0), shift(near, 0, 2)]
     near[3:] = after(near[3:], away)
     (sent,) = after((activations,), *near)
     near = ring_start(jnp.concatenate(near, axis=0), 1)
@@ -137,18 +138,22 @@
     gradient = gradient * token_scale
 
     squares = gradient * gradient + 1e-30
-    row_full = total_over(jnp.sum(squares, axis=1), ("x", "y"))
+    row_part, col_part = jnp.sum(squares, axis=1), jnp.sum(squares, axis=0)
+    row_part, gradient = lax.optimization_barrier((row_part, gradient))
+    scores_new = scores - 50.0 * weights * gradient
+    row_full = total_over(row_part, ("x", "y"))
     row_moment_new = 0.8 * row_moment + 0.2 * row_full / D
-    col_part = jnp.sum(squares, axis=0)
     sums = jnp.concatenate([col_part, jnp.sum(row_moment_new.reshape(8, 128), axis=0)])
     sums = total_over(sums, ("zl", "core", "zh"))
+    sums, scores_new, weights, gradient = lax.optimization_barrier(
+        (sums, scores_new, weights, gradient)
+    )
     col_moment_new = 0.8 * col_moment + 0.2 * sums[:512] / FF
     row_average = jnp.sum(sums[512:]) / FF
     row_scale, col_scale = lax.rsqrt(row_moment_new), lax.rsqrt(col_moment_new / row_average)
     update = gradient * (row_scale[:, None] * col_scale[None, :])
     momentum_new = (0.9 * momentum.astype(jnp.float32) + 0.1 * update).astype(jnp.bfloat16)
     weights_new = weights - 0.01 * momentum_new.astype(jnp.float32)
-    scores_new = scores - 50.0 * weights * gradient
     return (weights_new, momentum_new, scores_new, row_moment_new, col_moment_new)
 
 

time: 156 us -> 153 us (0.981)
  blocking collectives: 29.6 us -> 11.3 us
  starting transfers between devices: 27.9 us -> 42.7 us
  waiting for transfers between devices: 50.6 us -> 47.5 us
  other arithmetic: 6.8 us -> 9.68 us
    all_to_all x2 -> x1, blocking collectives: 29.6 us -> 11.3 us  [total_over(): return jnp.sum(lax.all_to_all(spread, axes, 0, 0, tiled=True), axis=0)]
    all_to_all x0 -> x1, starting transfers between devices: none -> 10.7 us  [total_over(): return jnp.sum(lax.all_to_all(spread, axes, 0, 0, tiled=True), axis=0)]
    ppermute x12, waiting for transfers between devices: 46.2 us -> 38.5 us  [shift(): return lax.ppermute(array, AXES, ring_pairs(phase, step))]
    ppermute x12, starting transfers between devices: 12.7 us -> 18.5 us  [shift(): return lax.ppermute(array, AXES, ring_pairs(phase, step))]
    sub x0 -> x1, other arithmetic: none -> 4.39 us  [local(): scores_new = scores - 50.0 * weights * gradient]
    all_to_all x0 -> x1, waiting for transfers between devices: none -> 3.09 us  [total_over(): return jnp.sum(lax.all_to_all(spread, axes, 0, 0, tiled=True), axis=0)]
    ppermute x4 -> x5, waiting for transfers between devices: 4.46 us -> 5.89 us  [swap(): return lax.ppermute(array, axis, [(0, 1), (1, 0)])]
    ppermute x4 -> x5, starting transfers between devices: 9.13 us -> 7.82 us  [swap(): return lax.ppermute(array, axis, [(0, 1), (1, 0)])]
  transfers between devices with their start and end apart: 18 -> 20, of which waited for: 10 -> 11; matrix products, arithmetic and copies ran while one was open for 13% -> 17% of each run, Pallas kernels for 7% -> 7%
where the time goes in v9:
time: 153 us
  waiting for transfers between devices  47.5 us (31%)
  starting transfers between devices  42.7 us (28%)
  matrix products  18.9 us (12%)
  blocking collectives  11.3 us (7%)
  Pallas kernels  10.9 us (7%)
  local copies, waits for them, and re-layouts  10.3 us (7%)
  other arithmetic  9.68 us (6%)
    ppermute x12, waiting for transfers between devices, shift(): return lax.ppermute(array, AXES, ring_pairs(phase, step))  38.5 us
    dot_general x8, matrix products, product(): lax.dot_general(grad_rows, act_rows, (((0,), (0,)), ((), ())), preferred_...  18.9 us
    ppermute x12, starting transfers between devices, shift(): return lax.ppermute(array, AXES, ring_pairs(phase, step))  18.5 us
    all_to_all x1, blocking collectives, total_over(): return jnp.sum(lax.all_to_all(spread, axes, 0, 0, tiled=True), axis=0)  11.3 us
    pallas_call x2, Pallas kernels, arranged(): pl.pallas_call(arrange_kernel, in_specs=[pl.BlockSpec(memory_space=pltpu....  10.9 us
    all_to_all x1, starting transfers between devices, total_over(): return jnp.sum(lax.all_to_all(spread, axes, 0, 0, tiled=True), axis=0)  10.7 us
    ppermute x5, starting transfers between devices, swap(): return lax.ppermute(array, axis, [(0, 1), (1, 0)])  7.82 us
    unnamed x18, local copies, waits for them, and re-layouts  6.9 us
  transfers between devices with their start and end apart: 20, of which 11 were waited for; matrix products, arithmetic and copies ran while one was open for 17% of the time, Pallas kernels for 7%

profile of v9, /device:TPU:1, one launch (start us, length us, event | category | flops | bytes accessed | tf_op | source)
XLA Modules:
  0.0 152.8 jit_solution(6718122589375078034)
XLA Ops:
  0.7 2.1 %constant_dynamic-update-slice_fusion.9 = (bf16[1024,1024]{1,0:T(8,128)(2,1)}, bf16[128,1024]{1,0:T(8,128)(2,1)S(1)}, bf16[128,1024]{1,0:T(8,128)(2,1)S(1)}, bf1...) fusion(bf16[128,4096]{1,0:T(8,128)(2,1)} %param.8, s32[]{:T(128)S(6)} %select_n.202, s32[]{:T(128)S(6)} %select_n.201, ...), kind=kLoop, calls=%fused_computation.35 | loop fusion | bytes 2359312
  2.8 2.6 %collective-permute-start = (bf16[256,1024]{1,0:T(8,128)(2,1)S(1)}, bf16[256,1024]{1,0:T(8,128)(2,1)S(1)}, u32[]{:S(2)}, u32[]{:S(2)}) collective-permute-start(bf16[256,1024]{1,0:T(8,128)(2,1)S(1)} %pad_maximum_fusion), channel_id=1, source_target_pairs={{0,128},{128,0},{1,129},{129,1},{2,130},{130,2},{3,131},{131,3},{4... | collective-permute-start | bytes 1572872 | tf_op jit(solution)/shard_map/ppermute | solution.py:39
  5.3 1.0 collective-permute-start.6
  6.3 1.2 collective-permute-done.6
  7.5 1.4 collective-permute-start.7
  8.8 1.5 %collective-permute-start.8 = (bf16[256,1024]{1,0:T(8,128)(2,1)S(1)}, bf16[256,1024]{1,0:T(8,128)(2,1)S(1)}, u32[]{:S(2)}, u32[]{:S(2)}) collective-permute-start(bf16[256,1024]{1,0:T(8,128)(2,1)S(1)} %pad_maximum_fusion.2), channel_id=1, source_target_pairs={{0,48},{4,52},{8,56},{12,60},{16,0},{20,4},{24,8},{28,12},{32,16},... | collective-permute-start | bytes 1572872 | tf_op jit(solution)/shard_map/ppermute | solution.py:30
  10.4 1.6 %collective-permute-start.9 = (bf16[256,1024]{1,0:T(8,128)(2,1)S(1)}, bf16[256,1024]{1,0:T(8,128)(2,1)S(1)}, u32[]{:S(2)}, u32[]{:S(2)}) collective-permute-start(bf16[256,1024]{1,0:T(8,128)(2,1)S(1)} %pad_maximum_fusion.2), channel_id=1, source_target_pairs={{0,32},{4,36},{8,40},{12,44},{16,48},{20,52},{24,56},{28,60},{32,0... | collective-permute-start | bytes 1572872 | tf_op jit(solution)/shard_map/ppermute | solution.py:30
  11.9 4.0 %collective-permute-done = bf16[256,1024]{1,0:T(8,128)(2,1)S(1)} collective-permute-done((bf16[256,1024]{1,0:T(8,128)(2,1)S(1)}, bf16[256,1024]{1,0:T(8,128)(2,1)S(1)}, u32[]{:S(2)}, u32[]{:S(2)}) %collective-permute-start) | collective-permute-done | bytes 524320 | tf_op jit(solution)/shard_map/ppermute | solution.py:39
  15.9 0.8 fusion.21
  16.7 2.3 %collective-permute-start.1 = (bf16[128,1024]{1,0:T(8,128)(2,1)S(1)}, bf16[128,1024]{1,0:T(8,128)(2,1)S(1)}, u32[]{:S(2)}, u32[]{:S(2)}) collective-permute-start(bf16[128,1024]{1,0:T(8,128)(2,1)S(1)} %get-tuple-element.52), channel_id=1, source_target_pairs={{0,64},{64,0},{1,65},{65,1},{2,66},{66,2},{3,67},{67,3},{4,68},{68... | collective-permute-start | bytes 786440 | tf_op jit(solution)/shard_map/ppermute | solution.py:39
  19.7 0.7 collective-permute-done.1
  20.5 2.8 %collective-permute-start.3 = (bf16[256,1024]{1,0:T(8,128)(2,1)S(1)}, bf16[256,1024]{1,0:T(8,128)(2,1)S(1)}, u32[]{:S(2)}, u32[]{:S(2)}) collective-permute-start(bf16[256,1024]{1,0:T(8,128)(2,1)S(1)} %pad_maximum_fusion.1), channel_id=1, source_target_pairs={{0,48},{4,52},{8,56},{12,60},{16,0},{20,4},{24,8},{28,12},{32,16},... | collective-permute-start | bytes 1572872 | tf_op jit(solution)/shard_map/ppermute | solution.py:30
  23.3 0.8 constant_dynamic-update-slice_fusion.7
  24.1 0.8 constant_dynamic-update-slice_fusion.6
  25.0 0.8 constant_dynamic-update-slice_fusion.5
  25.8 1.2 collective-permute-start.11
  27.0 1.5 collective-permute-start.12
  28.5 0.9 collective-permute-done.3
  29.4 3.4 %collective-permute-start.4 = (bf16[256,1024]{1,0:T(8,128)(2,1)S(1)}, bf16[256,1024]{1,0:T(8,128)(2,1)S(1)}, u32[]{:S(2)}, u32[]{:S(2)}) collective-permute-start(bf16[256,1024]{1,0:T(8,128)(2,1)S(1)} %collective-permute-done.3), channel_id=1, source_target_pairs={{0,48},{4,52},{8,56},{12,60},{16,0},{20,4},{24,8},{28,12},{32,16},... | collective-permute-start | bytes 1572872 | tf_op jit(solution)/shard_map/ppermute | solution.py:30
  33.5 1.0 collective-permute-done.2
  34.5 0.8 constant_dynamic-update-slice_fusion.2
  35.4 0.8 constant_dynamic-update-slice_fusion.1
  36.2 8.4 %collective-permute-done.4 = bf16[256,1024]{1,0:T(8,128)(2,1)S(1)} collective-permute-done((bf16[256,1024]{1,0:T(8,128)(2,1)S(1)}, bf16[256,1024]{1,0:T(8,128)(2,1)S(1)}, u32[]{:S(2)}, u32[]{:S(2)}) %collective-permute-start.4) | collective-permute-done | bytes 524320 | tf_op jit(solution)/shard_map/ppermute | solution.py:30
  44.6 0.8 constant_dynamic-update-slice_fusion
  45.5 2.5 %collective-permute-start.5 = (bf16[1024,1024]{1,0:T(8,128)(2,1)}, bf16[1024,1024]{1,0:T(8,128)(2,1)}, u32[]{:S(2)}, u32[]{:S(2)}) collective-permute-start(bf16[1024,1024]{1,0:T(8,128)(2,1)} %constant_dynamic-update-slice_fusion), channel_id=1, source_target_pairs={{0,12},{4,0},{8,4},{12,8},{16,28},{20,16},{24,20},{28,24},{32,44},... | collective-permute-start | bytes 6291464 | tf_op jit(solution)/shard_map/ppermute | solution.py:30
  48.2 1.5 %collective-permute-start.14 = (bf16[1024,512]{1,0:T(8,128)(2,1)S(1)}, bf16[1024,512]{1,0:T(8,128)(2,1)S(1)}, u32[]{:S(2)}, u32[]{:S(2)}) collective-permute-start(bf16[1024,512]{1,0:T(8,128)(2,1)S(1)} %get-tuple-element.46), channel_id=1, source_target_pairs={{0,128},{128,1},{1,129},{129,2},{2,130},{130,3},{3,131},{131,0},{4... | collective-permute-start | bytes 3145736 | tf_op jit(solution)/shard_map/ppermute | solution.py:35
  49.7 4.2 %collective-permute-start.15 = (bf16[1024,512]{1,0:T(8,128)(2,1)S(1)}, bf16[1024,512]{1,0:T(8,128)(2,1)S(1)}, u32[]{:S(2)}, u32[]{:S(2)}) collective-permute-start(bf16[1024,512]{1,0:T(8,128)(2,1)S(1)} %get-tuple-element.45), channel_id=1, source_target_pairs={{0,131},{128,0},{1,128},{129,1},{2,129},{130,2},{3,130},{131,3},{4... | collective-permute-start | bytes 3145736 | tf_op jit(solution)/shard_map/ppermute | solution.py:35
  53.9 4.5 %shard_map.110 = bf16[4096,512]{1,0:T(8,128)(2,1)S(1)} custom-call(s32[16]{0:T(128)S(1)} %stack.67.place, bf16[2048,512]{1,0:T(8,128)(2,1)S(1)} %copy-done, bf16[2048,512]{1,0:T(8,128)(2,1)} %collective-permute-done.10.second), custom_call_target="tpu_custom_call" | custom-call | bytes 8388608 | tf_op jit(solution)/shard_map/pallas_call | solution.py:77
  58.5 2.9 %fusion.17 = f32[1024,512]{1,0:T(8,128)S(1)} fusion(bf16[1024,1024]{1,0:T(8,128)(2,1)} %constant_dynamic-update-slice_fusion.5, bf16[4096,512]{1,0:T(8,128)(2,1)S(1)} %shard_map.110), kind=kOutput, calls=%fused_computation.21 | convolution fusion | flops 1073741824 | bytes 5242880 | tf_op jit(solution)/shard_map/dot_general | solution.py:55
  61.5 2.9 %fusion.15 = f32[1024,512]{1,0:T(8,128)S(1)} fusion(bf16[1024,1024]{1,0:T(8,128)(2,1)} %collective-permute-done.11, bf16[4096,512]{1,0:T(8,128)(2,1)S(1)} %shard_map.110), kind=kOutput, calls=%fused_computation.19 | convolution fusion | flops 1073741824 | bytes 5242880 | tf_op jit(solution)/shard_map/dot_general | solution.py:55
  64.4 3.0 %add_add_fusion = f32[1024,512]{1,0:T(8,128)S(1)} fusion(f32[1024,512]{1,0:T(8,128)S(1)} %fusion.17, f32[1024,512]{1,0:T(8,128)S(1)} %fusion.15, bf16[1024,1024]{1,0:T(8,128)(2,1)} %collective-permute-done.12, bf16[4096,512]{1,0:T(8,128)(2,1)S(1)} %shard_map.110), kind=kOutput, calls=%fused_computation.5 | convolution fusion | flops 1074790400 | bytes 9437184 | tf_op jit(solution)/shard_map/dot_general | solution.py:55
  67.3 13.3 %collective-permute-done.5 = bf16[1024,1024]{1,0:T(8,128)(2,1)} collective-permute-done((bf16[1024,1024]{1,0:T(8,128)(2,1)}, bf16[1024,1024]{1,0:T(8,128)(2,1)}, u32[]{:S(2)}, u32[]{:S(2)}) %collective-permute-start.5) | collective-permute-done | bytes 2097184 | tf_op jit(solution)/shard_map/ppermute | solution.py:30
  80.8 2.0 %collective-permute-start.16 = (bf16[2048,512]{1,0:T(8,128)(2,1)S(1)}, bf16[2048,512]{1,0:T(8,128)(2,1)S(1)}, u32[]{:S(2)}, u32[]{:S(2)}) collective-permute-start(bf16[2048,512]{1,0:T(8,128)(2,1)S(1)} %constant_dynamic-update-slice_fusion.10.first), channel_id=1, source_target_pairs={{0,64},{64,0},{1,65},{65,1},{2,66},{66,2},{3,67},{67,3},{4,68},{68... | collective-permute-start | bytes 6291464 | tf_op jit(solution)/shard_map/ppermute | solution.py:39
  82.8 2.6 %collective-permute-start.18 = (bf16[1024,1024]{1,0:T(8,128)(2,1)}, bf16[1024,1024]{1,0:T(8,128)(2,1)S(1)}, u32[]{:S(2)}, u32[]{:S(2)}) collective-permute-start(bf16[1024,1024]{1,0:T(8,128)(2,1)} %collective-permute-done.5), channel_id=1, source_target_pairs={{0,12},{4,0},{8,4},{12,8},{16,28},{20,16},{24,20},{28,24},{32,44},... | collective-permute-start | bytes 6291464 | tf_op jit(solution)/shard_map/ppermute | solution.py:30
  85.4 2.6 %collective-permute-done.13 = bf16[1024,1024]{1,0:T(8,128)(2,1)S(1)} collective-permute-done((bf16[1024,1024]{1,0:T(8,128)(2,1)}, bf16[1024,1024]{1,0:T(8,128)(2,1)S(1)}, u32[]{:S(2)}, u32[]{:S(2)}) %collective-permute-start.13) | collective-permute-done | bytes 2097184 | tf_op jit(solution)/shard_map/ppermute | solution.py:30
  88.0 1.3 fusion.9
  89.3 6.3 %shard_map.111 = bf16[4096,512]{1,0:T(8,128)(2,1)S(1)} custom-call(s32[16]{0:T(128)S(1)} %stack.67.place, bf16[2048,512]{1,0:T(8,128)(2,1)S(1)} %constant_dynamic-update-slice_fusion.10.first, bf16[2048,512]{1,0:T(8,128)(2,1)S(1)} %collective-permute-done.16.second), custom_call_target="tpu_custom_call" | custom-call | bytes 8388608 | tf_op jit(solution)/shard_map/pallas_call | solution.py:77
  95.7 2.9 %fusion.6 = f32[1024,512]{1,0:T(8,128)S(1)} fusion(bf16[1024,1024]{1,0:T(8,128)(2,1)} %collective-permute-done.5, bf16[4096,512]{1,0:T(8,128)(2,1)S(1)} %shard_map.111), kind=kOutput, calls=%fused_computation.12 | convolution fusion | flops 1073741824 | bytes 5242880 | tf_op jit(solution)/shard_map/dot_general | solution.py:55
  98.5 10.2 %collective-permute-done.18 = bf16[1024,1024]{1,0:T(8,128)(2,1)S(1)} collective-permute-done((bf16[1024,1024]{1,0:T(8,128)(2,1)}, bf16[1024,1024]{1,0:T(8,128)(2,1)S(1)}, u32[]{:S(2)}, u32[]{:S(2)}) %collective-permute-start.18) | collective-permute-done | bytes 2097184 | tf_op jit(solution)/shard_map/ppermute | solution.py:30
  108.7 1.3 fusion.2
  110.0 2.0 %collective-permute-done.17 = bf16[1024,1024]{1,0:T(8,128)(2,1)S(1)} collective-permute-done((bf16[1024,1024]{1,0:T(8,128)(2,1)}, bf16[1024,1024]{1,0:T(8,128)(2,1)S(1)}, u32[]{:S(2)}, u32[]{:S(2)}) %collective-permute-start.17) | collective-permute-done | bytes 2097184 | tf_op jit(solution)/shard_map/ppermute | solution.py:30
  112.0 1.3 fusion.4
  113.3 3.5 %fusion.1 = (f32[512]{0:T(512)S(1)}, f32[1024]{0:T(1024)S(1)}, f32[1024,512]{1,0:T(8,128)S(1)}) fusion(f32[1024,512]{1,0:T(8,128)S(1)} %fusion.4, f32[1024,512]{1,0:T(8,128)S(1)} %fusion.2, f32[1024,512]{1,0:T(8,128)S(1)} %fusion.6, bf16[1024,1024]{1,0:T(8,128)(2,1)} %constant_dynamic-update-slice_fusion, bf16[4096,512]{1,0:T(8,128)(2,1)S(1)} %shard_map.111, ...), kind=kOutput, calls=%fused_computation.7 | convolution fusion | flops 1078983168 | bytes 15734784 | tf_op jit(solution)/shard_map/dot_general | solution.py:55
  116.8 11.3 %all_to_all.12 = f32[16,1,1024]{2,1,0:T(1,128)S(1)} all-to-all(f32[16,1,1024]{2,1,0:T(1,128)S(1)} %broadcast_in_dim.4), channel_id=1, replica_groups=mesh['zl'=2,'core'=2,'x'=4,'y'=4,'zh'=4] {'x','y'}, dimensions={0} | all-to-all | bytes 131072 | tf_op jit(solution)/shard_map/all_to_all | solution.py:93
  128.9 10.7 %all-to-all-start.1 = ((f32[16,1,640]{2,1,0:T(1,128)}), f32[16,1,640]{2,1,0:T(1,128)S(1)}, u32[]{:S(2)}, u32[]{:S(2)}) async-start(f32[16,1,640]{2,1,0:T(1,128)} %broadcast_in_dim.5), calls=%async_computation.1 | async-start | bytes 81920 | tf_op jit(solution)/shard_map/all_to_all | solution.py:93
  139.6 4.4 %multiply_subtract_fusion.1 = f32[1024,512]{1,0:T(8,128)} fusion(f32[1024,512]{1,0:T(8,128)} %param.11, f32[1024,512]{1,0:T(8,128)S(1)} %get-tuple-element.32, f32[1024,512]{1,0:T(8,128)} %param.9), kind=kLoop, calls=%fused_computation.2 | loop fusion | flops 1572864 | bytes 8388608 | tf_op jit(solution)/shard_map/sub | solution.py:143
  144.0 3.1 %all-to-all-done.1 = f32[16,1,640]{2,1,0:T(1,128)S(1)} async-done(((f32[16,1,640]{2,1,0:T(1,128)}), f32[16,1,640]{2,1,0:T(1,128)S(1)}, u32[]{:S(2)}, u32[]{:S(2)}) %all-to-all-start.1) | async-done | bytes 40992 | tf_op jit(solution)/shard_map/all_to_all | solution.py:93
  148.9 3.9 %multiply_subtract_fusion = (f32[1024,512]{1,0:T(8,128)}, bf16[1024,512]{1,0:T(8,128)(2,1)}) fusion(f32[1024,512]{1,0:T(8,128)} %param.9, f32[1024,512]{1,0:T(8,128)S(1)} %get-tuple-element.32, f32[512]{0:T(512)S(1)} %get-tuple-element.41, f32[1024]{0:T(1024)S(1)} %get-tuple-element.39, bf16[1024,512]{1,0:T(8,128)(2,1)S(1)} %copy-done.1), kind=kLoop, calls=%fused_computation | loop fusion | flops 5242880 | bytes 8394752 | tf_op jit(solution)/shard_map/sub | solution.py:156
  (41 shorter events, 4.0 us)
Async XLA Ops:
  2.7 16.2 %copy-start = (bf16[2048,512]{1,0:T(8,128)(2,1)S(1)}, bf16[2048,512]{1,0:T(8,128)(2,1)}, u32[]{:S(2)}) copy-start(bf16[2048,512]{1,0:T(8,128)(2,1)} %first.1) | copy-start | bytes 6291460
  2.8 13.1 %collective-permute-start = (bf16[256,1024]{1,0:T(8,128)(2,1)S(1)}, bf16[256,1024]{1,0:T(8,128)(2,1)S(1)}, u32[]{:S(2)}, u32[]{:S(2)}) collective-permute-start(bf16[256,1024]{1,0:T(8,128)(2,1)S(1)} %pad_maximum_fusion), channel_id=1, source_target_pairs={{0,128},{128,0},{1,129},{129,1},{2,130},{130,2},{3,131},{131,3},{4... | collective-permute-start | bytes 1572872 | tf_op jit(solution)/shard_map/ppermute | solution.py:39
  5.3 2.1 %collective-permute-start.6 = (bf16[128,1024]{1,0:T(8,128)(2,1)S(1)}, bf16[128,1024]{1,0:T(8,128)(2,1)S(1)}, u32[]{:S(2)}, u32[]{:S(2)}) collective-permute-start(bf16[128,1024]{1,0:T(8,128)(2,1)S(1)} %get-tuple-element.49), channel_id=1, source_target_pairs={{0,64},{64,0},{1,65},{65,1},{2,66},{66,2},{3,67},{67,3},{4,68},{68... | collective-permute-start | bytes 786440 | tf_op jit(solution)/shard_map/ppermute | solution.py:39
  7.5 15.8 %collective-permute-start.7 = (bf16[256,1024]{1,0:T(8,128)(2,1)S(1)}, bf16[256,1024]{1,0:T(8,128)(2,1)S(1)}, u32[]{:S(2)}, u32[]{:S(2)}) collective-permute-start(bf16[256,1024]{1,0:T(8,128)(2,1)S(1)} %pad_maximum_fusion.2), channel_id=1, source_target_pairs={{0,16},{4,20},{8,24},{12,28},{16,32},{20,36},{24,40},{28,44},{32,4... | collective-permute-start | bytes 1572872 | tf_op jit(solution)/shard_map/ppermute | solution.py:30
  8.8 15.3 %collective-permute-start.8 = (bf16[256,1024]{1,0:T(8,128)(2,1)S(1)}, bf16[256,1024]{1,0:T(8,128)(2,1)S(1)}, u32[]{:S(2)}, u32[]{:S(2)}) collective-permute-start(bf16[256,1024]{1,0:T(8,128)(2,1)S(1)} %pad_maximum_fusion.2), channel_id=1, source_target_pairs={{0,48},{4,52},{8,56},{12,60},{16,0},{20,4},{24,8},{28,12},{32,16},... | collective-permute-start | bytes 1572872 | tf_op jit(solution)/shard_map/ppermute | solution.py:30
  10.4 13.8 %collective-permute-start.9 = (bf16[256,1024]{1,0:T(8,128)(2,1)S(1)}, bf16[256,1024]{1,0:T(8,128)(2,1)S(1)}, u32[]{:S(2)}, u32[]{:S(2)}) collective-permute-start(bf16[256,1024]{1,0:T(8,128)(2,1)S(1)} %pad_maximum_fusion.2), channel_id=1, source_target_pairs={{0,32},{4,36},{8,40},{12,44},{16,48},{20,52},{24,56},{28,60},{32,0... | collective-permute-start | bytes 1572872 | tf_op jit(solution)/shard_map/ppermute | solution.py:30
  16.7 3.8 %collective-permute-start.1 = (bf16[128,1024]{1,0:T(8,128)(2,1)S(1)}, bf16[128,1024]{1,0:T(8,128)(2,1)S(1)}, u32[]{:S(2)}, u32[]{:S(2)}) collective-permute-start(bf16[128,1024]{1,0:T(8,128)(2,1)S(1)} %get-tuple-element.52), channel_id=1, source_target_pairs={{0,64},{64,0},{1,65},{65,1},{2,66},{66,2},{3,67},{67,3},{4,68},{68... | collective-permute-start | bytes 786440 | tf_op jit(solution)/shard_map/ppermute | solution.py:39
  19.0 30.8 %collective-permute-start.10 = (bf16[2048,512]{1,0:T(8,128)(2,1)S(1)}, bf16[2048,512]{1,0:T(8,128)(2,1)}, u32[]{:S(2)}, u32[]{:S(2)}) collective-permute-start(bf16[2048,512]{1,0:T(8,128)(2,1)S(1)} %copy-done), channel_id=1, source_target_pairs={{0,64},{64,0},{1,65},{65,1},{2,66},{66,2},{3,67},{67,3},{4,68},{68... | collective-permute-start | bytes 6291464 | tf_op jit(solution)/shard_map/ppermute | solution.py:39
  20.5 8.9 %collective-permute-start.3 = (bf16[256,1024]{1,0:T(8,128)(2,1)S(1)}, bf16[256,1024]{1,0:T(8,128)(2,1)S(1)}, u32[]{:S(2)}, u32[]{:S(2)}) collective-permute-start(bf16[256,1024]{1,0:T(8,128)(2,1)S(1)} %pad_maximum_fusion.1), channel_id=1, source_target_pairs={{0,48},{4,52},{8,56},{12,60},{16,0},{20,4},{24,8},{28,12},{32,16},... | collective-permute-start | bytes 1572872 | tf_op jit(solution)/shard_map/ppermute | solution.py:30
  23.3 11.2 %collective-permute-start.2 = (bf16[256,1024]{1,0:T(8,128)(2,1)S(1)}, bf16[256,1024]{1,0:T(8,128)(2,1)S(1)}, u32[]{:S(2)}, u32[]{:S(2)}) collective-permute-start(bf16[256,1024]{1,0:T(8,128)(2,1)S(1)} %pad_maximum_fusion.1), channel_id=1, source_target_pairs={{0,16},{4,20},{8,24},{12,28},{16,32},{20,36},{24,40},{28,44},{32,4... | collective-permute-start | bytes 1572872 | tf_op jit(solution)/shard_map/ppermute | solution.py:30
  25.8 35.6 %collective-permute-start.11 = (bf16[1024,1024]{1,0:T(8,128)(2,1)}, bf16[1024,1024]{1,0:T(8,128)(2,1)}, u32[]{:S(2)}, u32[]{:S(2)}) collective-permute-start(bf16[1024,1024]{1,0:T(8,128)(2,1)} %constant_dynamic-update-slice_fusion.5), channel_id=1, source_target_pairs={{0,4},{4,8},{8,12},{12,0},{16,20},{20,24},{24,28},{28,16},{32,36},... | collective-permute-start | bytes 6291464 | tf_op jit(solution)/shard_map/ppermute | solution.py:30
  27.0 34.4 %collective-permute-start.12 = (bf16[1024,1024]{1,0:T(8,128)(2,1)}, bf16[1024,1024]{1,0:T(8,128)(2,1)}, u32[]{:S(2)}, u32[]{:S(2)}) collective-permute-start(bf16[1024,1024]{1,0:T(8,128)(2,1)} %constant_dynamic-update-slice_fusion.5), channel_id=1, source_target_pairs={{0,12},{4,0},{8,4},{12,8},{16,28},{20,16},{24,20},{28,24},{32,44},... | collective-permute-start | bytes 6291464 | tf_op jit(solution)/shard_map/ppermute | solution.py:30
  29.4 15.2 %collective-permute-start.4 = (bf16[256,1024]{1,0:T(8,128)(2,1)S(1)}, bf16[256,1024]{1,0:T(8,128)(2,1)S(1)}, u32[]{:S(2)}, u32[]{:S(2)}) collective-permute-start(bf16[256,1024]{1,0:T(8,128)(2,1)S(1)} %collective-permute-done.3), channel_id=1, source_target_pairs={{0,48},{4,52},{8,56},{12,60},{16,0},{20,4},{24,8},{28,12},{32,16},... | collective-permute-start | bytes 1572872 | tf_op jit(solution)/shard_map/ppermute | solution.py:30
  45.5 35.2 %collective-permute-start.5 = (bf16[1024,1024]{1,0:T(8,128)(2,1)}, bf16[1024,1024]{1,0:T(8,128)(2,1)}, u32[]{:S(2)}, u32[]{:S(2)}) collective-permute-start(bf16[1024,1024]{1,0:T(8,128)(2,1)} %constant_dynamic-update-slice_fusion), channel_id=1, source_target_pairs={{0,12},{4,0},{8,4},{12,8},{16,28},{20,16},{24,20},{28,24},{32,44},... | collective-permute-start | bytes 6291464 | tf_op jit(solution)/shard_map/ppermute | solution.py:30
  48.2 32.5 %collective-permute-start.14 = (bf16[1024,512]{1,0:T(8,128)(2,1)S(1)}, bf16[1024,512]{1,0:T(8,128)(2,1)S(1)}, u32[]{:S(2)}, u32[]{:S(2)}) collective-permute-start(bf16[1024,512]{1,0:T(8,128)(2,1)S(1)} %get-tuple-element.46), channel_id=1, source_target_pairs={{0,128},{128,1},{1,129},{129,2},{2,130},{130,3},{3,131},{131,0},{4... | collective-permute-start | bytes 3145736 | tf_op jit(solution)/shard_map/ppermute | solution.py:35
  49.7 30.9 %collective-permute-start.15 = (bf16[1024,512]{1,0:T(8,128)(2,1)S(1)}, bf16[1024,512]{1,0:T(8,128)(2,1)S(1)}, u32[]{:S(2)}, u32[]{:S(2)}) collective-permute-start(bf16[1024,512]{1,0:T(8,128)(2,1)S(1)} %get-tuple-element.45), channel_id=1, source_target_pairs={{0,131},{128,0},{1,128},{129,1},{2,129},{130,2},{3,130},{131,3},{4... | collective-permute-start | bytes 3145736 | tf_op jit(solution)/shard_map/ppermute | solution.py:35
  61.4 26.7 %collective-permute-start.13 = (bf16[1024,1024]{1,0:T(8,128)(2,1)}, bf16[1024,1024]{1,0:T(8,128)(2,1)S(1)}, u32[]{:S(2)}, u32[]{:S(2)}) collective-permute-start(bf16[1024,1024]{1,0:T(8,128)(2,1)} %collective-permute-done.11), channel_id=1, source_target_pairs={{0,4},{4,8},{8,12},{12,0},{16,20},{20,24},{24,28},{28,16},{32,36},... | collective-permute-start | bytes 6291464 | tf_op jit(solution)/shard_map/ppermute | solution.py:30
  80.8 8.5 %collective-permute-start.16 = (bf16[2048,512]{1,0:T(8,128)(2,1)S(1)}, bf16[2048,512]{1,0:T(8,128)(2,1)S(1)}, u32[]{:S(2)}, u32[]{:S(2)}) collective-permute-start(bf16[2048,512]{1,0:T(8,128)(2,1)S(1)} %constant_dynamic-update-slice_fusion.10.first), channel_id=1, source_target_pairs={{0,64},{64,0},{1,65},{65,1},{2,66},{66,2},{3,67},{67,3},{4,68},{68... | collective-permute-start | bytes 6291464 | tf_op jit(solution)/shard_map/ppermute | solution.py:39
  82.8 25.9 %collective-permute-start.18 = (bf16[1024,1024]{1,0:T(8,128)(2,1)}, bf16[1024,1024]{1,0:T(8,128)(2,1)S(1)}, u32[]{:S(2)}, u32[]{:S(2)}) collective-permute-start(bf16[1024,1024]{1,0:T(8,128)(2,1)} %collective-permute-done.5), channel_id=1, source_target_pairs={{0,12},{4,0},{8,4},{12,8},{16,28},{20,16},{24,20},{28,24},{32,44},... | collective-permute-start | bytes 6291464 | tf_op jit(solution)/shard_map/ppermute | solution.py:30
  85.4 26.6 %collective-permute-start.17 = (bf16[1024,1024]{1,0:T(8,128)(2,1)}, bf16[1024,1024]{1,0:T(8,128)(2,1)S(1)}, u32[]{:S(2)}, u32[]{:S(2)}) collective-permute-start(bf16[1024,1024]{1,0:T(8,128)(2,1)} %constant_dynamic-update-slice_fusion), channel_id=1, source_target_pairs={{0,4},{4,8},{8,12},{12,0},{16,20},{20,24},{24,28},{28,16},{32,36},... | collective-permute-start | bytes 6291464 | tf_op jit(solution)/shard_map/ppermute | solution.py:30
  113.3 14.9 %copy-start.3 = (f32[1024]{0:T(1024)S(1)}, f32[1024]{0:T(1024)}, u32[]{:S(2)}) copy-start(f32[1024]{0:T(1024)} %param.12) | copy-start | bytes 12292
  128.2 15.8 %copy-start.2 = (f32[1024]{0:T(1024)}, f32[1024]{0:T(1024)S(1)}, u32[]{:S(2)}) copy-start(f32[1024]{0:T(1024)S(1)} %get-tuple-element.40) | copy-start | bytes 12292
  128.9 18.2 %all-to-all-start.1 = ((f32[16,1,640]{2,1,0:T(1,128)}), f32[16,1,640]{2,1,0:T(1,128)S(1)}, u32[]{:S(2)}, u32[]{:S(2)}) async-start(f32[16,1,640]{2,1,0:T(1,128)} %broadcast_in_dim.5), calls=%async_computation.1 | async-start | bytes 81920 | tf_op jit(solution)/shard_map/all_to_all | solution.py:93
  139.5 8.8 %copy-start.4 = (f32[512]{0:T(512)S(1)}, f32[512]{0:T(512)}, u32[]{:S(2)}) copy-start(f32[512]{0:T(512)} %param.13) | copy-start | bytes 6148
  139.6 9.4 %copy-start.1 = (bf16[1024,512]{1,0:T(8,128)(2,1)S(1)}, bf16[1024,512]{1,0:T(8,128)(2,1)}, u32[]{:S(2)}) copy-start(bf16[1024,512]{1,0:T(8,128)(2,1)} %param.10) | copy-start | bytes 3145732

commit v10 on v9

--- a/solution.py
+++ b/solution.py
@@ -118,23 +118,26 @@
 
     near = [*ring_start(near, 0), shift(near, 0, 2)]
     near[3:] = after(near[3:], away)
-    (sent,) = after((activations,), *near)
     near = ring_start(jnp.concatenate(near, axis=0), 1)
     away = ring_end(ring_start(away, 0), 0, -1)
+    near = list(after(near, *away))
+    (sent,) = after((activations,), *near)
     half = sent.shape[0] // 2
     acts_low = (along_z(sent[:half], 1), along_z(sent[half:], -1))
     first = arranged(places, activations, acts_core)
     gradient = product(near[0], first[0]) + product(near[1], first[1]) + product(near[2], first[2])
-    near = ring_end(after(near, *away), 1, 1)
     away = ring_start(jnp.concatenate(away, axis=0), 1)
+    near[1], away[1] = lax.optimization_barrier((near[1], away[1]))
+    near = ring_end(near, 1, 1)
     away[2], gradient = lax.optimization_barrier((away[2], gradient))
     away = ring_end(away, 1, -1)
     acts_low = jnp.concatenate(after(acts_low, away[2]), axis=0)
     second = arranged(places, acts_low, swap(acts_low, "core"))
+    gradient = gradient + product(away[0], second[0])
+    gradient = gradient + product(away[1], second[1]) + product(away[2], second[2])
     gradient = gradient + product(near[3], first[3])
-    gradient = gradient + product(away[0], second[0]) + product(away[2], second[2])
-    last = lax.optimization_barrier((product(away[1], second[1]), product(away[3], second[3])))
-    gradient = gradient + (last[0] + last[1])
+    away[3], gradient = lax.optimization_barrier((away[3], gradient))
+    gradient = gradient + lax.optimization_barrier(product(away[3], second[3]))
     gradient = gradient * token_scale
 
     squares = gradient * gradient + 1e-30

time: 153 us -> 163 us (1.065)
  waiting for transfers between devices: 47.5 us -> 59.5 us
  starting transfers between devices: 42.7 us -> 38.7 us
    ppermute x2, waiting for transfers between devices: 0.01 us -> 6.89 us  [along_z(): lax.ppermute(array, ('zl', 'zh'), [(place(z), place((z + step) % 8)) for...]
    all_to_all x1, starting transfers between devices: 10.7 us -> 5.7 us  [total_over(): return jnp.sum(lax.all_to_all(spread, axes, 0, 0, tiled=True), axis=0)]
    ppermute x12, waiting for transfers between devices: 38.5 us -> 42.6 us  [shift(): return lax.ppermute(array, AXES, ring_pairs(phase, step))]
    ppermute x5, starting transfers between devices: 7.82 us -> 10.9 us  [swap(): return lax.ppermute(array, axis, [(0, 1), (1, 0)])]
    unnamed x18 -> x17, local copies, waits for them, and re-layouts: 6.9 us -> 4.85 us
    dynamic_slice x0 -> x1, local copies, waits for them, and re-layouts: none -> 2.05 us  [units(): lax.dynamic_slice_in_dim(out_grads, ((low ^ a) * 2 + (core ^ b)) * rows,...]
  transfers between devices with their start and end apart: 20 -> 20, of which waited for: 11 -> 12; matrix products, arithmetic and copies ran while one was open for 17% -> 18% of each run, Pallas kernels for 7% -> 7%
where the time goes in v10:
time: 163 us; the launch traced here: 162 us
  waiting for transfers between devices  59.5 us (37%)
  starting transfers between devices  38.7 us (24%)
  matrix products  18.5 us (11%)
  blocking collectives  12.4 us (8%)
  Pallas kernels  10.9 us (7%)
  local copies, waits for them, and re-layouts  10.3 us (6%)
  other arithmetic  10.3 us (6%)
    ppermute x12, waiting for transfers between devices, shift(): return lax.ppermute(array, AXES, ring_pairs(phase, step))  42.6 us
    dot_general x8, matrix products, product(): lax.dot_general(grad_rows, act_rows, (((0,), (0,)), ((), ())), preferred_...  18.5 us
    ppermute x12, starting transfers between devices, shift(): return lax.ppermute(array, AXES, ring_pairs(phase, step))  17.4 us
    all_to_all x1, blocking collectives, total_over(): return jnp.sum(lax.all_to_all(spread, axes, 0, 0, tiled=True), axis=0)  12.4 us
    ppermute x5, starting transfers between devices, swap(): return lax.ppermute(array, axis, [(0, 1), (1, 0)])  10.9 us
    pallas_call x2, Pallas kernels, arranged(): pl.pallas_call(arrange_kernel, in_specs=[pl.BlockSpec(memory_space=pltpu....  10.9 us
    ppermute x5, waiting for transfers between devices, swap(): return lax.ppermute(array, axis, [(0, 1), (1, 0)])  6.98 us
    ppermute x2, waiting for transfers between devices, along_z(): lax.ppermute(array, ('zl', 'zh'), [(place(z), place((z + step) % 8)) for...  6.89 us
  transfers between devices with their start and end apart: 20, of which 12 were waited for; matrix products, arithmetic and copies ran while one was open for 18% of the time, Pallas kernels for 7%

profile of v10, /device:TPU:1, one launch (start us, length us, event | category | flops | bytes accessed | tf_op | source)
XLA Modules:
  0.0 162.2 jit_solution(4134026591636743700)
XLA Ops:
  0.7 2.1 %constant_dynamic-slice_fusion = (bf16[128,1024]{1,0:T(8,128)(2,1)S(1)}, bf16[128,1024]{1,0:T(8,128)(2,1)S(1)}, bf16[128,1024]{1,0:T(8,128)(2,1)S(1)}, bf16[1024,1024]{1,0:T(8,128)(2,1)}, bf16[128,1024]{1,0:T(8,128)(2,1)S(1)}) fusion(bf16[128,4096]{1,0:T(8,128)(2,1)} %param.8, s32[]{:T(128)S(6)} %select_n.203, s32[]{:T(128)S(6)} %select_n.201, ...), kind=kLoop, calls=%fused_computation.44 | loop fusion | bytes 2359312 | tf_op jit(solution)/shard_map/dynamic_slice | solution.py:103
  2.8 2.6 %collective-permute-start = (bf16[256,1024]{1,0:T(8,128)(2,1)S(1)}, bf16[256,1024]{1,0:T(8,128)(2,1)S(1)}, u32[]{:S(2)}, u32[]{:S(2)}) collective-permute-start(bf16[256,1024]{1,0:T(8,128)(2,1)S(1)} %pad_maximum_fusion), channel_id=1, source_target_pairs={{0,128},{128,0},{1,129},{129,1},{2,130},{130,2},{3,131},{131,3},{4... | collective-permute-start | bytes 1572872 | tf_op jit(solution)/shard_map/ppermute | solution.py:39
  5.3 1.0 collective-permute-start.6
  6.3 1.2 collective-permute-done.6
  7.5 3.0 %collective-permute-start.9 = (bf16[256,1024]{1,0:T(8,128)(2,1)S(1)}, bf16[256,1024]{1,0:T(8,128)(2,1)S(1)}, u32[]{:S(2)}, u32[]{:S(2)}) collective-permute-start(bf16[256,1024]{1,0:T(8,128)(2,1)S(1)} %pad_maximum_fusion.2), channel_id=1, source_target_pairs={{0,32},{4,36},{8,40},{12,44},{16,48},{20,52},{24,56},{28,60},{32,0... | collective-permute-start | bytes 1572872 | tf_op jit(solution)/shard_map/ppermute | solution.py:30
  10.5 0.8 collective-permute-start.8
  11.9 4.0 %collective-permute-done = bf16[256,1024]{1,0:T(8,128)(2,1)S(1)} collective-permute-done((bf16[256,1024]{1,0:T(8,128)(2,1)S(1)}, bf16[256,1024]{1,0:T(8,128)(2,1)S(1)}, u32[]{:S(2)}, u32[]{:S(2)}) %collective-permute-start) | collective-permute-done | bytes 524320 | tf_op jit(solution)/shard_map/ppermute | solution.py:39
  15.9 0.8 fusion.21
  16.7 2.3 %collective-permute-start.1 = (bf16[128,1024]{1,0:T(8,128)(2,1)S(1)}, bf16[128,1024]{1,0:T(8,128)(2,1)S(1)}, u32[]{:S(2)}, u32[]{:S(2)}) collective-permute-start(bf16[128,1024]{1,0:T(8,128)(2,1)S(1)} %get-tuple-element.63), channel_id=1, source_target_pairs={{0,64},{64,0},{1,65},{65,1},{2,66},{66,2},{3,67},{67,3},{4,68},{68... | collective-permute-start | bytes 786440 | tf_op jit(solution)/shard_map/ppermute | solution.py:39
  19.0 0.7 constant_dynamic-update-slice_fusion.8
  19.7 0.7 collective-permute-done.1
  20.5 2.5 %collective-permute-done.7 = bf16[256,1024]{1,0:T(8,128)(2,1)S(1)} collective-permute-done((bf16[256,1024]{1,0:T(8,128)(2,1)S(1)}, bf16[256,1024]{1,0:T(8,128)(2,1)S(1)}, u32[]{:S(2)}, u32[]{:S(2)}) %collective-permute-start.7) | collective-permute-done | bytes 524320 | tf_op jit(solution)/shard_map/ppermute | solution.py:30
  23.0 0.8 constant_dynamic-update-slice_fusion.7
  23.8 0.8 constant_dynamic-update-slice_fusion.6
  24.7 0.8 constant_dynamic-update-slice_fusion.5
  25.5 2.5 %collective-permute-start.11 = (bf16[1024,1024]{1,0:T(8,128)(2,1)}, bf16[1024,1024]{1,0:T(8,128)(2,1)}, u32[]{:S(2)}, u32[]{:S(2)}) collective-permute-start(bf16[1024,1024]{1,0:T(8,128)(2,1)} %constant_dynamic-update-slice_fusion.5), channel_id=1, source_target_pairs={{0,12},{4,0},{8,4},{12,8},{16,28},{20,16},{24,20},{28,24},{32,44},... | collective-permute-start | bytes 6291464 | tf_op jit(solution)/shard_map/ppermute | solution.py:30
  28.0 1.9 %collective-permute-start.3 = (bf16[256,1024]{1,0:T(8,128)(2,1)S(1)}, bf16[256,1024]{1,0:T(8,128)(2,1)S(1)}, u32[]{:S(2)}, u32[]{:S(2)}) collective-permute-start(bf16[256,1024]{1,0:T(8,128)(2,1)S(1)} %pad_maximum_fusion.1), channel_id=1, source_target_pairs={{0,48},{4,52},{8,56},{12,60},{16,0},{20,4},{24,8},{28,12},{32,16},... | collective-permute-start | bytes 1572872 | tf_op jit(solution)/shard_map/ppermute | solution.py:30
  29.9 12.1 %collective-permute-done.3 = bf16[256,1024]{1,0:T(8,128)(2,1)S(1)} collective-permute-done((bf16[256,1024]{1,0:T(8,128)(2,1)S(1)}, bf16[256,1024]{1,0:T(8,128)(2,1)S(1)}, u32[]{:S(2)}, u32[]{:S(2)}) %collective-permute-start.3) | collective-permute-done | bytes 524320 | tf_op jit(solution)/shard_map/ppermute | solution.py:30
  42.0 2.9 %collective-permute-start.4 = (bf16[256,1024]{1,0:T(8,128)(2,1)S(1)}, bf16[256,1024]{1,0:T(8,128)(2,1)S(1)}, u32[]{:S(2)}, u32[]{:S(2)}) collective-permute-start(bf16[256,1024]{1,0:T(8,128)(2,1)S(1)} %collective-permute-done.3), channel_id=1, source_target_pairs={{0,48},{4,52},{8,56},{12,60},{16,0},{20,4},{24,8},{28,12},{32,16},... | collective-permute-start | bytes 1572872 | tf_op jit(solution)/shard_map/ppermute | solution.py:30
  44.9 0.7 constant_dynamic-update-slice_fusion.3
  45.6 0.8 constant_dynamic-update-slice_fusion.2
  46.4 0.8 constant_dynamic-update-slice_fusion.1
  47.3 9.4 %collective-permute-done.4 = bf16[256,1024]{1,0:T(8,128)(2,1)S(1)} collective-permute-done((bf16[256,1024]{1,0:T(8,128)(2,1)S(1)}, bf16[256,1024]{1,0:T(8,128)(2,1)S(1)}, u32[]{:S(2)}, u32[]{:S(2)}) %collective-permute-start.4) | collective-permute-done | bytes 524320 | tf_op jit(solution)/shard_map/ppermute | solution.py:30
  56.7 0.8 constant_dynamic-update-slice_fusion
  57.5 2.9 %collective-permute-start.5 = (bf16[1024,1024]{1,0:T(8,128)(2,1)}, bf16[1024,1024]{1,0:T(8,128)(2,1)}, u32[]{:S(2)}, u32[]{:S(2)}) collective-permute-start(bf16[1024,1024]{1,0:T(8,128)(2,1)} %constant_dynamic-update-slice_fusion), channel_id=1, source_target_pairs={{0,12},{4,0},{8,4},{12,8},{16,28},{20,16},{24,20},{28,24},{32,44},... | collective-permute-start | bytes 6291464 | tf_op jit(solution)/shard_map/ppermute | solution.py:30
  60.6 4.5 %shard_map.110 = bf16[4096,512]{1,0:T(8,128)(2,1)S(1)} custom-call(s32[16]{0:T(128)S(1)} %stack.67.place, bf16[2048,512]{1,0:T(8,128)(2,1)S(1)} %copy-done, bf16[2048,512]{1,0:T(8,128)(2,1)} %collective-permute-done.12.second), custom_call_target="tpu_custom_call" | custom-call | bytes 8388608 | tf_op jit(solution)/shard_map/pallas_call | solution.py:77
  65.3 4.7 %collective-permute-start.15 = (bf16[1024,512]{1,0:T(8,128)(2,1)S(1)}, bf16[1024,512]{1,0:T(8,128)(2,1)S(1)}, u32[]{:S(2)}, u32[]{:S(2)}) collective-permute-start(bf16[1024,512]{1,0:T(8,128)(2,1)S(1)} %get-tuple-element.54), channel_id=1, source_target_pairs={{0,131},{128,0},{1,128},{129,1},{2,129},{130,2},{3,130},{131,3},{4... | collective-permute-start | bytes 3145736 | tf_op jit(solution)/shard_map/ppermute | solution.py:35
  70.0 2.9 %fusion.17 = f32[1024,512]{1,0:T(8,128)S(1)} fusion(bf16[1024,1024]{1,0:T(8,128)(2,1)} %constant_dynamic-update-slice_fusion.5, bf16[4096,512]{1,0:T(8,128)(2,1)S(1)} %shard_map.110), kind=kOutput, calls=%fused_computation.22 | convolution fusion | flops 1073741824 | bytes 5242880 | tf_op jit(solution)/shard_map/dot_general | solution.py:55
  72.9 2.9 %fusion.15 = f32[1024,512]{1,0:T(8,128)S(1)} fusion(bf16[1024,1024]{1,0:T(8,128)(2,1)} %collective-permute-done.10, bf16[4096,512]{1,0:T(8,128)(2,1)S(1)} %shard_map.110), kind=kOutput, calls=%fused_computation.20 | convolution fusion | flops 1073741824 | bytes 5242880 | tf_op jit(solution)/shard_map/dot_general | solution.py:55
  75.8 2.9 %add_add_fusion.1 = f32[1024,512]{1,0:T(8,128)S(1)} fusion(f32[1024,512]{1,0:T(8,128)S(1)} %fusion.17, f32[1024,512]{1,0:T(8,128)S(1)} %fusion.15, bf16[1024,1024]{1,0:T(8,128)(2,1)} %collective-permute-done.11, bf16[4096,512]{1,0:T(8,128)(2,1)S(1)} %shard_map.110), kind=kOutput, calls=%fused_computation.6 | convolution fusion | flops 1074790400 | bytes 9437184 | tf_op jit(solution)/shard_map/dot_general | solution.py:55
  78.7 6.3 %collective-permute-done.5 = bf16[1024,1024]{1,0:T(8,128)(2,1)} collective-permute-done((bf16[1024,1024]{1,0:T(8,128)(2,1)}, bf16[1024,1024]{1,0:T(8,128)(2,1)}, u32[]{:S(2)}, u32[]{:S(2)}) %collective-permute-start.5) | collective-permute-done | bytes 2097184 | tf_op jit(solution)/shard_map/ppermute | solution.py:30
  85.0 3.8 %collective-permute-done.15 = bf16[1024,512]{1,0:T(8,128)(2,1)S(1)} collective-permute-done((bf16[1024,512]{1,0:T(8,128)(2,1)S(1)}, bf16[1024,512]{1,0:T(8,128)(2,1)S(1)}, u32[]{:S(2)}, u32[]{:S(2)}) %collective-permute-start.15) | collective-permute-done | bytes 1048608 | tf_op jit(solution)/shard_map/ppermute | solution.py:35
  88.7 3.1 %collective-permute-done.14 = bf16[1024,512]{1,0:T(8,128)(2,1)S(1)} collective-permute-done((bf16[1024,512]{1,0:T(8,128)(2,1)S(1)}, bf16[1024,512]{1,0:T(8,128)(2,1)S(1)}, u32[]{:S(2)}, u32[]{:S(2)}) %collective-permute-start.14) | collective-permute-done | bytes 1048608 | tf_op jit(solution)/shard_map/ppermute | solution.py:35
  92.0 5.1 %collective-permute-start.16 = (bf16[2048,512]{1,0:T(8,128)(2,1)S(1)}, bf16[2048,512]{1,0:T(8,128)(2,1)S(1)}, u32[]{:S(2)}, u32[]{:S(2)}) collective-permute-start(bf16[2048,512]{1,0:T(8,128)(2,1)S(1)} %constant_dynamic-update-slice_fusion.10.first), channel_id=1, source_target_pairs={{0,64},{64,0},{1,65},{65,1},{2,66},{66,2},{3,67},{67,3},{4,68},{68... | collective-permute-start | bytes 6291464 | tf_op jit(solution)/shard_map/ppermute | solution.py:39
  97.1 2.7 %collective-permute-start.13 = (bf16[1024,1024]{1,0:T(8,128)(2,1)}, bf16[1024,1024]{1,0:T(8,128)(2,1)S(1)}, u32[]{:S(2)}, u32[]{:S(2)}) collective-permute-start(bf16[1024,1024]{1,0:T(8,128)(2,1)} %collective-permute-done.5), channel_id=1, source_target_pairs={{0,12},{4,0},{8,4},{12,8},{16,28},{20,16},{24,20},{28,24},{32,44},... | collective-permute-start | bytes 6291464 | tf_op jit(solution)/shard_map/ppermute | solution.py:30
  99.8 1.1 collective-permute-done.16.second
  100.9 6.3 %shard_map.111 = bf16[4096,512]{1,0:T(8,128)(2,1)S(1)} custom-call(s32[16]{0:T(128)S(1)} %stack.67.place, bf16[2048,512]{1,0:T(8,128)(2,1)S(1)} %constant_dynamic-update-slice_fusion.10.first, bf16[2048,512]{1,0:T(8,128)(2,1)S(1)} %collective-permute-done.16.second), custom_call_target="tpu_custom_call" | custom-call | bytes 8388608 | tf_op jit(solution)/shard_map/pallas_call | solution.py:77
  107.2 2.9 %fusion.6 = f32[1024,512]{1,0:T(8,128)S(1)} fusion(bf16[1024,1024]{1,0:T(8,128)(2,1)} %collective-permute-done.5, bf16[4096,512]{1,0:T(8,128)(2,1)S(1)} %shard_map.111), kind=kOutput, calls=%fused_computation.13 | convolution fusion | flops 1073741824 | bytes 5242880 | tf_op jit(solution)/shard_map/dot_general | solution.py:55
  110.1 1.3 fusion.8
  111.4 12.3 %collective-permute-done.18 = bf16[1024,1024]{1,0:T(8,128)(2,1)S(1)} collective-permute-done((bf16[1024,1024]{1,0:T(8,128)(2,1)}, bf16[1024,1024]{1,0:T(8,128)(2,1)S(1)}, u32[]{:S(2)}, u32[]{:S(2)}) %collective-permute-start.18) | collective-permute-done | bytes 2097184 | tf_op jit(solution)/shard_map/ppermute | solution.py:30
  123.7 1.3 fusion.4
  125.0 3.2 %add_add_fusion = f32[1024,512]{1,0:T(8,128)S(1)} fusion(f32[1024,512]{1,0:T(8,128)S(1)} %fusion.4, f32[1024,512]{1,0:T(8,128)S(1)} %fusion.6, f32[1024,512]{1,0:T(8,128)S(1)} %fusion.8, f32[1024,512]{1,0:T(8,128)S(1)} %add_add_fusion.1, bf16[1024,1024]{1,0:T(8,128)(2,1)} %constant_dynamic-update-slice_fusion, bf16[4096,512]{1,0:T(8,128)(2,1)S(1)} %shard_map.111), kind=kOutput, calls=%fused_computation.5 | convolution fusion | flops 1075838976 | bytes 13631488 | tf_op jit(solution)/shard_map/dot_general | solution.py:55
  128.2 1.3 fusion.2
  130.1 12.4 %all_to_all.12 = f32[16,1,1024]{2,1,0:T(1,128)S(1)} all-to-all(f32[16,1,1024]{2,1,0:T(1,128)S(1)} %broadcast_in_dim.4), channel_id=1, replica_groups=mesh['zl'=2,'core'=2,'x'=4,'y'=4,'zh'=4] {'x','y'}, dimensions={0} | all-to-all | bytes 131072 | tf_op jit(solution)/shard_map/all_to_all | solution.py:93
  143.2 5.7 %all-to-all-start.1 = ((f32[16,1,640]{2,1,0:T(1,128)}), f32[16,1,640]{2,1,0:T(1,128)S(1)}, u32[]{:S(2)}, u32[]{:S(2)}) async-start(f32[16,1,640]{2,1,0:T(1,128)} %broadcast_in_dim.5), calls=%async_computation.1 | async-start | bytes 81920 | tf_op jit(solution)/shard_map/all_to_all | solution.py:93
  148.9 4.4 %multiply_subtract_fusion.1 = f32[1024,512]{1,0:T(8,128)} fusion(f32[1024,512]{1,0:T(8,128)} %param.11, f32[1024,512]{1,0:T(8,128)S(1)} %get-tuple-element.40, f32[1024,512]{1,0:T(8,128)} %param.9), kind=kLoop, calls=%fused_computation.2 | loop fusion | flops 1572864 | bytes 8388608 | tf_op jit(solution)/shard_map/sub | solution.py:146
  153.3 3.0 %all-to-all-done.1 = f32[16,1,640]{2,1,0:T(1,128)S(1)} async-done(((f32[16,1,640]{2,1,0:T(1,128)}), f32[16,1,640]{2,1,0:T(1,128)S(1)}, u32[]{:S(2)}, u32[]{:S(2)}) %all-to-all-start.1) | async-done | bytes 40992 | tf_op jit(solution)/shard_map/all_to_all | solution.py:93
  158.3 3.9 %multiply_subtract_fusion = (f32[1024,512]{1,0:T(8,128)}, bf16[1024,512]{1,0:T(8,128)(2,1)}) fusion(f32[1024,512]{1,0:T(8,128)} %param.9, f32[1024,512]{1,0:T(8,128)S(1)} %get-tuple-element.40, f32[512]{0:T(512)S(1)} %get-tuple-element.49, f32[1024]{0:T(1024)S(1)} %get-tuple-element.47, bf16[1024,512]{1,0:T(8,128)(2,1)S(1)} %copy-done.1), kind=kLoop, calls=%fused_computation | loop fusion | flops 5242880 | bytes 8394752 | tf_op jit(solution)/shard_map/sub | solution.py:159
  (42 shorter events, 3.9 us)
Async XLA Ops:
  2.7 16.3 %copy-start = (bf16[2048,512]{1,0:T(8,128)(2,1)S(1)}, bf16[2048,512]{1,0:T(8,128)(2,1)}, u32[]{:S(2)}) copy-start(bf16[2048,512]{1,0:T(8,128)(2,1)} %first.1) | copy-start | bytes 6291460
  2.8 13.1 %collective-permute-start = (bf16[256,1024]{1,0:T(8,128)(2,1)S(1)}, bf16[256,1024]{1,0:T(8,128)(2,1)S(1)}, u32[]{:S(2)}, u32[]{:S(2)}) collective-permute-start(bf16[256,1024]{1,0:T(8,128)(2,1)S(1)} %pad_maximum_fusion), channel_id=1, source_target_pairs={{0,128},{128,0},{1,129},{129,1},{2,130},{130,2},{3,131},{131,3},{4... | collective-permute-start | bytes 1572872 | tf_op jit(solution)/shard_map/ppermute | solution.py:39
  5.3 2.1 %collective-permute-start.6 = (bf16[128,1024]{1,0:T(8,128)(2,1)S(1)}, bf16[128,1024]{1,0:T(8,128)(2,1)S(1)}, u32[]{:S(2)}, u32[]{:S(2)}) collective-permute-start(bf16[128,1024]{1,0:T(8,128)(2,1)S(1)} %get-tuple-element.56), channel_id=1, source_target_pairs={{0,64},{64,0},{1,65},{65,1},{2,66},{66,2},{3,67},{67,3},{4,68},{68... | collective-permute-start | bytes 786440 | tf_op jit(solution)/shard_map/ppermute | solution.py:39
  7.5 13.0 %collective-permute-start.9 = (bf16[256,1024]{1,0:T(8,128)(2,1)S(1)}, bf16[256,1024]{1,0:T(8,128)(2,1)S(1)}, u32[]{:S(2)}, u32[]{:S(2)}) collective-permute-start(bf16[256,1024]{1,0:T(8,128)(2,1)S(1)} %pad_maximum_fusion.2), channel_id=1, source_target_pairs={{0,32},{4,36},{8,40},{12,44},{16,48},{20,52},{24,56},{28,60},{32,0... | collective-permute-start | bytes 1572872 | tf_op jit(solution)/shard_map/ppermute | solution.py:30
  10.5 13.4 %collective-permute-start.8 = (bf16[256,1024]{1,0:T(8,128)(2,1)S(1)}, bf16[256,1024]{1,0:T(8,128)(2,1)S(1)}, u32[]{:S(2)}, u32[]{:S(2)}) collective-permute-start(bf16[256,1024]{1,0:T(8,128)(2,1)S(1)} %pad_maximum_fusion.2), channel_id=1, source_target_pairs={{0,48},{4,52},{8,56},{12,60},{16,0},{20,4},{24,8},{28,12},{32,16},... | collective-permute-start | bytes 1572872 | tf_op jit(solution)/shard_map/ppermute | solution.py:30
  11.2 11.8 %collective-permute-start.7 = (bf16[256,1024]{1,0:T(8,128)(2,1)S(1)}, bf16[256,1024]{1,0:T(8,128)(2,1)S(1)}, u32[]{:S(2)}, u32[]{:S(2)}) collective-permute-start(bf16[256,1024]{1,0:T(8,128)(2,1)S(1)} %pad_maximum_fusion.2), channel_id=1, source_target_pairs={{0,16},{4,20},{8,24},{12,28},{16,32},{20,36},{24,40},{28,44},{32,4... | collective-permute-start | bytes 1572872 | tf_op jit(solution)/shard_map/ppermute | solution.py:30
  16.7 3.8 %collective-permute-start.1 = (bf16[128,1024]{1,0:T(8,128)(2,1)S(1)}, bf16[128,1024]{1,0:T(8,128)(2,1)S(1)}, u32[]{:S(2)}, u32[]{:S(2)}) collective-permute-start(bf16[128,1024]{1,0:T(8,128)(2,1)S(1)} %get-tuple-element.63), channel_id=1, source_target_pairs={{0,64},{64,0},{1,65},{65,1},{2,66},{66,2},{3,67},{67,3},{4,68},{68... | collective-permute-start | bytes 786440 | tf_op jit(solution)/shard_map/ppermute | solution.py:39
  19.0 41.6 %collective-permute-start.12 = (bf16[2048,512]{1,0:T(8,128)(2,1)S(1)}, bf16[2048,512]{1,0:T(8,128)(2,1)}, u32[]{:S(2)}, u32[]{:S(2)}) collective-permute-start(bf16[2048,512]{1,0:T(8,128)(2,1)S(1)} %copy-done), channel_id=1, source_target_pairs={{0,64},{64,0},{1,65},{65,1},{2,66},{66,2},{3,67},{67,3},{4,68},{68... | collective-permute-start | bytes 6291464 | tf_op jit(solution)/shard_map/ppermute | solution.py:39
  25.5 39.7 %collective-permute-start.11 = (bf16[1024,1024]{1,0:T(8,128)(2,1)}, bf16[1024,1024]{1,0:T(8,128)(2,1)}, u32[]{:S(2)}, u32[]{:S(2)}) collective-permute-start(bf16[1024,1024]{1,0:T(8,128)(2,1)} %constant_dynamic-update-slice_fusion.5), channel_id=1, source_target_pairs={{0,12},{4,0},{8,4},{12,8},{16,28},{20,16},{24,20},{28,24},{32,44},... | collective-permute-start | bytes 6291464 | tf_op jit(solution)/shard_map/ppermute | solution.py:30
  28.0 37.2 %collective-permute-start.10 = (bf16[1024,1024]{1,0:T(8,128)(2,1)}, bf16[1024,1024]{1,0:T(8,128)(2,1)}, u32[]{:S(2)}, u32[]{:S(2)}) collective-permute-start(bf16[1024,1024]{1,0:T(8,128)(2,1)} %constant_dynamic-update-slice_fusion.5), channel_id=1, source_target_pairs={{0,4},{4,8},{8,12},{12,0},{16,20},{20,24},{24,28},{28,16},{32,36},... | collective-permute-start | bytes 6291464 | tf_op jit(solution)/shard_map/ppermute | solution.py:30
  28.0 14.0 %collective-permute-start.3 = (bf16[256,1024]{1,0:T(8,128)(2,1)S(1)}, bf16[256,1024]{1,0:T(8,128)(2,1)S(1)}, u32[]{:S(2)}, u32[]{:S(2)}) collective-permute-start(bf16[256,1024]{1,0:T(8,128)(2,1)S(1)} %pad_maximum_fusion.1), channel_id=1, source_target_pairs={{0,48},{4,52},{8,56},{12,60},{16,0},{20,4},{24,8},{28,12},{32,16},... | collective-permute-start | bytes 1572872 | tf_op jit(solution)/shard_map/ppermute | solution.py:30
  29.9 15.7 %collective-permute-start.2 = (bf16[256,1024]{1,0:T(8,128)(2,1)S(1)}, bf16[256,1024]{1,0:T(8,128)(2,1)S(1)}, u32[]{:S(2)}, u32[]{:S(2)}) collective-permute-start(bf16[256,1024]{1,0:T(8,128)(2,1)S(1)} %pad_maximum_fusion.1), channel_id=1, source_target_pairs={{0,16},{4,20},{8,24},{12,28},{16,32},{20,36},{24,40},{28,44},{32,4... | collective-permute-start | bytes 1572872 | tf_op jit(solution)/shard_map/ppermute | solution.py:30
  42.0 14.7 %collective-permute-start.4 = (bf16[256,1024]{1,0:T(8,128)(2,1)S(1)}, bf16[256,1024]{1,0:T(8,128)(2,1)S(1)}, u32[]{:S(2)}, u32[]{:S(2)}) collective-permute-start(bf16[256,1024]{1,0:T(8,128)(2,1)S(1)} %collective-permute-done.3), channel_id=1, source_target_pairs={{0,48},{4,52},{8,56},{12,60},{16,0},{20,4},{24,8},{28,12},{32,16},... | collective-permute-start | bytes 1572872 | tf_op jit(solution)/shard_map/ppermute | solution.py:30
  57.5 27.5 %collective-permute-start.5 = (bf16[1024,1024]{1,0:T(8,128)(2,1)}, bf16[1024,1024]{1,0:T(8,128)(2,1)}, u32[]{:S(2)}, u32[]{:S(2)}) collective-permute-start(bf16[1024,1024]{1,0:T(8,128)(2,1)} %constant_dynamic-update-slice_fusion), channel_id=1, source_target_pairs={{0,12},{4,0},{8,4},{12,8},{16,28},{20,16},{24,20},{28,24},{32,44},... | collective-permute-start | bytes 6291464 | tf_op jit(solution)/shard_map/ppermute | solution.py:30
  60.5 36.6 %collective-permute-start.17 = (bf16[1024,1024]{1,0:T(8,128)(2,1)}, bf16[1024,1024]{1,0:T(8,128)(2,1)S(1)}, u32[]{:S(2)}, u32[]{:S(2)}) collective-permute-start(bf16[1024,1024]{1,0:T(8,128)(2,1)} %constant_dynamic-update-slice_fusion), channel_id=1, source_target_pairs={{0,4},{4,8},{8,12},{12,0},{16,20},{20,24},{24,28},{28,16},{32,36},... | collective-permute-start | bytes 6291464 | tf_op jit(solution)/shard_map/ppermute | solution.py:30
  65.3 23.4 %collective-permute-start.15 = (bf16[1024,512]{1,0:T(8,128)(2,1)S(1)}, bf16[1024,512]{1,0:T(8,128)(2,1)S(1)}, u32[]{:S(2)}, u32[]{:S(2)}) collective-permute-start(bf16[1024,512]{1,0:T(8,128)(2,1)S(1)} %get-tuple-element.54), channel_id=1, source_target_pairs={{0,131},{128,0},{1,128},{129,1},{2,129},{130,2},{3,130},{131,3},{4... | collective-permute-start | bytes 3145736 | tf_op jit(solution)/shard_map/ppermute | solution.py:35
  70.0 21.8 %collective-permute-start.14 = (bf16[1024,512]{1,0:T(8,128)(2,1)S(1)}, bf16[1024,512]{1,0:T(8,128)(2,1)S(1)}, u32[]{:S(2)}, u32[]{:S(2)}) collective-permute-start(bf16[1024,512]{1,0:T(8,128)(2,1)S(1)} %get-tuple-element.55), channel_id=1, source_target_pairs={{0,128},{128,1},{1,129},{129,2},{2,130},{130,3},{3,131},{131,0},{4... | collective-permute-start | bytes 3145736 | tf_op jit(solution)/shard_map/ppermute | solution.py:35
  92.0 8.8 %collective-permute-start.16 = (bf16[2048,512]{1,0:T(8,128)(2,1)S(1)}, bf16[2048,512]{1,0:T(8,128)(2,1)S(1)}, u32[]{:S(2)}, u32[]{:S(2)}) collective-permute-start(bf16[2048,512]{1,0:T(8,128)(2,1)S(1)} %constant_dynamic-update-slice_fusion.10.first), channel_id=1, source_target_pairs={{0,64},{64,0},{1,65},{65,1},{2,66},{66,2},{3,67},{67,3},{4,68},{68... | collective-permute-start | bytes 6291464 | tf_op jit(solution)/shard_map/ppermute | solution.py:39
  97.1 26.6 %collective-permute-start.18 = (bf16[1024,1024]{1,0:T(8,128)(2,1)}, bf16[1024,1024]{1,0:T(8,128)(2,1)S(1)}, u32[]{:S(2)}, u32[]{:S(2)}) collective-permute-start(bf16[1024,1024]{1,0:T(8,128)(2,1)} %collective-permute-done.10), channel_id=1, source_target_pairs={{0,4},{4,8},{8,12},{12,0},{16,20},{20,24},{24,28},{28,16},{32,36},... | collective-permute-start | bytes 6291464 | tf_op jit(solution)/shard_map/ppermute | solution.py:30
  97.1 31.1 %collective-permute-start.13 = (bf16[1024,1024]{1,0:T(8,128)(2,1)}, bf16[1024,1024]{1,0:T(8,128)(2,1)S(1)}, u32[]{:S(2)}, u32[]{:S(2)}) collective-permute-start(bf16[1024,1024]{1,0:T(8,128)(2,1)} %collective-permute-done.5), channel_id=1, source_target_pairs={{0,12},{4,0},{8,4},{12,8},{16,28},{20,16},{24,20},{28,24},{32,44},... | collective-permute-start | bytes 6291464 | tf_op jit(solution)/shard_map/ppermute | solution.py:30
  129.4 13.1 %copy-start.3 = (f32[1024]{0:T(1024)S(1)}, f32[1024]{0:T(1024)}, u32[]{:S(2)}) copy-start(f32[1024]{0:T(1024)} %param.12) | copy-start | bytes 12292
  142.5 10.8 %copy-start.2 = (f32[1024]{0:T(1024)}, f32[1024]{0:T(1024)S(1)}, u32[]{:S(2)}) copy-start(f32[1024]{0:T(1024)S(1)} %get-tuple-element.48) | copy-start | bytes 12292
  143.2 13.2 %all-to-all-start.1 = ((f32[16,1,640]{2,1,0:T(1,128)}), f32[16,1,640]{2,1,0:T(1,128)S(1)}, u32[]{:S(2)}, u32[]{:S(2)}) async-start(f32[16,1,640]{2,1,0:T(1,128)} %broadcast_in_dim.5), calls=%async_computation.1 | async-start | bytes 81920 | tf_op jit(solution)/shard_map/all_to_all | solution.py:93
  148.9 8.8 %copy-start.4 = (f32[512]{0:T(512)S(1)}, f32[512]{0:T(512)}, u32[]{:S(2)}) copy-start(f32[512]{0:T(512)} %param.13) | copy-start | bytes 6148
  148.9 9.3 %copy-start.1 = (bf16[1024,512]{1,0:T(8,128)(2,1)S(1)}, bf16[1024,512]{1,0:T(8,128)(2,1)}, u32[]{:S(2)}) copy-start(bf16[1024,512]{1,0:T(8,128)(2,1)} %param.10) | copy-start | bytes 3145732

commit v11 on v9

--- a/solution.py
+++ b/solution.py
@@ -120,7 +120,7 @@
     near[3:] = after(near[3:], away)
     (sent,) = after((activations,), *near)
     near = ring_start(jnp.concatenate(near, axis=0), 1)
-    away = ring_end(ring_start(away, 0), 0, -1)
+    away = ring_end(ring_start(away, 0), 0, 1)
     half = sent.shape[0] // 2
     acts_low = (along_z(sent[:half], 1), along_z(sent[half:], -1))
     first = arranged(places, activations, acts_core)
@@ -133,8 +133,10 @@
     second = arranged(places, acts_low, swap(acts_low, "core"))
     gradient = gradient + product(near[3], first[3])
     gradient = gradient + product(away[0], second[0]) + product(away[2], second[2])
-    last = lax.optimization_barrier((product(away[1], second[1]), product(away[3], second[3])))
-    gradient = gradient + (last[0] + last[1])
+    away[3], gradient = lax.optimization_barrier((away[3], gradient))
+    gradient = gradient + product(away[3], second[3])
+    away[1], gradient = lax.optimization_barrier((away[1], gradient))
+    gradient = gradient + lax.optimization_barrier(product(away[1], second[1]))
     gradient = gradient * token_scale
 
     squares = gradient * gradient + 1e-30

time: 153 us -> 150 us (0.980)
  starting transfers between devices: 42.7 us -> 39.7 us
    ppermute x12, starting transfers between devices: 18.5 us -> 13.8 us  [shift(): return lax.ppermute(array, AXES, ring_pairs(phase, step))]
    dynamic_slice x0 -> x1, local copies, waits for them, and re-layouts: none -> 2.05 us  [units(): lax.dynamic_slice_in_dim(out_grads, ((low ^ a) * 2 + (core ^ b)) * rows,...]
    unnamed x18 -> x17, local copies, waits for them, and re-layouts: 6.9 us -> 4.85 us
  transfers between devices with their start and end apart: 20 -> 20, of which waited for: 11 -> 12; matrix products, arithmetic and copies ran while one was open for 17% -> 20% of each run, Pallas kernels for 7% -> 7%
where the time goes in v11:
time: 150 us
  waiting for transfers between devices  47.7 us (32%)
  starting transfers between devices  39.7 us (26%)
  matrix products  18.4 us (12%)
  Pallas kernels  10.9 us (7%)
  other arithmetic  10.8 us (7%)
  blocking collectives  10.5 us (7%)
  local copies, waits for them, and re-layouts  10.3 us (7%)
  between operations  1.53 us (1%)
    ppermute x12, waiting for transfers between devices, shift(): return lax.ppermute(array, AXES, ring_pairs(phase, step))  38.8 us
    dot_general x8, matrix products, product(): lax.dot_general(grad_rows, act_rows, (((0,), (0,)), ((), ())), preferred_...  18.4 us
    ppermute x12, starting transfers between devices, shift(): return lax.ppermute(array, AXES, ring_pairs(phase, step))  13.8 us
    all_to_all x1, starting transfers between devices, total_over(): return jnp.sum(lax.all_to_all(spread, axes, 0, 0, tiled=True), axis=0)  11.7 us
    pallas_call x2, Pallas kernels, arranged(): pl.pallas_call(arrange_kernel, in_specs=[pl.BlockSpec(memory_space=pltpu....  10.9 us
    all_to_all x1, blocking collectives, total_over(): return jnp.sum(lax.all_to_all(spread, axes, 0, 0, tiled=True), axis=0)  10.5 us
    ppermute x5, starting transfers between devices, swap(): return lax.ppermute(array, axis, [(0, 1), (1, 0)])  7.83 us
    ppermute x2, starting transfers between devices, along_z(): lax.ppermute(array, ('zl', 'zh'), [(place(z), place((z + step) % 8)) for...  6.34 us
  transfers between devices with their start and end apart: 20, of which 12 were waited for; matrix products, arithmetic and copies ran while one was open for 20% of the time, Pallas kernels for 7%

profile of v11, /device:TPU:1, one launch (start us, length us, event | category | flops | bytes accessed | tf_op | source)
XLA Modules:
  0.0 149.8 jit_solution(18043954076894364079)
XLA Ops:
  0.7 2.1 %constant_dynamic-slice_fusion = (bf16[128,1024]{1,0:T(8,128)(2,1)S(1)}, bf16[128,1024]{1,0:T(8,128)(2,1)S(1)}, bf16[128,1024]{1,0:T(8,128)(2,1)S(1)}, bf16[1024,1024]{1,0:T(8,128)(2,1)}, bf16[128,1024]{1,0:T(8,128)(2,1)S(1)}) fusion(bf16[128,4096]{1,0:T(8,128)(2,1)} %param.8, s32[]{:T(128)S(6)} %select_n.203, s32[]{:T(128)S(6)} %select_n.201, ...), kind=kLoop, calls=%fused_computation.44 | loop fusion | bytes 2359312 | tf_op jit(solution)/shard_map/dynamic_slice | solution.py:103
  2.8 2.6 %collective-permute-start = (bf16[256,1024]{1,0:T(8,128)(2,1)S(1)}, bf16[256,1024]{1,0:T(8,128)(2,1)S(1)}, u32[]{:S(2)}, u32[]{:S(2)}) collective-permute-start(bf16[256,1024]{1,0:T(8,128)(2,1)S(1)} %pad_maximum_fusion), channel_id=1, source_target_pairs={{0,128},{128,0},{1,129},{129,1},{2,130},{130,2},{3,131},{131,3},{4... | collective-permute-start | bytes 1572872 | tf_op jit(solution)/shard_map/ppermute | solution.py:39
  5.3 1.0 collective-permute-start.7
  6.3 1.2 collective-permute-done.7
  7.5 1.4 collective-permute-start.8
  8.8 1.5 %collective-permute-start.9 = (bf16[256,1024]{1,0:T(8,128)(2,1)S(1)}, bf16[256,1024]{1,0:T(8,128)(2,1)S(1)}, u32[]{:S(2)}, u32[]{:S(2)}) collective-permute-start(bf16[256,1024]{1,0:T(8,128)(2,1)S(1)} %pad_maximum_fusion.2), channel_id=1, source_target_pairs={{0,48},{4,52},{8,56},{12,60},{16,0},{20,4},{24,8},{28,12},{32,16},... | collective-permute-start | bytes 1572872 | tf_op jit(solution)/shard_map/ppermute | solution.py:30
  10.4 1.6 %collective-permute-start.10 = (bf16[256,1024]{1,0:T(8,128)(2,1)S(1)}, bf16[256,1024]{1,0:T(8,128)(2,1)S(1)}, u32[]{:S(2)}, u32[]{:S(2)}) collective-permute-start(bf16[256,1024]{1,0:T(8,128)(2,1)S(1)} %pad_maximum_fusion.2), channel_id=1, source_target_pairs={{0,32},{4,36},{8,40},{12,44},{16,48},{20,52},{24,56},{28,60},{32,0... | collective-permute-start | bytes 1572872 | tf_op jit(solution)/shard_map/ppermute | solution.py:30
  11.9 4.0 %collective-permute-done = bf16[256,1024]{1,0:T(8,128)(2,1)S(1)} collective-permute-done((bf16[256,1024]{1,0:T(8,128)(2,1)S(1)}, bf16[256,1024]{1,0:T(8,128)(2,1)S(1)}, u32[]{:S(2)}, u32[]{:S(2)}) %collective-permute-start) | collective-permute-done | bytes 524320 | tf_op jit(solution)/shard_map/ppermute | solution.py:39
  15.9 0.8 fusion.21
  16.7 2.3 %collective-permute-start.1 = (bf16[128,1024]{1,0:T(8,128)(2,1)S(1)}, bf16[128,1024]{1,0:T(8,128)(2,1)S(1)}, u32[]{:S(2)}, u32[]{:S(2)}) collective-permute-start(bf16[128,1024]{1,0:T(8,128)(2,1)S(1)} %get-tuple-element.59), channel_id=1, source_target_pairs={{0,64},{64,0},{1,65},{65,1},{2,66},{66,2},{3,67},{67,3},{4,68},{68... | collective-permute-start | bytes 786440 | tf_op jit(solution)/shard_map/ppermute | solution.py:39
  19.7 0.7 collective-permute-done.1
  20.5 1.4 collective-permute-start.2
  21.9 0.8 constant_dynamic-update-slice_fusion.7
  22.7 1.2 collective-permute-done.10
  23.9 0.8 constant_dynamic-update-slice_fusion.6
  24.8 0.8 constant_dynamic-update-slice_fusion.5
  25.6 0.9 collective-permute-start.12
  26.5 1.8 %collective-permute-start.13 = (bf16[1024,1024]{1,0:T(8,128)(2,1)}, bf16[1024,1024]{1,0:T(8,128)(2,1)}, u32[]{:S(2)}, u32[]{:S(2)}) collective-permute-start(bf16[1024,1024]{1,0:T(8,128)(2,1)} %constant_dynamic-update-slice_fusion.5), channel_id=1, source_target_pairs={{0,12},{4,0},{8,4},{12,8},{16,28},{20,16},{24,20},{28,24},{32,44},... | collective-permute-start | bytes 6291464 | tf_op jit(solution)/shard_map/ppermute | solution.py:30
  28.3 1.6 %collective-permute-start.3 = (bf16[256,1024]{1,0:T(8,128)(2,1)S(1)}, bf16[256,1024]{1,0:T(8,128)(2,1)S(1)}, u32[]{:S(2)}, u32[]{:S(2)}) collective-permute-start(bf16[256,1024]{1,0:T(8,128)(2,1)S(1)} %pad_maximum_fusion.1), channel_id=1, source_target_pairs={{0,48},{4,52},{8,56},{12,60},{16,0},{20,4},{24,8},{28,12},{32,16},... | collective-permute-start | bytes 1572872 | tf_op jit(solution)/shard_map/ppermute | solution.py:30
  30.9 0.8 constant_dynamic-update-slice_fusion.2
  31.7 10.1 %collective-permute-done.3 = bf16[256,1024]{1,0:T(8,128)(2,1)S(1)} collective-permute-done((bf16[256,1024]{1,0:T(8,128)(2,1)S(1)}, bf16[256,1024]{1,0:T(8,128)(2,1)S(1)}, u32[]{:S(2)}, u32[]{:S(2)}) %collective-permute-start.3) | collective-permute-done | bytes 524320 | tf_op jit(solution)/shard_map/ppermute | solution.py:30
  41.8 0.8 constant_dynamic-update-slice_fusion.1
  42.7 2.8 %collective-permute-done.4 = bf16[256,1024]{1,0:T(8,128)(2,1)S(1)} collective-permute-done((bf16[256,1024]{1,0:T(8,128)(2,1)S(1)}, bf16[256,1024]{1,0:T(8,128)(2,1)S(1)}, u32[]{:S(2)}, u32[]{:S(2)}) %collective-permute-start.4) | collective-permute-done | bytes 524320 | tf_op jit(solution)/shard_map/ppermute | solution.py:30
  45.5 0.8 constant_dynamic-update-slice_fusion
  46.3 2.2 %collective-permute-start.6 = (bf16[1024,1024]{1,0:T(8,128)(2,1)}, bf16[1024,1024]{1,0:T(8,128)(2,1)}, u32[]{:S(2)}, u32[]{:S(2)}) collective-permute-start(bf16[1024,1024]{1,0:T(8,128)(2,1)} %constant_dynamic-update-slice_fusion), channel_id=1, source_target_pairs={{0,12},{4,0},{8,4},{12,8},{16,28},{20,16},{24,20},{28,24},{32,44},... | collective-permute-start | bytes 6291464 | tf_op jit(solution)/shard_map/ppermute | solution.py:30
  48.7 1.8 %collective-permute-start.16 = (bf16[1024,512]{1,0:T(8,128)(2,1)S(1)}, bf16[1024,512]{1,0:T(8,128)(2,1)S(1)}, u32[]{:S(2)}, u32[]{:S(2)}) collective-permute-start(bf16[1024,512]{1,0:T(8,128)(2,1)S(1)} %get-tuple-element.51), channel_id=1, source_target_pairs={{0,128},{128,1},{1,129},{129,2},{2,130},{130,3},{3,131},{131,0},{4... | collective-permute-start | bytes 3145736 | tf_op jit(solution)/shard_map/ppermute | solution.py:35
  50.5 4.6 %collective-permute-start.17 = (bf16[1024,512]{1,0:T(8,128)(2,1)S(1)}, bf16[1024,512]{1,0:T(8,128)(2,1)S(1)}, u32[]{:S(2)}, u32[]{:S(2)}) collective-permute-start(bf16[1024,512]{1,0:T(8,128)(2,1)S(1)} %get-tuple-element.50), channel_id=1, source_target_pairs={{0,131},{128,0},{1,128},{129,1},{2,129},{130,2},{3,130},{131,3},{4... | collective-permute-start | bytes 3145736 | tf_op jit(solution)/shard_map/ppermute | solution.py:35
  55.1 4.5 %shard_map.110 = bf16[4096,512]{1,0:T(8,128)(2,1)S(1)} custom-call(s32[16]{0:T(128)S(1)} %stack.67.place, bf16[2048,512]{1,0:T(8,128)(2,1)S(1)} %copy-done, bf16[2048,512]{1,0:T(8,128)(2,1)} %collective-permute-done.11.second), custom_call_target="tpu_custom_call" | custom-call | bytes 8388608 | tf_op jit(solution)/shard_map/pallas_call | solution.py:77
  59.6 2.9 %fusion.17 = f32[1024,512]{1,0:T(8,128)S(1)} fusion(bf16[1024,1024]{1,0:T(8,128)(2,1)} %constant_dynamic-update-slice_fusion.5, bf16[4096,512]{1,0:T(8,128)(2,1)S(1)} %shard_map.110), kind=kOutput, calls=%fused_computation.22 | convolution fusion | flops 1073741824 | bytes 5242880 | tf_op jit(solution)/shard_map/dot_general | solution.py:55
  62.6 2.9 %fusion.15 = f32[1024,512]{1,0:T(8,128)S(1)} fusion(bf16[1024,1024]{1,0:T(8,128)(2,1)} %collective-permute-done.12, bf16[4096,512]{1,0:T(8,128)(2,1)S(1)} %shard_map.110), kind=kOutput, calls=%fused_computation.20 | convolution fusion | flops 1073741824 | bytes 5242880 | tf_op jit(solution)/shard_map/dot_general | solution.py:55
  65.5 2.9 %add_add_fusion.1 = f32[1024,512]{1,0:T(8,128)S(1)} fusion(f32[1024,512]{1,0:T(8,128)S(1)} %fusion.17, f32[1024,512]{1,0:T(8,128)S(1)} %fusion.15, bf16[1024,1024]{1,0:T(8,128)(2,1)} %collective-permute-done.13, bf16[4096,512]{1,0:T(8,128)(2,1)S(1)} %shard_map.110), kind=kOutput, calls=%fused_computation.6 | convolution fusion | flops 1074790400 | bytes 9437184 | tf_op jit(solution)/shard_map/dot_general | solution.py:55
  68.4 11.7 %collective-permute-done.6 = bf16[1024,1024]{1,0:T(8,128)(2,1)} collective-permute-done((bf16[1024,1024]{1,0:T(8,128)(2,1)}, bf16[1024,1024]{1,0:T(8,128)(2,1)}, u32[]{:S(2)}, u32[]{:S(2)}) %collective-permute-start.6) | collective-permute-done | bytes 2097184 | tf_op jit(solution)/shard_map/ppermute | solution.py:30
  80.3 2.0 %collective-permute-start.18 = (bf16[2048,512]{1,0:T(8,128)(2,1)S(1)}, bf16[2048,512]{1,0:T(8,128)(2,1)S(1)}, u32[]{:S(2)}, u32[]{:S(2)}) collective-permute-start(bf16[2048,512]{1,0:T(8,128)(2,1)S(1)} %constant_dynamic-update-slice_fusion.10.first), channel_id=1, source_target_pairs={{0,64},{64,0},{1,65},{65,1},{2,66},{66,2},{3,67},{67,3},{4,68},{68... | collective-permute-start | bytes 6291464 | tf_op jit(solution)/shard_map/ppermute | solution.py:39
  82.3 1.1 collective-permute-start.14
  83.8 5.5 %collective-permute-done.15 = bf16[1024,1024]{1,0:T(8,128)(2,1)S(1)} collective-permute-done((bf16[1024,1024]{1,0:T(8,128)(2,1)}, bf16[1024,1024]{1,0:T(8,128)(2,1)S(1)}, u32[]{:S(2)}, u32[]{:S(2)}) %collective-permute-start.15) | collective-permute-done | bytes 2097184 | tf_op jit(solution)/shard_map/ppermute | solution.py:30
  89.2 1.3 fusion.9
  90.5 6.3 %shard_map.111 = bf16[4096,512]{1,0:T(8,128)(2,1)S(1)} custom-call(s32[16]{0:T(128)S(1)} %stack.67.place, bf16[2048,512]{1,0:T(8,128)(2,1)S(1)} %constant_dynamic-update-slice_fusion.10.first, bf16[2048,512]{1,0:T(8,128)(2,1)S(1)} %collective-permute-done.18.second), custom_call_target="tpu_custom_call" | custom-call | bytes 8388608 | tf_op jit(solution)/shard_map/pallas_call | solution.py:77
  96.9 2.9 %fusion.6 = f32[1024,512]{1,0:T(8,128)S(1)} fusion(bf16[1024,1024]{1,0:T(8,128)(2,1)} %collective-permute-done.6, bf16[4096,512]{1,0:T(8,128)(2,1)S(1)} %shard_map.111), kind=kOutput, calls=%fused_computation.13 | convolution fusion | flops 1073741824 | bytes 5242880 | tf_op jit(solution)/shard_map/dot_general | solution.py:55
  99.7 3.0 %add_add_fusion = f32[1024,512]{1,0:T(8,128)S(1)} fusion(f32[1024,512]{1,0:T(8,128)S(1)} %fusion.6, f32[1024,512]{1,0:T(8,128)S(1)} %add_add_fusion.1, f32[1024,512]{1,0:T(8,128)S(1)} %fusion.9, bf16[1024,1024]{1,0:T(8,128)(2,1)} %constant_dynamic-update-slice_fusion, bf16[4096,512]{1,0:T(8,128)(2,1)S(1)} %shard_map.111), kind=kOutput, calls=%fused_computation.5 | convolution fusion | flops 1075314688 | bytes 11534336 | tf_op jit(solution)/shard_map/dot_general | solution.py:55
  102.8 4.9 %collective-permute-done.14 = bf16[1024,1024]{1,0:T(8,128)(2,1)S(1)} collective-permute-done((bf16[1024,1024]{1,0:T(8,128)(2,1)}, bf16[1024,1024]{1,0:T(8,128)(2,1)S(1)}, u32[]{:S(2)}, u32[]{:S(2)}) %collective-permute-start.14) | collective-permute-done | bytes 2097184 | tf_op jit(solution)/shard_map/ppermute | solution.py:30
  107.7 1.3 fusion.4
  109.4 2.2 %collective-permute-done.5 = bf16[1024,1024]{1,0:T(8,128)(2,1)S(1)} collective-permute-done((bf16[1024,1024]{1,0:T(8,128)(2,1)}, bf16[1024,1024]{1,0:T(8,128)(2,1)S(1)}, u32[]{:S(2)}, u32[]{:S(2)}) %collective-permute-start.5) | collective-permute-done | bytes 2097184 | tf_op jit(solution)/shard_map/ppermute | solution.py:30
  111.7 1.3 fusion.2
  113.6 10.5 %all_to_all.12 = f32[16,1,1024]{2,1,0:T(1,128)S(1)} all-to-all(f32[16,1,1024]{2,1,0:T(1,128)S(1)} %broadcast_in_dim.4), channel_id=1, replica_groups=mesh['zl'=2,'core'=2,'x'=4,'y'=4,'zh'=4] {'x','y'}, dimensions={0} | all-to-all | bytes 131072 | tf_op jit(solution)/shard_map/all_to_all | solution.py:93
  124.8 11.7 %all-to-all-start.1 = ((f32[16,1,640]{2,1,0:T(1,128)}), f32[16,1,640]{2,1,0:T(1,128)S(1)}, u32[]{:S(2)}, u32[]{:S(2)}) async-start(f32[16,1,640]{2,1,0:T(1,128)} %broadcast_in_dim.5), calls=%async_computation.1 | async-start | bytes 81920 | tf_op jit(solution)/shard_map/all_to_all | solution.py:93
  136.5 4.4 %multiply_subtract_fusion.1 = f32[1024,512]{1,0:T(8,128)} fusion(f32[1024,512]{1,0:T(8,128)} %param.11, f32[1024,512]{1,0:T(8,128)S(1)} %get-tuple-element.36, f32[1024,512]{1,0:T(8,128)} %param.9), kind=kLoop, calls=%fused_computation.2 | loop fusion | flops 1572864 | bytes 8388608 | tf_op jit(solution)/shard_map/sub | solution.py:145
  140.9 3.1 %all-to-all-done.1 = f32[16,1,640]{2,1,0:T(1,128)S(1)} async-done(((f32[16,1,640]{2,1,0:T(1,128)}), f32[16,1,640]{2,1,0:T(1,128)S(1)}, u32[]{:S(2)}, u32[]{:S(2)}) %all-to-all-start.1) | async-done | bytes 40992 | tf_op jit(solution)/shard_map/all_to_all | solution.py:93
  145.9 3.9 %multiply_subtract_fusion = (f32[1024,512]{1,0:T(8,128)}, bf16[1024,512]{1,0:T(8,128)(2,1)}) fusion(f32[1024,512]{1,0:T(8,128)} %param.9, f32[1024,512]{1,0:T(8,128)S(1)} %get-tuple-element.36, f32[512]{0:T(512)S(1)} %get-tuple-element.45, f32[1024]{0:T(1024)S(1)} %get-tuple-element.43, bf16[1024,512]{1,0:T(8,128)(2,1)S(1)} %copy-done.1), kind=kLoop, calls=%fused_computation | loop fusion | flops 5242880 | bytes 8394752 | tf_op jit(solution)/shard_map/sub | solution.py:158
  (43 shorter events, 5.8 us)
Async XLA Ops:
  2.7 16.3 %copy-start = (bf16[2048,512]{1,0:T(8,128)(2,1)S(1)}, bf16[2048,512]{1,0:T(8,128)(2,1)}, u32[]{:S(2)}) copy-start(bf16[2048,512]{1,0:T(8,128)(2,1)} %first.1) | copy-start | bytes 6291460
  2.8 13.1 %collective-permute-start = (bf16[256,1024]{1,0:T(8,128)(2,1)S(1)}, bf16[256,1024]{1,0:T(8,128)(2,1)S(1)}, u32[]{:S(2)}, u32[]{:S(2)}) collective-permute-start(bf16[256,1024]{1,0:T(8,128)(2,1)S(1)} %pad_maximum_fusion), channel_id=1, source_target_pairs={{0,128},{128,0},{1,129},{129,1},{2,130},{130,2},{3,131},{131,3},{4... | collective-permute-start | bytes 1572872 | tf_op jit(solution)/shard_map/ppermute | solution.py:39
  5.3 2.1 %collective-permute-start.7 = (bf16[128,1024]{1,0:T(8,128)(2,1)S(1)}, bf16[128,1024]{1,0:T(8,128)(2,1)S(1)}, u32[]{:S(2)}, u32[]{:S(2)}) collective-permute-start(bf16[128,1024]{1,0:T(8,128)(2,1)S(1)} %get-tuple-element.52), channel_id=1, source_target_pairs={{0,64},{64,0},{1,65},{65,1},{2,66},{66,2},{3,67},{67,3},{4,68},{68... | collective-permute-start | bytes 786440 | tf_op jit(solution)/shard_map/ppermute | solution.py:39
  7.5 14.4 %collective-permute-start.8 = (bf16[256,1024]{1,0:T(8,128)(2,1)S(1)}, bf16[256,1024]{1,0:T(8,128)(2,1)S(1)}, u32[]{:S(2)}, u32[]{:S(2)}) collective-permute-start(bf16[256,1024]{1,0:T(8,128)(2,1)S(1)} %pad_maximum_fusion.2), channel_id=1, source_target_pairs={{0,16},{4,20},{8,24},{12,28},{16,32},{20,36},{24,40},{28,44},{32,4... | collective-permute-start | bytes 1572872 | tf_op jit(solution)/shard_map/ppermute | solution.py:30
  8.8 15.1 %collective-permute-start.9 = (bf16[256,1024]{1,0:T(8,128)(2,1)S(1)}, bf16[256,1024]{1,0:T(8,128)(2,1)S(1)}, u32[]{:S(2)}, u32[]{:S(2)}) collective-permute-start(bf16[256,1024]{1,0:T(8,128)(2,1)S(1)} %pad_maximum_fusion.2), channel_id=1, source_target_pairs={{0,48},{4,52},{8,56},{12,60},{16,0},{20,4},{24,8},{28,12},{32,16},... | collective-permute-start | bytes 1572872 | tf_op jit(solution)/shard_map/ppermute | solution.py:30
  10.4 13.6 %collective-permute-start.10 = (bf16[256,1024]{1,0:T(8,128)(2,1)S(1)}, bf16[256,1024]{1,0:T(8,128)(2,1)S(1)}, u32[]{:S(2)}, u32[]{:S(2)}) collective-permute-start(bf16[256,1024]{1,0:T(8,128)(2,1)S(1)} %pad_maximum_fusion.2), channel_id=1, source_target_pairs={{0,32},{4,36},{8,40},{12,44},{16,48},{20,52},{24,56},{28,60},{32,0... | collective-permute-start | bytes 1572872 | tf_op jit(solution)/shard_map/ppermute | solution.py:30
  16.7 3.8 %collective-permute-start.1 = (bf16[128,1024]{1,0:T(8,128)(2,1)S(1)}, bf16[128,1024]{1,0:T(8,128)(2,1)S(1)}, u32[]{:S(2)}, u32[]{:S(2)}) collective-permute-start(bf16[128,1024]{1,0:T(8,128)(2,1)S(1)} %get-tuple-element.59), channel_id=1, source_target_pairs={{0,64},{64,0},{1,65},{65,1},{2,66},{66,2},{3,67},{67,3},{4,68},{68... | collective-permute-start | bytes 786440 | tf_op jit(solution)/shard_map/ppermute | solution.py:39
  19.0 31.5 %collective-permute-start.11 = (bf16[2048,512]{1,0:T(8,128)(2,1)S(1)}, bf16[2048,512]{1,0:T(8,128)(2,1)}, u32[]{:S(2)}, u32[]{:S(2)}) collective-permute-start(bf16[2048,512]{1,0:T(8,128)(2,1)S(1)} %copy-done), channel_id=1, source_target_pairs={{0,64},{64,0},{1,65},{65,1},{2,66},{66,2},{3,67},{67,3},{4,68},{68... | collective-permute-start | bytes 6291464 | tf_op jit(solution)/shard_map/ppermute | solution.py:39
  20.5 9.7 %collective-permute-start.2 = (bf16[256,1024]{1,0:T(8,128)(2,1)S(1)}, bf16[256,1024]{1,0:T(8,128)(2,1)S(1)}, u32[]{:S(2)}, u32[]{:S(2)}) collective-permute-start(bf16[256,1024]{1,0:T(8,128)(2,1)S(1)} %pad_maximum_fusion.1), channel_id=1, source_target_pairs={{0,16},{4,20},{8,24},{12,28},{16,32},{20,36},{24,40},{28,44},{32,4... | collective-permute-start | bytes 1572872 | tf_op jit(solution)/shard_map/ppermute | solution.py:30
  25.6 36.9 %collective-permute-start.12 = (bf16[1024,1024]{1,0:T(8,128)(2,1)}, bf16[1024,1024]{1,0:T(8,128)(2,1)}, u32[]{:S(2)}, u32[]{:S(2)}) collective-permute-start(bf16[1024,1024]{1,0:T(8,128)(2,1)} %constant_dynamic-update-slice_fusion.5), channel_id=1, source_target_pairs={{0,4},{4,8},{8,12},{12,0},{16,20},{20,24},{24,28},{28,16},{32,36},... | collective-permute-start | bytes 6291464 | tf_op jit(solution)/shard_map/ppermute | solution.py:30
  26.5 36.0 %collective-permute-start.13 = (bf16[1024,1024]{1,0:T(8,128)(2,1)}, bf16[1024,1024]{1,0:T(8,128)(2,1)}, u32[]{:S(2)}, u32[]{:S(2)}) collective-permute-start(bf16[1024,1024]{1,0:T(8,128)(2,1)} %constant_dynamic-update-slice_fusion.5), channel_id=1, source_target_pairs={{0,12},{4,0},{8,4},{12,8},{16,28},{20,16},{24,20},{28,24},{32,44},... | collective-permute-start | bytes 6291464 | tf_op jit(solution)/shard_map/ppermute | solution.py:30
  28.3 13.6 %collective-permute-start.3 = (bf16[256,1024]{1,0:T(8,128)(2,1)S(1)}, bf16[256,1024]{1,0:T(8,128)(2,1)S(1)}, u32[]{:S(2)}, u32[]{:S(2)}) collective-permute-start(bf16[256,1024]{1,0:T(8,128)(2,1)S(1)} %pad_maximum_fusion.1), channel_id=1, source_target_pairs={{0,48},{4,52},{8,56},{12,60},{16,0},{20,4},{24,8},{28,12},{32,16},... | collective-permute-start | bytes 1572872 | tf_op jit(solution)/shard_map/ppermute | solution.py:30
  30.2 15.3 %collective-permute-start.4 = (bf16[256,1024]{1,0:T(8,128)(2,1)S(1)}, bf16[256,1024]{1,0:T(8,128)(2,1)S(1)}, u32[]{:S(2)}, u32[]{:S(2)}) collective-permute-start(bf16[256,1024]{1,0:T(8,128)(2,1)S(1)} %collective-permute-done.2), channel_id=1, source_target_pairs={{0,16},{4,20},{8,24},{12,28},{16,32},{20,36},{24,40},{28,44},{32,4... | collective-permute-start | bytes 1572872 | tf_op jit(solution)/shard_map/ppermute | solution.py:30
  46.3 33.8 %collective-permute-start.6 = (bf16[1024,1024]{1,0:T(8,128)(2,1)}, bf16[1024,1024]{1,0:T(8,128)(2,1)}, u32[]{:S(2)}, u32[]{:S(2)}) collective-permute-start(bf16[1024,1024]{1,0:T(8,128)(2,1)} %constant_dynamic-update-slice_fusion), channel_id=1, source_target_pairs={{0,12},{4,0},{8,4},{12,8},{16,28},{20,16},{24,20},{28,24},{32,44},... | collective-permute-start | bytes 6291464 | tf_op jit(solution)/shard_map/ppermute | solution.py:30
  48.7 31.4 %collective-permute-start.16 = (bf16[1024,512]{1,0:T(8,128)(2,1)S(1)}, bf16[1024,512]{1,0:T(8,128)(2,1)S(1)}, u32[]{:S(2)}, u32[]{:S(2)}) collective-permute-start(bf16[1024,512]{1,0:T(8,128)(2,1)S(1)} %get-tuple-element.51), channel_id=1, source_target_pairs={{0,128},{128,1},{1,129},{129,2},{2,130},{130,3},{3,131},{131,0},{4... | collective-permute-start | bytes 3145736 | tf_op jit(solution)/shard_map/ppermute | solution.py:35
  50.5 29.6 %collective-permute-start.17 = (bf16[1024,512]{1,0:T(8,128)(2,1)S(1)}, bf16[1024,512]{1,0:T(8,128)(2,1)S(1)}, u32[]{:S(2)}, u32[]{:S(2)}) collective-permute-start(bf16[1024,512]{1,0:T(8,128)(2,1)S(1)} %get-tuple-element.50), channel_id=1, source_target_pairs={{0,131},{128,0},{1,128},{129,1},{2,129},{130,2},{3,130},{131,3},{4... | collective-permute-start | bytes 3145736 | tf_op jit(solution)/shard_map/ppermute | solution.py:35
  62.5 26.7 %collective-permute-start.15 = (bf16[1024,1024]{1,0:T(8,128)(2,1)}, bf16[1024,1024]{1,0:T(8,128)(2,1)S(1)}, u32[]{:S(2)}, u32[]{:S(2)}) collective-permute-start(bf16[1024,1024]{1,0:T(8,128)(2,1)} %collective-permute-done.12), channel_id=1, source_target_pairs={{0,4},{4,8},{8,12},{12,0},{16,20},{20,24},{24,28},{28,16},{32,36},... | collective-permute-start | bytes 6291464 | tf_op jit(solution)/shard_map/ppermute | solution.py:30
  80.3 10.3 %collective-permute-start.18 = (bf16[2048,512]{1,0:T(8,128)(2,1)S(1)}, bf16[2048,512]{1,0:T(8,128)(2,1)S(1)}, u32[]{:S(2)}, u32[]{:S(2)}) collective-permute-start(bf16[2048,512]{1,0:T(8,128)(2,1)S(1)} %constant_dynamic-update-slice_fusion.10.first), channel_id=1, source_target_pairs={{0,64},{64,0},{1,65},{65,1},{2,66},{66,2},{3,67},{67,3},{4,68},{68... | collective-permute-start | bytes 6291464 | tf_op jit(solution)/shard_map/ppermute | solution.py:39
  82.3 25.4 %collective-permute-start.14 = (bf16[1024,1024]{1,0:T(8,128)(2,1)}, bf16[1024,1024]{1,0:T(8,128)(2,1)S(1)}, u32[]{:S(2)}, u32[]{:S(2)}) collective-permute-start(bf16[1024,1024]{1,0:T(8,128)(2,1)} %collective-permute-done.6), channel_id=1, source_target_pairs={{0,12},{4,0},{8,4},{12,8},{16,28},{20,16},{24,20},{28,24},{32,44},... | collective-permute-start | bytes 6291464 | tf_op jit(solution)/shard_map/ppermute | solution.py:30
  83.4 28.3 %collective-permute-start.5 = (bf16[1024,1024]{1,0:T(8,128)(2,1)}, bf16[1024,1024]{1,0:T(8,128)(2,1)S(1)}, u32[]{:S(2)}, u32[]{:S(2)}) collective-permute-start(bf16[1024,1024]{1,0:T(8,128)(2,1)} %constant_dynamic-update-slice_fusion), channel_id=1, source_target_pairs={{0,4},{4,8},{8,12},{12,0},{16,20},{20,24},{24,28},{28,16},{32,36},... | collective-permute-start | bytes 6291464 | tf_op jit(solution)/shard_map/ppermute | solution.py:30
  113.0 11.2 %copy-start.3 = (f32[1024]{0:T(1024)S(1)}, f32[1024]{0:T(1024)}, u32[]{:S(2)}) copy-start(f32[1024]{0:T(1024)} %param.12) | copy-start | bytes 12292
  124.1 16.8 %copy-start.2 = (f32[1024]{0:T(1024)}, f32[1024]{0:T(1024)S(1)}, u32[]{:S(2)}) copy-start(f32[1024]{0:T(1024)S(1)} %get-tuple-element.44) | copy-start | bytes 12292
  124.8 19.2 %all-to-all-start.1 = ((f32[16,1,640]{2,1,0:T(1,128)}), f32[16,1,640]{2,1,0:T(1,128)S(1)}, u32[]{:S(2)}, u32[]{:S(2)}) async-start(f32[16,1,640]{2,1,0:T(1,128)} %broadcast_in_dim.5), calls=%async_computation.1 | async-start | bytes 81920 | tf_op jit(solution)/shard_map/all_to_all | solution.py:93
  136.5 8.8 %copy-start.4 = (f32[512]{0:T(512)S(1)}, f32[512]{0:T(512)}, u32[]{:S(2)}) copy-start(f32[512]{0:T(512)} %param.13) | copy-start | bytes 6148
  136.5 9.4 %copy-start.1 = (bf16[1024,512]{1,0:T(8,128)(2,1)S(1)}, bf16[1024,512]{1,0:T(8,128)(2,1)}, u32[]{:S(2)}) copy-start(bf16[1024,512]{1,0:T(8,128)(2,1)} %param.10) | copy-start | bytes 3145732

commit v12 on v11

--- a/solution.py
+++ b/solution.py
@@ -121,9 +121,10 @@
     (sent,) = after((activations,), *near)
     near = ring_start(jnp.concatenate(near, axis=0), 1)
     away = ring_end(ring_start(away, 0), 0, 1)
+    first = arranged(places, activations, acts_core)
+    away[2], first = lax.optimization_barrier((away[2], first))
     half = sent.shape[0] // 2
     acts_low = (along_z(sent[:half], 1), along_z(sent[half:], -1))
-    first = arranged(places, activations, acts_core)
     gradient = product(near[0], first[0]) + product(near[1], first[1]) + product(near[2], first[2])
     near = ring_end(after(near, *away), 1, 1)
     away = ring_start(jnp.concatenate(away, axis=0), 1)

time: 150 us -> 151 us (level)
  waiting for transfers between devices: 47.7 us -> 52.3 us
  matrix products: 18.4 us -> 15.3 us
  starting transfers between devices: 39.7 us -> 37.1 us
  blocking collectives: 10.5 us -> 12.1 us
    ppermute x12, waiting for transfers between devices: 38.8 us -> 43.6 us  [shift(): return lax.ppermute(array, AXES, ring_pairs(phase, step))]
    dot_general x8, matrix products: 18.4 us -> 15.3 us  [product(): lax.dot_general(grad_rows, act_rows, (((0,), (0,)), ((), ())), preferred_...]
    all_to_all x1, starting transfers between devices: 11.7 us -> 9.96 us  [total_over(): return jnp.sum(lax.all_to_all(spread, axes, 0, 0, tiled=True), axis=0)]
    all_to_all x1, blocking collectives: 10.5 us -> 12.1 us  [total_over(): return jnp.sum(lax.all_to_all(spread, axes, 0, 0, tiled=True), axis=0)]
    unnamed x17 -> x19, local copies, waits for them, and re-layouts: 4.85 us -> 5.1 us
  transfers between devices with their start and end apart: 20 -> 20, of which waited for: 12 -> 12; matrix products, arithmetic and copies ran while one was open for 20% -> 18% of each run, Pallas kernels for 7% -> 7%
where the time goes in v12:
time: 151 us
  waiting for transfers between devices  52.3 us (35%)
  starting transfers between devices  37.1 us (25%)
  matrix products  15.3 us (10%)
  blocking collectives  12.1 us (8%)
  local copies, waits for them, and re-layouts  10.9 us (7%)
  Pallas kernels  10.9 us (7%)
  other arithmetic  10.8 us (7%)
  between operations  1.51 us (1%)
    ppermute x12, waiting for transfers between devices, shift(): return lax.ppermute(array, AXES, ring_pairs(phase, step))  43.6 us
    dot_general x8, matrix products, product(): lax.dot_general(grad_rows, act_rows, (((0,), (0,)), ((), ())), preferred_...  15.3 us
    ppermute x12, starting transfers between devices, shift(): return lax.ppermute(array, AXES, ring_pairs(phase, step))  14.3 us
    all_to_all x1, blocking collectives, total_over(): return jnp.sum(lax.all_to_all(spread, axes, 0, 0, tiled=True), axis=0)  12.1 us
    pallas_call x2, Pallas kernels, arranged(): pl.pallas_call(arrange_kernel, in_specs=[pl.BlockSpec(memory_space=pltpu....  10.9 us
    all_to_all x1, starting transfers between devices, total_over(): return jnp.sum(lax.all_to_all(spread, axes, 0, 0, tiled=True), axis=0)  9.96 us
    ppermute x5, starting transfers between devices, swap(): return lax.ppermute(array, axis, [(0, 1), (1, 0)])  7.79 us
    ppermute x5, waiting for transfers between devices, swap(): return lax.ppermute(array, axis, [(0, 1), (1, 0)])  5.59 us
  transfers between devices with their start and end apart: 20, of which 12 were waited for; matrix products, arithmetic and copies ran while one was open for 18% of the time, Pallas kernels for 7%

profile of v12, /device:TPU:1, one launch (start us, length us, event | category | flops | bytes accessed | tf_op | source)
XLA Modules:
  0.0 150.8 jit_solution(9045169359867356101)
XLA Ops:
  0.7 2.2 %constant_dynamic-slice_fusion = (bf16[128,1024]{1,0:T(8,128)(2,1)S(1)}, bf16[128,1024]{1,0:T(8,128)(2,1)S(1)}, bf16[128,1024]{1,0:T(8,128)(2,1)S(1)}, bf16[1024,1024]{1,0:T(8,128)(2,1)}, bf16[128,1024]{1,0:T(8,128)(2,1)S(1)}) fusion(bf16[128,4096]{1,0:T(8,128)(2,1)} %param.8, s32[]{:T(128)S(6)} %select_n.247, s32[]{:T(128)S(6)} %select_n.201, ...), kind=kLoop, calls=%fused_computation.48 | loop fusion | bytes 2359312 | tf_op jit(solution)/shard_map/dynamic_slice | solution.py:103
  2.9 2.6 %collective-permute-start = (bf16[256,1024]{1,0:T(8,128)(2,1)S(1)}, bf16[256,1024]{1,0:T(8,128)(2,1)S(1)}, u32[]{:S(2)}, u32[]{:S(2)}) collective-permute-start(bf16[256,1024]{1,0:T(8,128)(2,1)S(1)} %pad_maximum_fusion), channel_id=1, source_target_pairs={{0,128},{128,0},{1,129},{129,1},{2,130},{130,2},{3,131},{131,3},{4... | collective-permute-start | bytes 1572872 | tf_op jit(solution)/shard_map/ppermute | solution.py:39
  5.5 1.0 collective-permute-start.4
  6.4 4.0 %collective-permute-done.8 = bf16[128,1024]{1,0:T(8,128)(2,1)S(1)} collective-permute-done((bf16[128,1024]{1,0:T(8,128)(2,1)S(1)}, bf16[128,1024]{1,0:T(8,128)(2,1)S(1)}, u32[]{:S(2)}, u32[]{:S(2)}) %collective-permute-start.8) | collective-permute-done | bytes 262176 | tf_op jit(solution)/shard_map/ppermute | solution.py:39
  10.5 1.4 collective-permute-start.9
  11.9 1.5 %collective-permute-start.10 = (bf16[256,1024]{1,0:T(8,128)(2,1)S(1)}, bf16[256,1024]{1,0:T(8,128)(2,1)S(1)}, u32[]{:S(2)}, u32[]{:S(2)}) collective-permute-start(bf16[256,1024]{1,0:T(8,128)(2,1)S(1)} %pad_maximum_fusion.2), channel_id=1, source_target_pairs={{0,48},{4,52},{8,56},{12,60},{16,0},{20,4},{24,8},{28,12},{32,16},... | collective-permute-start | bytes 1572872 | tf_op jit(solution)/shard_map/ppermute | solution.py:30
  13.4 1.6 %collective-permute-start.11 = (bf16[256,1024]{1,0:T(8,128)(2,1)S(1)}, bf16[256,1024]{1,0:T(8,128)(2,1)S(1)}, u32[]{:S(2)}, u32[]{:S(2)}) collective-permute-start(bf16[256,1024]{1,0:T(8,128)(2,1)S(1)} %pad_maximum_fusion.2), channel_id=1, source_target_pairs={{0,32},{4,36},{8,40},{12,44},{16,48},{20,52},{24,56},{28,60},{32,0... | collective-permute-start | bytes 1572872 | tf_op jit(solution)/shard_map/ppermute | solution.py:30
  14.9 1.1 collective-permute-done
  16.0 0.8 fusion.25
  16.8 2.3 %collective-permute-start.1 = (bf16[128,1024]{1,0:T(8,128)(2,1)S(1)}, bf16[128,1024]{1,0:T(8,128)(2,1)S(1)}, u32[]{:S(2)}, u32[]{:S(2)}) collective-permute-start(bf16[128,1024]{1,0:T(8,128)(2,1)S(1)} %get-tuple-element.63), channel_id=1, source_target_pairs={{0,64},{64,0},{1,65},{65,1},{2,66},{66,2},{3,67},{67,3},{4,68},{68... | collective-permute-start | bytes 786440 | tf_op jit(solution)/shard_map/ppermute | solution.py:39
  20.3 1.4 collective-permute-start.2
  21.7 0.8 constant_dynamic-update-slice_fusion.7
  22.5 4.5 %collective-permute-done.11 = bf16[256,1024]{1,0:T(8,128)(2,1)S(1)} collective-permute-done((bf16[256,1024]{1,0:T(8,128)(2,1)S(1)}, bf16[256,1024]{1,0:T(8,128)(2,1)S(1)}, u32[]{:S(2)}, u32[]{:S(2)}) %collective-permute-start.11) | collective-permute-done | bytes 524320 | tf_op jit(solution)/shard_map/ppermute | solution.py:30
  27.0 0.8 constant_dynamic-update-slice_fusion.6
  27.8 0.8 constant_dynamic-update-slice_fusion.5
  28.7 1.0 collective-permute-start.12
  29.6 1.7 %collective-permute-start.13 = (bf16[1024,1024]{1,0:T(8,128)(2,1)}, bf16[1024,1024]{1,0:T(8,128)(2,1)}, u32[]{:S(2)}, u32[]{:S(2)}) collective-permute-start(bf16[1024,1024]{1,0:T(8,128)(2,1)} %constant_dynamic-update-slice_fusion.5), channel_id=1, source_target_pairs={{0,12},{4,0},{8,4},{12,8},{16,28},{20,16},{24,20},{28,24},{32,44},... | collective-permute-start | bytes 6291464 | tf_op jit(solution)/shard_map/ppermute | solution.py:30
  31.3 1.5 %collective-permute-start.3 = (bf16[256,1024]{1,0:T(8,128)(2,1)S(1)}, bf16[256,1024]{1,0:T(8,128)(2,1)}, u32[]{:S(2)}, u32[]{:S(2)}) collective-permute-start(bf16[256,1024]{1,0:T(8,128)(2,1)S(1)} %pad_maximum_fusion.1), channel_id=1, source_target_pairs={{0,48},{4,52},{8,56},{12,60},{16,0},{20,4},{24,8},{28,12},{32,16},... | collective-permute-start | bytes 1572872 | tf_op jit(solution)/shard_map/ppermute | solution.py:30
  33.0 0.7 constant_dynamic-update-slice_fusion.3
  33.7 0.8 constant_dynamic-update-slice_fusion.2
  34.5 4.5 %shard_map.110 = bf16[4096,512]{1,0:T(8,128)(2,1)S(1)} custom-call(s32[16]{0:T(128)S(1)} %stack.67.place, bf16[2048,512]{1,0:T(8,128)(2,1)S(1)} %copy-done, bf16[2048,512]{1,0:T(8,128)(2,1)} %collective-permute-done.4.second), custom_call_target="tpu_custom_call" | custom-call | bytes 8388608 | tf_op jit(solution)/shard_map/pallas_call | solution.py:77
  39.1 6.0 %collective-permute-done.3 = bf16[256,1024]{1,0:T(8,128)(2,1)} collective-permute-done((bf16[256,1024]{1,0:T(8,128)(2,1)S(1)}, bf16[256,1024]{1,0:T(8,128)(2,1)}, u32[]{:S(2)}, u32[]{:S(2)}) %collective-permute-start.3) | collective-permute-done | bytes 524320 | tf_op jit(solution)/shard_map/ppermute | solution.py:30
  45.1 1.1 constant_dynamic-update-slice_fusion.1
  46.2 2.0 %collective-permute-done.5 = bf16[256,1024]{1,0:T(8,128)(2,1)} collective-permute-done((bf16[256,1024]{1,0:T(8,128)(2,1)S(1)}, bf16[256,1024]{1,0:T(8,128)(2,1)}, u32[]{:S(2)}, u32[]{:S(2)}) %collective-permute-start.5) | collective-permute-done | bytes 524320 | tf_op jit(solution)/shard_map/ppermute | solution.py:30
  48.2 1.1 constant_dynamic-update-slice_fusion
  49.3 2.0 %collective-permute-start.7 = (bf16[1024,1024]{1,0:T(8,128)(2,1)S(1)}, bf16[1024,1024]{1,0:T(8,128)(2,1)S(1)}, u32[]{:S(2)}, u32[]{:S(2)}) collective-permute-start(bf16[1024,1024]{1,0:T(8,128)(2,1)S(1)} %constant_dynamic-update-slice_fusion), channel_id=1, source_target_pairs={{0,12},{4,0},{8,4},{12,8},{16,28},{20,16},{24,20},{28,24},{32,44},... | collective-permute-start | bytes 6291464 | tf_op jit(solution)/shard_map/ppermute | solution.py:30
  51.5 4.9 %collective-permute-start.17 = (bf16[1024,512]{1,0:T(8,128)(2,1)S(1)}, bf16[1024,512]{1,0:T(8,128)(2,1)S(1)}, u32[]{:S(2)}, u32[]{:S(2)}) collective-permute-start(bf16[1024,512]{1,0:T(8,128)(2,1)S(1)} %get-tuple-element.54), channel_id=1, source_target_pairs={{0,131},{128,0},{1,128},{129,1},{2,129},{130,2},{3,130},{131,3},{4... | collective-permute-start | bytes 3145736 | tf_op jit(solution)/shard_map/ppermute | solution.py:35
  56.4 2.9 %fusion.17 = f32[1024,512]{1,0:T(8,128)S(1)} fusion(bf16[1024,1024]{1,0:T(8,128)(2,1)} %constant_dynamic-update-slice_fusion.5, bf16[4,1024,512]{2,1,0:T(8,128)(2,1)S(1)} %bitcast.41), kind=kOutput, calls=%fused_computation.22 | convolution fusion | flops 1073741824 | bytes 5242880 | tf_op jit(solution)/shard_map/dot_general | solution.py:55
  59.3 1.8 %collective-permute-done.12 = bf16[1024,1024]{1,0:T(8,128)(2,1)} collective-permute-done((bf16[1024,1024]{1,0:T(8,128)(2,1)}, bf16[1024,1024]{1,0:T(8,128)(2,1)}, u32[]{:S(2)}, u32[]{:S(2)}) %collective-permute-start.12) | collective-permute-done | bytes 2097184 | tf_op jit(solution)/shard_map/ppermute | solution.py:30
  61.1 0.9 collective-permute-start.15
  62.0 2.9 %fusion.15 = f32[1024,512]{1,0:T(8,128)S(1)} fusion(bf16[1024,1024]{1,0:T(8,128)(2,1)} %collective-permute-done.12, bf16[4,1024,512]{2,1,0:T(8,128)(2,1)S(1)} %bitcast.42), kind=kOutput, calls=%fused_computation.20 | convolution fusion | flops 1073741824 | bytes 5242880 | tf_op jit(solution)/shard_map/dot_general | solution.py:55
  64.9 2.9 %add_add_fusion.1 = f32[1024,512]{1,0:T(8,128)S(1)} fusion(f32[1024,512]{1,0:T(8,128)S(1)} %fusion.17, f32[1024,512]{1,0:T(8,128)S(1)} %fusion.15, bf16[1024,1024]{1,0:T(8,128)(2,1)} %collective-permute-done.13, bf16[4,1024,512]{2,1,0:T(8,128)(2,1)S(1)} %bitcast.43), kind=kOutput, calls=%fused_computation.6 | convolution fusion | flops 1074790400 | bytes 9437184 | tf_op jit(solution)/shard_map/dot_general | solution.py:55
  67.8 15.3 %collective-permute-done.7 = bf16[1024,1024]{1,0:T(8,128)(2,1)S(1)} collective-permute-done((bf16[1024,1024]{1,0:T(8,128)(2,1)S(1)}, bf16[1024,1024]{1,0:T(8,128)(2,1)S(1)}, u32[]{:S(2)}, u32[]{:S(2)}) %collective-permute-start.7) | collective-permute-done | bytes 2097184 | tf_op jit(solution)/shard_map/ppermute | solution.py:30
  83.3 2.0 %collective-permute-start.18 = (bf16[2048,512]{1,0:T(8,128)(2,1)S(1)}, bf16[2048,512]{1,0:T(8,128)(2,1)S(1)}, u32[]{:S(2)}, u32[]{:S(2)}) collective-permute-start(bf16[2048,512]{1,0:T(8,128)(2,1)S(1)} %constant_dynamic-update-slice_fusion.10.first), channel_id=1, source_target_pairs={{0,64},{64,0},{1,65},{65,1},{2,66},{66,2},{3,67},{67,3},{4,68},{68... | collective-permute-start | bytes 6291464 | tf_op jit(solution)/shard_map/ppermute | solution.py:39
  85.2 1.1 collective-permute-start.14
  86.7 1.0 collective-permute-done.15
  87.7 1.3 fusion.9
  89.0 6.3 %shard_map.111 = bf16[4096,512]{1,0:T(8,128)(2,1)S(1)} custom-call(s32[16]{0:T(128)S(1)} %stack.67.place, bf16[2048,512]{1,0:T(8,128)(2,1)S(1)} %constant_dynamic-update-slice_fusion.10.first, bf16[2048,512]{1,0:T(8,128)(2,1)S(1)} %collective-permute-done.18.second), custom_call_target="tpu_custom_call" | custom-call | bytes 8388608 | tf_op jit(solution)/shard_map/pallas_call | solution.py:77
  95.4 1.3 fusion.6
  96.6 1.4 add_add_fusion
  98.1 12.4 %collective-permute-done.14 = bf16[1024,1024]{1,0:T(8,128)(2,1)S(1)} collective-permute-done((bf16[1024,1024]{1,0:T(8,128)(2,1)S(1)}, bf16[1024,1024]{1,0:T(8,128)(2,1)S(1)}, u32[]{:S(2)}, u32[]{:S(2)}) %collective-permute-start.14) | collective-permute-done | bytes 2097184 | tf_op jit(solution)/shard_map/ppermute | solution.py:30
  110.4 1.3 fusion.4
  112.7 1.3 fusion.2
  114.7 12.1 %all_to_all.12 = f32[16,1,1024]{2,1,0:T(1,128)S(1)} all-to-all(f32[16,1,1024]{2,1,0:T(1,128)S(1)} %broadcast_in_dim.4), channel_id=1, replica_groups=mesh['zl'=2,'core'=2,'x'=4,'y'=4,'zh'=4] {'x','y'}, dimensions={0} | all-to-all | bytes 131072 | tf_op jit(solution)/shard_map/all_to_all | solution.py:93
  127.5 10.0 %all-to-all-start.1 = ((f32[16,1,640]{2,1,0:T(1,128)}), f32[16,1,640]{2,1,0:T(1,128)S(1)}, u32[]{:S(2)}, u32[]{:S(2)}) async-start(f32[16,1,640]{2,1,0:T(1,128)} %broadcast_in_dim.5), calls=%async_computation.1 | async-start | bytes 81920 | tf_op jit(solution)/shard_map/all_to_all | solution.py:93
  137.5 4.4 %multiply_subtract_fusion.1 = f32[1024,512]{1,0:T(8,128)} fusion(f32[1024,512]{1,0:T(8,128)} %param.11, f32[1024,512]{1,0:T(8,128)S(1)} %get-tuple-element.40, f32[1024,512]{1,0:T(8,128)} %param.9), kind=kLoop, calls=%fused_computation.2 | loop fusion | flops 1572864 | bytes 8388608 | tf_op jit(solution)/shard_map/sub | solution.py:146
  141.9 3.1 %all-to-all-done.1 = f32[16,1,640]{2,1,0:T(1,128)S(1)} async-done(((f32[16,1,640]{2,1,0:T(1,128)}), f32[16,1,640]{2,1,0:T(1,128)S(1)}, u32[]{:S(2)}, u32[]{:S(2)}) %all-to-all-start.1) | async-done | bytes 40992 | tf_op jit(solution)/shard_map/all_to_all | solution.py:93
  146.9 3.9 %multiply_subtract_fusion = (f32[1024,512]{1,0:T(8,128)}, bf16[1024,512]{1,0:T(8,128)(2,1)}) fusion(f32[1024,512]{1,0:T(8,128)} %param.9, f32[1024,512]{1,0:T(8,128)S(1)} %get-tuple-element.40, f32[512]{0:T(512)S(1)} %get-tuple-element.49, f32[1024]{0:T(1024)S(1)} %get-tuple-element.47, bf16[1024,512]{1,0:T(8,128)(2,1)S(1)} %copy-done.2), kind=kLoop, calls=%fused_computation | loop fusion | flops 5242880 | bytes 8394752 | tf_op jit(solution)/shard_map/sub | solution.py:159
  (45 shorter events, 5.8 us)
Async XLA Ops:
  0.6 4.8 %copy-start = (bf16[2048,512]{1,0:T(8,128)(2,1)S(1)}, bf16[2048,512]{1,0:T(8,128)(2,1)}, u32[]{:S(2)}) copy-start(bf16[2048,512]{1,0:T(8,128)(2,1)} %first.1) | copy-start | bytes 6291460
  2.9 13.1 %collective-permute-start = (bf16[256,1024]{1,0:T(8,128)(2,1)S(1)}, bf16[256,1024]{1,0:T(8,128)(2,1)S(1)}, u32[]{:S(2)}, u32[]{:S(2)}) collective-permute-start(bf16[256,1024]{1,0:T(8,128)(2,1)S(1)} %pad_maximum_fusion), channel_id=1, source_target_pairs={{0,128},{128,0},{1,129},{129,1},{2,130},{130,2},{3,131},{131,3},{4... | collective-permute-start | bytes 1572872 | tf_op jit(solution)/shard_map/ppermute | solution.py:39
  5.5 29.1 %collective-permute-start.4 = (bf16[2048,512]{1,0:T(8,128)(2,1)S(1)}, bf16[2048,512]{1,0:T(8,128)(2,1)}, u32[]{:S(2)}, u32[]{:S(2)}) collective-permute-start(bf16[2048,512]{1,0:T(8,128)(2,1)S(1)} %copy-done), channel_id=1, source_target_pairs={{0,64},{64,0},{1,65},{65,1},{2,66},{66,2},{3,67},{67,3},{4,68},{68... | collective-permute-start | bytes 6291464 | tf_op jit(solution)/shard_map/ppermute | solution.py:39
  6.4 4.0 %collective-permute-start.8 = (bf16[128,1024]{1,0:T(8,128)(2,1)S(1)}, bf16[128,1024]{1,0:T(8,128)(2,1)S(1)}, u32[]{:S(2)}, u32[]{:S(2)}) collective-permute-start(bf16[128,1024]{1,0:T(8,128)(2,1)S(1)} %get-tuple-element.56), channel_id=1, source_target_pairs={{0,64},{64,0},{1,65},{65,1},{2,66},{66,2},{3,67},{67,3},{4,68},{68... | collective-permute-start | bytes 786440 | tf_op jit(solution)/shard_map/ppermute | solution.py:39
  10.5 11.2 %collective-permute-start.9 = (bf16[256,1024]{1,0:T(8,128)(2,1)S(1)}, bf16[256,1024]{1,0:T(8,128)(2,1)S(1)}, u32[]{:S(2)}, u32[]{:S(2)}) collective-permute-start(bf16[256,1024]{1,0:T(8,128)(2,1)S(1)} %pad_maximum_fusion.2), channel_id=1, source_target_pairs={{0,16},{4,20},{8,24},{12,28},{16,32},{20,36},{24,40},{28,44},{32,4... | collective-permute-start | bytes 1572872 | tf_op jit(solution)/shard_map/ppermute | solution.py:30
  11.9 15.1 %collective-permute-start.10 = (bf16[256,1024]{1,0:T(8,128)(2,1)S(1)}, bf16[256,1024]{1,0:T(8,128)(2,1)S(1)}, u32[]{:S(2)}, u32[]{:S(2)}) collective-permute-start(bf16[256,1024]{1,0:T(8,128)(2,1)S(1)} %pad_maximum_fusion.2), channel_id=1, source_target_pairs={{0,48},{4,52},{8,56},{12,60},{16,0},{20,4},{24,8},{28,12},{32,16},... | collective-permute-start | bytes 1572872 | tf_op jit(solution)/shard_map/ppermute | solution.py:30
  13.4 13.6 %collective-permute-start.11 = (bf16[256,1024]{1,0:T(8,128)(2,1)S(1)}, bf16[256,1024]{1,0:T(8,128)(2,1)S(1)}, u32[]{:S(2)}, u32[]{:S(2)}) collective-permute-start(bf16[256,1024]{1,0:T(8,128)(2,1)S(1)} %pad_maximum_fusion.2), channel_id=1, source_target_pairs={{0,32},{4,36},{8,40},{12,44},{16,48},{20,52},{24,56},{28,60},{32,0... | collective-permute-start | bytes 1572872 | tf_op jit(solution)/shard_map/ppermute | solution.py:30
  16.8 3.5 %collective-permute-start.1 = (bf16[128,1024]{1,0:T(8,128)(2,1)S(1)}, bf16[128,1024]{1,0:T(8,128)(2,1)S(1)}, u32[]{:S(2)}, u32[]{:S(2)}) collective-permute-start(bf16[128,1024]{1,0:T(8,128)(2,1)S(1)} %get-tuple-element.63), channel_id=1, source_target_pairs={{0,64},{64,0},{1,65},{65,1},{2,66},{66,2},{3,67},{67,3},{4,68},{68... | collective-permute-start | bytes 786440 | tf_op jit(solution)/shard_map/ppermute | solution.py:39
  20.3 12.6 %collective-permute-start.2 = (bf16[256,1024]{1,0:T(8,128)(2,1)S(1)}, bf16[256,1024]{1,0:T(8,128)(2,1)S(1)}, u32[]{:S(2)}, u32[]{:S(2)}) collective-permute-start(bf16[256,1024]{1,0:T(8,128)(2,1)S(1)} %pad_maximum_fusion.1), channel_id=1, source_target_pairs={{0,16},{4,20},{8,24},{12,28},{16,32},{20,36},{24,40},{28,44},{32,4... | collective-permute-start | bytes 1572872 | tf_op jit(solution)/shard_map/ppermute | solution.py:30
  28.7 32.4 %collective-permute-start.12 = (bf16[1024,1024]{1,0:T(8,128)(2,1)}, bf16[1024,1024]{1,0:T(8,128)(2,1)}, u32[]{:S(2)}, u32[]{:S(2)}) collective-permute-start(bf16[1024,1024]{1,0:T(8,128)(2,1)} %constant_dynamic-update-slice_fusion.5), channel_id=1, source_target_pairs={{0,4},{4,8},{8,12},{12,0},{16,20},{20,24},{24,28},{28,16},{32,36},... | collective-permute-start | bytes 6291464 | tf_op jit(solution)/shard_map/ppermute | solution.py:30
  29.6 31.5 %collective-permute-start.13 = (bf16[1024,1024]{1,0:T(8,128)(2,1)}, bf16[1024,1024]{1,0:T(8,128)(2,1)}, u32[]{:S(2)}, u32[]{:S(2)}) collective-permute-start(bf16[1024,1024]{1,0:T(8,128)(2,1)} %constant_dynamic-update-slice_fusion.5), channel_id=1, source_target_pairs={{0,12},{4,0},{8,4},{12,8},{16,28},{20,16},{24,20},{28,24},{32,44},... | collective-permute-start | bytes 6291464 | tf_op jit(solution)/shard_map/ppermute | solution.py:30
  31.3 13.8 %collective-permute-start.3 = (bf16[256,1024]{1,0:T(8,128)(2,1)S(1)}, bf16[256,1024]{1,0:T(8,128)(2,1)}, u32[]{:S(2)}, u32[]{:S(2)}) collective-permute-start(bf16[256,1024]{1,0:T(8,128)(2,1)S(1)} %pad_maximum_fusion.1), channel_id=1, source_target_pairs={{0,48},{4,52},{8,56},{12,60},{16,0},{20,4},{24,8},{28,12},{32,16},... | collective-permute-start | bytes 1572872 | tf_op jit(solution)/shard_map/ppermute | solution.py:30
  32.9 15.3 %collective-permute-start.5 = (bf16[256,1024]{1,0:T(8,128)(2,1)S(1)}, bf16[256,1024]{1,0:T(8,128)(2,1)}, u32[]{:S(2)}, u32[]{:S(2)}) collective-permute-start(bf16[256,1024]{1,0:T(8,128)(2,1)S(1)} %collective-permute-done.2), channel_id=1, source_target_pairs={{0,16},{4,20},{8,24},{12,28},{16,32},{20,36},{24,40},{28,44},{32,4... | collective-permute-start | bytes 1572872 | tf_op jit(solution)/shard_map/ppermute | solution.py:30
  34.5 10.6 %copy-start.1 = (bf16[1024,1024]{1,0:T(8,128)(2,1)S(1)}, bf16[1024,1024]{1,0:T(8,128)(2,1)}, u32[]{:S(2)}) copy-start(bf16[1024,1024]{1,0:T(8,128)(2,1)} %constant_dynamic-update-slice_fusion.2) | copy-start | bytes 6291460
  49.3 33.8 %collective-permute-start.7 = (bf16[1024,1024]{1,0:T(8,128)(2,1)S(1)}, bf16[1024,1024]{1,0:T(8,128)(2,1)S(1)}, u32[]{:S(2)}, u32[]{:S(2)}) collective-permute-start(bf16[1024,1024]{1,0:T(8,128)(2,1)S(1)} %constant_dynamic-update-slice_fusion), channel_id=1, source_target_pairs={{0,12},{4,0},{8,4},{12,8},{16,28},{20,16},{24,20},{28,24},{32,44},... | collective-permute-start | bytes 6291464 | tf_op jit(solution)/shard_map/ppermute | solution.py:30
  51.4 31.7 %collective-permute-start.16 = (bf16[1024,512]{1,0:T(8,128)(2,1)S(1)}, bf16[1024,512]{1,0:T(8,128)(2,1)S(1)}, u32[]{:S(2)}, u32[]{:S(2)}) collective-permute-start(bf16[1024,512]{1,0:T(8,128)(2,1)S(1)} %get-tuple-element.55), channel_id=1, source_target_pairs={{0,128},{128,1},{1,129},{129,2},{2,130},{130,3},{3,131},{131,0},{4... | collective-permute-start | bytes 3145736 | tf_op jit(solution)/shard_map/ppermute | solution.py:35
  51.5 31.7 %collective-permute-start.17 = (bf16[1024,512]{1,0:T(8,128)(2,1)S(1)}, bf16[1024,512]{1,0:T(8,128)(2,1)S(1)}, u32[]{:S(2)}, u32[]{:S(2)}) collective-permute-start(bf16[1024,512]{1,0:T(8,128)(2,1)S(1)} %get-tuple-element.54), channel_id=1, source_target_pairs={{0,131},{128,0},{1,128},{129,1},{2,129},{130,2},{3,130},{131,3},{4... | collective-permute-start | bytes 3145736 | tf_op jit(solution)/shard_map/ppermute | solution.py:35
  61.1 26.6 %collective-permute-start.15 = (bf16[1024,1024]{1,0:T(8,128)(2,1)}, bf16[1024,1024]{1,0:T(8,128)(2,1)S(1)}, u32[]{:S(2)}, u32[]{:S(2)}) collective-permute-start(bf16[1024,1024]{1,0:T(8,128)(2,1)} %collective-permute-done.12), channel_id=1, source_target_pairs={{0,4},{4,8},{8,12},{12,0},{16,20},{20,24},{24,28},{28,16},{32,36},... | collective-permute-start | bytes 6291464 | tf_op jit(solution)/shard_map/ppermute | solution.py:30
  83.3 5.8 %collective-permute-start.18 = (bf16[2048,512]{1,0:T(8,128)(2,1)S(1)}, bf16[2048,512]{1,0:T(8,128)(2,1)S(1)}, u32[]{:S(2)}, u32[]{:S(2)}) collective-permute-start(bf16[2048,512]{1,0:T(8,128)(2,1)S(1)} %constant_dynamic-update-slice_fusion.10.first), channel_id=1, source_target_pairs={{0,64},{64,0},{1,65},{65,1},{2,66},{66,2},{3,67},{67,3},{4,68},{68... | collective-permute-start | bytes 6291464 | tf_op jit(solution)/shard_map/ppermute | solution.py:39
  85.2 25.2 %collective-permute-start.14 = (bf16[1024,1024]{1,0:T(8,128)(2,1)S(1)}, bf16[1024,1024]{1,0:T(8,128)(2,1)S(1)}, u32[]{:S(2)}, u32[]{:S(2)}) collective-permute-start(bf16[1024,1024]{1,0:T(8,128)(2,1)S(1)} %collective-permute-done.7), channel_id=1, source_target_pairs={{0,12},{4,0},{8,4},{12,8},{16,28},{20,16},{24,20},{28,24},{32,44},... | collective-permute-start | bytes 6291464 | tf_op jit(solution)/shard_map/ppermute | solution.py:30
  86.4 26.4 %collective-permute-start.6 = (bf16[1024,1024]{1,0:T(8,128)(2,1)S(1)}, bf16[1024,1024]{1,0:T(8,128)(2,1)S(1)}, u32[]{:S(2)}, u32[]{:S(2)}) collective-permute-start(bf16[1024,1024]{1,0:T(8,128)(2,1)S(1)} %constant_dynamic-update-slice_fusion), channel_id=1, source_target_pairs={{0,4},{4,8},{8,12},{12,0},{16,20},{20,24},{24,28},{28,16},{32,36},... | collective-permute-start | bytes 6291464 | tf_op jit(solution)/shard_map/ppermute | solution.py:30
  114.0 12.8 %copy-start.4 = (f32[1024]{0:T(1024)S(1)}, f32[1024]{0:T(1024)}, u32[]{:S(2)}) copy-start(f32[1024]{0:T(1024)} %param.12) | copy-start | bytes 12292
  126.9 15.0 %copy-start.3 = (f32[1024]{0:T(1024)}, f32[1024]{0:T(1024)S(1)}, u32[]{:S(2)}) copy-start(f32[1024]{0:T(1024)S(1)} %get-tuple-element.48) | copy-start | bytes 12292
  127.5 17.5 %all-to-all-start.1 = ((f32[16,1,640]{2,1,0:T(1,128)}), f32[16,1,640]{2,1,0:T(1,128)S(1)}, u32[]{:S(2)}, u32[]{:S(2)}) async-start(f32[16,1,640]{2,1,0:T(1,128)} %broadcast_in_dim.5), calls=%async_computation.1 | async-start | bytes 81920 | tf_op jit(solution)/shard_map/all_to_all | solution.py:93
  137.5 8.8 %copy-start.5 = (f32[512]{0:T(512)S(1)}, f32[512]{0:T(512)}, u32[]{:S(2)}) copy-start(f32[512]{0:T(512)} %param.13) | copy-start | bytes 6148
  137.5 9.4 %copy-start.2 = (bf16[1024,512]{1,0:T(8,128)(2,1)S(1)}, bf16[1024,512]{1,0:T(8,128)(2,1)}, u32[]{:S(2)}) copy-start(bf16[1024,512]{1,0:T(8,128)(2,1)} %param.10) | copy-start | bytes 3145732
